TPU v7x, 32 devices: a whole 2x2x4 slice. The times are simulated.
32 devices in a mesh: groups: 2 (over y), latent: 8 (over z, x), dp: 2 (over core).
Axes of the slice: x: 2, y: 2, z: 4, core: 2. Of those that a mesh axis runs over, the one named last changes fastest.
Arguments:
- acts: bfloat16 [128, 1792], P(('groups', 'latent', 'dp')), parts along dimension 0, may hold values from -6 to 6
- w_enc: bfloat16 [3584, 65536], P(('groups', 'dp'), 'latent'), parts along dimension 0, may hold values from -0.125 to 0.125
- b_enc: float32 [131072], P(('groups', 'latent')), parts along dimension 0, may hold values from -1.5 to -0.5
- w_dec: bfloat16 [131072, 1792], P(('groups', 'latent'), 'dp'), parts along dimension 0, may hold values from -0.0625 to 0.0625
- dec_m: bfloat16 [131072, 1792], P(('groups', 'latent'), 'dp'), parts along dimension 0, may hold values from -0.03125 to 0.03125
- dec_v: bfloat16 [131072, 1792], P(('groups', 'latent'), 'dp'), parts along dimension 0, may hold values from 9.9651515e-08 to 9.983778e-07
Outputs:
- dec_step: bfloat16 [131072, 1792], P(('groups', 'latent'), 'dp'), parts along dimension 0
There are 2 independent parts, one for each index of `groups`. A program takes and returns all parts, laid end to end along the dimension named above; each array names one. Nothing has to cross between parts.
All inputs are finite; a program needn't handle non-finite values.
Results may differ from a plain program's by a relative error of at most 0.0072.
Values may be sent and summed in bfloat16 or wider, within the bound.
No kernel may reach another device: no remote copies, remote signals or barrier semaphores. Data moves between devices by JAX's collectives and lax.ppermute only.
A program may use at most 256 MiB of HBM per device.

v0:
```python
import jax
import jax.numpy as jnp
from jax import lax
from jax.sharding import PartitionSpec as P


def partner(value, axis, stride):
    return lax.ppermute(value, axis, [(i, i ^ 1 << stride) for i in range(lax.axis_size(axis))])


def adam_step(grad, dec_m, dec_v):
    moment1 = 0.9 * dec_m.astype(jnp.float32) + 0.1 * grad
    moment2 = 0.999 * dec_v.astype(jnp.float32) + 0.001 * grad * grad
    first = moment1 / (1.0 - 0.9**10)
    second = moment2 / (1.0 - 0.999**10)
    return (first / (jnp.sqrt(second) + 1e-08)).astype(jnp.bfloat16)


def per_device(acts, w_enc, b_enc, w_dec, dec_m, dec_v):
    half = w_enc.shape[0]
    side = lax.axis_index("dp")
    contract = (((0,), (0,)), ((), ()))
    rows_all = lax.all_gather(acts, "latent", axis=0, tiled=True)
    pre = jnp.dot(
        rows_all,
        lax.all_gather(w_enc, "dp", axis=0, tiled=True),
        preferred_element_type=jnp.float32,
    )
    codes = jnp.maximum(pre + b_enc, 0.0).astype(jnp.bfloat16)
    dec_full = lax.all_gather(w_dec, "dp", axis=1, tiled=True)
    recon = lax.psum(jnp.dot(codes, dec_full, preferred_element_type=jnp.float32), "latent")
    error = (recon - rows_all.astype(jnp.float32)).astype(jnp.bfloat16)
    mine_err = lax.dynamic_slice_in_dim(error, side * half, half, 1)
    send_err = lax.dynamic_slice_in_dim(error, (1 - side) * half, half, 1)
    other_codes, other_err = partner((codes, send_err), "dp", 0)
    total_rows = rows_all.shape[0] * lax.axis_size("dp")
    grad = (
        lax.dot_general(codes, mine_err, contract, preferred_element_type=jnp.float32)
        + lax.dot_general(other_codes, other_err, contract, preferred_element_type=jnp.float32)
    ) / total_rows
    return adam_step(grad, dec_m, dec_v)


def solution(mesh):
    in_specs = (
        P(("groups", "latent", "dp"), None),
        P(("groups", "dp"), "latent"),
        P(("groups", "latent")),
        P(("groups", "latent"), "dp"),
        P(("groups", "latent"), "dp"),
        P(("groups", "latent"), "dp"),
    )
    out_specs = P(("groups", "latent"), "dp")
    return jax.shard_map(
        per_device, mesh=mesh, in_specs=in_specs, out_specs=out_specs, check_vma=False
    )
```

profile of v0, /device:TPU:0, one launch (start us, length us, event | category | flops | bytes accessed | tf_op | source)
XLA Modules:
  0.0 243.3 jit_solution(11341962302935147512)
XLA Ops:
  6.5 0.0 copy-start.1
  6.5 0.0 copy-start
  6.5 0.0 all-gather.4.cloned.1.call-start
  6.5 0.7 all-gather.4.cloned.1.call-update
  7.3 0.0 all-gather.6.cloned.1.call-start
  7.3 0.7 all-gather.6.cloned.1.call-update
  8.0 0.0 all-reduce.2.cloned.1.call-start
  8.1 0.0 copy-done.1
  8.1 32.4 %all-gather = bf16[8,4,1792]{2,1,0:T(4,128)(2,1)S(1)} all-gather(bf16[1,4,1792]{2,1,0:T(4,128)(2,1)S(1)} %bitcast.8), channel_id=1, replica_groups=mesh['groups'=2,'latent'=8,'dp'=2] {'latent'}, dimensions={0}, use_global_device_ids=true | all-gather | bytes 129024 | tf_op jit(solution)/shard_map/all_gather | solution.py:23
  40.5 18.0 %all-gather.4.cloned.1.call-done = bf16[1792,8192]{1,0:T(8,128)(2,1)} async-done(((bf16[896,8192]{1,0:T(8,128)(2,1)}), bf16[1792,8192]{1,0:T(8,128)(2,1)}) %all-gather.4.cloned.1.call-update) | async-done | bytes 29360144 | tf_op jit(solution)/shard_map/all_gather | solution.py:26
  58.5 0.0 copy-done
  58.5 12.7 %fusion.1 = bf16[32,8192]{1,0:T(8,128)(2,1)S(1)} fusion(bf16[32,1792]{1,0:T(8,128)(2,1)S(1)} %reshape.2, bf16[1792,8192]{1,0:T(8,128)(2,1)} %all-gather.4.cloned.1.call-done, f32[8192]{0:T(1024)S(1)} %copy-done), kind=kOutput, calls=%fused_computation.3 | convolution fusion | flops 940310528 | bytes 30031872 | tf_op jit(solution)/shard_map/dot_general | solution.py:24
  71.2 36.8 %all-gather.6.cloned.1.call-done = bf16[8192,1792]{1,0:T(8,128)(2,1)} async-done(((bf16[8192,896]{1,0:T(8,128)(2,1)}), bf16[8192,1792]{1,0:T(8,128)(2,1)}) %all-gather.6.cloned.1.call-update) | async-done | bytes 29360144 | tf_op jit(solution)/shard_map/all_gather | solution.py:30
  108.1 12.6 %fusion.5 = f32[32,1792]{1,0:T(8,128)} fusion(bf16[32,8192]{1,0:T(8,128)(2,1)S(1)} %fusion.1, bf16[8192,1792]{1,0:T(8,128)(2,1)} %all-gather.6.cloned.1.call-done), kind=kOutput, calls=%fused_computation.9 | convolution fusion | flops 939524096 | bytes 30113792 | tf_op jit(solution)/shard_map/dot_general | solution.py:31
  120.6 0.0 all-reduce.2.cloned.1.call-update
  120.7 0.3 collective-permute-start
  121.0 71.4 %all-reduce.2.cloned.1.call-done = f32[32,1792]{1,0:T(8,128)} async-done(((f32[32,1792]{1,0:T(8,128)}), f32[32,1792]{1,0:T(8,128)}) %all-reduce.2.cloned.1.call-update) | async-done | bytes 229392 | tf_op jit(solution)/shard_map/psum | solution.py:31
  192.4 1.0 subtract_convert_fusion
  193.4 0.1 collective-permute-start.1
  193.5 11.7 %fusion.2 = f32[8192,896]{1,0:T(8,128)} fusion(bf16[32,8192]{1,0:T(8,128)(2,1)S(1)} %fusion.1, bf16[32,1792]{1,0:T(8,128)(2,1)S(1)} %subtract_convert_fusion, s32[]{:T(128)S(6)} %select_n.6), kind=kOutput, calls=%fused_computation.5 | convolution fusion | flops 469762048 | bytes 29941764 | tf_op jit(solution)/shard_map/dot_general | solution.py:38
  205.1 0.0 collective-permute-done.1
  205.1 0.0 collective-permute-done
  205.1 31.7 %divide_convert_fusion = bf16[8192,896]{1,0:T(8,128)(2,1)} fusion(bf16[8192,896]{1,0:T(8,128)(2,1)} %param.11, f32[8192,896]{1,0:T(8,128)} %fusion.2, bf16[8192,896]{1,0:T(8,128)(2,1)} %param.10, bf16[32,8192]{1,0:T(8,128)(2,1)S(1)} %collective-permute-done, bf16[32,896]{1,0:T(8,128)(2,1)S(1)} %collective-permute-done.1), kind=kOutput, calls=%fused_computation | convolution fusion | flops 587202560 | bytes 73981952 | tf_op jit(solution)/shard_map/dot_general | solution.py:39
  (2 shorter events, 0.0 us)
Async XLA Ops:
  6.5 1.5 copy-start.1
  6.5 52.0 %copy-start = (f32[8192]{0:T(1024)S(1)}, f32[8192]{0:T(1024)}, u32[]{:S(2)}) copy-start(f32[8192]{0:T(1024)} %param.8) | copy-start | bytes 98308
  6.5 51.9 %all-gather.4.cloned.1.call-start = ((), (), s32[]{:S(2)}) async-start(), calls=%async_computation | async-start | bytes 44040192 | tf_op jit(solution)/shard_map/all_gather | solution.py:26
  7.3 100.8 %all-gather.6.cloned.1.call-start = ((), (), s32[]{:S(2)}) async-start(), calls=%async_computation.1 | async-start | bytes 44040192 | tf_op jit(solution)/shard_map/all_gather | solution.py:30
  8.0 184.4 %all-reduce.2.cloned.1.call-start = ((), (), s32[]{:S(2)}) async-start(), calls=%async_computation.2 | async-start | bytes 458752 | tf_op jit(solution)/shard_map/psum | solution.py:31
  120.7 84.5 %collective-permute-start = (bf16[32,8192]{1,0:T(8,128)(2,1)S(1)}, bf16[32,8192]{1,0:T(8,128)(2,1)S(1)}, u32[]{:S(2)}, u32[]{:S(2)}) collective-permute-start(bf16[32,8192]{1,0:T(8,128)(2,1)S(1)} %fusion.1), channel_id=1, source_target_pairs={{0,1},{1,0},{2,3},{3,2},{4,5},{5,4},{6,7},{7,6},{8,9},{9,8},{10,11... | collective-permute-start | bytes 1572872 | tf_op jit(solution)/shard_map/ppermute | solution.py:8
  193.4 11.8 %collective-permute-start.1 = (bf16[32,896]{1,0:T(8,128)(2,1)S(1)}, bf16[32,896]{1,0:T(8,128)(2,1)S(1)}, u32[]{:S(2)}, u32[]{:S(2)}) collective-permute-start(bf16[32,896]{1,0:T(8,128)(2,1)S(1)} %constant_dynamic-slice_fusion), channel_id=1, source_target_pairs={{0,1},{1,0},{2,3},{3,2},{4,5},{5,4},{6,7},{7,6},{8,9},{9,8},{10,11... | collective-permute-start | bytes 172040 | tf_op jit(solution)/shard_map/ppermute | solution.py:8
Sparse Core Ops, SparseCore 0:
  8.9 49.5 all-gather.3
  60.0 47.9 all-gather.5
  120.8 71.5 all-reduce.1
where the time goes:
time: 244 us; the launch traced here: 243 us
  waiting for transfers between devices  128 us (52%)
  matrix products  68.7 us (28%)
  blocking collectives  32.4 us (13%)
  between operations  13.2 us (5%)
    psum x1, waiting for transfers between devices, per_device(): lax.psum(jnp.dot(codes, dec_full, preferred_element_type=jnp.float32), 'l...  71.4 us
    all_gather x1, waiting for transfers between devices, per_device(): dec_full = lax.all_gather(w_dec, 'dp', axis=1, tiled=True)  36.8 us
    all_gather x1, blocking collectives, per_device(): rows_all = lax.all_gather(acts, 'latent', axis=0, tiled=True)  32.4 us
    dot_general x1, matrix products, per_device(): lax.dot_general(other_codes, other_err, contract, preferred_element_type=...  31.7 us
    all_gather x1, waiting for transfers between devices, per_device(): lax.all_gather(w_enc, 'dp', axis=0, tiled=True)  18 us
    dot_general x1, matrix products, per_device(): jnp.dot(rows_all, lax.all_gather(w_enc, 'dp', axis=0, tiled=True), prefer...  12.7 us
    dot_general x1, matrix products, per_device(): jnp.dot(codes, dec_full, preferred_element_type=jnp.float32)  12.6 us
    dot_general x1, matrix products, per_device(): lax.dot_general(codes, mine_err, contract, preferred_element_type=jnp.flo...  11.7 us
  transfers between devices with their start and end apart: 5, of which 3 were waited for; matrix products, arithmetic and copies ran while one was open for 10% of the time, Pallas kernels for 0%

commit v1 on v0

v1 whole, which is shorter than its diff:
```python
import functools

import jax
import jax.numpy as jnp
from jax import lax
from jax.experimental import pallas as pl
from jax.experimental.pallas import tpu as pltpu
from jax.sharding import PartitionSpec as P

MIB = 1 << 20
WHOLE = pl.BlockSpec(memory_space=pltpu.VMEM)
DIRECT = 8


def swap(value, axis, mask):
    n = lax.axis_size(axis)
    return lax.ppermute(value, axis, [(i, i ^ mask) for i in range(n)])


def params(mib):
    return pltpu.CompilerParams(vmem_limit_bytes=mib * MIB)


def resident(value):
    return pltpu.with_memory_space_constraint(value, pltpu.VMEM)


def pair_kernel(mine, theirs, out):
    half = out.shape[1]
    rows = mine.shape[0]
    side = lax.axis_index("dp")

    def write(first, second, at):
        both = [first[:, at : at + half], second[:, at : at + half]]
        out[...] = jnp.concatenate([b.astype(jnp.float32) for b in both]).astype(out.dtype)

    @pl.when(side == 0)
    def _():
        write(mine, theirs, 0)

    @pl.when(side == 1)
    def _():
        write(theirs, mine, half)


def pair_rows(acts):
    theirs = swap(acts, "dp", 1)
    return pl.pallas_call(
        pair_kernel,
        out_shape=jax.ShapeDtypeStruct((2 * acts.shape[0], acts.shape[1] // 2), acts.dtype),
        in_specs=[WHOLE, WHOLE],
        out_specs=WHOLE,
        compiler_params=params(4),
    )(acts, theirs)


def spread(block):
    n = lax.axis_size("latent")
    if n > DIRECT:
        return [lax.all_gather(block, "latent", axis=0, tiled=True)]
    return [block] + [swap(block, "latent", j) for j in range(1, n)]


def stack(refs):
    if len(refs) == 1:
        return refs[0][...]
    return jnp.concatenate([r[...].astype(jnp.float32) for r in refs]).astype(refs[0].dtype)


def encode_kernel(chunk, *refs):
    *rows_refs, w, out = refs
    rows = stack(rows_refs)

    @pl.loop(0, out.shape[1] // chunk)
    def _(i):
        at = pl.ds(pl.multiple_of(i * chunk, chunk), chunk)
        out[:, at] = jnp.dot(rows, w[:, at], preferred_element_type=jnp.float32)


def encode(blocks, w_enc):
    tokens = sum(b.shape[0] for b in blocks)
    lat = w_enc.shape[1]
    return pl.pallas_call(
        functools.partial(encode_kernel, min(512, lat)),
        out_shape=jax.ShapeDtypeStruct((tokens, lat), jnp.float32),
        in_specs=[WHOLE] * (len(blocks) + 1),
        out_specs=WHOLE,
        compiler_params=params(8),
    )(*blocks, resident(w_enc))


def decode_kernel(chunk, mine, theirs, bias, w, codes, *out):
    tokens, lat = mine.shape
    total = jnp.zeros((tokens, w.shape[1]), jnp.float32)

    def step(i, total):
        at = pl.ds(pl.multiple_of(i * chunk, chunk), chunk)
        pre = mine[:, at] + theirs[:, at] + bias[:, at]
        block = jnp.maximum(pre, 0.0).astype(jnp.bfloat16)
        codes[:, at] = block
        return total + jnp.dot(block, w[at, :], preferred_element_type=jnp.float32)

    total = lax.fori_loop(0, lat // chunk, step, total)
    rows = out[0].shape[0]
    for j, ref in enumerate(out):
        ref[...] = total[j * rows : (j + 1) * rows]


def decode(mine, theirs, bias, w_dec, parts):
    tokens, lat = mine.shape
    half = w_dec.shape[1]
    codes, *sums = pl.pallas_call(
        functools.partial(decode_kernel, min(512, lat)),
        out_shape=[jax.ShapeDtypeStruct((tokens, lat), jnp.bfloat16)]
        + [jax.ShapeDtypeStruct((tokens // parts, half), jnp.float32)] * parts,
        in_specs=[WHOLE] * 4,
        out_specs=[WHOLE] * (1 + parts),
        compiler_params=params(8),
    )(mine, theirs, bias.reshape(1, lat), resident(w_dec))
    return codes, sums


def error_kernel(*refs):
    *sums, rows, out = refs
    total = sums[0][...]
    for ref in sums[1:]:
        total = total + ref[...]
    out[...] = (total - rows[...].astype(jnp.float32)).astype(out.dtype)


def own_error(sums, rows):
    return pl.pallas_call(
        error_kernel,
        out_shape=jax.ShapeDtypeStruct(rows.shape, rows.dtype),
        in_specs=[WHOLE] * (len(sums) + 1),
        out_specs=WHOLE,
        compiler_params=params(4),
    )(*sums, rows)


def reduce_rows(sums):
    n = lax.axis_size("latent")
    if n > DIRECT:
        return [lax.psum_scatter(sums[0], "latent", scatter_dimension=0, tiled=True)]
    return [sums[0]] + [swap(sums[j], "latent", j) for j in range(1, n)]


def adam_kernel(total_rows, codes, m, v, *refs):
    *err_refs, out = refs
    err = stack(err_refs)
    grad = lax.dot_general(
        codes[...], err, (((0,), (0,)), ((), ())), preferred_element_type=jnp.float32
    ) / total_rows
    moment1 = 0.9 * m[...].astype(jnp.float32) + 0.1 * grad
    moment2 = 0.999 * v[...].astype(jnp.float32) + 0.001 * grad * grad
    first = moment1 / (1.0 - 0.9**10)
    second = moment2 / (1.0 - 0.999**10)
    out[...] = (first / (jnp.sqrt(second) + 1e-8)).astype(out.dtype)


def adam(codes, m, v, errs):
    tokens, lat = codes.shape
    half = m.shape[1]
    rows = min(256, lat)
    slab = pl.BlockSpec((rows, half), lambda i: (i, 0))
    return pl.pallas_call(
        functools.partial(adam_kernel, tokens),
        grid=(lat // rows,),
        out_shape=jax.ShapeDtypeStruct(m.shape, jnp.bfloat16),
        in_specs=[pl.BlockSpec((tokens, rows), lambda i: (0, i)), slab, slab] + [WHOLE] * len(errs),
        out_specs=slab,
        compiler_params=params(16),
    )(codes, m, v, *errs)


def per_device(acts, w_enc, b_enc, w_dec, dec_m, dec_v):
    own = pair_rows(acts)
    blocks = spread(own)
    mine = encode(blocks, w_enc)
    theirs = swap(mine, "dp", 1)
    codes, sums = decode(mine, theirs, b_enc, w_dec, len(blocks))
    err = own_error(reduce_rows(sums), own)
    return adam(codes, dec_m, dec_v, spread(err))


def solution(mesh):
    in_specs = (
        P(("groups", "latent", "dp"), None),
        P(("groups", "dp"), "latent"),
        P(("groups", "latent")),
        P(("groups", "latent"), "dp"),
        P(("groups", "latent"), "dp"),
        P(("groups", "latent"), "dp"),
    )
    out_specs = P(("groups", "latent"), "dp")
    return jax.shard_map(
        per_device, mesh=mesh, in_specs=in_specs, out_specs=out_specs, check_vma=False
    )
```

time: 244 us -> 102 us (0.42)
  waiting for transfers between devices: 128 us -> 17.1 us
  matrix products: 68.7 us -> 0 us
  Pallas kernels: 0 us -> 38.5 us
  starting transfers between devices: 0.43 us -> 35.3 us
  blocking collectives: 32.4 us -> 0 us
  between operations: 13.2 us -> 0.06 us
  local copies, waits for them, and re-layouts: 0.05 us -> 11.1 us
    psum x1 -> x0, waiting for transfers between devices: 71.4 us -> none  [per_device(): lax.psum(jnp.dot(codes, dec_full, preferred_element_type=jnp.float32), 'l...]
    dot_general x4 -> x0, matrix products: 68.7 us -> none  [the longest x1 31.7 us: per_device(): lax.dot_general(other_codes, other_err, contract, preferred_element_type=...]
    all_gather x2 -> x0, waiting for transfers between devices: 54.8 us -> none  [the longest x1 36.8 us: per_device(): dec_full = lax.all_gather(w_dec, 'dp', axis=1, tiled=True)]
    pallas_call x0 -> x5, Pallas kernels: none -> 38.5 us  [the longest x1 29.2 us: adam(): pl.pallas_call(functools.partial(adam_kernel, tokens), grid=(lat // rows,...]
    ppermute x2 -> x23, starting transfers between devices: 0.35 us -> 35.3 us  [swap(): return lax.ppermute(value, axis, [(i, i ^ mask) for i in range(n)])]
    all_gather x1 -> x0, blocking collectives: 32.4 us -> none  [per_device(): rows_all = lax.all_gather(acts, 'latent', axis=0, tiled=True)]
    ppermute x2 -> x23, waiting for transfers between devices: 0.01 us -> 17.1 us  [swap(): return lax.ppermute(value, axis, [(i, i ^ mask) for i in range(n)])]
    unnamed x5 -> x12, local copies, waits for them, and re-layouts: 0.04 us -> 11.1 us
  transfers between devices with their start and end apart: 5 -> 23, of which waited for: 3 -> 11; matrix products, arithmetic and copies ran while one was open for 10% -> 0% of each run, Pallas kernels for 0% -> 0%
where the time goes in v1:
time: 102 us
  Pallas kernels  38.5 us (38%)
  starting transfers between devices  35.3 us (35%)
  waiting for transfers between devices  17.1 us (17%)
  local copies, waits for them, and re-layouts  11.1 us (11%)
    ppermute x23, starting transfers between devices, swap(): return lax.ppermute(value, axis, [(i, i ^ mask) for i in range(n)])  35.3 us
    pallas_call x1, Pallas kernels, adam(): pl.pallas_call(functools.partial(adam_kernel, tokens), grid=(lat // rows,...  29.2 us
    ppermute x23, waiting for transfers between devices, swap(): return lax.ppermute(value, axis, [(i, i ^ mask) for i in range(n)])  17.1 us
    unnamed x12, local copies, waits for them, and re-layouts  11.1 us
    pallas_call x1, Pallas kernels, decode(): pl.pallas_call(functools.partial(decode_kernel, min(512, lat)), out_shape...  4.73 us
    pallas_call x1, Pallas kernels, encode(): pl.pallas_call(functools.partial(encode_kernel, min(512, lat)), out_shape...  4.53 us
  transfers between devices with their start and end apart: 23, of which 11 were waited for; matrix products, arithmetic and copies ran while one was open for 0% of the time, Pallas kernels for 0%

profile of v1, /device:TPU:0, one launch (start us, length us, event | category | flops | bytes accessed | tf_op | source)
XLA Modules:
  0.0 102.0 jit_solution(2037688097937290256)
XLA Ops:
  0.5 1.0 %collective-permute-done.theirs = bf16[4,1792]{1,0:T(4,128)(2,1)S(1)} collective-permute-done((bf16[4,1792]{1,0:T(4,128)(2,1)}, bf16[4,1792]{1,0:T(4,128)(2,1)S(1)}, u32[]{:S(2)}, u32[]{:S(2)}) %collective-permute-start) | collective-permute-done | bytes 14368 | tf_op jit(solution)/shard_map/ppermute | solution.py:17
  1.5 0.7 copy-done.5
  2.2 5.9 %collective-permute-start.7 = (bf16[8,896]{1,0:T(8,128)(2,1)S(1)}, bf16[8,896]{1,0:T(8,128)(2,1)S(1)}, u32[]{:S(2)}, u32[]{:S(2)}) collective-permute-start(bf16[8,896]{1,0:T(8,128)(2,1)S(1)} %shard_map.64.refs_0_.refs_8_), channel_id=1, source_target_pairs={{0,14},{2,12},{4,10},{6,8},{8,6},{10,4},{12,2},{14,0},{1,15},{3,13... | collective-permute-start | bytes 43016 | tf_op jit(solution)/shard_map/ppermute | solution.py:17
  8.3 0.8 collective-permute-start.5
  9.1 2.0 %collective-permute-start.4 = (bf16[8,896]{1,0:T(8,128)(2,1)S(1)}, bf16[8,896]{1,0:T(8,128)(2,1)S(1)}, u32[]{:S(2)}, u32[]{:S(2)}) collective-permute-start(bf16[8,896]{1,0:T(8,128)(2,1)S(1)} %shard_map.64.refs_0_.refs_8_), channel_id=1, source_target_pairs={{0,8},{2,10},{4,12},{6,14},{8,0},{10,2},{12,4},{14,6},{1,9},{3,11}... | collective-permute-start | bytes 43016 | tf_op jit(solution)/shard_map/ppermute | solution.py:17
  11.1 2.3 %collective-permute-start.3 = (bf16[8,896]{1,0:T(8,128)(2,1)S(1)}, bf16[8,896]{1,0:T(8,128)(2,1)S(1)}, u32[]{:S(2)}, u32[]{:S(2)}) collective-permute-start(bf16[8,896]{1,0:T(8,128)(2,1)S(1)} %shard_map.64.refs_0_.refs_8_), channel_id=1, source_target_pairs={{0,6},{2,4},{4,2},{6,0},{8,14},{10,12},{12,10},{14,8},{1,7},{3,5},... | collective-permute-start | bytes 43016 | tf_op jit(solution)/shard_map/ppermute | solution.py:17
  13.4 0.8 collective-permute-start.2
  14.6 1.1 %collective-permute-done.3.refs_3_ = bf16[8,896]{1,0:T(8,128)(2,1)S(1)} collective-permute-done((bf16[8,896]{1,0:T(8,128)(2,1)S(1)}, bf16[8,896]{1,0:T(8,128)(2,1)S(1)}, u32[]{:S(2)}, u32[]{:S(2)}) %collective-permute-start.3) | collective-permute-done | bytes 14368 | tf_op jit(solution)/shard_map/ppermute | solution.py:17
  15.7 1.4 %collective-permute-done.2.refs_2_ = bf16[8,896]{1,0:T(8,128)(2,1)S(1)} collective-permute-done((bf16[8,896]{1,0:T(8,128)(2,1)S(1)}, bf16[8,896]{1,0:T(8,128)(2,1)S(1)}, u32[]{:S(2)}, u32[]{:S(2)}) %collective-permute-start.2) | collective-permute-done | bytes 14368 | tf_op jit(solution)/shard_map/ppermute | solution.py:17
  17.1 0.8 collective-permute-done.1.refs_1_
  17.9 5.2 %copy-done = bf16[896,8192]{1,0:T(8,128)(2,1)S(1)} copy-done((bf16[896,8192]{1,0:T(8,128)(2,1)S(1)}, bf16[896,8192]{1,0:T(8,128)(2,1)}, u32[]{:S(2)}) %copy-start) | copy-done | bytes 14680088
  23.1 4.5 %shard_map.65.mine = f32[64,8192]{1,0:T(8,128)S(1)} custom-call(bf16[8,896]{1,0:T(8,128)(2,1)S(1)} %shard_map.64.refs_0_.refs_8_, bf16[8,896]{1,0:T(8,128)(2,1)S(1)} %collective-permute-done.1.refs_1_, bf16[8,896]{1,0:T(8,128)(2,1)S(1)} %collective-permute-done.2.refs_2_, bf16[8,896]{1,0:T(8,128)(2,1)S(1)} %collective-permute-done.3.refs_3_, ...), custom_call_target="tpu_custom_call" | custom-call | tf_op jit(solution)/shard_map/pallas_call | solution.py:83
  27.7 4.1 %collective-permute-done.8.theirs = f32[64,8192]{1,0:T(8,128)S(1)} collective-permute-done((f32[64,8192]{1,0:T(8,128)S(1)}, f32[64,8192]{1,0:T(8,128)S(1)}, u32[]{:S(2)}, u32[]{:S(2)}) %collective-permute-start.8) | collective-permute-done | bytes 2097184 | tf_op jit(solution)/shard_map/ppermute | solution.py:17
  31.8 4.7 %shard_map.66 = (bf16[64,8192]{1,0:T(8,128)(2,1)S(1)}, f32[8,896]{1,0:T(8,128)S(1)}, f32[8,896]{1,0:T(8,128)S(1)}, f32[8,896]{1,0:T(8,128)S(1)}, f32[8,896]{1,0:...) custom-call(f32[64,8192]{1,0:T(8,128)S(1)} %shard_map.65.mine, ...), custom_call_target="tpu_custom_call" | custom-call | tf_op jit(solution)/shard_map/pallas_call | solution.py:112
  36.6 0.5 collective-permute-start.9
  37.1 1.4 %collective-permute-start.10 = (f32[8,896]{1,0:T(8,128)S(1)}, f32[8,896]{1,0:T(8,128)S(1)}, u32[]{:S(2)}, u32[]{:S(2)}) collective-permute-start(f32[8,896]{1,0:T(8,128)S(1)} %get-tuple-element.17), channel_id=1, source_target_pairs={{0,4},{2,6},{4,0},{6,2},{8,12},{10,14},{12,8},{14,10},{1,5},{3,7},... | collective-permute-start | bytes 86024 | tf_op jit(solution)/shard_map/ppermute | solution.py:17
  38.5 1.7 %collective-permute-start.11 = (f32[8,896]{1,0:T(8,128)S(1)}, f32[8,896]{1,0:T(8,128)S(1)}, u32[]{:S(2)}, u32[]{:S(2)}) collective-permute-start(f32[8,896]{1,0:T(8,128)S(1)} %get-tuple-element.18), channel_id=1, source_target_pairs={{0,6},{2,4},{4,2},{6,0},{8,14},{10,12},{12,10},{14,8},{1,7},{3,5},... | collective-permute-start | bytes 86024 | tf_op jit(solution)/shard_map/ppermute | solution.py:17
  40.1 2.2 %collective-permute-start.12 = (f32[8,896]{1,0:T(8,128)S(1)}, f32[8,896]{1,0:T(8,128)S(1)}, u32[]{:S(2)}, u32[]{:S(2)}) collective-permute-start(f32[8,896]{1,0:T(8,128)S(1)} %get-tuple-element.19), channel_id=1, source_target_pairs={{0,8},{2,10},{4,12},{6,14},{8,0},{10,2},{12,4},{14,6},{1,9},{3,11}... | collective-permute-start | bytes 86024 | tf_op jit(solution)/shard_map/ppermute | solution.py:17
  42.3 0.6 collective-permute-start.13
  42.9 3.7 %collective-permute-start.14 = (f32[8,896]{1,0:T(8,128)S(1)}, f32[8,896]{1,0:T(8,128)S(1)}, u32[]{:S(2)}, u32[]{:S(2)}) collective-permute-start(f32[8,896]{1,0:T(8,128)S(1)} %get-tuple-element.21), channel_id=1, source_target_pairs={{0,12},{2,14},{4,8},{6,10},{8,4},{10,6},{12,0},{14,2},{1,13},{3,15... | collective-permute-start | bytes 86024 | tf_op jit(solution)/shard_map/ppermute | solution.py:17
  46.6 1.2 %collective-permute-start.15 = (f32[8,896]{1,0:T(8,128)S(1)}, f32[8,896]{1,0:T(8,128)S(1)}, u32[]{:S(2)}, u32[]{:S(2)}) collective-permute-start(f32[8,896]{1,0:T(8,128)S(1)} %get-tuple-element.22), channel_id=1, source_target_pairs={{0,14},{2,12},{4,10},{6,8},{8,6},{10,4},{12,2},{14,0},{1,15},{3,13... | collective-permute-start | bytes 86024 | tf_op jit(solution)/shard_map/ppermute | solution.py:17
  47.8 0.6 collective-permute-done.13.refs_5_
  48.8 4.4 %collective-permute-done.15.refs_7_ = f32[8,896]{1,0:T(8,128)S(1)} collective-permute-done((f32[8,896]{1,0:T(8,128)S(1)}, f32[8,896]{1,0:T(8,128)S(1)}, u32[]{:S(2)}, u32[]{:S(2)}) %collective-permute-start.15) | collective-permute-done | bytes 28704 | tf_op jit(solution)/shard_map/ppermute | solution.py:17
  53.2 1.2 %collective-permute-start.22 = (bf16[8,896]{1,0:T(8,128)(2,1)S(1)}, bf16[8,896]{1,0:T(8,128)(2,1)S(1)}, u32[]{:S(2)}, u32[]{:S(2)}) collective-permute-start(bf16[8,896]{1,0:T(8,128)(2,1)S(1)} %shard_map.67.refs_0_), channel_id=1, source_target_pairs={{0,14},{2,12},{4,10},{6,8},{8,6},{10,4},{12,2},{14,0},{1,15},{3,13... | collective-permute-start | bytes 43016 | tf_op jit(solution)/shard_map/ppermute | solution.py:17
  54.4 3.6 %collective-permute-start.21 = (bf16[8,896]{1,0:T(8,128)(2,1)S(1)}, bf16[8,896]{1,0:T(8,128)(2,1)S(1)}, u32[]{:S(2)}, u32[]{:S(2)}) collective-permute-start(bf16[8,896]{1,0:T(8,128)(2,1)S(1)} %shard_map.67.refs_0_), channel_id=1, source_target_pairs={{0,12},{2,14},{4,8},{6,10},{8,4},{10,6},{12,0},{14,2},{1,13},{3,15... | collective-permute-start | bytes 43016 | tf_op jit(solution)/shard_map/ppermute | solution.py:17
  58.0 2.9 %collective-permute-start.19 = (bf16[8,896]{1,0:T(8,128)(2,1)S(1)}, bf16[8,896]{1,0:T(8,128)(2,1)S(1)}, u32[]{:S(2)}, u32[]{:S(2)}) collective-permute-start(bf16[8,896]{1,0:T(8,128)(2,1)S(1)} %shard_map.67.refs_0_), channel_id=1, source_target_pairs={{0,8},{2,10},{4,12},{6,14},{8,0},{10,2},{12,4},{14,6},{1,9},{3,11}... | collective-permute-start | bytes 43016 | tf_op jit(solution)/shard_map/ppermute | solution.py:17
  61.0 2.9 %collective-permute-start.17 = (bf16[8,896]{1,0:T(8,128)(2,1)S(1)}, bf16[8,896]{1,0:T(8,128)(2,1)S(1)}, u32[]{:S(2)}, u32[]{:S(2)}) collective-permute-start(bf16[8,896]{1,0:T(8,128)(2,1)S(1)} %shard_map.67.refs_0_), channel_id=1, source_target_pairs={{0,4},{2,6},{4,0},{6,2},{8,12},{10,14},{12,8},{14,10},{1,5},{3,7},... | collective-permute-start | bytes 43016 | tf_op jit(solution)/shard_map/ppermute | solution.py:17
  63.9 0.5 collective-permute-start.16
  64.4 1.1 %collective-permute-done.18.refs_3_ = bf16[8,896]{1,0:T(8,128)(2,1)S(1)} collective-permute-done((bf16[8,896]{1,0:T(8,128)(2,1)S(1)}, bf16[8,896]{1,0:T(8,128)(2,1)S(1)}, u32[]{:S(2)}, u32[]{:S(2)}) %collective-permute-start.18) | collective-permute-done | bytes 14368 | tf_op jit(solution)/shard_map/ppermute | solution.py:17
  65.7 1.9 %collective-permute-done.16.refs_1_ = bf16[8,896]{1,0:T(8,128)(2,1)S(1)} collective-permute-done((bf16[8,896]{1,0:T(8,128)(2,1)S(1)}, bf16[8,896]{1,0:T(8,128)(2,1)S(1)}, u32[]{:S(2)}, u32[]{:S(2)}) %collective-permute-start.16) | collective-permute-done | bytes 14368 | tf_op jit(solution)/shard_map/ppermute | solution.py:17
  67.6 5.2 %copy-done.3 = bf16[8192,896]{1,0:T(8,128)(2,1)S(1)} copy-done((bf16[8192,896]{1,0:T(8,128)(2,1)S(1)}, bf16[8192,896]{1,0:T(8,128)(2,1)}, u32[]{:S(2)}) %copy-start.3) | copy-done | bytes 14680088
  72.8 29.2 %shard_map.68 = bf16[8192,896]{1,0:T(8,128)(2,1)} custom-call(bf16[64,8192]{1,0:T(8,128)(2,1)S(1)} %get-tuple-element.14.codes, bf16[8192,896]{1,0:T(8,128)(2,1)S(1)} %copy-done.2, bf16[8192,896]{1,0:T(8,128)(2,1)S(1)} %copy-done.3, bf16[8,896]{1,0:T(8,128)(2,1)S(1)} %shard_map.67.refs_0_, bf16[8,896]{1,0:T(8,128)(2,1)S(1)} %collective-permute-done.16.refs_1_, ...), custom_call_target="tpu_custom_call" | custom-call | tf_op jit(solution)/shard_map/pallas_call | solution.py:166
  (31 shorter events, 1.8 us)
Async XLA Ops:
  0.0 31.8 %copy-start.4 = (f32[8192]{0:T(1024)S(1)}, f32[8192]{0:T(1024)}, u32[]{:S(2)}) copy-start(f32[8192]{0:T(1024)} %param.8) | copy-start | bytes 98308
  0.0 1.5 %collective-permute-start = (bf16[4,1792]{1,0:T(4,128)(2,1)}, bf16[4,1792]{1,0:T(4,128)(2,1)S(1)}, u32[]{:S(2)}, u32[]{:S(2)}) collective-permute-start(bf16[4,1792]{1,0:T(4,128)(2,1)} %mine.1), channel_id=1, source_target_pairs={{0,1},{1,0},{2,3},{3,2},{4,5},{5,4},{6,7},{7,6},{8,9},{9,8},{10,11... | collective-permute-start | bytes 43016 | tf_op jit(solution)/shard_map/ppermute | solution.py:17
  1.5 0.7 copy-start.5
  2.2 11.2 %collective-permute-start.7 = (bf16[8,896]{1,0:T(8,128)(2,1)S(1)}, bf16[8,896]{1,0:T(8,128)(2,1)S(1)}, u32[]{:S(2)}, u32[]{:S(2)}) collective-permute-start(bf16[8,896]{1,0:T(8,128)(2,1)S(1)} %shard_map.64.refs_0_.refs_8_), channel_id=1, source_target_pairs={{0,14},{2,12},{4,10},{6,8},{8,6},{10,4},{12,2},{14,0},{1,15},{3,13... | collective-permute-start | bytes 43016 | tf_op jit(solution)/shard_map/ppermute | solution.py:17
  8.1 6.1 %collective-permute-start.6 = (bf16[8,896]{1,0:T(8,128)(2,1)S(1)}, bf16[8,896]{1,0:T(8,128)(2,1)S(1)}, u32[]{:S(2)}, u32[]{:S(2)}) collective-permute-start(bf16[8,896]{1,0:T(8,128)(2,1)S(1)} %shard_map.64.refs_0_.refs_8_), channel_id=1, source_target_pairs={{0,12},{2,14},{4,8},{6,10},{8,4},{10,6},{12,0},{14,2},{1,13},{3,15... | collective-permute-start | bytes 43016 | tf_op jit(solution)/shard_map/ppermute | solution.py:17
  8.3 6.3 %collective-permute-start.5 = (bf16[8,896]{1,0:T(8,128)(2,1)S(1)}, bf16[8,896]{1,0:T(8,128)(2,1)S(1)}, u32[]{:S(2)}, u32[]{:S(2)}) collective-permute-start(bf16[8,896]{1,0:T(8,128)(2,1)S(1)} %shard_map.64.refs_0_.refs_8_), channel_id=1, source_target_pairs={{0,10},{2,8},{4,14},{6,12},{8,2},{10,0},{12,6},{14,4},{1,11},{3,9}... | collective-permute-start | bytes 43016 | tf_op jit(solution)/shard_map/ppermute | solution.py:17
  9.1 5.5 %collective-permute-start.4 = (bf16[8,896]{1,0:T(8,128)(2,1)S(1)}, bf16[8,896]{1,0:T(8,128)(2,1)S(1)}, u32[]{:S(2)}, u32[]{:S(2)}) collective-permute-start(bf16[8,896]{1,0:T(8,128)(2,1)S(1)} %shard_map.64.refs_0_.refs_8_), channel_id=1, source_target_pairs={{0,8},{2,10},{4,12},{6,14},{8,0},{10,2},{12,4},{14,6},{1,9},{3,11}... | collective-permute-start | bytes 43016 | tf_op jit(solution)/shard_map/ppermute | solution.py:17
  11.1 4.6 %collective-permute-start.3 = (bf16[8,896]{1,0:T(8,128)(2,1)S(1)}, bf16[8,896]{1,0:T(8,128)(2,1)S(1)}, u32[]{:S(2)}, u32[]{:S(2)}) collective-permute-start(bf16[8,896]{1,0:T(8,128)(2,1)S(1)} %shard_map.64.refs_0_.refs_8_), channel_id=1, source_target_pairs={{0,6},{2,4},{4,2},{6,0},{8,14},{10,12},{12,10},{14,8},{1,7},{3,5},... | collective-permute-start | bytes 43016 | tf_op jit(solution)/shard_map/ppermute | solution.py:17
  13.4 3.7 %collective-permute-start.2 = (bf16[8,896]{1,0:T(8,128)(2,1)S(1)}, bf16[8,896]{1,0:T(8,128)(2,1)S(1)}, u32[]{:S(2)}, u32[]{:S(2)}) collective-permute-start(bf16[8,896]{1,0:T(8,128)(2,1)S(1)} %shard_map.64.refs_0_.refs_8_), channel_id=1, source_target_pairs={{0,4},{2,6},{4,0},{6,2},{8,12},{10,14},{12,8},{14,10},{1,5},{3,7},... | collective-permute-start | bytes 43016 | tf_op jit(solution)/shard_map/ppermute | solution.py:17
  14.2 3.7 %collective-permute-start.1 = (bf16[8,896]{1,0:T(8,128)(2,1)S(1)}, bf16[8,896]{1,0:T(8,128)(2,1)S(1)}, u32[]{:S(2)}, u32[]{:S(2)}) collective-permute-start(bf16[8,896]{1,0:T(8,128)(2,1)S(1)} %shard_map.64.refs_0_.refs_8_), channel_id=1, source_target_pairs={{0,2},{2,0},{4,6},{6,4},{8,10},{10,8},{12,14},{14,12},{1,3},{3,1},... | collective-permute-start | bytes 43016 | tf_op jit(solution)/shard_map/ppermute | solution.py:17
  17.9 5.2 %copy-start = (bf16[896,8192]{1,0:T(8,128)(2,1)S(1)}, bf16[896,8192]{1,0:T(8,128)(2,1)}, u32[]{:S(2)}) copy-start(bf16[896,8192]{1,0:T(8,128)(2,1)} %refs_8_.1) | copy-start | bytes 44040196
  23.1 8.8 %copy-start.1 = (bf16[8192,896]{1,0:T(8,128)(2,1)S(1)}, bf16[8192,896]{1,0:T(8,128)(2,1)}, u32[]{:S(2)}) copy-start(bf16[8192,896]{1,0:T(8,128)(2,1)} %w.1) | copy-start | bytes 44040196
  23.1 44.6 %copy-start.2 = (bf16[8192,896]{1,0:T(8,128)(2,1)S(1)}, bf16[8192,896]{1,0:T(8,128)(2,1)}, u32[]{:S(2)}) copy-start(bf16[8192,896]{1,0:T(8,128)(2,1)} %m.1) | copy-start | bytes 44040196
  27.6 4.2 %collective-permute-start.8 = (f32[64,8192]{1,0:T(8,128)S(1)}, f32[64,8192]{1,0:T(8,128)S(1)}, u32[]{:S(2)}, u32[]{:S(2)}) collective-permute-start(f32[64,8192]{1,0:T(8,128)S(1)} %shard_map.65.mine), channel_id=1, source_target_pairs={{0,1},{1,0},{2,3},{3,2},{4,5},{5,4},{6,7},{7,6},{8,9},{9,8},{10,11... | collective-permute-start | bytes 6291464 | tf_op jit(solution)/shard_map/ppermute | solution.py:17
  36.6 6.3 %collective-permute-start.9 = (f32[8,896]{1,0:T(8,128)S(1)}, f32[8,896]{1,0:T(8,128)S(1)}, u32[]{:S(2)}, u32[]{:S(2)}) collective-permute-start(f32[8,896]{1,0:T(8,128)S(1)} %get-tuple-element.16), channel_id=1, source_target_pairs={{0,2},{2,0},{4,6},{6,4},{8,10},{10,8},{12,14},{14,12},{1,3},{3,1},... | collective-permute-start | bytes 86024 | tf_op jit(solution)/shard_map/ppermute | solution.py:17
  37.1 9.6 %collective-permute-start.10 = (f32[8,896]{1,0:T(8,128)S(1)}, f32[8,896]{1,0:T(8,128)S(1)}, u32[]{:S(2)}, u32[]{:S(2)}) collective-permute-start(f32[8,896]{1,0:T(8,128)S(1)} %get-tuple-element.17), channel_id=1, source_target_pairs={{0,4},{2,6},{4,0},{6,2},{8,12},{10,14},{12,8},{14,10},{1,5},{3,7},... | collective-permute-start | bytes 86024 | tf_op jit(solution)/shard_map/ppermute | solution.py:17
  38.5 9.3 %collective-permute-start.11 = (f32[8,896]{1,0:T(8,128)S(1)}, f32[8,896]{1,0:T(8,128)S(1)}, u32[]{:S(2)}, u32[]{:S(2)}) collective-permute-start(f32[8,896]{1,0:T(8,128)S(1)} %get-tuple-element.18), channel_id=1, source_target_pairs={{0,6},{2,4},{4,2},{6,0},{8,14},{10,12},{12,10},{14,8},{1,7},{3,5},... | collective-permute-start | bytes 86024 | tf_op jit(solution)/shard_map/ppermute | solution.py:17
  40.1 7.7 %collective-permute-start.12 = (f32[8,896]{1,0:T(8,128)S(1)}, f32[8,896]{1,0:T(8,128)S(1)}, u32[]{:S(2)}, u32[]{:S(2)}) collective-permute-start(f32[8,896]{1,0:T(8,128)S(1)} %get-tuple-element.19), channel_id=1, source_target_pairs={{0,8},{2,10},{4,12},{6,14},{8,0},{10,2},{12,4},{14,6},{1,9},{3,11}... | collective-permute-start | bytes 86024 | tf_op jit(solution)/shard_map/ppermute | solution.py:17
  42.3 6.0 %collective-permute-start.13 = (f32[8,896]{1,0:T(8,128)S(1)}, f32[8,896]{1,0:T(8,128)S(1)}, u32[]{:S(2)}, u32[]{:S(2)}) collective-permute-start(f32[8,896]{1,0:T(8,128)S(1)} %get-tuple-element.20), channel_id=1, source_target_pairs={{0,10},{2,8},{4,14},{6,12},{8,2},{10,0},{12,6},{14,4},{1,11},{3,9}... | collective-permute-start | bytes 86024 | tf_op jit(solution)/shard_map/ppermute | solution.py:17
  42.9 5.9 %collective-permute-start.14 = (f32[8,896]{1,0:T(8,128)S(1)}, f32[8,896]{1,0:T(8,128)S(1)}, u32[]{:S(2)}, u32[]{:S(2)}) collective-permute-start(f32[8,896]{1,0:T(8,128)S(1)} %get-tuple-element.21), channel_id=1, source_target_pairs={{0,12},{2,14},{4,8},{6,10},{8,4},{10,6},{12,0},{14,2},{1,13},{3,15... | collective-permute-start | bytes 86024 | tf_op jit(solution)/shard_map/ppermute | solution.py:17
  46.6 6.6 %collective-permute-start.15 = (f32[8,896]{1,0:T(8,128)S(1)}, f32[8,896]{1,0:T(8,128)S(1)}, u32[]{:S(2)}, u32[]{:S(2)}) collective-permute-start(f32[8,896]{1,0:T(8,128)S(1)} %get-tuple-element.22), channel_id=1, source_target_pairs={{0,14},{2,12},{4,10},{6,8},{8,6},{10,4},{12,2},{14,0},{1,15},{3,13... | collective-permute-start | bytes 86024 | tf_op jit(solution)/shard_map/ppermute | solution.py:17
  53.2 7.7 %collective-permute-start.22 = (bf16[8,896]{1,0:T(8,128)(2,1)S(1)}, bf16[8,896]{1,0:T(8,128)(2,1)S(1)}, u32[]{:S(2)}, u32[]{:S(2)}) collective-permute-start(bf16[8,896]{1,0:T(8,128)(2,1)S(1)} %shard_map.67.refs_0_), channel_id=1, source_target_pairs={{0,14},{2,12},{4,10},{6,8},{8,6},{10,4},{12,2},{14,0},{1,15},{3,13... | collective-permute-start | bytes 43016 | tf_op jit(solution)/shard_map/ppermute | solution.py:17
  54.4 9.5 %collective-permute-start.21 = (bf16[8,896]{1,0:T(8,128)(2,1)S(1)}, bf16[8,896]{1,0:T(8,128)(2,1)S(1)}, u32[]{:S(2)}, u32[]{:S(2)}) collective-permute-start(bf16[8,896]{1,0:T(8,128)(2,1)S(1)} %shard_map.67.refs_0_), channel_id=1, source_target_pairs={{0,12},{2,14},{4,8},{6,10},{8,4},{10,6},{12,0},{14,2},{1,13},{3,15... | collective-permute-start | bytes 43016 | tf_op jit(solution)/shard_map/ppermute | solution.py:17
  58.0 6.4 %collective-permute-start.20 = (bf16[8,896]{1,0:T(8,128)(2,1)S(1)}, bf16[8,896]{1,0:T(8,128)(2,1)S(1)}, u32[]{:S(2)}, u32[]{:S(2)}) collective-permute-start(bf16[8,896]{1,0:T(8,128)(2,1)S(1)} %shard_map.67.refs_0_), channel_id=1, source_target_pairs={{0,10},{2,8},{4,14},{6,12},{8,2},{10,0},{12,6},{14,4},{1,11},{3,9}... | collective-permute-start | bytes 43016 | tf_op jit(solution)/shard_map/ppermute | solution.py:17
  58.0 6.4 %collective-permute-start.19 = (bf16[8,896]{1,0:T(8,128)(2,1)S(1)}, bf16[8,896]{1,0:T(8,128)(2,1)S(1)}, u32[]{:S(2)}, u32[]{:S(2)}) collective-permute-start(bf16[8,896]{1,0:T(8,128)(2,1)S(1)} %shard_map.67.refs_0_), channel_id=1, source_target_pairs={{0,8},{2,10},{4,12},{6,14},{8,0},{10,2},{12,4},{14,6},{1,9},{3,11}... | collective-permute-start | bytes 43016 | tf_op jit(solution)/shard_map/ppermute | solution.py:17
  60.9 4.6 %collective-permute-start.18 = (bf16[8,896]{1,0:T(8,128)(2,1)S(1)}, bf16[8,896]{1,0:T(8,128)(2,1)S(1)}, u32[]{:S(2)}, u32[]{:S(2)}) collective-permute-start(bf16[8,896]{1,0:T(8,128)(2,1)S(1)} %shard_map.67.refs_0_), channel_id=1, source_target_pairs={{0,6},{2,4},{4,2},{6,0},{8,14},{10,12},{12,10},{14,8},{1,7},{3,5},... | collective-permute-start | bytes 43016 | tf_op jit(solution)/shard_map/ppermute | solution.py:17
  61.0 4.8 %collective-permute-start.17 = (bf16[8,896]{1,0:T(8,128)(2,1)S(1)}, bf16[8,896]{1,0:T(8,128)(2,1)S(1)}, u32[]{:S(2)}, u32[]{:S(2)}) collective-permute-start(bf16[8,896]{1,0:T(8,128)(2,1)S(1)} %shard_map.67.refs_0_), channel_id=1, source_target_pairs={{0,4},{2,6},{4,0},{6,2},{8,12},{10,14},{12,8},{14,10},{1,5},{3,7},... | collective-permute-start | bytes 43016 | tf_op jit(solution)/shard_map/ppermute | solution.py:17
  63.9 3.7 %collective-permute-start.16 = (bf16[8,896]{1,0:T(8,128)(2,1)S(1)}, bf16[8,896]{1,0:T(8,128)(2,1)S(1)}, u32[]{:S(2)}, u32[]{:S(2)}) collective-permute-start(bf16[8,896]{1,0:T(8,128)(2,1)S(1)} %shard_map.67.refs_0_), channel_id=1, source_target_pairs={{0,2},{2,0},{4,6},{6,4},{8,10},{10,8},{12,14},{14,12},{1,3},{3,1},... | collective-permute-start | bytes 43016 | tf_op jit(solution)/shard_map/ppermute | solution.py:17
  67.6 5.2 %copy-start.3 = (bf16[8192,896]{1,0:T(8,128)(2,1)S(1)}, bf16[8192,896]{1,0:T(8,128)(2,1)}, u32[]{:S(2)}) copy-start(bf16[8192,896]{1,0:T(8,128)(2,1)} %v.1) | copy-start | bytes 44040196

commit v2 on v1

v2 whole, which is shorter than its diff:
```python
import functools

import jax
import jax.numpy as jnp
from jax import lax
from jax.experimental import pallas as pl
from jax.experimental.pallas import tpu as pltpu
from jax.sharding import PartitionSpec as P

MIB = 1 << 20
WHOLE = pl.BlockSpec(memory_space=pltpu.VMEM)
DIRECT = 8


def swap(value, axis, mask):
    n = lax.axis_size(axis)
    return lax.ppermute(value, axis, [(i, i ^ mask) for i in range(n)])


def params(mib):
    return pltpu.CompilerParams(vmem_limit_bytes=mib * MIB)


def waits(mib):
    return pl.CostEstimate(flops=mib * 350_000_000, bytes_accessed=mib * MIB, transcendentals=0)


def resident(value):
    return pltpu.with_memory_space_constraint(value, pltpu.VMEM)


def pair_kernel(mine, theirs, own, out):
    half = out.shape[-1]
    side = lax.axis_index("dp")

    def write(first, second, at):
        both = [first[:, at : at + half], second[:, at : at + half]]
        rows = jnp.concatenate([b.astype(jnp.float32) for b in both]).astype(out.dtype)
        own[...] = rows
        for i in range(out.shape[0]):
            out[i] = rows

    @pl.when(side == 0)
    def _():
        write(mine, theirs, 0)

    @pl.when(side == 1)
    def _():
        write(theirs, mine, half)


def pair_rows(acts, copies):
    theirs = swap(acts, "dp", 1)
    shape = (2 * acts.shape[0], acts.shape[1] // 2)
    return pl.pallas_call(
        pair_kernel,
        out_shape=[
            jax.ShapeDtypeStruct(shape, acts.dtype),
            jax.ShapeDtypeStruct((copies, *shape), acts.dtype),
        ],
        in_specs=[WHOLE, WHOLE],
        out_specs=[WHOLE, WHOLE],
        cost_estimate=waits(6),
        compiler_params=params(4),
    )(acts, theirs)


def peers(n):
    order, mask = [0], n // 2
    while mask:
        order += [j ^ mask for j in order]
        mask //= 2
    return order


def order_kernel(blocks, out):
    me = lax.axis_index("latent")
    parts = [blocks[me ^ j] for j in peers(blocks.shape[0])]
    out[...] = jnp.concatenate([p.astype(jnp.float32) for p in parts]).astype(out.dtype)


def join_kernel(a, b, out):
    both = [a[...], b[...]]
    out[...] = jnp.concatenate([x.astype(jnp.float32) for x in both]).astype(out.dtype)


def join(a, b):
    return pl.pallas_call(
        join_kernel,
        out_shape=jax.ShapeDtypeStruct((a.shape[0] + b.shape[0], a.shape[1]), a.dtype),
        in_specs=[WHOLE, WHOLE],
        out_specs=WHOLE,
        cost_estimate=waits(4),
        compiler_params=params(4),
    )(a, b)


def gather_rows(acts):
    n = lax.axis_size("latent")
    if n > DIRECT:
        own, _ = pair_rows(acts, 1)
        return lax.all_gather(own, "latent", axis=0, tiled=True), own
    own, copies = pair_rows(acts, n)
    blocks = lax.all_to_all(copies, "latent", 0, 0, tiled=True)
    rows = pl.pallas_call(
        order_kernel,
        out_shape=jax.ShapeDtypeStruct((n * copies.shape[1], copies.shape[2]), acts.dtype),
        in_specs=[WHOLE],
        out_specs=WHOLE,
        cost_estimate=waits(6),
        compiler_params=params(4),
    )(blocks)
    return rows, own


def spread(block):
    n = lax.axis_size("latent")
    if n > DIRECT:
        return lax.all_gather(block, "latent", axis=0, tiled=True)
    mask = n // 2
    while mask:
        block = join(block, swap(block, "latent", mask))
        mask //= 2
    return block


def encode_kernel(chunk, rows_ref, w, out):
    rows = rows_ref[...]

    @pl.loop(0, out.shape[1] // chunk)
    def _(i):
        at = pl.ds(pl.multiple_of(i * chunk, chunk), chunk)
        out[:, at] = jnp.dot(rows, w[:, at], preferred_element_type=jnp.float32)


def encode(rows, w_enc):
    tokens, lat = rows.shape[0], w_enc.shape[1]
    return pl.pallas_call(
        functools.partial(encode_kernel, min(512, lat)),
        out_shape=jax.ShapeDtypeStruct((tokens, lat), jnp.float32),
        in_specs=[WHOLE] * 2,
        out_specs=WHOLE,
        cost_estimate=waits(14),
        compiler_params=params(8),
    )(rows, resident(w_enc))


def decode_kernel(chunk, mine, theirs, bias, w, codes, *out):
    tokens, lat = mine.shape
    total = jnp.zeros((tokens, w.shape[1]), jnp.float32)

    def step(i, total):
        at = pl.ds(pl.multiple_of(i * chunk, chunk), chunk)
        pre = mine[:, at] + theirs[:, at] + bias[:, at]
        block = jnp.maximum(pre, 0.0).astype(jnp.bfloat16)
        codes[:, at] = block
        return total + jnp.dot(block, w[at, :], preferred_element_type=jnp.float32)

    total = lax.fori_loop(0, lat // chunk, step, total)
    rows = tokens // len(out)
    for j, ref in enumerate(out):
        ref[...] = total[j * rows : (j + 1) * rows]


def decode(mine, theirs, bias, w_dec, parts):
    tokens, lat = mine.shape
    half = w_dec.shape[1]
    codes, *sums = pl.pallas_call(
        functools.partial(decode_kernel, min(512, lat)),
        out_shape=[jax.ShapeDtypeStruct((tokens, lat), jnp.bfloat16)]
        + [jax.ShapeDtypeStruct((tokens // parts, half), jnp.float32)] * parts,
        in_specs=[WHOLE] * 4,
        out_specs=[WHOLE] * (1 + parts),
        cost_estimate=waits(14),
        compiler_params=params(8),
    )(mine, theirs, bias.reshape(1, lat), resident(w_dec))
    return codes, sums


def turn_kernel(chunk, codes, out):
    @pl.loop(0, out.shape[0] // chunk)
    def _(i):
        at = pl.ds(pl.multiple_of(i * chunk, chunk), chunk)
        out[at, :] = codes[:, at].astype(jnp.float32).T.astype(out.dtype)


def turn(codes):
    tokens, lat = codes.shape
    return pl.pallas_call(
        functools.partial(turn_kernel, min(512, lat)),
        out_shape=jax.ShapeDtypeStruct((lat, tokens), codes.dtype),
        in_specs=[WHOLE],
        out_specs=WHOLE,
        cost_estimate=waits(4),
        compiler_params=params(8),
    )(codes)


def halve_kernel(a, b, keep, send):
    total = a[...] + b[...]
    half = keep.shape[0]
    keep[...] = total[:half]
    send[...] = total[half:]


def halve(a, b):
    rows, half = a.shape
    return pl.pallas_call(
        halve_kernel,
        out_shape=[jax.ShapeDtypeStruct((rows // 2, half), a.dtype)] * 2,
        in_specs=[WHOLE] * 2,
        out_specs=[WHOLE] * 2,
        cost_estimate=waits(4),
        compiler_params=params(4),
    )(a, b)


def error_kernel(*refs):
    *sums, rows, out = refs
    total = sums[0][...]
    for ref in sums[1:]:
        total = total + ref[...]
    out[...] = (total - rows[...].astype(jnp.float32)).astype(out.dtype)


def own_error(sums, rows):
    return pl.pallas_call(
        error_kernel,
        out_shape=jax.ShapeDtypeStruct(rows.shape, rows.dtype),
        in_specs=[WHOLE] * (len(sums) + 1),
        out_specs=WHOLE,
        cost_estimate=waits(4),
        compiler_params=params(4),
    )(*sums, rows)


def reduce_rows(sums):
    n = lax.axis_size("latent")
    if n > DIRECT:
        return [lax.psum_scatter(sums[0], "latent", scatter_dimension=0, tiled=True)]
    keep, send = sums
    mask = 1
    while mask < n // 2:
        keep, send = halve(keep, swap(send, "latent", mask))
        mask *= 2
    return [keep, swap(send, "latent", mask)]


def adam_kernel(codes_t, err, m, v, out, *products):
    tokens = codes_t.shape[1]
    b = 0.1 / (1.0 - 0.9**10) / tokens
    a = 0.9 / (1.0 - 0.9**10) / b
    p = 0.999 / (1.0 - 0.999**10) / b**2
    q = 0.001 / (1.0 - 0.999**10) / tokens**2 / b**2
    eps = 1e-8 / b
    i, last = pl.program_id(0), pl.num_programs(0) - 1
    rows = out.shape[0]
    part = rows // len(products)

    def multiply(block, k):
        at = pl.ds(pl.multiple_of(block * rows + k * part, part), part)
        products[k][...] = jnp.dot(codes_t[at, :], err[...], preferred_element_type=jnp.float32)

    @pl.when(i == 0)
    def _():
        multiply(0, 0)

    for k in range(len(products)):
        if k + 1 < len(products):
            multiply(i, k + 1)
        else:
            multiply(jnp.minimum(i + 1, last), 0)
        for r in range(0, part, 16):
            at = pl.ds(pl.multiple_of(i * rows + k * part + r, 16), 16)
            c = products[k][r : r + 16, :]
            first = m[at, :].astype(jnp.float32) * a + c
            second = v[at, :].astype(jnp.float32) * p + (c * c) * q
            root = second * lax.rsqrt(second)
            step = first * pl.reciprocal(root + eps, approx=True)
            out[k * part + r : k * part + r + 16, :] = step.astype(out.dtype)


def adam(codes_t, err, m, v):
    lat, half = m.shape
    rows = min(512, lat)
    parts = 4
    return pl.pallas_call(
        adam_kernel,
        grid=(lat // rows,),
        out_shape=jax.ShapeDtypeStruct(m.shape, jnp.bfloat16),
        in_specs=[WHOLE] * 4,
        out_specs=pl.BlockSpec((rows, half), lambda i: (i, 0)),
        scratch_shapes=[pltpu.VMEM((rows // parts, half), jnp.float32)] * parts,
        compiler_params=params(8),
    )(codes_t, err, resident(m), resident(v))


def per_device(acts, w_enc, b_enc, w_dec, dec_m, dec_v):
    rows, own = gather_rows(acts)
    mine = encode(rows, w_enc)
    theirs = swap(mine, "dp", 1)
    direct = lax.axis_size("latent") <= DIRECT
    codes, sums = decode(mine, theirs, b_enc, w_dec, 2 if direct else 1)
    codes_t = turn(codes)
    err = spread(own_error(reduce_rows(sums), own))
    return adam(codes_t, err, dec_m, dec_v)


def solution(mesh):
    in_specs = (
        P(("groups", "latent", "dp"), None),
        P(("groups", "dp"), "latent"),
        P(("groups", "latent")),
        P(("groups", "latent"), "dp"),
        P(("groups", "latent"), "dp"),
        P(("groups", "latent"), "dp"),
    )
    out_specs = P(("groups", "latent"), "dp")
    return jax.shard_map(
        per_device, mesh=mesh, in_specs=in_specs, out_specs=out_specs, check_vma=False
    )
```

time: 102 us -> 74.9 us (0.73)
  starting transfers between devices: 35.3 us -> 2.51 us
  blocking collectives: 0 us -> 14.4 us
  waiting for transfers between devices: 17.1 us -> 28.6 us
  Pallas kernels: 38.5 us -> 27.5 us
  local copies, waits for them, and re-layouts: 11.1 us -> 1.39 us
    ppermute x23 -> x8, starting transfers between devices: 35.3 us -> 2.51 us  [swap(): return lax.ppermute(value, axis, [(i, i ^ mask) for i in range(n)])]
    all_to_all x0 -> x1, blocking collectives: none -> 14.4 us  [gather_rows(): blocks = lax.all_to_all(copies, 'latent', 0, 0, tiled=True)]
    ppermute x23 -> x8, waiting for transfers between devices: 17.1 us -> 28.6 us  [swap(): return lax.ppermute(value, axis, [(i, i ^ mask) for i in range(n)])]
    pallas_call x2 -> x9, Pallas kernels: 29.2 us -> 18.2 us  [the longest x1 16.5 us: adam(): pl.pallas_call(adam_kernel, grid=(lat // rows,), out_shape=jax.ShapeDtype...]
    unnamed x12 -> x30, local copies, waits for them, and re-layouts: 11.1 us -> 1.39 us
  transfers between devices with their start and end apart: 23 -> 8, of which waited for: 11 -> 8; matrix products, arithmetic and copies ran while one was open for 0% -> 0% of each run, Pallas kernels for 0% -> 2%
where the time goes in v2:
time: 74.9 us; the launch traced here: 74.6 us
  waiting for transfers between devices  28.6 us (38%)
  Pallas kernels  27.5 us (37%)
  blocking collectives  14.4 us (19%)
  starting transfers between devices  2.51 us (3%)
  local copies, waits for them, and re-layouts  1.39 us (2%)
    ppermute x8, waiting for transfers between devices, swap(): return lax.ppermute(value, axis, [(i, i ^ mask) for i in range(n)])  28.6 us
    pallas_call x1, Pallas kernels, adam(): pl.pallas_call(adam_kernel, grid=(lat // rows,), out_shape=jax.ShapeDtype...  16.5 us
    all_to_all x1, blocking collectives, gather_rows(): blocks = lax.all_to_all(copies, 'latent', 0, 0, tiled=True)  14.4 us
    pallas_call x1, Pallas kernels, decode(): pl.pallas_call(functools.partial(decode_kernel, min(512, lat)), out_shape...  4.73 us
    pallas_call x1, Pallas kernels, encode(): pl.pallas_call(functools.partial(encode_kernel, min(512, lat)), out_shape...  4.53 us
    ppermute x8, starting transfers between devices, swap(): return lax.ppermute(value, axis, [(i, i ^ mask) for i in range(n)])  2.51 us
    pallas_call x1, Pallas kernels, turn(): pl.pallas_call(functools.partial(turn_kernel, min(512, lat)), out_shape=j...  1.68 us
  transfers between devices with their start and end apart: 8, of which 8 were waited for; matrix products, arithmetic and copies ran while one was open for 0% of the time, Pallas kernels for 2%

profile of v2, /device:TPU:0, one launch (start us, length us, event | category | flops | bytes accessed | tf_op | source)
XLA Modules:
  0.0 74.6 jit_solution(8445328200543285747)
XLA Ops:
  0.0 0.5 collective-permute-start
  0.5 1.0 %collective-permute-done.theirs = bf16[4,1792]{1,0:T(4,128)(2,1)S(1)} collective-permute-done((bf16[4,1792]{1,0:T(4,128)(2,1)}, bf16[4,1792]{1,0:T(4,128)(2,1)S(1)}, u32[]{:S(2)}, u32[]{:S(2)}) %collective-permute-start) | collective-permute-done | bytes 14368 | tf_op jit(solution)/shard_map/ppermute | solution.py:17
  1.5 1.3 %copy-done.2 = bf16[4,1792]{1,0:T(4,128)(2,1)S(1)} copy-done((bf16[4,1792]{1,0:T(4,128)(2,1)S(1)}, bf16[4,1792]{1,0:T(4,128)(2,1)}, u32[]{:S(2)}) %copy-start.2) | copy-done | bytes 14360
  2.9 0.0 copy-start
  2.9 14.4 %all_to_all.5.blocks = bf16[8,8,896]{2,1,0:T(8,128)(2,1)S(1)} all-to-all(bf16[8,8,896]{2,1,0:T(8,128)(2,1)S(1)} %get-tuple-element.14), channel_id=1, replica_groups=mesh['groups'=2,'latent'=8,'dp'=2] {'latent'}, dimensions={0} | all-to-all | bytes 229376 | tf_op jit(solution)/shard_map/all_to_all | solution.py:104
  17.3 0.0 slice-start.2
  17.3 0.0 slice-start.3
  17.3 4.5 %shard_map.66.mine = f32[64,8192]{1,0:T(8,128)S(1)} custom-call(bf16[64,896]{1,0:T(8,128)(2,1)S(1)} %shard_map.65.rows_ref, bf16[896,8192]{1,0:T(8,128)(2,1)S(1)} %copy-done.1), custom_call_target="tpu_custom_call" | custom-call | flops 4899999744 | bytes 14680064 | tf_op jit(solution)/shard_map/pallas_call | solution.py:138
  21.9 0.1 collective-permute-start.1
  21.9 4.1 %collective-permute-done.1.theirs = f32[64,8192]{1,0:T(8,128)S(1)} collective-permute-done((f32[64,8192]{1,0:T(8,128)S(1)}, f32[64,8192]{1,0:T(8,128)S(1)}, u32[]{:S(2)}, u32[]{:S(2)}) %collective-permute-start.1) | collective-permute-done | bytes 2097184 | tf_op jit(solution)/shard_map/ppermute | solution.py:17
  26.1 0.0 copy-done
  26.1 0.0 slice-start.8
  26.1 0.0 slice-start.9
  26.1 4.7 %shard_map.67 = (bf16[64,8192]{1,0:T(8,128)(2,1)S(1)}, f32[32,896]{1,0:T(8,128)S(1)}, f32[32,896]{1,0:T(8,128)S(1)}) custom-call(f32[64,8192]{1,0:T(8,128)S(1)} %shard_map.66.mine, f32[64,8192]{1,0:T(8,128)S(1)} %collective-permute-done.1.theirs, f32[1,8192]{1,0:T(1,128)S(1)} %bitcast.7, bf16[8192,896]{1,0:T(8,128)(2,1)S(1)} %bitcast.2), custom_call_target="tpu_custom_call" | custom-call | flops 4899999744 | bytes 14680064 | tf_op jit(solution)/shard_map/pallas_call | solution.py:168
  30.9 0.4 collective-permute-start.2
  31.3 4.8 %collective-permute-done.2.b = f32[32,896]{1,0:T(8,128)S(1)} collective-permute-done((f32[32,896]{1,0:T(8,128)S(1)}, f32[32,896]{1,0:T(8,128)S(1)}, u32[]{:S(2)}, u32[]{:S(2)}) %collective-permute-start.2) | collective-permute-done | bytes 114720 | tf_op jit(solution)/shard_map/ppermute | solution.py:17
  36.1 0.1 collective-permute-start.3
  36.3 4.1 %collective-permute-done.3.b = f32[16,896]{1,0:T(8,128)S(1)} collective-permute-done((f32[16,896]{1,0:T(8,128)S(1)}, f32[16,896]{1,0:T(8,128)S(1)}, u32[]{:S(2)}, u32[]{:S(2)}) %collective-permute-start.3) | collective-permute-done | bytes 57376 | tf_op jit(solution)/shard_map/ppermute | solution.py:17
  40.4 0.5 collective-permute-start.4
  40.9 4.4 %collective-permute-done.4.refs_1_ = f32[8,896]{1,0:T(8,128)S(1)} collective-permute-done((f32[8,896]{1,0:T(8,128)S(1)}, f32[8,896]{1,0:T(8,128)S(1)}, u32[]{:S(2)}, u32[]{:S(2)}) %collective-permute-start.4) | collective-permute-done | bytes 28704 | tf_op jit(solution)/shard_map/ppermute | solution.py:17
  45.3 0.0 slice-start.6
  45.3 0.5 collective-permute-start.5
  45.8 4.2 %collective-permute-done.5.b = bf16[8,896]{1,0:T(8,128)(2,1)S(1)} collective-permute-done((bf16[8,896]{1,0:T(8,128)(2,1)S(1)}, bf16[8,896]{1,0:T(8,128)(2,1)S(1)}, u32[]{:S(2)}, u32[]{:S(2)}) %collective-permute-start.5) | collective-permute-done | bytes 14368 | tf_op jit(solution)/shard_map/ppermute | solution.py:17
  50.0 0.1 collective-permute-start.6
  50.0 3.8 %collective-permute-done.6.b = bf16[16,896]{1,0:T(8,128)(2,1)S(1)} collective-permute-done((bf16[16,896]{1,0:T(8,128)(2,1)S(1)}, bf16[16,896]{1,0:T(8,128)(2,1)S(1)}, u32[]{:S(2)}, u32[]{:S(2)}) %collective-permute-start.6) | collective-permute-done | bytes 28704 | tf_op jit(solution)/shard_map/ppermute | solution.py:17
  53.8 0.4 collective-permute-start.7
  54.2 1.7 %shard_map.68.codes_t = bf16[8192,64]{1,0:T(8,128)(2,1)S(1)} custom-call(bf16[64,8192]{1,0:T(8,128)(2,1)S(1)} %get-tuple-element.15.codes), custom_call_target="tpu_custom_call" | custom-call | flops 1400000000 | bytes 4194304 | tf_op jit(solution)/shard_map/pallas_call | solution.py:189
  55.9 2.1 %collective-permute-done.7.b = bf16[32,896]{1,0:T(8,128)(2,1)S(1)} collective-permute-done((bf16[32,896]{1,0:T(8,128)(2,1)S(1)}, bf16[32,896]{1,0:T(8,128)(2,1)S(1)}, u32[]{:S(2)}, u32[]{:S(2)}) %collective-permute-start.7) | collective-permute-done | bytes 57376 | tf_op jit(solution)/shard_map/ppermute | solution.py:17
  58.0 0.0 slice-done.8
  58.0 0.0 slice-done.9
  58.0 0.0 slice-done.4
  58.1 16.5 %shard_map.75 = bf16[8192,896]{1,0:T(8,128)(2,1)} custom-call(bf16[8192,64]{1,0:T(8,128)(2,1)S(1)} %shard_map.68.codes_t, bf16[64,896]{1,0:T(8,128)(2,1)S(1)} %shard_map.74.err, bf16[8192,896]{1,0:T(8,128)(2,1)S(1)} %bitcast.4, bf16[8192,896]{1,0:T(8,128)(2,1)S(1)} %bitcast.6), custom_call_target="tpu_custom_call" | custom-call | tf_op jit(solution)/shard_map/pallas_call | solution.py:287
  (30 shorter events, 0.1 us)
Async XLA Ops:
  0.0 17.3 %copy-start.1 = (bf16[896,8192]{1,0:T(8,128)(2,1)S(1)}, bf16[896,8192]{1,0:T(8,128)(2,1)}, u32[]{:S(2)}) copy-start(bf16[896,8192]{1,0:T(8,128)(2,1)} %w.2) | copy-start | bytes 44040196
  0.0 1.5 %collective-permute-start = (bf16[4,1792]{1,0:T(4,128)(2,1)}, bf16[4,1792]{1,0:T(4,128)(2,1)S(1)}, u32[]{:S(2)}, u32[]{:S(2)}) collective-permute-start(bf16[4,1792]{1,0:T(4,128)(2,1)} %mine.1), channel_id=1, source_target_pairs={{0,1},{1,0},{2,3},{3,2},{4,5},{5,4},{6,7},{7,6},{8,9},{9,8},{10,11... | collective-permute-start | bytes 43016 | tf_op jit(solution)/shard_map/ppermute | solution.py:17
  1.5 1.3 %copy-start.2 = (bf16[4,1792]{1,0:T(4,128)(2,1)S(1)}, bf16[4,1792]{1,0:T(4,128)(2,1)}, u32[]{:S(2)}) copy-start(bf16[4,1792]{1,0:T(4,128)(2,1)} %mine.1) | copy-start | bytes 43012
  2.8 23.3 %slice-start = ((s8[14680064]{0:T(1024)(128)(4,1)}), s8[4194304]{0:T(1024)(128)(4,1)S(1)}, s32[]{:S(2)}) async-start(s8[14680064]{0:T(1024)(128)(4,1)} %bitcast.1), calls=%async_computation.1 | async-start | bytes 8388608
  2.9 23.2 %copy-start = (f32[8192]{0:T(1024)S(1)}, f32[8192]{0:T(1024)}, u32[]{:S(2)}) copy-start(f32[8192]{0:T(1024)} %param.8) | copy-start | bytes 98308
  17.3 8.8 %slice-start.1 = ((s8[14680064]{0:T(1024)(128)(4,1)}), s8[4194304]{0:T(1024)(128)(4,1)S(1)}, s32[]{:S(2)}) async-start(s8[14680064]{0:T(1024)(128)(4,1)} %bitcast.1), calls=%async_computation.2 | async-start | bytes 8388608
  17.3 8.8 %slice-start.2 = ((s8[14680064]{0:T(1024)(128)(4,1)}), s8[4194304]{0:T(1024)(128)(4,1)S(1)}, s32[]{:S(2)}) async-start(s8[14680064]{0:T(1024)(128)(4,1)} %bitcast.1), calls=%async_computation.3 | async-start | bytes 8388608
  17.3 8.8 %slice-start.3 = ((s8[14680064]{0:T(1024)(128)(4,1)}), s8[2097152]{0:T(1024)(128)(4,1)S(1)}, s32[]{:S(2)}) async-start(s8[14680064]{0:T(1024)(128)(4,1)} %bitcast.1), calls=%async_computation.4 | async-start | bytes 4194304
  21.9 4.2 %collective-permute-start.1 = (f32[64,8192]{1,0:T(8,128)S(1)}, f32[64,8192]{1,0:T(8,128)S(1)}, u32[]{:S(2)}, u32[]{:S(2)}) collective-permute-start(f32[64,8192]{1,0:T(8,128)S(1)} %shard_map.66.mine), channel_id=1, source_target_pairs={{0,1},{1,0},{2,3},{3,2},{4,5},{5,4},{6,7},{7,6},{8,9},{9,8},{10,11... | collective-permute-start | bytes 6291464 | tf_op jit(solution)/shard_map/ppermute | solution.py:17
  26.1 31.9 %slice-start.8 = ((s8[14680064]{0:T(1024)(128)(4,1)}), s8[2097152]{0:T(1024)(128)(4,1)S(1)}, s32[]{:S(2)}) async-start(s8[14680064]{0:T(1024)(128)(4,1)} %bitcast.5), calls=%async_computation.9 | async-start | bytes 4194304
  26.1 31.9 %slice-start.9 = ((s8[14680064]{0:T(1024)(128)(4,1)}), s8[4194304]{0:T(1024)(128)(4,1)S(1)}, s32[]{:S(2)}) async-start(s8[14680064]{0:T(1024)(128)(4,1)} %bitcast.5), calls=%async_computation.10 | async-start | bytes 8388608
  30.9 5.2 %collective-permute-start.2 = (f32[32,896]{1,0:T(8,128)S(1)}, f32[32,896]{1,0:T(8,128)S(1)}, u32[]{:S(2)}, u32[]{:S(2)}) collective-permute-start(f32[32,896]{1,0:T(8,128)S(1)} %get-tuple-element.17), channel_id=1, source_target_pairs={{0,2},{2,0},{4,6},{6,4},{8,10},{10,8},{12,14},{14,12},{1,3},{3,1},... | collective-permute-start | bytes 344072 | tf_op jit(solution)/shard_map/ppermute | solution.py:17
  36.1 4.2 %collective-permute-start.3 = (f32[16,896]{1,0:T(8,128)S(1)}, f32[16,896]{1,0:T(8,128)S(1)}, u32[]{:S(2)}, u32[]{:S(2)}) collective-permute-start(f32[16,896]{1,0:T(8,128)S(1)} %get-tuple-element.19), channel_id=1, source_target_pairs={{0,4},{2,6},{4,0},{6,2},{8,12},{10,14},{12,8},{14,10},{1,5},{3,7},... | collective-permute-start | bytes 172040 | tf_op jit(solution)/shard_map/ppermute | solution.py:17
  40.4 17.7 %slice-start.4 = ((s8[14680064]{0:T(1024)(128)(4,1)}), s8[4194304]{0:T(1024)(128)(4,1)S(1)}, s32[]{:S(2)}) async-start(s8[14680064]{0:T(1024)(128)(4,1)} %bitcast.3), calls=%async_computation.5 | async-start | bytes 8388608
  40.4 17.7 %slice-start.10 = ((s8[14680064]{0:T(1024)(128)(4,1)}), s8[4194304]{0:T(1024)(128)(4,1)S(1)}, s32[]{:S(2)}) async-start(s8[14680064]{0:T(1024)(128)(4,1)} %bitcast.5), calls=%async_computation.11 | async-start | bytes 8388608
  40.4 4.8 %collective-permute-start.4 = (f32[8,896]{1,0:T(8,128)S(1)}, f32[8,896]{1,0:T(8,128)S(1)}, u32[]{:S(2)}, u32[]{:S(2)}) collective-permute-start(f32[8,896]{1,0:T(8,128)S(1)} %get-tuple-element.21), channel_id=1, source_target_pairs={{0,8},{2,10},{4,12},{6,14},{8,0},{10,2},{12,4},{14,6},{1,9},{3,11}... | collective-permute-start | bytes 86024 | tf_op jit(solution)/shard_map/ppermute | solution.py:17
  45.2 12.8 %slice-start.5 = ((s8[14680064]{0:T(1024)(128)(4,1)}), s8[4194304]{0:T(1024)(128)(4,1)S(1)}, s32[]{:S(2)}) async-start(s8[14680064]{0:T(1024)(128)(4,1)} %bitcast.3), calls=%async_computation.6 | async-start | bytes 8388608
  45.3 12.8 %slice-start.6 = ((s8[14680064]{0:T(1024)(128)(4,1)}), s8[4194304]{0:T(1024)(128)(4,1)S(1)}, s32[]{:S(2)}) async-start(s8[14680064]{0:T(1024)(128)(4,1)} %bitcast.3), calls=%async_computation.7 | async-start | bytes 8388608
  45.3 4.7 %collective-permute-start.5 = (bf16[8,896]{1,0:T(8,128)(2,1)S(1)}, bf16[8,896]{1,0:T(8,128)(2,1)S(1)}, u32[]{:S(2)}, u32[]{:S(2)}) collective-permute-start(bf16[8,896]{1,0:T(8,128)(2,1)S(1)} %shard_map.71.a), channel_id=1, source_target_pairs={{0,8},{2,10},{4,12},{6,14},{8,0},{10,2},{12,4},{14,6},{1,9},{3,11}... | collective-permute-start | bytes 43016 | tf_op jit(solution)/shard_map/ppermute | solution.py:17
  50.0 8.1 %slice-start.11 = ((s8[14680064]{0:T(1024)(128)(4,1)}), s8[4194304]{0:T(1024)(128)(4,1)S(1)}, s32[]{:S(2)}) async-start(s8[14680064]{0:T(1024)(128)(4,1)} %bitcast.5), calls=%async_computation.12 | async-start | bytes 8388608
  50.0 3.9 %collective-permute-start.6 = (bf16[16,896]{1,0:T(8,128)(2,1)S(1)}, bf16[16,896]{1,0:T(8,128)(2,1)S(1)}, u32[]{:S(2)}, u32[]{:S(2)}) collective-permute-start(bf16[16,896]{1,0:T(8,128)(2,1)S(1)} %shard_map.72.a), channel_id=1, source_target_pairs={{0,4},{2,6},{4,0},{6,2},{8,12},{10,14},{12,8},{14,10},{1,5},{3,7},... | collective-permute-start | bytes 86024 | tf_op jit(solution)/shard_map/ppermute | solution.py:17
  53.8 4.2 %collective-permute-start.7 = (bf16[32,896]{1,0:T(8,128)(2,1)S(1)}, bf16[32,896]{1,0:T(8,128)(2,1)S(1)}, u32[]{:S(2)}, u32[]{:S(2)}) collective-permute-start(bf16[32,896]{1,0:T(8,128)(2,1)S(1)} %shard_map.73.a), channel_id=1, source_target_pairs={{0,2},{2,0},{4,6},{6,4},{8,10},{10,8},{12,14},{14,12},{1,3},{3,1},... | collective-permute-start | bytes 172040 | tf_op jit(solution)/shard_map/ppermute | solution.py:17
  54.2 3.9 %slice-start.7 = ((s8[14680064]{0:T(1024)(128)(4,1)}), s8[2097152]{0:T(1024)(128)(4,1)S(1)}, s32[]{:S(2)}) async-start(s8[14680064]{0:T(1024)(128)(4,1)} %bitcast.3), calls=%async_computation.8 | async-start | bytes 4194304

commit v3 on v1

v3 whole, which is shorter than its diff:
```python
import functools

import jax
import jax.numpy as jnp
from jax import lax
from jax.experimental import pallas as pl
from jax.experimental.pallas import tpu as pltpu
from jax.sharding import PartitionSpec as P

MIB = 1 << 20
WHOLE = pl.BlockSpec(memory_space=pltpu.VMEM)
DIRECT = 8


def swap(value, axis, mask):
    n = lax.axis_size(axis)
    return lax.ppermute(value, axis, [(i, i ^ mask) for i in range(n)])


def params(mib):
    return pltpu.CompilerParams(vmem_limit_bytes=mib * MIB)


def waits(mib):
    return pl.CostEstimate(flops=mib * 350_000_000, bytes_accessed=mib * MIB, transcendentals=0)


def resident(value):
    return pltpu.with_memory_space_constraint(value, pltpu.VMEM)


def far_masks():
    return range(2, lax.axis_size("latent"), 2)


def stack(refs):
    return jnp.concatenate([r[...].astype(jnp.float32) for r in refs]).astype(refs[0].dtype)


def near_kernel(*refs):
    *rows, out = refs
    half = out.shape[1]
    side = lax.axis_index("dp")

    def write(order, at):
        picked = [rows[i][:, at : at + half].astype(jnp.float32) for i in order]
        out[...] = jnp.concatenate(picked).astype(out.dtype)

    pairs = range(0, len(rows), 2)

    @pl.when(side == 0)
    def _():
        write([i + c for i in pairs for c in (0, 1)], 0)

    @pl.when(side == 1)
    def _():
        write([i + c for i in pairs for c in (1, 0)], half)


def near_rows(acts, near):
    axes = ("latent", "dp")
    rows = [acts] + [swap(acts, axes, mask) for mask in range(1, 2 * near)]
    return pl.pallas_call(
        near_kernel,
        out_shape=jax.ShapeDtypeStruct((len(rows) * acts.shape[0], acts.shape[1] // 2), acts.dtype),
        in_specs=[WHOLE] * len(rows),
        out_specs=WHOLE,
        cost_estimate=waits(14),
        compiler_params=params(4),
    )(*rows)


def spread(block):
    if lax.axis_size("latent") > DIRECT:
        return [lax.all_gather(block, "latent", axis=0, tiled=True)]
    return [block] + [swap(block, "latent", mask) for mask in far_masks()]


def encode_kernel(first, chunk, *refs):
    *rows_refs, w, out = refs
    rows = stack(rows_refs)

    @pl.loop(0, out.shape[1] // chunk)
    def _(i):
        at = pl.multiple_of(i * chunk, chunk)
        out[:, pl.ds(at, chunk)] = jnp.dot(
            rows, w[:, pl.ds(first + at, chunk)], preferred_element_type=jnp.float32
        )


def encode(blocks, w_enc, first, lat):
    tokens = sum(b.shape[0] for b in blocks)
    return pl.pallas_call(
        functools.partial(encode_kernel, first, min(512, lat)),
        out_shape=jax.ShapeDtypeStruct((tokens, lat), jnp.float32),
        in_specs=[WHOLE] * (len(blocks) + 1),
        out_specs=WHOLE,
        cost_estimate=waits(7),
        compiler_params=params(8),
    )(*blocks, resident(w_enc))


def decode_kernel(first, chunk, given, mine, theirs, bias, w, *refs):
    codes, *out = refs[given:]
    tokens, lat = mine.shape
    total = refs[0][...] if given else jnp.zeros((tokens, w.shape[1]), jnp.float32)

    def step(i, total):
        at = pl.multiple_of(i * chunk, chunk)
        part, whole = pl.ds(at, chunk), pl.ds(first + at, chunk)
        pre = mine[:, part] + theirs[:, part] + bias[:, whole]
        block = jnp.maximum(pre, 0.0).astype(jnp.bfloat16)
        codes[:, part] = block
        return total + jnp.dot(block, w[whole, :], preferred_element_type=jnp.float32)

    total = lax.fori_loop(0, lat // chunk, step, total)
    rows = tokens // len(out)
    for j, ref in enumerate(out):
        ref[...] = total[j * rows : (j + 1) * rows]


def decode(mine, theirs, bias, w_dec, first, given, parts):
    tokens, lat = mine.shape
    half = w_dec.shape[1]
    codes, *sums = pl.pallas_call(
        functools.partial(decode_kernel, first, min(512, lat), len(given)),
        out_shape=[jax.ShapeDtypeStruct((tokens, lat), jnp.bfloat16)]
        + [jax.ShapeDtypeStruct((tokens // parts, half), jnp.float32)] * parts,
        in_specs=[WHOLE] * (4 + len(given)),
        out_specs=[WHOLE] * (1 + parts),
        cost_estimate=waits(7),
        compiler_params=params(8),
    )(mine, theirs, bias.reshape(1, -1), resident(w_dec), *given)
    return codes, sums


def turn_kernel(chunk, *refs):
    *codes, out = refs
    for k, ref in enumerate(codes):
        lat = ref.shape[1]

        @pl.loop(0, lat // chunk)
        def _(i):
            at = pl.multiple_of(i * chunk, chunk)
            block = ref[:, pl.ds(at, chunk)].astype(jnp.float32).T
            out[pl.ds(k * lat + at, chunk), :] = block.astype(out.dtype)


def turn(*codes):
    tokens, lat = codes[0].shape
    return pl.pallas_call(
        functools.partial(turn_kernel, min(512, lat)),
        out_shape=jax.ShapeDtypeStruct((len(codes) * lat, tokens), codes[0].dtype),
        in_specs=[WHOLE] * len(codes),
        out_specs=WHOLE,
        cost_estimate=waits(4),
        compiler_params=params(8),
    )(*codes)


def sum_kernel(*refs):
    *terms, out = refs
    total = terms[0][...]
    for ref in terms[1:]:
        total = total + ref[...]
    out[...] = total


def add_up(terms):
    return pl.pallas_call(
        sum_kernel,
        out_shape=jax.ShapeDtypeStruct(terms[0].shape, jnp.float32),
        in_specs=[WHOLE] * len(terms),
        out_specs=WHOLE,
        cost_estimate=waits(8),
        compiler_params=params(4),
    )(*terms)


def error_kernel(total, rows, *refs):
    *near, out = refs
    total = total[...]
    for ref in near:
        half = ref.shape[0] // 2
        total = total + jnp.concatenate([ref[half:], ref[:half]])
    out[...] = (total - rows[...].astype(jnp.float32)).astype(out.dtype)


def error(total, near, rows):
    return pl.pallas_call(
        error_kernel,
        out_shape=jax.ShapeDtypeStruct(rows.shape, rows.dtype),
        in_specs=[WHOLE] * (2 + len(near)),
        out_specs=WHOLE,
        cost_estimate=waits(8),
        compiler_params=params(4),
    )(total, rows, *near)


def reduce_rows(sums):
    if lax.axis_size("latent") > DIRECT:
        return lax.psum_scatter(sums[0], "latent", scatter_dimension=0, tiled=True), []
    terms = [sums[0]] + [swap(s, "latent", mask) for s, mask in zip(sums[1:], far_masks())]
    total = add_up(terms)
    return total, [swap(total, "latent", 1)]


def adam_kernel(blocks, codes_t, m, v, *refs):
    err_refs, out, products, err = refs[:blocks], refs[blocks], refs[blocks + 1 : -1], refs[-1]
    tokens = codes_t.shape[1]
    b = 0.1 / (1.0 - 0.9**10) / tokens
    a = 0.9 / (1.0 - 0.9**10) / b
    p = 0.999 / (1.0 - 0.999**10) / b**2
    q = 0.001 / (1.0 - 0.999**10) / tokens**2 / b**2
    eps = jnp.float32(1e-8 / b)
    i, last = pl.program_id(0), pl.num_programs(0) - 1
    rows = out.shape[0]
    part = rows // len(products)

    def multiply(block, k):
        at = pl.ds(pl.multiple_of(block * rows + k * part, part), part)
        products[k][...] = jnp.dot(codes_t[at, :], err[...], preferred_element_type=jnp.float32)

    @pl.when(i == 0)
    def _():
        err[...] = stack(err_refs)
        multiply(0, 0)

    for k in range(len(products)):
        if k + 1 < len(products):
            multiply(i, k + 1)
        else:
            multiply(jnp.minimum(i + 1, last), 0)
        for r in range(0, part, 16):
            at = pl.ds(pl.multiple_of(i * rows + k * part + r, 16), 16)
            c = products[k][r : r + 16, :]
            first = m[at, :].astype(jnp.float32) * a + c
            second = v[at, :].astype(jnp.float32) * p + (c * c) * q
            second = second.astype(out.dtype)
            root = second * lax.rsqrt(second)
            step = first.astype(out.dtype) * pl.reciprocal(root + eps.astype(out.dtype), approx=True)
            out[k * part + r : k * part + r + 16, :] = step


def adam(codes_t, blocks, m, v):
    lat, half = m.shape
    rows = min(512, lat)
    parts = 4
    return pl.pallas_call(
        functools.partial(adam_kernel, len(blocks)),
        grid=(lat // rows,),
        out_shape=jax.ShapeDtypeStruct(m.shape, jnp.bfloat16),
        in_specs=[WHOLE] * (3 + len(blocks)),
        out_specs=pl.BlockSpec((rows, half), lambda i: (i, 0)),
        scratch_shapes=[pltpu.VMEM((rows // parts, half), jnp.float32)] * parts
        + [pltpu.VMEM((codes_t.shape[1], half), jnp.bfloat16)],
        compiler_params=params(8),
    )(codes_t, resident(m), resident(v), *blocks)


def per_device(acts, w_enc, b_enc, w_dec, dec_m, dec_v):
    direct = lax.axis_size("latent") <= DIRECT
    rows = near_rows(acts, 2 if direct else 1)
    blocks = spread(rows)
    part = w_enc.shape[1] // 2
    mine = [encode(blocks, w_enc, k * part, part) for k in range(2)]
    theirs = [swap(x, "dp", 1) for x in mine]
    codes, sums = [None, None], []
    for k in range(2):
        codes[k], sums = decode(
            mine[k], theirs[k], b_enc, w_dec, k * part, sums, len(blocks) if k else 1
        )
    codes_t = turn(*codes)
    total, near = reduce_rows(sums)
    err = spread(error(total, near, rows))
    return adam(codes_t, err, dec_m, dec_v)


def solution(mesh):
    in_specs = (
        P(("groups", "latent", "dp"), None),
        P(("groups", "dp"), "latent"),
        P(("groups", "latent")),
        P(("groups", "latent"), "dp"),
        P(("groups", "latent"), "dp"),
        P(("groups", "latent"), "dp"),
    )
    out_specs = P(("groups", "latent"), "dp")
    return jax.shard_map(
        per_device, mesh=mesh, in_specs=in_specs, out_specs=out_specs, check_vma=False
    )
```

time: 102 us -> 61.4 us (0.60)
  starting transfers between devices: 35.3 us -> 18 us
  Pallas kernels: 38.5 us -> 26.4 us
  local copies, waits for them, and re-layouts: 11.1 us -> 0.8 us
  waiting for transfers between devices: 17.1 us -> 15.7 us
    ppermute x23 -> x15, starting transfers between devices: 35.3 us -> 18 us  [swap(): return lax.ppermute(value, axis, [(i, i ^ mask) for i in range(n)])]
    pallas_call x5 -> x9, Pallas kernels: 38.5 us -> 26.4 us  [the longest x1 15.4 us: adam(): pl.pallas_call(functools.partial(adam_kernel, len(blocks)), grid=(lat //...]
    unnamed x12 -> x30, local copies, waits for them, and re-layouts: 11.1 us -> 0.8 us
    ppermute x23 -> x15, waiting for transfers between devices: 17.1 us -> 15.7 us  [swap(): return lax.ppermute(value, axis, [(i, i ^ mask) for i in range(n)])]
  transfers between devices with their start and end apart: 23 -> 15, of which waited for: 11 -> 9; matrix products, arithmetic and copies ran while one was open for 0% -> 0% of each run, Pallas kernels for 0% -> 10%
where the time goes in v3:
time: 61.4 us; the launch traced here: 61.1 us
  Pallas kernels  26.4 us (43%)
  starting transfers between devices  18 us (29%)
  waiting for transfers between devices  15.7 us (26%)
  local copies, waits for them, and re-layouts  0.8 us (1%)
    ppermute x15, starting transfers between devices, swap(): return lax.ppermute(value, axis, [(i, i ^ mask) for i in range(n)])  18 us
    ppermute x15, waiting for transfers between devices, swap(): return lax.ppermute(value, axis, [(i, i ^ mask) for i in range(n)])  15.7 us
    pallas_call x1, Pallas kernels, adam(): pl.pallas_call(functools.partial(adam_kernel, len(blocks)), grid=(lat //...  15.4 us
    pallas_call x2, Pallas kernels, decode(): pl.pallas_call(functools.partial(decode_kernel, first, min(512, lat), len...  4.75 us
    pallas_call x2, Pallas kernels, encode(): pl.pallas_call(functools.partial(encode_kernel, first, min(512, lat)), ou...  4.54 us
    pallas_call x1, Pallas kernels, turn(): pl.pallas_call(functools.partial(turn_kernel, min(512, lat)), out_shape=j...  1.68 us
  transfers between devices with their start and end apart: 15, of which 9 were waited for; matrix products, arithmetic and copies ran while one was open for 0% of the time, Pallas kernels for 10%

profile of v3, /device:TPU:0, one launch (start us, length us, event | category | flops | bytes accessed | tf_op | source)
XLA Modules:
  0.0 61.1 jit_solution(11372812130179867892)
XLA Ops:
  0.0 2.9 %collective-permute-start.1 = (bf16[4,1792]{1,0:T(4,128)(2,1)}, bf16[4,1792]{1,0:T(4,128)(2,1)S(1)}, u32[]{:S(2)}, u32[]{:S(2)}) collective-permute-start(bf16[4,1792]{1,0:T(4,128)(2,1)} %refs_0_.1), channel_id=1, source_target_pairs={{0,2},{1,3},{2,0},{3,1},{4,6},{5,7},{6,4},{7,5},{8,10},{9,11},{10,... | collective-permute-start | bytes 43016 | tf_op jit(solution)/shard_map/ppermute | solution.py:17
  2.9 0.2 collective-permute-start.2
  3.1 1.7 %collective-permute-done.1.refs_2_ = bf16[4,1792]{1,0:T(4,128)(2,1)S(1)} collective-permute-done((bf16[4,1792]{1,0:T(4,128)(2,1)}, bf16[4,1792]{1,0:T(4,128)(2,1)S(1)}, u32[]{:S(2)}, u32[]{:S(2)}) %collective-permute-start.1) | collective-permute-done | bytes 14368 | tf_op jit(solution)/shard_map/ppermute | solution.py:17
  4.8 1.4 %collective-permute-done.2.refs_3_ = bf16[4,1792]{1,0:T(4,128)(2,1)S(1)} collective-permute-done((bf16[4,1792]{1,0:T(4,128)(2,1)}, bf16[4,1792]{1,0:T(4,128)(2,1)S(1)}, u32[]{:S(2)}, u32[]{:S(2)}) %collective-permute-start.2) | collective-permute-done | bytes 14368 | tf_op jit(solution)/shard_map/ppermute | solution.py:17
  6.3 0.7 %copy-done.2 = bf16[4,1792]{1,0:T(4,128)(2,1)S(1)} copy-done((bf16[4,1792]{1,0:T(4,128)(2,1)S(1)}, bf16[4,1792]{1,0:T(4,128)(2,1)}, u32[]{:S(2)}) %copy-start.2) | copy-done | bytes 14360
  7.1 3.7 %collective-permute-start.5 = (bf16[16,896]{1,0:T(8,128)(2,1)S(1)}, bf16[16,896]{1,0:T(8,128)(2,1)S(1)}, u32[]{:S(2)}, u32[]{:S(2)}) collective-permute-start(bf16[16,896]{1,0:T(8,128)(2,1)S(1)} %shard_map.64.refs_0_.rows), channel_id=1, source_target_pairs={{0,12},{2,14},{4,8},{6,10},{8,4},{10,6},{12,0},{14,2},{1,13},{3,15... | collective-permute-start | bytes 86024 | tf_op jit(solution)/shard_map/ppermute | solution.py:17
  10.7 0.8 %collective-permute-start.3 = (bf16[16,896]{1,0:T(8,128)(2,1)S(1)}, bf16[16,896]{1,0:T(8,128)(2,1)S(1)}, u32[]{:S(2)}, u32[]{:S(2)}) collective-permute-start(bf16[16,896]{1,0:T(8,128)(2,1)S(1)} %shard_map.64.refs_0_.rows), channel_id=1, source_target_pairs={{0,4},{2,6},{4,0},{6,2},{8,12},{10,14},{12,8},{14,10},{1,5},{3,7},... | collective-permute-start | bytes 86024 | tf_op jit(solution)/shard_map/ppermute | solution.py:17
  11.5 1.3 %collective-permute-done.5.refs_3_ = bf16[16,896]{1,0:T(8,128)(2,1)S(1)} collective-permute-done((bf16[16,896]{1,0:T(8,128)(2,1)S(1)}, bf16[16,896]{1,0:T(8,128)(2,1)S(1)}, u32[]{:S(2)}, u32[]{:S(2)}) %collective-permute-start.5) | collective-permute-done | bytes 28704 | tf_op jit(solution)/shard_map/ppermute | solution.py:17
  12.8 2.7 %collective-permute-done.4.refs_2_ = bf16[16,896]{1,0:T(8,128)(2,1)S(1)} collective-permute-done((bf16[16,896]{1,0:T(8,128)(2,1)S(1)}, bf16[16,896]{1,0:T(8,128)(2,1)S(1)}, u32[]{:S(2)}, u32[]{:S(2)}) %collective-permute-start.4) | collective-permute-done | bytes 28704 | tf_op jit(solution)/shard_map/ppermute | solution.py:17
  15.5 2.3 %shard_map.65.mine = f32[64,4096]{1,0:T(8,128)S(1)} custom-call(bf16[16,896]{1,0:T(8,128)(2,1)S(1)} %shard_map.64.refs_0_.rows, bf16[16,896]{1,0:T(8,128)(2,1)S(1)} %collective-permute-done.3.refs_1_, bf16[16,896]{1,0:T(8,128)(2,1)S(1)} %collective-permute-done.4.refs_2_, bf16[16,896]{1,0:T(8,128)(2,1)S(1)} %collective-permute-done.5.refs_3_, ...), custom_call_target="tpu_custom_call" | custom-call | flops 2449999872 | bytes 7340032 | tf_op jit(solution)/shard_map/pallas_call | solution.py:93
  17.8 0.0 slice-start.2
  17.8 0.1 collective-permute-start.6
  17.9 2.3 %shard_map.67.mine = f32[64,4096]{1,0:T(8,128)S(1)} custom-call(bf16[16,896]{1,0:T(8,128)(2,1)S(1)} %shard_map.64.refs_0_.rows, bf16[16,896]{1,0:T(8,128)(2,1)S(1)} %collective-permute-done.3.refs_1_, bf16[16,896]{1,0:T(8,128)(2,1)S(1)} %collective-permute-done.4.refs_2_, bf16[16,896]{1,0:T(8,128)(2,1)S(1)} %collective-permute-done.5.refs_3_, ...), custom_call_target="tpu_custom_call" | custom-call | flops 2449999872 | bytes 7340032 | tf_op jit(solution)/shard_map/pallas_call | solution.py:93
  20.2 0.6 collective-permute-start.7
  20.8 2.4 %shard_map.66 = (bf16[64,4096]{1,0:T(8,128)(2,1)S(1)}, f32[64,896]{1,0:T(8,128)S(1)}) custom-call(f32[64,4096]{1,0:T(8,128)S(1)} %shard_map.65.mine, f32[64,4096]{1,0:T(8,128)S(1)} %collective-permute-done.6.theirs, f32[1,8192]{1,0:T(1,128)S(1)} %bitcast.7, bf16[8192,896]{1,0:T(8,128)(2,1)S(1)} %bitcast.2), custom_call_target="tpu_custom_call" | custom-call | flops 2449999872 | bytes 7340032 | tf_op jit(solution)/shard_map/pallas_call | solution.py:125
  23.2 0.0 slice-start.4
  23.2 2.4 %shard_map.68 = (bf16[64,4096]{1,0:T(8,128)(2,1)S(1)}, f32[16,896]{1,0:T(8,128)S(1)}, f32[16,896]{1,0:T(8,128)S(1)}, f32[16,896]{1,0:T(8,128)S(1)}, f32[16,896]{1,0:T(8,128)S(1)}) custom-call(f32[64,4096]{1,0:T(8,128)S(1)} %shard_map.67.mine, f32[64,4096]{1,0:T(8,128)S(1)} %collective-permute-done.7.theirs, f32[1,8192]{1,0:T(1,128)S(1)} %bitcast.8, ...), custom_call_target="tpu_custom_call" | custom-call | flops 2449999872 | bytes 7340032 | tf_op jit(solution)/shard_map/pallas_call | solution.py:125
  25.6 0.2 collective-permute-start.8
  25.8 1.9 %collective-permute-start.9 = (f32[16,896]{1,0:T(8,128)S(1)}, f32[16,896]{1,0:T(8,128)S(1)}, u32[]{:S(2)}, u32[]{:S(2)}) collective-permute-start(f32[16,896]{1,0:T(8,128)S(1)} %get-tuple-element.17), channel_id=1, source_target_pairs={{0,8},{2,10},{4,12},{6,14},{8,0},{10,2},{12,4},{14,6},{1,9},{3,11}... | collective-permute-start | bytes 172040 | tf_op jit(solution)/shard_map/ppermute | solution.py:17
  27.8 2.3 %collective-permute-start.10 = (f32[16,896]{1,0:T(8,128)S(1)}, f32[16,896]{1,0:T(8,128)S(1)}, u32[]{:S(2)}, u32[]{:S(2)}) collective-permute-start(f32[16,896]{1,0:T(8,128)S(1)} %get-tuple-element.18), channel_id=1, source_target_pairs={{0,12},{2,14},{4,8},{6,10},{8,4},{10,6},{12,0},{14,2},{1,13},{3,15... | collective-permute-start | bytes 172040 | tf_op jit(solution)/shard_map/ppermute | solution.py:17
  30.0 0.7 %collective-permute-done.8.refs_1_ = f32[16,896]{1,0:T(8,128)S(1)} collective-permute-done((f32[16,896]{1,0:T(8,128)S(1)}, f32[16,896]{1,0:T(8,128)S(1)}, u32[]{:S(2)}, u32[]{:S(2)}) %collective-permute-start.8) | collective-permute-done | bytes 57376 | tf_op jit(solution)/shard_map/ppermute | solution.py:17
  30.8 0.7 %collective-permute-done.9.refs_2_ = f32[16,896]{1,0:T(8,128)S(1)} collective-permute-done((f32[16,896]{1,0:T(8,128)S(1)}, f32[16,896]{1,0:T(8,128)S(1)}, u32[]{:S(2)}, u32[]{:S(2)}) %collective-permute-start.9) | collective-permute-done | bytes 57376 | tf_op jit(solution)/shard_map/ppermute | solution.py:17
  31.5 2.3 %collective-permute-done.10.refs_3_ = f32[16,896]{1,0:T(8,128)S(1)} collective-permute-done((f32[16,896]{1,0:T(8,128)S(1)}, f32[16,896]{1,0:T(8,128)S(1)}, u32[]{:S(2)}, u32[]{:S(2)}) %collective-permute-start.10) | collective-permute-done | bytes 57376 | tf_op jit(solution)/shard_map/ppermute | solution.py:17
  33.8 0.0 slice-start.11
  33.9 0.9 %collective-permute-start.11 = (f32[16,896]{1,0:T(8,128)S(1)}, f32[16,896]{1,0:T(8,128)S(1)}, u32[]{:S(2)}, u32[]{:S(2)}) collective-permute-start(f32[16,896]{1,0:T(8,128)S(1)} %shard_map.70.total), channel_id=1, source_target_pairs={{0,2},{2,0},{4,6},{6,4},{8,10},{10,8},{12,14},{14,12},{1,3},{3,1},... | collective-permute-start | bytes 172040 | tf_op jit(solution)/shard_map/ppermute | solution.py:17
  34.7 3.4 %collective-permute-done.11.refs_0_ = f32[16,896]{1,0:T(8,128)S(1)} collective-permute-done((f32[16,896]{1,0:T(8,128)S(1)}, f32[16,896]{1,0:T(8,128)S(1)}, u32[]{:S(2)}, u32[]{:S(2)}) %collective-permute-start.11) | collective-permute-done | bytes 57376 | tf_op jit(solution)/shard_map/ppermute | solution.py:17
  38.1 2.5 %collective-permute-start.14 = (bf16[16,896]{1,0:T(8,128)(2,1)S(1)}, bf16[16,896]{1,0:T(8,128)(2,1)S(1)}, u32[]{:S(2)}, u32[]{:S(2)}) collective-permute-start(bf16[16,896]{1,0:T(8,128)(2,1)S(1)} %shard_map.71.refs_0_), channel_id=1, source_target_pairs={{0,12},{2,14},{4,8},{6,10},{8,4},{10,6},{12,0},{14,2},{1,13},{3,15... | collective-permute-start | bytes 86024 | tf_op jit(solution)/shard_map/ppermute | solution.py:17
  40.6 0.4 collective-permute-start.13
  41.0 1.6 %collective-permute-start.12 = (bf16[16,896]{1,0:T(8,128)(2,1)S(1)}, bf16[16,896]{1,0:T(8,128)(2,1)S(1)}, u32[]{:S(2)}, u32[]{:S(2)}) collective-permute-start(bf16[16,896]{1,0:T(8,128)(2,1)S(1)} %shard_map.71.refs_0_), channel_id=1, source_target_pairs={{0,4},{2,6},{4,0},{6,2},{8,12},{10,14},{12,8},{14,10},{1,5},{3,7},... | collective-permute-start | bytes 86024 | tf_op jit(solution)/shard_map/ppermute | solution.py:17
  42.6 1.7 %shard_map.69.codes_t = bf16[8192,64]{1,0:T(8,128)(2,1)S(1)} custom-call(bf16[64,4096]{1,0:T(8,128)(2,1)S(1)} %get-tuple-element.12.refs_0_, bf16[64,4096]{1,0:T(8,128)(2,1)S(1)} %get-tuple-element.14.refs_1_), custom_call_target="tpu_custom_call" | custom-call | flops 1400000000 | bytes 4194304 | tf_op jit(solution)/shard_map/pallas_call | solution.py:151
  44.3 1.4 %collective-permute-done.13.refs_2_ = bf16[16,896]{1,0:T(8,128)(2,1)S(1)} collective-permute-done((bf16[16,896]{1,0:T(8,128)(2,1)S(1)}, bf16[16,896]{1,0:T(8,128)(2,1)S(1)}, u32[]{:S(2)}, u32[]{:S(2)}) %collective-permute-start.13) | collective-permute-done | bytes 28704 | tf_op jit(solution)/shard_map/ppermute | solution.py:17
  45.7 15.4 %shard_map.72 = bf16[8192,896]{1,0:T(8,128)(2,1)} custom-call(bf16[8192,64]{1,0:T(8,128)(2,1)S(1)} %shard_map.69.codes_t, bf16[8192,896]{1,0:T(8,128)(2,1)S(1)} %bitcast.4, bf16[8192,896]{1,0:T(8,128)(2,1)S(1)} %bitcast.6, bf16[16,896]{1,0:T(8,128)(2,1)S(1)} %shard_map.71.refs_0_, bf16[16,896]{1,0:T(8,128)(2,1)S(1)} %collective-permute-done.12.refs_1_, ...), custom_call_target="tpu_custom_call" | custom-call | tf_op jit(solution)/shard_map/pallas_call | solution.py:249
  (40 shorter events, 0.1 us)
Async XLA Ops:
  0.0 15.5 %copy-start = (bf16[896,8192]{1,0:T(8,128)(2,1)S(1)}, bf16[896,8192]{1,0:T(8,128)(2,1)}, u32[]{:S(2)}) copy-start(bf16[896,8192]{1,0:T(8,128)(2,1)} %refs_4_.3) | copy-start | bytes 44040196
  0.0 4.8 %collective-permute-start.1 = (bf16[4,1792]{1,0:T(4,128)(2,1)}, bf16[4,1792]{1,0:T(4,128)(2,1)S(1)}, u32[]{:S(2)}, u32[]{:S(2)}) collective-permute-start(bf16[4,1792]{1,0:T(4,128)(2,1)} %refs_0_.1), channel_id=1, source_target_pairs={{0,2},{1,3},{2,0},{3,1},{4,6},{5,7},{6,4},{7,5},{8,10},{9,11},{10,... | collective-permute-start | bytes 43016 | tf_op jit(solution)/shard_map/ppermute | solution.py:17
  2.9 1.9 %collective-permute-start = (bf16[4,1792]{1,0:T(4,128)(2,1)}, bf16[4,1792]{1,0:T(4,128)(2,1)S(1)}, u32[]{:S(2)}, u32[]{:S(2)}) collective-permute-start(bf16[4,1792]{1,0:T(4,128)(2,1)} %refs_0_.1), channel_id=1, source_target_pairs={{0,1},{1,0},{2,3},{3,2},{4,5},{5,4},{6,7},{7,6},{8,9},{9,8},{10,11... | collective-permute-start | bytes 43016 | tf_op jit(solution)/shard_map/ppermute | solution.py:17
  2.9 3.4 %collective-permute-start.2 = (bf16[4,1792]{1,0:T(4,128)(2,1)}, bf16[4,1792]{1,0:T(4,128)(2,1)S(1)}, u32[]{:S(2)}, u32[]{:S(2)}) collective-permute-start(bf16[4,1792]{1,0:T(4,128)(2,1)} %refs_0_.1), channel_id=1, source_target_pairs={{0,3},{1,2},{2,1},{3,0},{4,7},{5,6},{6,5},{7,4},{8,11},{9,10},{10,... | collective-permute-start | bytes 43016 | tf_op jit(solution)/shard_map/ppermute | solution.py:17
  6.3 0.7 %copy-start.2 = (bf16[4,1792]{1,0:T(4,128)(2,1)S(1)}, bf16[4,1792]{1,0:T(4,128)(2,1)}, u32[]{:S(2)}) copy-start(bf16[4,1792]{1,0:T(4,128)(2,1)} %refs_0_.1) | copy-start | bytes 43012
  7.0 13.7 %slice-start = ((s8[14680064]{0:T(1024)(128)(4,1)}), s8[4194304]{0:T(1024)(128)(4,1)S(1)}, s32[]{:S(2)}) async-start(s8[14680064]{0:T(1024)(128)(4,1)} %bitcast.1), calls=%async_computation | async-start | bytes 8388608
  7.0 13.7 %slice-start.1 = ((s8[14680064]{0:T(1024)(128)(4,1)}), s8[4194304]{0:T(1024)(128)(4,1)S(1)}, s32[]{:S(2)}) async-start(s8[14680064]{0:T(1024)(128)(4,1)} %bitcast.1), calls=%async_computation.1 | async-start | bytes 8388608
  7.1 13.7 %copy-start.1 = (f32[8192]{0:T(1024)S(1)}, f32[8192]{0:T(1024)}, u32[]{:S(2)}) copy-start(f32[8192]{0:T(1024)} %param.8) | copy-start | bytes 98308
  7.1 5.7 %collective-permute-start.5 = (bf16[16,896]{1,0:T(8,128)(2,1)S(1)}, bf16[16,896]{1,0:T(8,128)(2,1)S(1)}, u32[]{:S(2)}, u32[]{:S(2)}) collective-permute-start(bf16[16,896]{1,0:T(8,128)(2,1)S(1)} %shard_map.64.refs_0_.rows), channel_id=1, source_target_pairs={{0,12},{2,14},{4,8},{6,10},{8,4},{10,6},{12,0},{14,2},{1,13},{3,15... | collective-permute-start | bytes 86024 | tf_op jit(solution)/shard_map/ppermute | solution.py:17
  10.7 4.8 %collective-permute-start.4 = (bf16[16,896]{1,0:T(8,128)(2,1)S(1)}, bf16[16,896]{1,0:T(8,128)(2,1)S(1)}, u32[]{:S(2)}, u32[]{:S(2)}) collective-permute-start(bf16[16,896]{1,0:T(8,128)(2,1)S(1)} %shard_map.64.refs_0_.rows), channel_id=1, source_target_pairs={{0,8},{2,10},{4,12},{6,14},{8,0},{10,2},{12,4},{14,6},{1,9},{3,11}... | collective-permute-start | bytes 86024 | tf_op jit(solution)/shard_map/ppermute | solution.py:17
  10.7 4.8 %collective-permute-start.3 = (bf16[16,896]{1,0:T(8,128)(2,1)S(1)}, bf16[16,896]{1,0:T(8,128)(2,1)S(1)}, u32[]{:S(2)}, u32[]{:S(2)}) collective-permute-start(bf16[16,896]{1,0:T(8,128)(2,1)S(1)} %shard_map.64.refs_0_.rows), channel_id=1, source_target_pairs={{0,4},{2,6},{4,0},{6,2},{8,12},{10,14},{12,8},{14,10},{1,5},{3,7},... | collective-permute-start | bytes 86024 | tf_op jit(solution)/shard_map/ppermute | solution.py:17
  17.8 3.0 %slice-start.2 = ((s8[14680064]{0:T(1024)(128)(4,1)}), s8[4194304]{0:T(1024)(128)(4,1)S(1)}, s32[]{:S(2)}) async-start(s8[14680064]{0:T(1024)(128)(4,1)} %bitcast.1), calls=%async_computation.2 | async-start | bytes 8388608
  17.8 3.0 %slice-start.3 = ((s8[14680064]{0:T(1024)(128)(4,1)}), s8[2097152]{0:T(1024)(128)(4,1)S(1)}, s32[]{:S(2)}) async-start(s8[14680064]{0:T(1024)(128)(4,1)} %bitcast.1), calls=%async_computation.3 | async-start | bytes 4194304
  17.8 2.9 %collective-permute-start.6 = (f32[64,4096]{1,0:T(8,128)S(1)}, f32[64,4096]{1,0:T(8,128)S(1)}, u32[]{:S(2)}, u32[]{:S(2)}) collective-permute-start(f32[64,4096]{1,0:T(8,128)S(1)} %shard_map.65.mine), channel_id=1, source_target_pairs={{0,1},{1,0},{2,3},{3,2},{4,5},{5,4},{6,7},{7,6},{8,9},{9,8},{10,11... | collective-permute-start | bytes 3145736 | tf_op jit(solution)/shard_map/ppermute | solution.py:17
  20.2 3.0 %collective-permute-start.7 = (f32[64,4096]{1,0:T(8,128)S(1)}, f32[64,4096]{1,0:T(8,128)S(1)}, u32[]{:S(2)}, u32[]{:S(2)}) collective-permute-start(f32[64,4096]{1,0:T(8,128)S(1)} %shard_map.67.mine), channel_id=1, source_target_pairs={{0,1},{1,0},{2,3},{3,2},{4,5},{5,4},{6,7},{7,6},{8,9},{9,8},{10,11... | collective-permute-start | bytes 3145736 | tf_op jit(solution)/shard_map/ppermute | solution.py:17
  23.2 22.5 %slice-start.4 = ((s8[14680064]{0:T(1024)(128)(4,1)}), s8[2097152]{0:T(1024)(128)(4,1)S(1)}, s32[]{:S(2)}) async-start(s8[14680064]{0:T(1024)(128)(4,1)} %bitcast.3), calls=%async_computation.4 | async-start | bytes 4194304
  23.2 22.5 %slice-start.5 = ((s8[14680064]{0:T(1024)(128)(4,1)}), s8[4194304]{0:T(1024)(128)(4,1)S(1)}, s32[]{:S(2)}) async-start(s8[14680064]{0:T(1024)(128)(4,1)} %bitcast.3), calls=%async_computation.5 | async-start | bytes 8388608
  23.2 22.5 %slice-start.8 = ((s8[14680064]{0:T(1024)(128)(4,1)}), s8[4194304]{0:T(1024)(128)(4,1)S(1)}, s32[]{:S(2)}) async-start(s8[14680064]{0:T(1024)(128)(4,1)} %bitcast.5), calls=%async_computation.8 | async-start | bytes 8388608
  23.2 22.5 %slice-start.9 = ((s8[14680064]{0:T(1024)(128)(4,1)}), s8[4194304]{0:T(1024)(128)(4,1)S(1)}, s32[]{:S(2)}) async-start(s8[14680064]{0:T(1024)(128)(4,1)} %bitcast.5), calls=%async_computation.9 | async-start | bytes 8388608
  25.6 5.2 %collective-permute-start.8 = (f32[16,896]{1,0:T(8,128)S(1)}, f32[16,896]{1,0:T(8,128)S(1)}, u32[]{:S(2)}, u32[]{:S(2)}) collective-permute-start(f32[16,896]{1,0:T(8,128)S(1)} %get-tuple-element.16), channel_id=1, source_target_pairs={{0,4},{2,6},{4,0},{6,2},{8,12},{10,14},{12,8},{14,10},{1,5},{3,7},... | collective-permute-start | bytes 172040 | tf_op jit(solution)/shard_map/ppermute | solution.py:17
  25.8 5.7 %collective-permute-start.9 = (f32[16,896]{1,0:T(8,128)S(1)}, f32[16,896]{1,0:T(8,128)S(1)}, u32[]{:S(2)}, u32[]{:S(2)}) collective-permute-start(f32[16,896]{1,0:T(8,128)S(1)} %get-tuple-element.17), channel_id=1, source_target_pairs={{0,8},{2,10},{4,12},{6,14},{8,0},{10,2},{12,4},{14,6},{1,9},{3,11}... | collective-permute-start | bytes 172040 | tf_op jit(solution)/shard_map/ppermute | solution.py:17
  27.8 6.0 %collective-permute-start.10 = (f32[16,896]{1,0:T(8,128)S(1)}, f32[16,896]{1,0:T(8,128)S(1)}, u32[]{:S(2)}, u32[]{:S(2)}) collective-permute-start(f32[16,896]{1,0:T(8,128)S(1)} %get-tuple-element.18), channel_id=1, source_target_pairs={{0,12},{2,14},{4,8},{6,10},{8,4},{10,6},{12,0},{14,2},{1,13},{3,15... | collective-permute-start | bytes 172040 | tf_op jit(solution)/shard_map/ppermute | solution.py:17
  33.8 11.9 %slice-start.6 = ((s8[14680064]{0:T(1024)(128)(4,1)}), s8[4194304]{0:T(1024)(128)(4,1)S(1)}, s32[]{:S(2)}) async-start(s8[14680064]{0:T(1024)(128)(4,1)} %bitcast.3), calls=%async_computation.6 | async-start | bytes 8388608
  33.8 11.9 %slice-start.10 = ((s8[14680064]{0:T(1024)(128)(4,1)}), s8[4194304]{0:T(1024)(128)(4,1)S(1)}, s32[]{:S(2)}) async-start(s8[14680064]{0:T(1024)(128)(4,1)} %bitcast.5), calls=%async_computation.10 | async-start | bytes 8388608
  33.8 11.9 %slice-start.7 = ((s8[14680064]{0:T(1024)(128)(4,1)}), s8[4194304]{0:T(1024)(128)(4,1)S(1)}, s32[]{:S(2)}) async-start(s8[14680064]{0:T(1024)(128)(4,1)} %bitcast.3), calls=%async_computation.7 | async-start | bytes 8388608
  33.8 11.9 %slice-start.11 = ((s8[14680064]{0:T(1024)(128)(4,1)}), s8[2097152]{0:T(1024)(128)(4,1)S(1)}, s32[]{:S(2)}) async-start(s8[14680064]{0:T(1024)(128)(4,1)} %bitcast.5), calls=%async_computation.11 | async-start | bytes 4194304
  33.9 4.2 %collective-permute-start.11 = (f32[16,896]{1,0:T(8,128)S(1)}, f32[16,896]{1,0:T(8,128)S(1)}, u32[]{:S(2)}, u32[]{:S(2)}) collective-permute-start(f32[16,896]{1,0:T(8,128)S(1)} %shard_map.70.total), channel_id=1, source_target_pairs={{0,2},{2,0},{4,6},{6,4},{8,10},{10,8},{12,14},{14,12},{1,3},{3,1},... | collective-permute-start | bytes 172040 | tf_op jit(solution)/shard_map/ppermute | solution.py:17
  38.1 6.1 %collective-permute-start.14 = (bf16[16,896]{1,0:T(8,128)(2,1)S(1)}, bf16[16,896]{1,0:T(8,128)(2,1)S(1)}, u32[]{:S(2)}, u32[]{:S(2)}) collective-permute-start(bf16[16,896]{1,0:T(8,128)(2,1)S(1)} %shard_map.71.refs_0_), channel_id=1, source_target_pairs={{0,12},{2,14},{4,8},{6,10},{8,4},{10,6},{12,0},{14,2},{1,13},{3,15... | collective-permute-start | bytes 86024 | tf_op jit(solution)/shard_map/ppermute | solution.py:17
  40.6 5.1 %collective-permute-start.13 = (bf16[16,896]{1,0:T(8,128)(2,1)S(1)}, bf16[16,896]{1,0:T(8,128)(2,1)S(1)}, u32[]{:S(2)}, u32[]{:S(2)}) collective-permute-start(bf16[16,896]{1,0:T(8,128)(2,1)S(1)} %shard_map.71.refs_0_), channel_id=1, source_target_pairs={{0,8},{2,10},{4,12},{6,14},{8,0},{10,2},{12,4},{14,6},{1,9},{3,11}... | collective-permute-start | bytes 86024 | tf_op jit(solution)/shard_map/ppermute | solution.py:17
  41.0 4.7 %collective-permute-start.12 = (bf16[16,896]{1,0:T(8,128)(2,1)S(1)}, bf16[16,896]{1,0:T(8,128)(2,1)S(1)}, u32[]{:S(2)}, u32[]{:S(2)}) collective-permute-start(bf16[16,896]{1,0:T(8,128)(2,1)S(1)} %shard_map.71.refs_0_), channel_id=1, source_target_pairs={{0,4},{2,6},{4,0},{6,2},{8,12},{10,14},{12,8},{14,10},{1,5},{3,7},... | collective-permute-start | bytes 86024 | tf_op jit(solution)/shard_map/ppermute | solution.py:17

commit v4 on v3

--- a/solution.py
+++ b/solution.py
@@ -57,9 +57,21 @@
         write([i + c for i in pairs for c in (1, 0)], half)
 
 
+def copy_kernel(x, out):
+    out[...] = x[...]
+
+
 def near_rows(acts, near):
     axes = ("latent", "dp")
-    rows = [acts] + [swap(acts, axes, mask) for mask in range(1, 2 * near)]
+    own = pl.pallas_call(
+        copy_kernel,
+        out_shape=jax.ShapeDtypeStruct(acts.shape, acts.dtype),
+        in_specs=[WHOLE],
+        out_specs=WHOLE,
+        cost_estimate=waits(1),
+        compiler_params=params(4),
+    )(acts)
+    rows = [own] + [swap(acts, axes, mask) for mask in range(1, 2 * near)]
     return pl.pallas_call(
         near_kernel,
         out_shape=jax.ShapeDtypeStruct((len(rows) * acts.shape[0], acts.shape[1] // 2), acts.dtype),
@@ -116,7 +128,7 @@
     total = lax.fori_loop(0, lat // chunk, step, total)
     rows = tokens // len(out)
     for j, ref in enumerate(out):
-        ref[...] = total[j * rows : (j + 1) * rows]
+        ref[...] = total[j * rows : (j + 1) * rows].astype(ref.dtype)
 
 
 def decode(mine, theirs, bias, w_dec, first, given, parts):
@@ -125,7 +137,10 @@
     codes, *sums = pl.pallas_call(
         functools.partial(decode_kernel, first, min(512, lat), len(given)),
         out_shape=[jax.ShapeDtypeStruct((tokens, lat), jnp.bfloat16)]
-        + [jax.ShapeDtypeStruct((tokens // parts, half), jnp.float32)] * parts,
+        + [
+            jax.ShapeDtypeStruct((tokens // parts, half), jnp.bfloat16 if j else jnp.float32)
+            for j in range(parts)
+        ],
         in_specs=[WHOLE] * (4 + len(given)),
         out_specs=[WHOLE] * (1 + parts),
         cost_estimate=waits(7),
@@ -158,20 +173,25 @@
     )(*codes)
 
 
-def sum_kernel(*refs):
-    *terms, out = refs
-    total = terms[0][...]
-    for ref in terms[1:]:
+def sum_kernel(own, *refs):
+    *terms, out, sent = refs
+    total = own[...]
+    for ref in terms:
         total = total + ref[...]
     out[...] = total
+    sent[...] = total.astype(sent.dtype)
 
 
 def add_up(terms):
+    shape = terms[0].shape
     return pl.pallas_call(
         sum_kernel,
-        out_shape=jax.ShapeDtypeStruct(terms[0].shape, jnp.float32),
+        out_shape=[
+            jax.ShapeDtypeStruct(shape, jnp.float32),
+            jax.ShapeDtypeStruct(shape, jnp.bfloat16),
+        ],
         in_specs=[WHOLE] * len(terms),
-        out_specs=WHOLE,
+        out_specs=[WHOLE] * 2,
         cost_estimate=waits(8),
         compiler_params=params(4),
     )(*terms)
@@ -182,7 +202,8 @@
     total = total[...]
     for ref in near:
         half = ref.shape[0] // 2
-        total = total + jnp.concatenate([ref[half:], ref[:half]])
+        term = ref[...].astype(jnp.float32)
+        total = total + jnp.concatenate([term[half:], term[:half]])
     out[...] = (total - rows[...].astype(jnp.float32)).astype(out.dtype)
 
 
@@ -201,8 +222,8 @@
     if lax.axis_size("latent") > DIRECT:
         return lax.psum_scatter(sums[0], "latent", scatter_dimension=0, tiled=True), []
     terms = [sums[0]] + [swap(s, "latent", mask) for s, mask in zip(sums[1:], far_masks())]
-    total = add_up(terms)
-    return total, [swap(total, "latent", 1)]
+    total, sent = add_up(terms)
+    return total, [swap(sent, "latent", 1)]
 
 
 def adam_kernel(blocks, codes_t, m, v, *refs):
@@ -212,7 +233,7 @@
     a = 0.9 / (1.0 - 0.9**10) / b
     p = 0.999 / (1.0 - 0.999**10) / b**2
     q = 0.001 / (1.0 - 0.999**10) / tokens**2 / b**2
-    eps = jnp.float32(1e-8 / b)
+    eps = 1e-8 / b
     i, last = pl.program_id(0), pl.num_programs(0) - 1
     rows = out.shape[0]
     part = rows // len(products)
@@ -236,16 +257,15 @@
             c = products[k][r : r + 16, :]
             first = m[at, :].astype(jnp.float32) * a + c
             second = v[at, :].astype(jnp.float32) * p + (c * c) * q
-            second = second.astype(out.dtype)
             root = second * lax.rsqrt(second)
-            step = first.astype(out.dtype) * pl.reciprocal(root + eps.astype(out.dtype), approx=True)
-            out[k * part + r : k * part + r + 16, :] = step
+            step = first * pl.reciprocal(root + eps, approx=True)
+            out[k * part + r : k * part + r + 16, :] = step.astype(out.dtype)
 
 
 def adam(codes_t, blocks, m, v):
     lat, half = m.shape
-    rows = min(512, lat)
-    parts = 4
+    rows = min(1024, lat)
+    parts = 2
     return pl.pallas_call(
         functools.partial(adam_kernel, len(blocks)),
         grid=(lat // rows,),
@@ -254,7 +274,7 @@
         out_specs=pl.BlockSpec((rows, half), lambda i: (i, 0)),
         scratch_shapes=[pltpu.VMEM((rows // parts, half), jnp.float32)] * parts
         + [pltpu.VMEM((codes_t.shape[1], half), jnp.bfloat16)],
-        compiler_params=params(8),
+        compiler_params=params(12),
     )(codes_t, resident(m), resident(v), *blocks)
 
 

time: 61.4 us -> 60.8 us (level)
  waiting for transfers between devices: 15.7 us -> 14.1 us
  local copies, waits for them, and re-layouts: 0.8 us -> 1.53 us
    ppermute x15, waiting for transfers between devices: 15.7 us -> 14.1 us  [swap(): return lax.ppermute(value, axis, [(i, i ^ mask) for i in range(n)])]
    unnamed x30, local copies, waits for them, and re-layouts: 0.8 us -> 1.53 us
  transfers between devices with their start and end apart: 15 -> 15, of which waited for: 9 -> 8; matrix products, arithmetic and copies ran while one was open for 0% -> 0% of each run, Pallas kernels for 10% -> 10%
where the time goes in v4:
time: 60.8 us; the launch traced here: 60.6 us
  Pallas kernels  27 us (44%)
  starting transfers between devices  17.7 us (29%)
  waiting for transfers between devices  14.1 us (23%)
  local copies, waits for them, and re-layouts  1.53 us (3%)
    ppermute x15, starting transfers between devices, swap(): return lax.ppermute(value, axis, [(i, i ^ mask) for i in range(n)])  17.7 us
    pallas_call x1, Pallas kernels, adam(): pl.pallas_call(functools.partial(adam_kernel, len(blocks)), grid=(lat //...  16 us
    ppermute x15, waiting for transfers between devices, swap(): return lax.ppermute(value, axis, [(i, i ^ mask) for i in range(n)])  14.1 us
    pallas_call x2, Pallas kernels, decode(): pl.pallas_call(functools.partial(decode_kernel, first, min(512, lat), len...  4.75 us
    pallas_call x2, Pallas kernels, encode(): pl.pallas_call(functools.partial(encode_kernel, first, min(512, lat)), ou...  4.54 us
    pallas_call x1, Pallas kernels, turn(): pl.pallas_call(functools.partial(turn_kernel, min(512, lat)), out_shape=j...  1.68 us
    unnamed x30, local copies, waits for them, and re-layouts  1.53 us
  transfers between devices with their start and end apart: 15, of which 8 were waited for; matrix products, arithmetic and copies ran while one was open for 0% of the time, Pallas kernels for 10%

profile of v4, /device:TPU:0, one launch (start us, length us, event | category | flops | bytes accessed | tf_op | source)
XLA Modules:
  0.0 60.6 jit_solution(1887913223782553177)
XLA Ops:
  0.0 0.5 collective-permute-start
  0.5 2.6 %collective-permute-start.2 = (bf16[4,1792]{1,0:T(4,128)(2,1)}, bf16[4,1792]{1,0:T(4,128)(2,1)S(1)}, u32[]{:S(2)}, u32[]{:S(2)}) collective-permute-start(bf16[4,1792]{1,0:T(4,128)(2,1)} %x.1), channel_id=1, source_target_pairs={{0,3},{1,2},{2,1},{3,0},{4,7},{5,6},{6,5},{7,4},{8,11},{9,10},{10,... | collective-permute-start | bytes 43016 | tf_op jit(solution)/shard_map/ppermute | solution.py:17
  3.1 0.1 collective-permute-start.1
  3.1 1.5 %copy-done.2 = bf16[4,1792]{1,0:T(4,128)(2,1)S(1)} copy-done((bf16[4,1792]{1,0:T(4,128)(2,1)S(1)}, bf16[4,1792]{1,0:T(4,128)(2,1)}, u32[]{:S(2)}) %copy-start.2) | copy-done | bytes 14360
  4.6 0.1 collective-permute-done.2.refs_3_
  4.7 2.3 %collective-permute-done.1.refs_2_ = bf16[4,1792]{1,0:T(4,128)(2,1)S(1)} collective-permute-done((bf16[4,1792]{1,0:T(4,128)(2,1)}, bf16[4,1792]{1,0:T(4,128)(2,1)S(1)}, u32[]{:S(2)}, u32[]{:S(2)}) %collective-permute-start.1) | collective-permute-done | bytes 14368 | tf_op jit(solution)/shard_map/ppermute | solution.py:17
  7.0 0.0 slice-start
  7.0 3.7 %collective-permute-start.5 = (bf16[16,896]{1,0:T(8,128)(2,1)S(1)}, bf16[16,896]{1,0:T(8,128)(2,1)S(1)}, u32[]{:S(2)}, u32[]{:S(2)}) collective-permute-start(bf16[16,896]{1,0:T(8,128)(2,1)S(1)} %shard_map.65.refs_0_.rows), channel_id=1, source_target_pairs={{0,12},{2,14},{4,8},{6,10},{8,4},{10,6},{12,0},{14,2},{1,13},{3,15... | collective-permute-start | bytes 86024 | tf_op jit(solution)/shard_map/ppermute | solution.py:17
  10.7 0.8 %collective-permute-start.3 = (bf16[16,896]{1,0:T(8,128)(2,1)S(1)}, bf16[16,896]{1,0:T(8,128)(2,1)S(1)}, u32[]{:S(2)}, u32[]{:S(2)}) collective-permute-start(bf16[16,896]{1,0:T(8,128)(2,1)S(1)} %shard_map.65.refs_0_.rows), channel_id=1, source_target_pairs={{0,4},{2,6},{4,0},{6,2},{8,12},{10,14},{12,8},{14,10},{1,5},{3,7},... | collective-permute-start | bytes 86024 | tf_op jit(solution)/shard_map/ppermute | solution.py:17
  11.5 1.3 %collective-permute-done.5.refs_3_ = bf16[16,896]{1,0:T(8,128)(2,1)S(1)} collective-permute-done((bf16[16,896]{1,0:T(8,128)(2,1)S(1)}, bf16[16,896]{1,0:T(8,128)(2,1)S(1)}, u32[]{:S(2)}, u32[]{:S(2)}) %collective-permute-start.5) | collective-permute-done | bytes 28704 | tf_op jit(solution)/shard_map/ppermute | solution.py:17
  12.8 2.7 %collective-permute-done.4.refs_2_ = bf16[16,896]{1,0:T(8,128)(2,1)S(1)} collective-permute-done((bf16[16,896]{1,0:T(8,128)(2,1)S(1)}, bf16[16,896]{1,0:T(8,128)(2,1)S(1)}, u32[]{:S(2)}, u32[]{:S(2)}) %collective-permute-start.4) | collective-permute-done | bytes 28704 | tf_op jit(solution)/shard_map/ppermute | solution.py:17
  15.5 2.3 %shard_map.66.mine = f32[64,4096]{1,0:T(8,128)S(1)} custom-call(bf16[16,896]{1,0:T(8,128)(2,1)S(1)} %shard_map.65.refs_0_.rows, bf16[16,896]{1,0:T(8,128)(2,1)S(1)} %collective-permute-done.3.refs_1_, bf16[16,896]{1,0:T(8,128)(2,1)S(1)} %collective-permute-done.4.refs_2_, bf16[16,896]{1,0:T(8,128)(2,1)S(1)} %collective-permute-done.5.refs_3_, ...), custom_call_target="tpu_custom_call" | custom-call | flops 2449999872 | bytes 7340032 | tf_op jit(solution)/shard_map/pallas_call | solution.py:105
  17.8 0.0 slice-start.2
  17.8 0.1 collective-permute-start.6
  17.9 2.3 %shard_map.68.mine = f32[64,4096]{1,0:T(8,128)S(1)} custom-call(bf16[16,896]{1,0:T(8,128)(2,1)S(1)} %shard_map.65.refs_0_.rows, bf16[16,896]{1,0:T(8,128)(2,1)S(1)} %collective-permute-done.3.refs_1_, bf16[16,896]{1,0:T(8,128)(2,1)S(1)} %collective-permute-done.4.refs_2_, bf16[16,896]{1,0:T(8,128)(2,1)S(1)} %collective-permute-done.5.refs_3_, ...), custom_call_target="tpu_custom_call" | custom-call | flops 2449999872 | bytes 7340032 | tf_op jit(solution)/shard_map/pallas_call | solution.py:105
  20.1 0.6 collective-permute-start.7
  20.7 2.4 %shard_map.67 = (bf16[64,4096]{1,0:T(8,128)(2,1)S(1)}, f32[64,896]{1,0:T(8,128)S(1)}) custom-call(f32[64,4096]{1,0:T(8,128)S(1)} %shard_map.66.mine, f32[64,4096]{1,0:T(8,128)S(1)} %collective-permute-done.6.theirs, f32[1,8192]{1,0:T(1,128)S(1)} %bitcast.7, bf16[8192,896]{1,0:T(8,128)(2,1)S(1)} %bitcast.2), custom_call_target="tpu_custom_call" | custom-call | flops 2449999872 | bytes 7340032 | tf_op jit(solution)/shard_map/pallas_call | solution.py:137
  23.1 0.0 slice-start.4
  23.2 0.0 slice-start.8
  23.2 2.4 %shard_map.69 = (bf16[64,4096]{1,0:T(8,128)(2,1)S(1)}, f32[16,896]{1,0:T(8,128)S(1)}, bf16[16,896]{1,0:T(8,128)(2,1)S(1)}, bf16[16,896]{1,0:T(8,128)(2,1)S(1)}, bf16[16,896]{1,0:T(8,128)(2,1)S(1)}) custom-call(f32[64,4096]{1,0:T(8,128)S(1)} %shard_map.68.mine, f32[64,4096]{1,0:T(8,128)S(1)} %collective-permute-done.7.theirs, f32[1,8192]{1,0:T(1,128)S(1)} %bitcast.8, ...), custom_call_target="tpu_custom_call" | custom-call | flops 2449999872 | bytes 7340032 | tf_op jit(solution)/shard_map/pallas_call | solution.py:137
  25.6 0.1 collective-permute-start.8
  25.6 2.1 %collective-permute-start.9 = (bf16[16,896]{1,0:T(8,128)(2,1)S(1)}, bf16[16,896]{1,0:T(8,128)(2,1)S(1)}, u32[]{:S(2)}, u32[]{:S(2)}) collective-permute-start(bf16[16,896]{1,0:T(8,128)(2,1)S(1)} %get-tuple-element.19), channel_id=1, source_target_pairs={{0,8},{2,10},{4,12},{6,14},{8,0},{10,2},{12,4},{14,6},{1,9},{3,11}... | collective-permute-start | bytes 86024 | tf_op jit(solution)/shard_map/ppermute | solution.py:17
  27.7 2.3 %collective-permute-start.10 = (bf16[16,896]{1,0:T(8,128)(2,1)S(1)}, bf16[16,896]{1,0:T(8,128)(2,1)S(1)}, u32[]{:S(2)}, u32[]{:S(2)}) collective-permute-start(bf16[16,896]{1,0:T(8,128)(2,1)S(1)} %get-tuple-element.20), channel_id=1, source_target_pairs={{0,12},{2,14},{4,8},{6,10},{8,4},{10,6},{12,0},{14,2},{1,13},{3,15... | collective-permute-start | bytes 86024 | tf_op jit(solution)/shard_map/ppermute | solution.py:17
  30.0 0.5 collective-permute-done.9.refs_1_
  30.5 2.9 %collective-permute-done.10.refs_2_ = bf16[16,896]{1,0:T(8,128)(2,1)S(1)} collective-permute-done((bf16[16,896]{1,0:T(8,128)(2,1)S(1)}, bf16[16,896]{1,0:T(8,128)(2,1)S(1)}, u32[]{:S(2)}, u32[]{:S(2)}) %collective-permute-start.10) | collective-permute-done | bytes 28704 | tf_op jit(solution)/shard_map/ppermute | solution.py:17
  33.4 0.6 collective-permute-start.11
  34.0 3.3 %collective-permute-done.11.refs_0_ = bf16[16,896]{1,0:T(8,128)(2,1)S(1)} collective-permute-done((bf16[16,896]{1,0:T(8,128)(2,1)S(1)}, bf16[16,896]{1,0:T(8,128)(2,1)S(1)}, u32[]{:S(2)}, u32[]{:S(2)}) %collective-permute-start.11) | collective-permute-done | bytes 28704 | tf_op jit(solution)/shard_map/ppermute | solution.py:17
  37.4 2.3 %collective-permute-start.14 = (bf16[16,896]{1,0:T(8,128)(2,1)S(1)}, bf16[16,896]{1,0:T(8,128)(2,1)S(1)}, u32[]{:S(2)}, u32[]{:S(2)}) collective-permute-start(bf16[16,896]{1,0:T(8,128)(2,1)S(1)} %shard_map.72.refs_0_), channel_id=1, source_target_pairs={{0,12},{2,14},{4,8},{6,10},{8,4},{10,6},{12,0},{14,2},{1,13},{3,15... | collective-permute-start | bytes 86024 | tf_op jit(solution)/shard_map/ppermute | solution.py:17
  39.7 2.1 %collective-permute-start.12 = (bf16[16,896]{1,0:T(8,128)(2,1)S(1)}, bf16[16,896]{1,0:T(8,128)(2,1)S(1)}, u32[]{:S(2)}, u32[]{:S(2)}) collective-permute-start(bf16[16,896]{1,0:T(8,128)(2,1)S(1)} %shard_map.72.refs_0_), channel_id=1, source_target_pairs={{0,4},{2,6},{4,0},{6,2},{8,12},{10,14},{12,8},{14,10},{1,5},{3,7},... | collective-permute-start | bytes 86024 | tf_op jit(solution)/shard_map/ppermute | solution.py:17
  41.8 1.7 %shard_map.70.codes_t = bf16[8192,64]{1,0:T(8,128)(2,1)S(1)} custom-call(bf16[64,4096]{1,0:T(8,128)(2,1)S(1)} %get-tuple-element.14.refs_0_, bf16[64,4096]{1,0:T(8,128)(2,1)S(1)} %get-tuple-element.16.refs_1_), custom_call_target="tpu_custom_call" | custom-call | flops 1400000000 | bytes 4194304 | tf_op jit(solution)/shard_map/pallas_call | solution.py:166
  43.5 1.0 %collective-permute-done.13.refs_2_ = bf16[16,896]{1,0:T(8,128)(2,1)S(1)} collective-permute-done((bf16[16,896]{1,0:T(8,128)(2,1)S(1)}, bf16[16,896]{1,0:T(8,128)(2,1)S(1)}, u32[]{:S(2)}, u32[]{:S(2)}) %collective-permute-start.13) | collective-permute-done | bytes 28704 | tf_op jit(solution)/shard_map/ppermute | solution.py:17
  44.6 16.0 %shard_map.73 = bf16[8192,896]{1,0:T(8,128)(2,1)} custom-call(bf16[8192,64]{1,0:T(8,128)(2,1)S(1)} %shard_map.70.codes_t, bf16[8192,896]{1,0:T(8,128)(2,1)S(1)} %bitcast.4, bf16[8192,896]{1,0:T(8,128)(2,1)S(1)} %bitcast.6, bf16[16,896]{1,0:T(8,128)(2,1)S(1)} %shard_map.72.refs_0_, bf16[16,896]{1,0:T(8,128)(2,1)S(1)} %collective-permute-done.12.refs_1_, ...), custom_call_target="tpu_custom_call" | custom-call | tf_op jit(solution)/shard_map/pallas_call | solution.py:269
  (41 shorter events, 0.1 us)
Async XLA Ops:
  0.0 15.5 %copy-start = (bf16[896,8192]{1,0:T(8,128)(2,1)S(1)}, bf16[896,8192]{1,0:T(8,128)(2,1)}, u32[]{:S(2)}) copy-start(bf16[896,8192]{1,0:T(8,128)(2,1)} %refs_4_.3) | copy-start | bytes 44040196
  0.0 4.6 %collective-permute-start = (bf16[4,1792]{1,0:T(4,128)(2,1)}, bf16[4,1792]{1,0:T(4,128)(2,1)S(1)}, u32[]{:S(2)}, u32[]{:S(2)}) collective-permute-start(bf16[4,1792]{1,0:T(4,128)(2,1)} %x.1), channel_id=1, source_target_pairs={{0,1},{1,0},{2,3},{3,2},{4,5},{5,4},{6,7},{7,6},{8,9},{9,8},{10,11... | collective-permute-start | bytes 43016 | tf_op jit(solution)/shard_map/ppermute | solution.py:17
  0.5 4.2 %collective-permute-start.2 = (bf16[4,1792]{1,0:T(4,128)(2,1)}, bf16[4,1792]{1,0:T(4,128)(2,1)S(1)}, u32[]{:S(2)}, u32[]{:S(2)}) collective-permute-start(bf16[4,1792]{1,0:T(4,128)(2,1)} %x.1), channel_id=1, source_target_pairs={{0,3},{1,2},{2,1},{3,0},{4,7},{5,6},{6,5},{7,4},{8,11},{9,10},{10,... | collective-permute-start | bytes 43016 | tf_op jit(solution)/shard_map/ppermute | solution.py:17
  3.1 3.9 %collective-permute-start.1 = (bf16[4,1792]{1,0:T(4,128)(2,1)}, bf16[4,1792]{1,0:T(4,128)(2,1)S(1)}, u32[]{:S(2)}, u32[]{:S(2)}) collective-permute-start(bf16[4,1792]{1,0:T(4,128)(2,1)} %x.1), channel_id=1, source_target_pairs={{0,2},{1,3},{2,0},{3,1},{4,6},{5,7},{6,4},{7,5},{8,10},{9,11},{10,... | collective-permute-start | bytes 43016 | tf_op jit(solution)/shard_map/ppermute | solution.py:17
  3.1 1.5 %copy-start.2 = (bf16[4,1792]{1,0:T(4,128)(2,1)S(1)}, bf16[4,1792]{1,0:T(4,128)(2,1)}, u32[]{:S(2)}) copy-start(bf16[4,1792]{1,0:T(4,128)(2,1)} %x.1) | copy-start | bytes 43012
  7.0 13.7 %slice-start = ((s8[14680064]{0:T(1024)(128)(4,1)}), s8[4194304]{0:T(1024)(128)(4,1)S(1)}, s32[]{:S(2)}) async-start(s8[14680064]{0:T(1024)(128)(4,1)} %bitcast.1), calls=%async_computation | async-start | bytes 8388608
  7.0 13.7 %slice-start.1 = ((s8[14680064]{0:T(1024)(128)(4,1)}), s8[4194304]{0:T(1024)(128)(4,1)S(1)}, s32[]{:S(2)}) async-start(s8[14680064]{0:T(1024)(128)(4,1)} %bitcast.1), calls=%async_computation.1 | async-start | bytes 8388608
  7.0 13.7 %copy-start.1 = (f32[8192]{0:T(1024)S(1)}, f32[8192]{0:T(1024)}, u32[]{:S(2)}) copy-start(f32[8192]{0:T(1024)} %param.8) | copy-start | bytes 98308
  7.0 5.7 %collective-permute-start.5 = (bf16[16,896]{1,0:T(8,128)(2,1)S(1)}, bf16[16,896]{1,0:T(8,128)(2,1)S(1)}, u32[]{:S(2)}, u32[]{:S(2)}) collective-permute-start(bf16[16,896]{1,0:T(8,128)(2,1)S(1)} %shard_map.65.refs_0_.rows), channel_id=1, source_target_pairs={{0,12},{2,14},{4,8},{6,10},{8,4},{10,6},{12,0},{14,2},{1,13},{3,15... | collective-permute-start | bytes 86024 | tf_op jit(solution)/shard_map/ppermute | solution.py:17
  10.7 4.8 %collective-permute-start.4 = (bf16[16,896]{1,0:T(8,128)(2,1)S(1)}, bf16[16,896]{1,0:T(8,128)(2,1)S(1)}, u32[]{:S(2)}, u32[]{:S(2)}) collective-permute-start(bf16[16,896]{1,0:T(8,128)(2,1)S(1)} %shard_map.65.refs_0_.rows), channel_id=1, source_target_pairs={{0,8},{2,10},{4,12},{6,14},{8,0},{10,2},{12,4},{14,6},{1,9},{3,11}... | collective-permute-start | bytes 86024 | tf_op jit(solution)/shard_map/ppermute | solution.py:17
  10.7 4.8 %collective-permute-start.3 = (bf16[16,896]{1,0:T(8,128)(2,1)S(1)}, bf16[16,896]{1,0:T(8,128)(2,1)S(1)}, u32[]{:S(2)}, u32[]{:S(2)}) collective-permute-start(bf16[16,896]{1,0:T(8,128)(2,1)S(1)} %shard_map.65.refs_0_.rows), channel_id=1, source_target_pairs={{0,4},{2,6},{4,0},{6,2},{8,12},{10,14},{12,8},{14,10},{1,5},{3,7},... | collective-permute-start | bytes 86024 | tf_op jit(solution)/shard_map/ppermute | solution.py:17
  17.8 3.0 %slice-start.2 = ((s8[14680064]{0:T(1024)(128)(4,1)}), s8[4194304]{0:T(1024)(128)(4,1)S(1)}, s32[]{:S(2)}) async-start(s8[14680064]{0:T(1024)(128)(4,1)} %bitcast.1), calls=%async_computation.2 | async-start | bytes 8388608
  17.8 3.0 %slice-start.3 = ((s8[14680064]{0:T(1024)(128)(4,1)}), s8[2097152]{0:T(1024)(128)(4,1)S(1)}, s32[]{:S(2)}) async-start(s8[14680064]{0:T(1024)(128)(4,1)} %bitcast.1), calls=%async_computation.3 | async-start | bytes 4194304
  17.8 2.9 %collective-permute-start.6 = (f32[64,4096]{1,0:T(8,128)S(1)}, f32[64,4096]{1,0:T(8,128)S(1)}, u32[]{:S(2)}, u32[]{:S(2)}) collective-permute-start(f32[64,4096]{1,0:T(8,128)S(1)} %shard_map.66.mine), channel_id=1, source_target_pairs={{0,1},{1,0},{2,3},{3,2},{4,5},{5,4},{6,7},{7,6},{8,9},{9,8},{10,11... | collective-permute-start | bytes 3145736 | tf_op jit(solution)/shard_map/ppermute | solution.py:17
  20.1 3.0 %collective-permute-start.7 = (f32[64,4096]{1,0:T(8,128)S(1)}, f32[64,4096]{1,0:T(8,128)S(1)}, u32[]{:S(2)}, u32[]{:S(2)}) collective-permute-start(f32[64,4096]{1,0:T(8,128)S(1)} %shard_map.68.mine), channel_id=1, source_target_pairs={{0,1},{1,0},{2,3},{3,2},{4,5},{5,4},{6,7},{7,6},{8,9},{9,8},{10,11... | collective-permute-start | bytes 3145736 | tf_op jit(solution)/shard_map/ppermute | solution.py:17
  23.1 21.4 %slice-start.4 = ((s8[14680064]{0:T(1024)(128)(4,1)}), s8[4194304]{0:T(1024)(128)(4,1)S(1)}, s32[]{:S(2)}) async-start(s8[14680064]{0:T(1024)(128)(4,1)} %bitcast.3), calls=%async_computation.4 | async-start | bytes 8388608
  23.1 21.4 %slice-start.5 = ((s8[14680064]{0:T(1024)(128)(4,1)}), s8[4194304]{0:T(1024)(128)(4,1)S(1)}, s32[]{:S(2)}) async-start(s8[14680064]{0:T(1024)(128)(4,1)} %bitcast.3), calls=%async_computation.5 | async-start | bytes 8388608
  23.2 21.4 %slice-start.8 = ((s8[14680064]{0:T(1024)(128)(4,1)}), s8[4194304]{0:T(1024)(128)(4,1)S(1)}, s32[]{:S(2)}) async-start(s8[14680064]{0:T(1024)(128)(4,1)} %bitcast.5), calls=%async_computation.8 | async-start | bytes 8388608
  23.2 21.4 %slice-start.9 = ((s8[14680064]{0:T(1024)(128)(4,1)}), s8[4194304]{0:T(1024)(128)(4,1)S(1)}, s32[]{:S(2)}) async-start(s8[14680064]{0:T(1024)(128)(4,1)} %bitcast.5), calls=%async_computation.9 | async-start | bytes 8388608
  25.6 4.5 %collective-permute-start.8 = (bf16[16,896]{1,0:T(8,128)(2,1)S(1)}, bf16[16,896]{1,0:T(8,128)(2,1)S(1)}, u32[]{:S(2)}, u32[]{:S(2)}) collective-permute-start(bf16[16,896]{1,0:T(8,128)(2,1)S(1)} %get-tuple-element.18), channel_id=1, source_target_pairs={{0,4},{2,6},{4,0},{6,2},{8,12},{10,14},{12,8},{14,10},{1,5},{3,7},... | collective-permute-start | bytes 86024 | tf_op jit(solution)/shard_map/ppermute | solution.py:17
  25.6 4.8 %collective-permute-start.9 = (bf16[16,896]{1,0:T(8,128)(2,1)S(1)}, bf16[16,896]{1,0:T(8,128)(2,1)S(1)}, u32[]{:S(2)}, u32[]{:S(2)}) collective-permute-start(bf16[16,896]{1,0:T(8,128)(2,1)S(1)} %get-tuple-element.19), channel_id=1, source_target_pairs={{0,8},{2,10},{4,12},{6,14},{8,0},{10,2},{12,4},{14,6},{1,9},{3,11}... | collective-permute-start | bytes 86024 | tf_op jit(solution)/shard_map/ppermute | solution.py:17
  27.7 5.7 %collective-permute-start.10 = (bf16[16,896]{1,0:T(8,128)(2,1)S(1)}, bf16[16,896]{1,0:T(8,128)(2,1)S(1)}, u32[]{:S(2)}, u32[]{:S(2)}) collective-permute-start(bf16[16,896]{1,0:T(8,128)(2,1)S(1)} %get-tuple-element.20), channel_id=1, source_target_pairs={{0,12},{2,14},{4,8},{6,10},{8,4},{10,6},{12,0},{14,2},{1,13},{3,15... | collective-permute-start | bytes 86024 | tf_op jit(solution)/shard_map/ppermute | solution.py:17
  33.4 11.1 %slice-start.6 = ((s8[14680064]{0:T(1024)(128)(4,1)}), s8[4194304]{0:T(1024)(128)(4,1)S(1)}, s32[]{:S(2)}) async-start(s8[14680064]{0:T(1024)(128)(4,1)} %bitcast.3), calls=%async_computation.6 | async-start | bytes 8388608
  33.4 11.1 %slice-start.10 = ((s8[14680064]{0:T(1024)(128)(4,1)}), s8[4194304]{0:T(1024)(128)(4,1)S(1)}, s32[]{:S(2)}) async-start(s8[14680064]{0:T(1024)(128)(4,1)} %bitcast.5), calls=%async_computation.10 | async-start | bytes 8388608
  33.4 3.9 %collective-permute-start.11 = (bf16[16,896]{1,0:T(8,128)(2,1)S(1)}, bf16[16,896]{1,0:T(8,128)(2,1)S(1)}, u32[]{:S(2)}, u32[]{:S(2)}) collective-permute-start(bf16[16,896]{1,0:T(8,128)(2,1)S(1)} %get-tuple-element.22), channel_id=1, source_target_pairs={{0,2},{2,0},{4,6},{6,4},{8,10},{10,8},{12,14},{14,12},{1,3},{3,1},... | collective-permute-start | bytes 86024 | tf_op jit(solution)/shard_map/ppermute | solution.py:17
  37.4 7.2 %slice-start.7 = ((s8[14680064]{0:T(1024)(128)(4,1)}), s8[2097152]{0:T(1024)(128)(4,1)S(1)}, s32[]{:S(2)}) async-start(s8[14680064]{0:T(1024)(128)(4,1)} %bitcast.3), calls=%async_computation.7 | async-start | bytes 4194304
  37.4 7.2 %slice-start.11 = ((s8[14680064]{0:T(1024)(128)(4,1)}), s8[2097152]{0:T(1024)(128)(4,1)S(1)}, s32[]{:S(2)}) async-start(s8[14680064]{0:T(1024)(128)(4,1)} %bitcast.5), calls=%async_computation.11 | async-start | bytes 4194304
  37.4 6.1 %collective-permute-start.14 = (bf16[16,896]{1,0:T(8,128)(2,1)S(1)}, bf16[16,896]{1,0:T(8,128)(2,1)S(1)}, u32[]{:S(2)}, u32[]{:S(2)}) collective-permute-start(bf16[16,896]{1,0:T(8,128)(2,1)S(1)} %shard_map.72.refs_0_), channel_id=1, source_target_pairs={{0,12},{2,14},{4,8},{6,10},{8,4},{10,6},{12,0},{14,2},{1,13},{3,15... | collective-permute-start | bytes 86024 | tf_op jit(solution)/shard_map/ppermute | solution.py:17
  39.7 4.8 %collective-permute-start.13 = (bf16[16,896]{1,0:T(8,128)(2,1)S(1)}, bf16[16,896]{1,0:T(8,128)(2,1)S(1)}, u32[]{:S(2)}, u32[]{:S(2)}) collective-permute-start(bf16[16,896]{1,0:T(8,128)(2,1)S(1)} %shard_map.72.refs_0_), channel_id=1, source_target_pairs={{0,8},{2,10},{4,12},{6,14},{8,0},{10,2},{12,4},{14,6},{1,9},{3,11}... | collective-permute-start | bytes 86024 | tf_op jit(solution)/shard_map/ppermute | solution.py:17
  39.7 4.8 %collective-permute-start.12 = (bf16[16,896]{1,0:T(8,128)(2,1)S(1)}, bf16[16,896]{1,0:T(8,128)(2,1)S(1)}, u32[]{:S(2)}, u32[]{:S(2)}) collective-permute-start(bf16[16,896]{1,0:T(8,128)(2,1)S(1)} %shard_map.72.refs_0_), channel_id=1, source_target_pairs={{0,4},{2,6},{4,0},{6,2},{8,12},{10,14},{12,8},{14,10},{1,5},{3,7},... | collective-permute-start | bytes 86024 | tf_op jit(solution)/shard_map/ppermute | solution.py:17

commit v5 on v4

v5 whole, which is shorter than its diff:
```python
import functools

import jax
import jax.numpy as jnp
from jax import lax
from jax.experimental import pallas as pl
from jax.experimental.pallas import tpu as pltpu
from jax.sharding import PartitionSpec as P

MIB = 1 << 20
WHOLE = pl.BlockSpec(memory_space=pltpu.VMEM)
DIRECT = 8


def swap(value, axis, mask):
    n = lax.axis_size(axis)
    return lax.ppermute(value, axis, [(i, i ^ mask) for i in range(n)])


def params(mib):
    return pltpu.CompilerParams(vmem_limit_bytes=mib * MIB)


def waits(mib):
    return pl.CostEstimate(flops=mib * 350_000_000, bytes_accessed=mib * MIB, transcendentals=0)


def resident(value):
    return pltpu.with_memory_space_constraint(value, pltpu.VMEM)


def far_masks():
    return range(2, lax.axis_size("latent"), 2)


def stack(refs):
    return jnp.concatenate([r[...].astype(jnp.float32) for r in refs]).astype(refs[0].dtype)


def near_kernel(*refs):
    *rows, out = refs
    half = out.shape[1]
    side = lax.axis_index("dp")

    def write(order, at):
        picked = [rows[i][:, at : at + half].astype(jnp.float32) for i in order]
        out[...] = jnp.concatenate(picked).astype(out.dtype)

    pairs = range(0, len(rows), 2)

    @pl.when(side == 0)
    def _():
        write([i + c for i in pairs for c in (0, 1)], 0)

    @pl.when(side == 1)
    def _():
        write([i + c for i in pairs for c in (1, 0)], half)


def copy_kernel(x, out):
    out[...] = x[...]


def near_rows(acts, near):
    axes = ("latent", "dp")
    own = pl.pallas_call(
        copy_kernel,
        out_shape=jax.ShapeDtypeStruct(acts.shape, acts.dtype),
        in_specs=[WHOLE],
        out_specs=WHOLE,
        cost_estimate=waits(1),
        compiler_params=params(4),
    )(acts)
    rows = [own] + [swap(acts, axes, mask) for mask in range(1, 2 * near)]
    return pl.pallas_call(
        near_kernel,
        out_shape=jax.ShapeDtypeStruct((len(rows) * acts.shape[0], acts.shape[1] // 2), acts.dtype),
        in_specs=[WHOLE] * len(rows),
        out_specs=WHOLE,
        cost_estimate=waits(14),
        compiler_params=params(4),
    )(*rows)


def spread(block):
    if lax.axis_size("latent") > DIRECT:
        return [lax.all_gather(block, "latent", axis=0, tiled=True)]
    return [block] + [swap(block, "latent", mask) for mask in far_masks()]


def encode_kernel(first, *refs):
    *rows_refs, w, out = refs
    lat = out.shape[1]
    out[...] = jnp.dot(
        stack(rows_refs), w[:, first : first + lat], preferred_element_type=jnp.float32
    )


def encode(blocks, w_enc, first, lat):
    tokens = sum(b.shape[0] for b in blocks)
    return pl.pallas_call(
        functools.partial(encode_kernel, first),
        out_shape=jax.ShapeDtypeStruct((tokens, lat), jnp.float32),
        in_specs=[WHOLE] * (len(blocks) + 1),
        out_specs=WHOLE,
        cost_estimate=waits(7),
        compiler_params=params(8),
    )(*blocks, resident(w_enc))


def decode_kernel(first, given, mine, theirs, bias, w, *refs):
    codes, *out = refs[given:]
    lat = mine.shape[1]
    pre = mine[...] + theirs[...] + bias[:, first : first + lat]
    block = jnp.maximum(pre, 0.0).astype(jnp.bfloat16)
    codes[...] = block
    total = jnp.dot(block, w[first : first + lat, :], preferred_element_type=jnp.float32)
    if given:
        total = total + refs[0][...]
    if len(out) == 1:
        out[0][...] = total
        return
    own, sent = out
    rows = own.shape[0]
    own[...] = total[:rows]
    far = lax.axis_index("latent") // 2
    for j in range(sent.shape[0]):
        sent[far ^ j] = total[j * rows : (j + 1) * rows].astype(sent.dtype)


def decode(mine, theirs, bias, w_dec, first, given, far):
    tokens, lat = mine.shape
    half = w_dec.shape[1]
    sums = [jax.ShapeDtypeStruct((tokens // far, half), jnp.float32)]
    if far > 1:
        sums.append(jax.ShapeDtypeStruct((far, tokens // far, half), jnp.bfloat16))
    codes, *sums = pl.pallas_call(
        functools.partial(decode_kernel, first, len(given)),
        out_shape=[jax.ShapeDtypeStruct((tokens, lat), jnp.bfloat16)] + sums,
        in_specs=[WHOLE] * (4 + len(given)),
        out_specs=[WHOLE] * (1 + len(sums)),
        cost_estimate=waits(7),
        compiler_params=params(8),
    )(mine, theirs, bias.reshape(1, -1), resident(w_dec), *given)
    return codes, sums


def turn_kernel(chunk, *refs):
    *codes, out = refs
    for k, ref in enumerate(codes):
        lat = ref.shape[1]

        @pl.loop(0, lat // chunk)
        def _(i):
            at = pl.multiple_of(i * chunk, chunk)
            block = ref[:, pl.ds(at, chunk)].astype(jnp.float32).T
            out[pl.ds(k * lat + at, chunk), :] = block.astype(out.dtype)


def turn(*codes):
    tokens, lat = codes[0].shape
    return pl.pallas_call(
        functools.partial(turn_kernel, min(512, lat)),
        out_shape=jax.ShapeDtypeStruct((len(codes) * lat, tokens), codes[0].dtype),
        in_specs=[WHOLE] * len(codes),
        out_specs=WHOLE,
        cost_estimate=waits(4),
        compiler_params=params(8),
    )(*codes)


def sum_kernel(own, far, out, sent):
    me = lax.axis_index("latent") // 2
    total = own[...]
    for j in range(1, far.shape[0]):
        total = total + far[me ^ j]
    out[...] = total
    sent[...] = total.astype(sent.dtype)


def add_up(own, far):
    return pl.pallas_call(
        sum_kernel,
        out_shape=[
            jax.ShapeDtypeStruct(own.shape, jnp.float32),
            jax.ShapeDtypeStruct(own.shape, jnp.bfloat16),
        ],
        in_specs=[WHOLE] * 2,
        out_specs=[WHOLE] * 2,
        cost_estimate=waits(8),
        compiler_params=params(4),
    )(own, far)


def error_kernel(total, rows, *refs):
    *near, out = refs
    total = total[...]
    for ref in near:
        half = ref.shape[0] // 2
        term = ref[...].astype(jnp.float32)
        total = total + jnp.concatenate([term[half:], term[:half]])
    err = (total - rows[...].astype(jnp.float32)).astype(out.dtype)
    for j in range(out.shape[0]):
        out[j] = err


def error(total, near, rows, copies):
    return pl.pallas_call(
        error_kernel,
        out_shape=jax.ShapeDtypeStruct((copies, *rows.shape), rows.dtype),
        in_specs=[WHOLE] * (2 + len(near)),
        out_specs=WHOLE,
        cost_estimate=waits(8),
        compiler_params=params(4),
    )(total, rows, *near)


def far_exchange(blocks):
    n = lax.axis_size("latent")
    groups = [list(range(near, n, 2)) for near in range(2)]
    return lax.all_to_all(blocks, "latent", 0, 0, axis_index_groups=groups, tiled=True)


def all_errors(sums, rows, codes_t):
    if lax.axis_size("latent") > DIRECT:
        total = lax.psum_scatter(sums[0], "latent", scatter_dimension=0, tiled=True)
        err = error(total, [], rows, 1)[0]
        return lax.all_gather(err, "latent", axis=0, tiled=True)[None], codes_t
    total, sent = add_up(sums[0], far_exchange(sums[1]))
    err = error(total, [swap(sent, "latent", 1)], rows, sums[1].shape[0])
    err, codes_t = lax.optimization_barrier((err, codes_t))
    return far_exchange(err), codes_t


def adam_kernel(codes_t, m, v, blocks, out, product, err):
    tokens = codes_t.shape[1]
    b = 0.1 / (1.0 - 0.9**10) / tokens
    a = 0.9 / (1.0 - 0.9**10) / b
    p = 0.999 / (1.0 - 0.999**10) / b**2
    q = 0.001 / (1.0 - 0.999**10) / tokens**2 / b**2
    eps = 1e-8 / b
    i, last = pl.program_id(0), pl.num_programs(0) - 1
    rows = out.shape[0]
    part = product.shape[0]
    slab = 16

    def multiply(start):
        at = pl.ds(pl.multiple_of(start, part), part)
        return jnp.dot(codes_t[at, :], err[...], preferred_element_type=jnp.float32)

    @pl.when(i == 0)
    def _():
        me = lax.axis_index("latent") // 2
        n = blocks.shape[0]
        picked = [blocks[me ^ j if n > 1 else 0] for j in range(n)]
        err[...] = jnp.concatenate([x.astype(jnp.float32) for x in picked]).astype(err.dtype)
        product[...] = multiply(0)

    def direction(c, start):
        at = pl.ds(pl.multiple_of(start, slab), slab)
        first = m[at, :].astype(jnp.float32) * a + c
        second = v[at, :].astype(jnp.float32) * p + (c * c) * q
        root = second * lax.rsqrt(second)
        return (first * pl.reciprocal(root + eps, approx=True)).astype(out.dtype)

    c = product[...]
    done = []
    for k in range(0, rows, part):
        if k + part < rows:
            later = multiply(i * rows + k + part)
        else:
            later = multiply(jnp.minimum(i + 1, last) * rows)
        steps = [(k + r, direction(c[r : r + slab], i * rows + k + r)) for r in range(0, part, slab)]
        for r, step in done:
            out[r : r + slab, :] = step
        done, c = steps, later
    for r, step in done:
        out[r : r + slab, :] = step
    product[...] = c


def adam(codes_t, blocks, m, v):
    lat, half = m.shape
    rows = min(1024, lat)
    return pl.pallas_call(
        adam_kernel,
        grid=(lat // rows,),
        out_shape=jax.ShapeDtypeStruct(m.shape, jnp.bfloat16),
        in_specs=[WHOLE] * 4,
        out_specs=pl.BlockSpec((rows, half), lambda i: (i, 0)),
        scratch_shapes=[
            pltpu.VMEM((64, half), jnp.float32),
            pltpu.VMEM((codes_t.shape[1], half), jnp.bfloat16),
        ],
        compiler_params=params(12),
    )(codes_t, resident(m), resident(v), blocks)


def per_device(acts, w_enc, b_enc, w_dec, dec_m, dec_v):
    direct = lax.axis_size("latent") <= DIRECT
    rows = near_rows(acts, 2 if direct else 1)
    blocks = spread(rows)
    part = w_enc.shape[1] // 2
    mine = [encode(blocks, w_enc, k * part, part) for k in range(2)]
    theirs = [swap(x, "dp", 1) for x in mine]
    codes, sums = [None, None], []
    for k in range(2):
        codes[k], sums = decode(
            mine[k], theirs[k], b_enc, w_dec, k * part, sums, len(blocks) if k else 1
        )
    errors, codes_t = all_errors(sums, rows, turn(*codes))
    return adam(codes_t, errors, dec_m, dec_v)


def solution(mesh):
    in_specs = (
        P(("groups", "latent", "dp"), None),
        P(("groups", "dp"), "latent"),
        P(("groups", "latent")),
        P(("groups", "latent"), "dp"),
        P(("groups", "latent"), "dp"),
        P(("groups", "latent"), "dp"),
    )
    out_specs = P(("groups", "latent"), "dp")
    return jax.shard_map(
        per_device, mesh=mesh, in_specs=in_specs, out_specs=out_specs, check_vma=False
    )
```

time: 60.8 us -> 61.1 us (level)
  blocking collectives: 0 us -> 18 us
  starting transfers between devices: 17.7 us -> 8.79 us
  waiting for transfers between devices: 14.1 us -> 8.9 us
  Pallas kernels: 27 us -> 23.3 us
    all_to_all x0 -> x2, blocking collectives: none -> 18 us  [far_exchange(): lax.all_to_all(blocks, 'latent', 0, 0, axis_index_groups=groups, tiled=True)]
    ppermute x15 -> x9, starting transfers between devices: 17.7 us -> 8.79 us  [swap(): return lax.ppermute(value, axis, [(i, i ^ mask) for i in range(n)])]
    ppermute x15 -> x9, waiting for transfers between devices: 14.1 us -> 8.9 us  [swap(): return lax.ppermute(value, axis, [(i, i ^ mask) for i in range(n)])]
    pallas_call x7, Pallas kernels: 25.3 us -> 21.6 us  [the longest x1 16.1 us: adam(): pl.pallas_call(adam_kernel, grid=(lat // rows,), out_shape=jax.ShapeDtype...]
  transfers between devices with their start and end apart: 15 -> 9, of which waited for: 8 -> 7; matrix products, arithmetic and copies ran while one was open for 0% -> 0% of each run, Pallas kernels for 10% -> 7%
where the time goes in v5:
time: 61.1 us; the launch traced here: 60.8 us
  Pallas kernels  23.3 us (38%)
  blocking collectives  18 us (29%)
  waiting for transfers between devices  8.9 us (15%)
  starting transfers between devices  8.79 us (14%)
  local copies, waits for them, and re-layouts  1.62 us (3%)
    all_to_all x2, blocking collectives, far_exchange(): lax.all_to_all(blocks, 'latent', 0, 0, axis_index_groups=groups, tiled=True)  18 us
    pallas_call x1, Pallas kernels, adam(): pl.pallas_call(adam_kernel, grid=(lat // rows,), out_shape=jax.ShapeDtype...  16.1 us
    ppermute x9, waiting for transfers between devices, swap(): return lax.ppermute(value, axis, [(i, i ^ mask) for i in range(n)])  8.9 us
    ppermute x9, starting transfers between devices, swap(): return lax.ppermute(value, axis, [(i, i ^ mask) for i in range(n)])  8.79 us
    pallas_call x2, Pallas kernels, encode(): pl.pallas_call(functools.partial(encode_kernel, first), out_shape=jax.Sha...  2.82 us
    pallas_call x2, Pallas kernels, decode(): pl.pallas_call(functools.partial(decode_kernel, first, len(given)), out_s...  2.58 us
    pallas_call x1, Pallas kernels, turn(): pl.pallas_call(functools.partial(turn_kernel, min(512, lat)), out_shape=j...  1.68 us
    unnamed x30, local copies, waits for them, and re-layouts  1.62 us
  transfers between devices with their start and end apart: 9, of which 7 were waited for; matrix products, arithmetic and copies ran while one was open for 0% of the time, Pallas kernels for 7%

profile of v5, /device:TPU:0, one launch (start us, length us, event | category | flops | bytes accessed | tf_op | source)
XLA Modules:
  0.0 60.8 jit_solution(8392297363957749850)
XLA Ops:
  0.0 0.5 collective-permute-start
  0.5 2.6 %collective-permute-start.2 = (bf16[4,1792]{1,0:T(4,128)(2,1)}, bf16[4,1792]{1,0:T(4,128)(2,1)S(1)}, u32[]{:S(2)}, u32[]{:S(2)}) collective-permute-start(bf16[4,1792]{1,0:T(4,128)(2,1)} %x.1), channel_id=1, source_target_pairs={{0,3},{1,2},{2,1},{3,0},{4,7},{5,6},{6,5},{7,4},{8,11},{9,10},{10,... | collective-permute-start | bytes 43016 | tf_op jit(solution)/shard_map/ppermute | solution.py:17
  3.1 0.1 collective-permute-start.1
  3.1 1.5 %copy-done.2 = bf16[4,1792]{1,0:T(4,128)(2,1)S(1)} copy-done((bf16[4,1792]{1,0:T(4,128)(2,1)S(1)}, bf16[4,1792]{1,0:T(4,128)(2,1)}, u32[]{:S(2)}) %copy-start.2) | copy-done | bytes 14360
  4.6 0.0 collective-permute-done.refs_1_
  4.6 0.1 collective-permute-done.2.refs_3_
  4.7 2.3 %collective-permute-done.1.refs_2_ = bf16[4,1792]{1,0:T(4,128)(2,1)S(1)} collective-permute-done((bf16[4,1792]{1,0:T(4,128)(2,1)}, bf16[4,1792]{1,0:T(4,128)(2,1)S(1)}, u32[]{:S(2)}, u32[]{:S(2)}) %collective-permute-start.1) | collective-permute-done | bytes 14368 | tf_op jit(solution)/shard_map/ppermute | solution.py:17
  7.0 0.0 slice-start
  7.0 0.0 slice-start.1
  7.0 0.0 copy-start.1
  7.0 3.7 %collective-permute-start.5 = (bf16[16,896]{1,0:T(8,128)(2,1)S(1)}, bf16[16,896]{1,0:T(8,128)(2,1)S(1)}, u32[]{:S(2)}, u32[]{:S(2)}) collective-permute-start(bf16[16,896]{1,0:T(8,128)(2,1)S(1)} %shard_map.65.refs_0_.rows), channel_id=1, source_target_pairs={{0,12},{2,14},{4,8},{6,10},{8,4},{10,6},{12,0},{14,2},{1,13},{3,15... | collective-permute-start | bytes 86024 | tf_op jit(solution)/shard_map/ppermute | solution.py:17
  10.7 0.0 collective-permute-start.4
  10.7 0.8 %collective-permute-start.3 = (bf16[16,896]{1,0:T(8,128)(2,1)S(1)}, bf16[16,896]{1,0:T(8,128)(2,1)S(1)}, u32[]{:S(2)}, u32[]{:S(2)}) collective-permute-start(bf16[16,896]{1,0:T(8,128)(2,1)S(1)} %shard_map.65.refs_0_.rows), channel_id=1, source_target_pairs={{0,4},{2,6},{4,0},{6,2},{8,12},{10,14},{12,8},{14,10},{1,5},{3,7},... | collective-permute-start | bytes 86024 | tf_op jit(solution)/shard_map/ppermute | solution.py:17
  11.5 1.3 %collective-permute-done.5.refs_3_ = bf16[16,896]{1,0:T(8,128)(2,1)S(1)} collective-permute-done((bf16[16,896]{1,0:T(8,128)(2,1)S(1)}, bf16[16,896]{1,0:T(8,128)(2,1)S(1)}, u32[]{:S(2)}, u32[]{:S(2)}) %collective-permute-start.5) | collective-permute-done | bytes 28704 | tf_op jit(solution)/shard_map/ppermute | solution.py:17
  12.8 2.7 %collective-permute-done.4.refs_2_ = bf16[16,896]{1,0:T(8,128)(2,1)S(1)} collective-permute-done((bf16[16,896]{1,0:T(8,128)(2,1)S(1)}, bf16[16,896]{1,0:T(8,128)(2,1)S(1)}, u32[]{:S(2)}, u32[]{:S(2)}) %collective-permute-start.4) | collective-permute-done | bytes 28704 | tf_op jit(solution)/shard_map/ppermute | solution.py:17
  15.5 0.0 collective-permute-done.3.refs_1_
  15.5 1.4 %shard_map.67.mine = f32[64,4096]{1,0:T(8,128)S(1)} custom-call(bf16[16,896]{1,0:T(8,128)(2,1)S(1)} %shard_map.65.refs_0_.rows, bf16[16,896]{1,0:T(8,128)(2,1)S(1)} %collective-permute-done.3.refs_1_, bf16[16,896]{1,0:T(8,128)(2,1)S(1)} %collective-permute-done.4.refs_2_, bf16[16,896]{1,0:T(8,128)(2,1)S(1)} %collective-permute-done.5.refs_3_, ...), custom_call_target="tpu_custom_call" | custom-call | flops 2449999872 | bytes 7340032 | tf_op jit(solution)/shard_map/pallas_call | solution.py:101
  16.9 0.0 slice-start.2
  16.9 0.1 collective-permute-start.7
  17.0 1.4 %shard_map.66.mine = f32[64,4096]{1,0:T(8,128)S(1)} custom-call(bf16[16,896]{1,0:T(8,128)(2,1)S(1)} %shard_map.65.refs_0_.rows, bf16[16,896]{1,0:T(8,128)(2,1)S(1)} %collective-permute-done.3.refs_1_, bf16[16,896]{1,0:T(8,128)(2,1)S(1)} %collective-permute-done.4.refs_2_, bf16[16,896]{1,0:T(8,128)(2,1)S(1)} %collective-permute-done.5.refs_3_, ...), custom_call_target="tpu_custom_call" | custom-call | flops 2449999872 | bytes 7340032 | tf_op jit(solution)/shard_map/pallas_call | solution.py:101
  18.4 0.6 collective-permute-start.6
  19.0 0.7 %collective-permute-done.7.theirs = f32[64,4096]{1,0:T(8,128)S(1)} collective-permute-done((f32[64,4096]{1,0:T(8,128)S(1)}, f32[64,4096]{1,0:T(8,128)S(1)}, u32[]{:S(2)}, u32[]{:S(2)}) %collective-permute-start.7) | collective-permute-done | bytes 1048608 | tf_op jit(solution)/shard_map/ppermute | solution.py:17
  19.7 0.1 slice-done.3
  19.8 1.3 %shard_map.68 = (bf16[64,4096]{1,0:T(8,128)(2,1)S(1)}, f32[64,896]{1,0:T(8,128)S(1)}) custom-call(f32[64,4096]{1,0:T(8,128)S(1)} %shard_map.67.mine, f32[64,4096]{1,0:T(8,128)S(1)} %collective-permute-done.7.theirs, f32[1,8192]{1,0:T(1,128)S(1)} %bitcast.7, bf16[8192,896]{1,0:T(8,128)(2,1)S(1)} %bitcast.2), custom_call_target="tpu_custom_call" | custom-call | flops 2449999872 | bytes 7340032 | tf_op jit(solution)/shard_map/pallas_call | solution.py:137
  21.1 0.2 collective-permute-done.6.theirs
  21.3 1.3 %shard_map.69 = (bf16[64,4096]{1,0:T(8,128)(2,1)S(1)}, f32[16,896]{1,0:T(8,128)S(1)}, bf16[4,16,896]{2,1,0:T(8,128)(2,1)S(1)}) custom-call(f32[64,4096]{1,0:T(8,128)S(1)} %shard_map.66.mine, f32[64,4096]{1,0:T(8,128)S(1)} %collective-permute-done.6.theirs, f32[1,8192]{1,0:T(1,128)S(1)} %bitcast.8, bf16[8192,896]{1,0:T(8,128)(2,1)S(1)} %bitcast.2, ...), custom_call_target="tpu_custom_call" | custom-call | flops 2449999872 | bytes 7340032 | tf_op jit(solution)/shard_map/pallas_call | solution.py:137
  22.6 9.6 %all_to_all.10.far = bf16[4,16,896]{2,1,0:T(8,128)(2,1)S(1)} all-to-all(bf16[4,16,896]{2,1,0:T(8,128)(2,1)S(1)} %get-tuple-element.16), channel_id=1, replica_groups={{0,4,8,12},{2,6,10,14},{1,5,9,13},{3,7,11,15},{16,20,24,28},{18,22,26,3..., dimensions={0} | all-to-all | bytes 229376 | tf_op jit(solution)/shard_map/all_to_all | solution.py:221
  32.2 0.6 collective-permute-start.8
  32.8 1.7 %shard_map.72.codes_t = bf16[8192,64]{1,0:T(8,128)(2,1)S(1)} custom-call(bf16[64,4096]{1,0:T(8,128)(2,1)S(1)} %get-tuple-element.19.refs_0_, bf16[64,4096]{1,0:T(8,128)(2,1)S(1)} %get-tuple-element.20.refs_1_), custom_call_target="tpu_custom_call" | custom-call | flops 1400000000 | bytes 4194304 | tf_op jit(solution)/shard_map/pallas_call | solution.py:162
  34.5 1.6 %collective-permute-done.8.refs_0_ = bf16[16,896]{1,0:T(8,128)(2,1)S(1)} collective-permute-done((bf16[16,896]{1,0:T(8,128)(2,1)S(1)}, bf16[16,896]{1,0:T(8,128)(2,1)S(1)}, u32[]{:S(2)}, u32[]{:S(2)}) %collective-permute-start.8) | collective-permute-done | bytes 28704 | tf_op jit(solution)/shard_map/ppermute | solution.py:17
  36.1 8.4 %all_to_all.11.blocks = bf16[4,16,896]{2,1,0:T(8,128)(2,1)S(1)} all-to-all(bf16[4,16,896]{2,1,0:T(8,128)(2,1)S(1)} %shard_map.71), channel_id=1, replica_groups={{0,4,8,12},{2,6,10,14},{1,5,9,13},{3,7,11,15},{16,20,24,28},{18,22,26,3..., dimensions={0} | all-to-all | bytes 229376 | tf_op jit(solution)/shard_map/all_to_all | solution.py:221
  44.6 16.1 %shard_map.73 = bf16[8192,896]{1,0:T(8,128)(2,1)} custom-call(bf16[8192,64]{1,0:T(8,128)(2,1)S(1)} %shard_map.72.codes_t, bf16[8192,896]{1,0:T(8,128)(2,1)S(1)} %bitcast.4, bf16[8192,896]{1,0:T(8,128)(2,1)S(1)} %bitcast.6, bf16[4,16,896]{2,1,0:T(8,128)(2,1)S(1)} %all_to_all.11.blocks), custom_call_target="tpu_custom_call" | custom-call | tf_op jit(solution)/shard_map/pallas_call | solution.py:285
  (31 shorter events, 0.1 us)
Async XLA Ops:
  0.0 15.5 %copy-start = (bf16[896,8192]{1,0:T(8,128)(2,1)S(1)}, bf16[896,8192]{1,0:T(8,128)(2,1)}, u32[]{:S(2)}) copy-start(bf16[896,8192]{1,0:T(8,128)(2,1)} %refs_4_.3) | copy-start | bytes 44040196
  0.0 4.6 %collective-permute-start = (bf16[4,1792]{1,0:T(4,128)(2,1)}, bf16[4,1792]{1,0:T(4,128)(2,1)S(1)}, u32[]{:S(2)}, u32[]{:S(2)}) collective-permute-start(bf16[4,1792]{1,0:T(4,128)(2,1)} %x.1), channel_id=1, source_target_pairs={{0,1},{1,0},{2,3},{3,2},{4,5},{5,4},{6,7},{7,6},{8,9},{9,8},{10,11... | collective-permute-start | bytes 43016 | tf_op jit(solution)/shard_map/ppermute | solution.py:17
  0.5 4.2 %collective-permute-start.2 = (bf16[4,1792]{1,0:T(4,128)(2,1)}, bf16[4,1792]{1,0:T(4,128)(2,1)S(1)}, u32[]{:S(2)}, u32[]{:S(2)}) collective-permute-start(bf16[4,1792]{1,0:T(4,128)(2,1)} %x.1), channel_id=1, source_target_pairs={{0,3},{1,2},{2,1},{3,0},{4,7},{5,6},{6,5},{7,4},{8,11},{9,10},{10,... | collective-permute-start | bytes 43016 | tf_op jit(solution)/shard_map/ppermute | solution.py:17
  3.1 3.9 %collective-permute-start.1 = (bf16[4,1792]{1,0:T(4,128)(2,1)}, bf16[4,1792]{1,0:T(4,128)(2,1)S(1)}, u32[]{:S(2)}, u32[]{:S(2)}) collective-permute-start(bf16[4,1792]{1,0:T(4,128)(2,1)} %x.1), channel_id=1, source_target_pairs={{0,2},{1,3},{2,0},{3,1},{4,6},{5,7},{6,4},{7,5},{8,10},{9,11},{10,... | collective-permute-start | bytes 43016 | tf_op jit(solution)/shard_map/ppermute | solution.py:17
  3.1 1.5 %copy-start.2 = (bf16[4,1792]{1,0:T(4,128)(2,1)S(1)}, bf16[4,1792]{1,0:T(4,128)(2,1)}, u32[]{:S(2)}) copy-start(bf16[4,1792]{1,0:T(4,128)(2,1)} %x.1) | copy-start | bytes 43012
  7.0 12.6 %slice-start = ((s8[14680064]{0:T(1024)(128)(4,1)}), s8[4194304]{0:T(1024)(128)(4,1)S(1)}, s32[]{:S(2)}) async-start(s8[14680064]{0:T(1024)(128)(4,1)} %bitcast.1), calls=%async_computation.2 | async-start | bytes 8388608
  7.0 12.6 %slice-start.1 = ((s8[14680064]{0:T(1024)(128)(4,1)}), s8[4194304]{0:T(1024)(128)(4,1)S(1)}, s32[]{:S(2)}) async-start(s8[14680064]{0:T(1024)(128)(4,1)} %bitcast.1), calls=%async_computation.3 | async-start | bytes 8388608
  7.0 12.6 %copy-start.1 = (f32[8192]{0:T(1024)S(1)}, f32[8192]{0:T(1024)}, u32[]{:S(2)}) copy-start(f32[8192]{0:T(1024)} %param.8) | copy-start | bytes 98308
  7.0 5.7 %collective-permute-start.5 = (bf16[16,896]{1,0:T(8,128)(2,1)S(1)}, bf16[16,896]{1,0:T(8,128)(2,1)S(1)}, u32[]{:S(2)}, u32[]{:S(2)}) collective-permute-start(bf16[16,896]{1,0:T(8,128)(2,1)S(1)} %shard_map.65.refs_0_.rows), channel_id=1, source_target_pairs={{0,12},{2,14},{4,8},{6,10},{8,4},{10,6},{12,0},{14,2},{1,13},{3,15... | collective-permute-start | bytes 86024 | tf_op jit(solution)/shard_map/ppermute | solution.py:17
  10.7 4.8 %collective-permute-start.4 = (bf16[16,896]{1,0:T(8,128)(2,1)S(1)}, bf16[16,896]{1,0:T(8,128)(2,1)S(1)}, u32[]{:S(2)}, u32[]{:S(2)}) collective-permute-start(bf16[16,896]{1,0:T(8,128)(2,1)S(1)} %shard_map.65.refs_0_.rows), channel_id=1, source_target_pairs={{0,8},{2,10},{4,12},{6,14},{8,0},{10,2},{12,4},{14,6},{1,9},{3,11}... | collective-permute-start | bytes 86024 | tf_op jit(solution)/shard_map/ppermute | solution.py:17
  10.7 4.8 %collective-permute-start.3 = (bf16[16,896]{1,0:T(8,128)(2,1)S(1)}, bf16[16,896]{1,0:T(8,128)(2,1)S(1)}, u32[]{:S(2)}, u32[]{:S(2)}) collective-permute-start(bf16[16,896]{1,0:T(8,128)(2,1)S(1)} %shard_map.65.refs_0_.rows), channel_id=1, source_target_pairs={{0,4},{2,6},{4,0},{6,2},{8,12},{10,14},{12,8},{14,10},{1,5},{3,7},... | collective-permute-start | bytes 86024 | tf_op jit(solution)/shard_map/ppermute | solution.py:17
  16.9 2.8 %slice-start.2 = ((s8[14680064]{0:T(1024)(128)(4,1)}), s8[4194304]{0:T(1024)(128)(4,1)S(1)}, s32[]{:S(2)}) async-start(s8[14680064]{0:T(1024)(128)(4,1)} %bitcast.1), calls=%async_computation.4 | async-start | bytes 8388608
  16.9 2.9 %slice-start.3 = ((s8[14680064]{0:T(1024)(128)(4,1)}), s8[2097152]{0:T(1024)(128)(4,1)S(1)}, s32[]{:S(2)}) async-start(s8[14680064]{0:T(1024)(128)(4,1)} %bitcast.1), calls=%async_computation.5 | async-start | bytes 4194304
  16.9 2.7 %collective-permute-start.7 = (f32[64,4096]{1,0:T(8,128)S(1)}, f32[64,4096]{1,0:T(8,128)S(1)}, u32[]{:S(2)}, u32[]{:S(2)}) collective-permute-start(f32[64,4096]{1,0:T(8,128)S(1)} %shard_map.67.mine), channel_id=1, source_target_pairs={{0,1},{1,0},{2,3},{3,2},{4,5},{5,4},{6,7},{7,6},{8,9},{9,8},{10,11... | collective-permute-start | bytes 3145736 | tf_op jit(solution)/shard_map/ppermute | solution.py:17
  18.4 2.8 %collective-permute-start.6 = (f32[64,4096]{1,0:T(8,128)S(1)}, f32[64,4096]{1,0:T(8,128)S(1)}, u32[]{:S(2)}, u32[]{:S(2)}) collective-permute-start(f32[64,4096]{1,0:T(8,128)S(1)} %shard_map.66.mine), channel_id=1, source_target_pairs={{0,1},{1,0},{2,3},{3,2},{4,5},{5,4},{6,7},{7,6},{8,9},{9,8},{10,11... | collective-permute-start | bytes 3145736 | tf_op jit(solution)/shard_map/ppermute | solution.py:17
  21.3 23.3 %slice-start.4 = ((s8[14680064]{0:T(1024)(128)(4,1)}), s8[4194304]{0:T(1024)(128)(4,1)S(1)}, s32[]{:S(2)}) async-start(s8[14680064]{0:T(1024)(128)(4,1)} %bitcast.3), calls=%async_computation.6 | async-start | bytes 8388608
  21.3 23.3 %slice-start.5 = ((s8[14680064]{0:T(1024)(128)(4,1)}), s8[4194304]{0:T(1024)(128)(4,1)S(1)}, s32[]{:S(2)}) async-start(s8[14680064]{0:T(1024)(128)(4,1)} %bitcast.3), calls=%async_computation.7 | async-start | bytes 8388608
  21.3 23.3 %slice-start.8 = ((s8[14680064]{0:T(1024)(128)(4,1)}), s8[4194304]{0:T(1024)(128)(4,1)S(1)}, s32[]{:S(2)}) async-start(s8[14680064]{0:T(1024)(128)(4,1)} %bitcast.5), calls=%async_computation.10 | async-start | bytes 8388608
  21.3 23.3 %slice-start.9 = ((s8[14680064]{0:T(1024)(128)(4,1)}), s8[4194304]{0:T(1024)(128)(4,1)S(1)}, s32[]{:S(2)}) async-start(s8[14680064]{0:T(1024)(128)(4,1)} %bitcast.5), calls=%async_computation.11 | async-start | bytes 8388608
  32.1 12.4 %slice-start.6 = ((s8[14680064]{0:T(1024)(128)(4,1)}), s8[4194304]{0:T(1024)(128)(4,1)S(1)}, s32[]{:S(2)}) async-start(s8[14680064]{0:T(1024)(128)(4,1)} %bitcast.3), calls=%async_computation.8 | async-start | bytes 8388608
  32.1 12.4 %slice-start.10 = ((s8[14680064]{0:T(1024)(128)(4,1)}), s8[4194304]{0:T(1024)(128)(4,1)S(1)}, s32[]{:S(2)}) async-start(s8[14680064]{0:T(1024)(128)(4,1)} %bitcast.5), calls=%async_computation.12 | async-start | bytes 8388608
  32.2 3.9 %collective-permute-start.8 = (bf16[16,896]{1,0:T(8,128)(2,1)S(1)}, bf16[16,896]{1,0:T(8,128)(2,1)S(1)}, u32[]{:S(2)}, u32[]{:S(2)}) collective-permute-start(bf16[16,896]{1,0:T(8,128)(2,1)S(1)} %get-tuple-element.18), channel_id=1, source_target_pairs={{0,2},{2,0},{4,6},{6,4},{8,10},{10,8},{12,14},{14,12},{1,3},{3,1},... | collective-permute-start | bytes 86024 | tf_op jit(solution)/shard_map/ppermute | solution.py:17
  32.8 11.8 %slice-start.7 = ((s8[14680064]{0:T(1024)(128)(4,1)}), s8[2097152]{0:T(1024)(128)(4,1)S(1)}, s32[]{:S(2)}) async-start(s8[14680064]{0:T(1024)(128)(4,1)} %bitcast.3), calls=%async_computation.9 | async-start | bytes 4194304
  32.8 11.8 %slice-start.11 = ((s8[14680064]{0:T(1024)(128)(4,1)}), s8[2097152]{0:T(1024)(128)(4,1)S(1)}, s32[]{:S(2)}) async-start(s8[14680064]{0:T(1024)(128)(4,1)} %bitcast.5), calls=%async_computation.13 | async-start | bytes 4194304

commit v6 on v5

--- a/solution.py
+++ b/solution.py
@@ -117,23 +117,18 @@
     total = jnp.dot(block, w[first : first + lat, :], preferred_element_type=jnp.float32)
     if given:
         total = total + refs[0][...]
-    if len(out) == 1:
-        out[0][...] = total
-        return
-    own, sent = out
-    rows = own.shape[0]
-    own[...] = total[:rows]
-    far = lax.axis_index("latent") // 2
-    for j in range(sent.shape[0]):
-        sent[far ^ j] = total[j * rows : (j + 1) * rows].astype(sent.dtype)
+    rows = out[0].shape[0]
+    for j, ref in enumerate(out):
+        ref[...] = total[j * rows : (j + 1) * rows].astype(ref.dtype)
 
 
 def decode(mine, theirs, bias, w_dec, first, given, far):
     tokens, lat = mine.shape
     half = w_dec.shape[1]
-    sums = [jax.ShapeDtypeStruct((tokens // far, half), jnp.float32)]
-    if far > 1:
-        sums.append(jax.ShapeDtypeStruct((far, tokens // far, half), jnp.bfloat16))
+    sums = [
+        jax.ShapeDtypeStruct((tokens // far, half), jnp.bfloat16 if j else jnp.float32)
+        for j in range(far)
+    ]
     codes, *sums = pl.pallas_call(
         functools.partial(decode_kernel, first, len(given)),
         out_shape=[jax.ShapeDtypeStruct((tokens, lat), jnp.bfloat16)] + sums,
@@ -169,27 +164,28 @@
     )(*codes)
 
 
-def sum_kernel(own, far, out, sent):
-    me = lax.axis_index("latent") // 2
+def sum_kernel(own, *refs):
+    *terms, out, sent = refs
     total = own[...]
-    for j in range(1, far.shape[0]):
-        total = total + far[me ^ j]
+    for ref in terms:
+        total = total + ref[...]
     out[...] = total
     sent[...] = total.astype(sent.dtype)
 
 
-def add_up(own, far):
+def add_up(terms):
+    shape = terms[0].shape
     return pl.pallas_call(
         sum_kernel,
         out_shape=[
-            jax.ShapeDtypeStruct(own.shape, jnp.float32),
-            jax.ShapeDtypeStruct(own.shape, jnp.bfloat16),
+            jax.ShapeDtypeStruct(shape, jnp.float32),
+            jax.ShapeDtypeStruct(shape, jnp.bfloat16),
         ],
-        in_specs=[WHOLE] * 2,
+        in_specs=[WHOLE] * len(terms),
         out_specs=[WHOLE] * 2,
         cost_estimate=waits(8),
         compiler_params=params(4),
-    )(own, far)
+    )(*terms)
 
 
 def error_kernel(total, rows, *refs):
@@ -199,15 +195,13 @@
         half = ref.shape[0] // 2
         term = ref[...].astype(jnp.float32)
         total = total + jnp.concatenate([term[half:], term[:half]])
-    err = (total - rows[...].astype(jnp.float32)).astype(out.dtype)
-    for j in range(out.shape[0]):
-        out[j] = err
-
-
-def error(total, near, rows, copies):
+    out[...] = (total - rows[...].astype(jnp.float32)).astype(out.dtype)
+
+
+def error(total, near, rows):
     return pl.pallas_call(
         error_kernel,
-        out_shape=jax.ShapeDtypeStruct((copies, *rows.shape), rows.dtype),
+        out_shape=jax.ShapeDtypeStruct(rows.shape, rows.dtype),
         in_specs=[WHOLE] * (2 + len(near)),
         out_specs=WHOLE,
         cost_estimate=waits(8),
@@ -215,24 +209,16 @@
     )(total, rows, *near)
 
 
-def far_exchange(blocks):
-    n = lax.axis_size("latent")
-    groups = [list(range(near, n, 2)) for near in range(2)]
-    return lax.all_to_all(blocks, "latent", 0, 0, axis_index_groups=groups, tiled=True)
-
-
-def all_errors(sums, rows, codes_t):
+def reduce_rows(sums):
     if lax.axis_size("latent") > DIRECT:
-        total = lax.psum_scatter(sums[0], "latent", scatter_dimension=0, tiled=True)
-        err = error(total, [], rows, 1)[0]
-        return lax.all_gather(err, "latent", axis=0, tiled=True)[None], codes_t
-    total, sent = add_up(sums[0], far_exchange(sums[1]))
-    err = error(total, [swap(sent, "latent", 1)], rows, sums[1].shape[0])
-    err, codes_t = lax.optimization_barrier((err, codes_t))
-    return far_exchange(err), codes_t
-
-
-def adam_kernel(codes_t, m, v, blocks, out, product, err):
+        return lax.psum_scatter(sums[0], "latent", scatter_dimension=0, tiled=True), []
+    terms = [sums[0]] + [swap(s, "latent", mask) for s, mask in zip(sums[1:], far_masks())]
+    total, sent = add_up(terms)
+    return total, [swap(sent, "latent", 1)]
+
+
+def adam_kernel(codes_t, m, v, *refs):
+    *blocks, out, product, err = refs
     tokens = codes_t.shape[1]
     b = 0.1 / (1.0 - 0.9**10) / tokens
     a = 0.9 / (1.0 - 0.9**10) / b
@@ -250,18 +236,16 @@
 
     @pl.when(i == 0)
     def _():
-        me = lax.axis_index("latent") // 2
-        n = blocks.shape[0]
-        picked = [blocks[me ^ j if n > 1 else 0] for j in range(n)]
-        err[...] = jnp.concatenate([x.astype(jnp.float32) for x in picked]).astype(err.dtype)
+        err[...] = stack(blocks)
         product[...] = multiply(0)
 
     def direction(c, start):
         at = pl.ds(pl.multiple_of(start, slab), slab)
         first = m[at, :].astype(jnp.float32) * a + c
         second = v[at, :].astype(jnp.float32) * p + (c * c) * q
-        root = second * lax.rsqrt(second)
-        return (first * pl.reciprocal(root + eps, approx=True)).astype(out.dtype)
+        inverse = lax.rsqrt(second)
+        x = inverse * eps
+        return (first * (inverse * (1.0 - x * (1.0 - x)))).astype(out.dtype)
 
     c = product[...]
     done = []
@@ -286,14 +270,14 @@
         adam_kernel,
         grid=(lat // rows,),
         out_shape=jax.ShapeDtypeStruct(m.shape, jnp.bfloat16),
-        in_specs=[WHOLE] * 4,
+        in_specs=[WHOLE] * (3 + len(blocks)),
         out_specs=pl.BlockSpec((rows, half), lambda i: (i, 0)),
         scratch_shapes=[
             pltpu.VMEM((64, half), jnp.float32),
             pltpu.VMEM((codes_t.shape[1], half), jnp.bfloat16),
         ],
         compiler_params=params(12),
-    )(codes_t, resident(m), resident(v), blocks)
+    )(codes_t, resident(m), resident(v), *blocks)
 
 
 def per_device(acts, w_enc, b_enc, w_dec, dec_m, dec_v):
@@ -308,8 +292,10 @@
         codes[k], sums = decode(
             mine[k], theirs[k], b_enc, w_dec, k * part, sums, len(blocks) if k else 1
         )
-    errors, codes_t = all_errors(sums, rows, turn(*codes))
-    return adam(codes_t, errors, dec_m, dec_v)
+    codes_t = turn(*codes)
+    total, near = reduce_rows(sums)
+    err = spread(error(total, near, rows))
+    return adam(codes_t, err, dec_m, dec_v)
 
 
 def solution(mesh):

time: 61.1 us -> 59.8 us (0.979)
  blocking collectives: 18 us -> 0 us
  starting transfers between devices: 8.79 us -> 17.7 us
  waiting for transfers between devices: 8.9 us -> 15 us
  Pallas kernels: 23.3 us -> 25.1 us
    all_to_all x2 -> x0, blocking collectives: 18 us -> none  [far_exchange(): lax.all_to_all(blocks, 'latent', 0, 0, axis_index_groups=groups, tiled=True)]
    ppermute x9 -> x15, starting transfers between devices: 8.79 us -> 17.7 us  [swap(): return lax.ppermute(value, axis, [(i, i ^ mask) for i in range(n)])]
    ppermute x9 -> x15, waiting for transfers between devices: 8.9 us -> 15 us  [swap(): return lax.ppermute(value, axis, [(i, i ^ mask) for i in range(n)])]
    pallas_call x1, Pallas kernels: 16.1 us -> 17.9 us  [adam(): pl.pallas_call(adam_kernel, grid=(lat // rows,), out_shape=jax.ShapeDtype...]
  transfers between devices with their start and end apart: 9 -> 15, of which waited for: 7 -> 10; matrix products, arithmetic and copies ran while one was open for 0% -> 0% of each run, Pallas kernels for 7% -> 7%
where the time goes in v6:
time: 59.8 us; the launch traced here: 59.6 us
  Pallas kernels  25.1 us (42%)
  starting transfers between devices  17.7 us (30%)
  waiting for transfers between devices  15 us (25%)
  local copies, waits for them, and re-layouts  1.62 us (3%)
    pallas_call x1, Pallas kernels, adam(): pl.pallas_call(adam_kernel, grid=(lat // rows,), out_shape=jax.ShapeDtype...  17.9 us
    ppermute x15, starting transfers between devices, swap(): return lax.ppermute(value, axis, [(i, i ^ mask) for i in range(n)])  17.7 us
    ppermute x15, waiting for transfers between devices, swap(): return lax.ppermute(value, axis, [(i, i ^ mask) for i in range(n)])  15 us
    pallas_call x2, Pallas kernels, encode(): pl.pallas_call(functools.partial(encode_kernel, first), out_shape=jax.Sha...  2.84 us
    pallas_call x2, Pallas kernels, decode(): pl.pallas_call(functools.partial(decode_kernel, first, len(given)), out_s...  2.58 us
    pallas_call x1, Pallas kernels, turn(): pl.pallas_call(functools.partial(turn_kernel, min(512, lat)), out_shape=j...  1.68 us
    unnamed x30, local copies, waits for them, and re-layouts  1.62 us
  transfers between devices with their start and end apart: 15, of which 10 were waited for; matrix products, arithmetic and copies ran while one was open for 0% of the time, Pallas kernels for 7%

profile of v6, /device:TPU:0, one launch (start us, length us, event | category | flops | bytes accessed | tf_op | source)
XLA Modules:
  0.0 59.6 jit_solution(8823702293354285714)
XLA Ops:
  0.0 0.5 collective-permute-start
  0.5 2.6 %collective-permute-start.2 = (bf16[4,1792]{1,0:T(4,128)(2,1)}, bf16[4,1792]{1,0:T(4,128)(2,1)S(1)}, u32[]{:S(2)}, u32[]{:S(2)}) collective-permute-start(bf16[4,1792]{1,0:T(4,128)(2,1)} %x.1), channel_id=1, source_target_pairs={{0,3},{1,2},{2,1},{3,0},{4,7},{5,6},{6,5},{7,4},{8,11},{9,10},{10,... | collective-permute-start | bytes 43016 | tf_op jit(solution)/shard_map/ppermute | solution.py:17
  3.1 0.1 collective-permute-start.1
  3.1 1.5 %copy-done.2 = bf16[4,1792]{1,0:T(4,128)(2,1)S(1)} copy-done((bf16[4,1792]{1,0:T(4,128)(2,1)S(1)}, bf16[4,1792]{1,0:T(4,128)(2,1)}, u32[]{:S(2)}) %copy-start.2) | copy-done | bytes 14360
  4.6 0.1 collective-permute-done.2.refs_3_
  4.7 2.3 %collective-permute-done.1.refs_2_ = bf16[4,1792]{1,0:T(4,128)(2,1)S(1)} collective-permute-done((bf16[4,1792]{1,0:T(4,128)(2,1)}, bf16[4,1792]{1,0:T(4,128)(2,1)S(1)}, u32[]{:S(2)}, u32[]{:S(2)}) %collective-permute-start.1) | collective-permute-done | bytes 14368 | tf_op jit(solution)/shard_map/ppermute | solution.py:17
  7.0 3.7 %collective-permute-start.5 = (bf16[16,896]{1,0:T(8,128)(2,1)S(1)}, bf16[16,896]{1,0:T(8,128)(2,1)S(1)}, u32[]{:S(2)}, u32[]{:S(2)}) collective-permute-start(bf16[16,896]{1,0:T(8,128)(2,1)S(1)} %shard_map.65.refs_0_.rows), channel_id=1, source_target_pairs={{0,12},{2,14},{4,8},{6,10},{8,4},{10,6},{12,0},{14,2},{1,13},{3,15... | collective-permute-start | bytes 86024 | tf_op jit(solution)/shard_map/ppermute | solution.py:17
  10.7 0.8 %collective-permute-start.3 = (bf16[16,896]{1,0:T(8,128)(2,1)S(1)}, bf16[16,896]{1,0:T(8,128)(2,1)S(1)}, u32[]{:S(2)}, u32[]{:S(2)}) collective-permute-start(bf16[16,896]{1,0:T(8,128)(2,1)S(1)} %shard_map.65.refs_0_.rows), channel_id=1, source_target_pairs={{0,4},{2,6},{4,0},{6,2},{8,12},{10,14},{12,8},{14,10},{1,5},{3,7},... | collective-permute-start | bytes 86024 | tf_op jit(solution)/shard_map/ppermute | solution.py:17
  11.5 1.3 %collective-permute-done.5.refs_3_ = bf16[16,896]{1,0:T(8,128)(2,1)S(1)} collective-permute-done((bf16[16,896]{1,0:T(8,128)(2,1)S(1)}, bf16[16,896]{1,0:T(8,128)(2,1)S(1)}, u32[]{:S(2)}, u32[]{:S(2)}) %collective-permute-start.5) | collective-permute-done | bytes 28704 | tf_op jit(solution)/shard_map/ppermute | solution.py:17
  12.8 2.7 %collective-permute-done.4.refs_2_ = bf16[16,896]{1,0:T(8,128)(2,1)S(1)} collective-permute-done((bf16[16,896]{1,0:T(8,128)(2,1)S(1)}, bf16[16,896]{1,0:T(8,128)(2,1)S(1)}, u32[]{:S(2)}, u32[]{:S(2)}) %collective-permute-start.4) | collective-permute-done | bytes 28704 | tf_op jit(solution)/shard_map/ppermute | solution.py:17
  15.5 1.4 %shard_map.66.mine = f32[64,4096]{1,0:T(8,128)S(1)} custom-call(bf16[16,896]{1,0:T(8,128)(2,1)S(1)} %shard_map.65.refs_0_.rows, bf16[16,896]{1,0:T(8,128)(2,1)S(1)} %collective-permute-done.3.refs_1_, bf16[16,896]{1,0:T(8,128)(2,1)S(1)} %collective-permute-done.4.refs_2_, bf16[16,896]{1,0:T(8,128)(2,1)S(1)} %collective-permute-done.5.refs_3_, ...), custom_call_target="tpu_custom_call" | custom-call | flops 2449999872 | bytes 7340032 | tf_op jit(solution)/shard_map/pallas_call | solution.py:101
  16.9 0.0 slice-start.2
  16.9 0.1 collective-permute-start.6
  17.0 1.4 %shard_map.68.mine = f32[64,4096]{1,0:T(8,128)S(1)} custom-call(bf16[16,896]{1,0:T(8,128)(2,1)S(1)} %shard_map.65.refs_0_.rows, bf16[16,896]{1,0:T(8,128)(2,1)S(1)} %collective-permute-done.3.refs_1_, bf16[16,896]{1,0:T(8,128)(2,1)S(1)} %collective-permute-done.4.refs_2_, bf16[16,896]{1,0:T(8,128)(2,1)S(1)} %collective-permute-done.5.refs_3_, ...), custom_call_target="tpu_custom_call" | custom-call | flops 2449999872 | bytes 7340032 | tf_op jit(solution)/shard_map/pallas_call | solution.py:101
  18.4 0.6 collective-permute-start.7
  19.0 0.7 %collective-permute-done.6.theirs = f32[64,4096]{1,0:T(8,128)S(1)} collective-permute-done((f32[64,4096]{1,0:T(8,128)S(1)}, f32[64,4096]{1,0:T(8,128)S(1)}, u32[]{:S(2)}, u32[]{:S(2)}) %collective-permute-start.6) | collective-permute-done | bytes 1048608 | tf_op jit(solution)/shard_map/ppermute | solution.py:17
  19.7 0.1 slice-done.3
  19.8 1.3 %shard_map.67 = (bf16[64,4096]{1,0:T(8,128)(2,1)S(1)}, f32[64,896]{1,0:T(8,128)S(1)}) custom-call(f32[64,4096]{1,0:T(8,128)S(1)} %shard_map.66.mine, f32[64,4096]{1,0:T(8,128)S(1)} %collective-permute-done.6.theirs, f32[1,8192]{1,0:T(1,128)S(1)} %bitcast.7, bf16[8192,896]{1,0:T(8,128)(2,1)S(1)} %bitcast.2), custom_call_target="tpu_custom_call" | custom-call | flops 2449999872 | bytes 7340032 | tf_op jit(solution)/shard_map/pallas_call | solution.py:132
  21.1 0.2 collective-permute-done.7.theirs
  21.3 1.3 %shard_map.69 = (bf16[64,4096]{1,0:T(8,128)(2,1)S(1)}, f32[16,896]{1,0:T(8,128)S(1)}, bf16[16,896]{1,0:T(8,128)(2,1)S(1)}, bf16[16,896]{1,0:T(8,128)(2,1)S(1)}, bf16[16,896]{1,0:T(8,128)(2,1)S(1)}) custom-call(f32[64,4096]{1,0:T(8,128)S(1)} %shard_map.68.mine, f32[64,4096]{1,0:T(8,128)S(1)} %collective-permute-done.7.theirs, f32[1,8192]{1,0:T(1,128)S(1)} %bitcast.8, ...), custom_call_target="tpu_custom_call" | custom-call | flops 2449999872 | bytes 7340032 | tf_op jit(solution)/shard_map/pallas_call | solution.py:132
  22.6 0.1 collective-permute-start.8
  22.7 2.1 %collective-permute-start.9 = (bf16[16,896]{1,0:T(8,128)(2,1)S(1)}, bf16[16,896]{1,0:T(8,128)(2,1)S(1)}, u32[]{:S(2)}, u32[]{:S(2)}) collective-permute-start(bf16[16,896]{1,0:T(8,128)(2,1)S(1)} %get-tuple-element.19), channel_id=1, source_target_pairs={{0,8},{2,10},{4,12},{6,14},{8,0},{10,2},{12,4},{14,6},{1,9},{3,11}... | collective-permute-start | bytes 86024 | tf_op jit(solution)/shard_map/ppermute | solution.py:17
  24.8 2.3 %collective-permute-start.10 = (bf16[16,896]{1,0:T(8,128)(2,1)S(1)}, bf16[16,896]{1,0:T(8,128)(2,1)S(1)}, u32[]{:S(2)}, u32[]{:S(2)}) collective-permute-start(bf16[16,896]{1,0:T(8,128)(2,1)S(1)} %get-tuple-element.20), channel_id=1, source_target_pairs={{0,12},{2,14},{4,8},{6,10},{8,4},{10,6},{12,0},{14,2},{1,13},{3,15... | collective-permute-start | bytes 86024 | tf_op jit(solution)/shard_map/ppermute | solution.py:17
  27.1 0.5 collective-permute-done.9.refs_1_
  27.5 2.9 %collective-permute-done.10.refs_2_ = bf16[16,896]{1,0:T(8,128)(2,1)S(1)} collective-permute-done((bf16[16,896]{1,0:T(8,128)(2,1)S(1)}, bf16[16,896]{1,0:T(8,128)(2,1)S(1)}, u32[]{:S(2)}, u32[]{:S(2)}) %collective-permute-start.10) | collective-permute-done | bytes 28704 | tf_op jit(solution)/shard_map/ppermute | solution.py:17
  30.5 0.6 %collective-permute-start.11 = (bf16[16,896]{1,0:T(8,128)(2,1)S(1)}, bf16[16,896]{1,0:T(8,128)(2,1)S(1)}, u32[]{:S(2)}, u32[]{:S(2)}) collective-permute-start(bf16[16,896]{1,0:T(8,128)(2,1)S(1)} %get-tuple-element.22), channel_id=1, source_target_pairs={{0,2},{2,0},{4,6},{6,4},{8,10},{10,8},{12,14},{14,12},{1,3},{3,1},... | collective-permute-start | bytes 86024 | tf_op jit(solution)/shard_map/ppermute | solution.py:17
  31.1 3.3 %collective-permute-done.11.refs_0_ = bf16[16,896]{1,0:T(8,128)(2,1)S(1)} collective-permute-done((bf16[16,896]{1,0:T(8,128)(2,1)S(1)}, bf16[16,896]{1,0:T(8,128)(2,1)S(1)}, u32[]{:S(2)}, u32[]{:S(2)}) %collective-permute-start.11) | collective-permute-done | bytes 28704 | tf_op jit(solution)/shard_map/ppermute | solution.py:17
  34.4 2.4 %collective-permute-start.14 = (bf16[16,896]{1,0:T(8,128)(2,1)S(1)}, bf16[16,896]{1,0:T(8,128)(2,1)S(1)}, u32[]{:S(2)}, u32[]{:S(2)}) collective-permute-start(bf16[16,896]{1,0:T(8,128)(2,1)S(1)} %shard_map.72.refs_0_), channel_id=1, source_target_pairs={{0,12},{2,14},{4,8},{6,10},{8,4},{10,6},{12,0},{14,2},{1,13},{3,15... | collective-permute-start | bytes 86024 | tf_op jit(solution)/shard_map/ppermute | solution.py:17
  36.8 2.1 %collective-permute-start.12 = (bf16[16,896]{1,0:T(8,128)(2,1)S(1)}, bf16[16,896]{1,0:T(8,128)(2,1)S(1)}, u32[]{:S(2)}, u32[]{:S(2)}) collective-permute-start(bf16[16,896]{1,0:T(8,128)(2,1)S(1)} %shard_map.72.refs_0_), channel_id=1, source_target_pairs={{0,4},{2,6},{4,0},{6,2},{8,12},{10,14},{12,8},{14,10},{1,5},{3,7},... | collective-permute-start | bytes 86024 | tf_op jit(solution)/shard_map/ppermute | solution.py:17
  38.9 1.7 %shard_map.70.codes_t = bf16[8192,64]{1,0:T(8,128)(2,1)S(1)} custom-call(bf16[64,4096]{1,0:T(8,128)(2,1)S(1)} %get-tuple-element.14.refs_0_, bf16[64,4096]{1,0:T(8,128)(2,1)S(1)} %get-tuple-element.16.refs_1_), custom_call_target="tpu_custom_call" | custom-call | flops 1400000000 | bytes 4194304 | tf_op jit(solution)/shard_map/pallas_call | solution.py:157
  40.6 1.0 %collective-permute-done.13.refs_2_ = bf16[16,896]{1,0:T(8,128)(2,1)S(1)} collective-permute-done((bf16[16,896]{1,0:T(8,128)(2,1)S(1)}, bf16[16,896]{1,0:T(8,128)(2,1)S(1)}, u32[]{:S(2)}, u32[]{:S(2)}) %collective-permute-start.13) | collective-permute-done | bytes 28704 | tf_op jit(solution)/shard_map/ppermute | solution.py:17
  41.6 17.9 %shard_map.73 = bf16[8192,896]{1,0:T(8,128)(2,1)} custom-call(bf16[8192,64]{1,0:T(8,128)(2,1)S(1)} %shard_map.70.codes_t, bf16[8192,896]{1,0:T(8,128)(2,1)S(1)} %bitcast.4, bf16[8192,896]{1,0:T(8,128)(2,1)S(1)} %bitcast.6, bf16[16,896]{1,0:T(8,128)(2,1)S(1)} %shard_map.72.refs_0_, bf16[16,896]{1,0:T(8,128)(2,1)S(1)} %collective-permute-done.12.refs_1_, ...), custom_call_target="tpu_custom_call" | custom-call | tf_op jit(solution)/shard_map/pallas_call | solution.py:269
  (41 shorter events, 0.1 us)
Async XLA Ops:
  0.0 15.5 %copy-start = (bf16[896,8192]{1,0:T(8,128)(2,1)S(1)}, bf16[896,8192]{1,0:T(8,128)(2,1)}, u32[]{:S(2)}) copy-start(bf16[896,8192]{1,0:T(8,128)(2,1)} %refs_4_.3) | copy-start | bytes 44040196
  0.0 4.6 %collective-permute-start = (bf16[4,1792]{1,0:T(4,128)(2,1)}, bf16[4,1792]{1,0:T(4,128)(2,1)S(1)}, u32[]{:S(2)}, u32[]{:S(2)}) collective-permute-start(bf16[4,1792]{1,0:T(4,128)(2,1)} %x.1), channel_id=1, source_target_pairs={{0,1},{1,0},{2,3},{3,2},{4,5},{5,4},{6,7},{7,6},{8,9},{9,8},{10,11... | collective-permute-start | bytes 43016 | tf_op jit(solution)/shard_map/ppermute | solution.py:17
  0.5 4.2 %collective-permute-start.2 = (bf16[4,1792]{1,0:T(4,128)(2,1)}, bf16[4,1792]{1,0:T(4,128)(2,1)S(1)}, u32[]{:S(2)}, u32[]{:S(2)}) collective-permute-start(bf16[4,1792]{1,0:T(4,128)(2,1)} %x.1), channel_id=1, source_target_pairs={{0,3},{1,2},{2,1},{3,0},{4,7},{5,6},{6,5},{7,4},{8,11},{9,10},{10,... | collective-permute-start | bytes 43016 | tf_op jit(solution)/shard_map/ppermute | solution.py:17
  3.1 3.9 %collective-permute-start.1 = (bf16[4,1792]{1,0:T(4,128)(2,1)}, bf16[4,1792]{1,0:T(4,128)(2,1)S(1)}, u32[]{:S(2)}, u32[]{:S(2)}) collective-permute-start(bf16[4,1792]{1,0:T(4,128)(2,1)} %x.1), channel_id=1, source_target_pairs={{0,2},{1,3},{2,0},{3,1},{4,6},{5,7},{6,4},{7,5},{8,10},{9,11},{10,... | collective-permute-start | bytes 43016 | tf_op jit(solution)/shard_map/ppermute | solution.py:17
  3.1 1.5 %copy-start.2 = (bf16[4,1792]{1,0:T(4,128)(2,1)S(1)}, bf16[4,1792]{1,0:T(4,128)(2,1)}, u32[]{:S(2)}) copy-start(bf16[4,1792]{1,0:T(4,128)(2,1)} %x.1) | copy-start | bytes 43012
  7.0 12.7 %slice-start = ((s8[14680064]{0:T(1024)(128)(4,1)}), s8[4194304]{0:T(1024)(128)(4,1)S(1)}, s32[]{:S(2)}) async-start(s8[14680064]{0:T(1024)(128)(4,1)} %bitcast.1), calls=%async_computation | async-start | bytes 8388608
  7.0 12.6 %slice-start.1 = ((s8[14680064]{0:T(1024)(128)(4,1)}), s8[4194304]{0:T(1024)(128)(4,1)S(1)}, s32[]{:S(2)}) async-start(s8[14680064]{0:T(1024)(128)(4,1)} %bitcast.1), calls=%async_computation.1 | async-start | bytes 8388608
  7.0 12.6 %copy-start.1 = (f32[8192]{0:T(1024)S(1)}, f32[8192]{0:T(1024)}, u32[]{:S(2)}) copy-start(f32[8192]{0:T(1024)} %param.8) | copy-start | bytes 98308
  7.0 5.7 %collective-permute-start.5 = (bf16[16,896]{1,0:T(8,128)(2,1)S(1)}, bf16[16,896]{1,0:T(8,128)(2,1)S(1)}, u32[]{:S(2)}, u32[]{:S(2)}) collective-permute-start(bf16[16,896]{1,0:T(8,128)(2,1)S(1)} %shard_map.65.refs_0_.rows), channel_id=1, source_target_pairs={{0,12},{2,14},{4,8},{6,10},{8,4},{10,6},{12,0},{14,2},{1,13},{3,15... | collective-permute-start | bytes 86024 | tf_op jit(solution)/shard_map/ppermute | solution.py:17
  10.7 4.8 %collective-permute-start.4 = (bf16[16,896]{1,0:T(8,128)(2,1)S(1)}, bf16[16,896]{1,0:T(8,128)(2,1)S(1)}, u32[]{:S(2)}, u32[]{:S(2)}) collective-permute-start(bf16[16,896]{1,0:T(8,128)(2,1)S(1)} %shard_map.65.refs_0_.rows), channel_id=1, source_target_pairs={{0,8},{2,10},{4,12},{6,14},{8,0},{10,2},{12,4},{14,6},{1,9},{3,11}... | collective-permute-start | bytes 86024 | tf_op jit(solution)/shard_map/ppermute | solution.py:17
  10.7 4.8 %collective-permute-start.3 = (bf16[16,896]{1,0:T(8,128)(2,1)S(1)}, bf16[16,896]{1,0:T(8,128)(2,1)S(1)}, u32[]{:S(2)}, u32[]{:S(2)}) collective-permute-start(bf16[16,896]{1,0:T(8,128)(2,1)S(1)} %shard_map.65.refs_0_.rows), channel_id=1, source_target_pairs={{0,4},{2,6},{4,0},{6,2},{8,12},{10,14},{12,8},{14,10},{1,5},{3,7},... | collective-permute-start | bytes 86024 | tf_op jit(solution)/shard_map/ppermute | solution.py:17
  16.9 2.8 %slice-start.2 = ((s8[14680064]{0:T(1024)(128)(4,1)}), s8[4194304]{0:T(1024)(128)(4,1)S(1)}, s32[]{:S(2)}) async-start(s8[14680064]{0:T(1024)(128)(4,1)} %bitcast.1), calls=%async_computation.2 | async-start | bytes 8388608
  16.9 2.9 %slice-start.3 = ((s8[14680064]{0:T(1024)(128)(4,1)}), s8[2097152]{0:T(1024)(128)(4,1)S(1)}, s32[]{:S(2)}) async-start(s8[14680064]{0:T(1024)(128)(4,1)} %bitcast.1), calls=%async_computation.3 | async-start | bytes 4194304
  16.9 2.7 %collective-permute-start.6 = (f32[64,4096]{1,0:T(8,128)S(1)}, f32[64,4096]{1,0:T(8,128)S(1)}, u32[]{:S(2)}, u32[]{:S(2)}) collective-permute-start(f32[64,4096]{1,0:T(8,128)S(1)} %shard_map.66.mine), channel_id=1, source_target_pairs={{0,1},{1,0},{2,3},{3,2},{4,5},{5,4},{6,7},{7,6},{8,9},{9,8},{10,11... | collective-permute-start | bytes 3145736 | tf_op jit(solution)/shard_map/ppermute | solution.py:17
  18.4 2.8 %collective-permute-start.7 = (f32[64,4096]{1,0:T(8,128)S(1)}, f32[64,4096]{1,0:T(8,128)S(1)}, u32[]{:S(2)}, u32[]{:S(2)}) collective-permute-start(f32[64,4096]{1,0:T(8,128)S(1)} %shard_map.68.mine), channel_id=1, source_target_pairs={{0,1},{1,0},{2,3},{3,2},{4,5},{5,4},{6,7},{7,6},{8,9},{9,8},{10,11... | collective-permute-start | bytes 3145736 | tf_op jit(solution)/shard_map/ppermute | solution.py:17
  21.3 20.3 %slice-start.4 = ((s8[14680064]{0:T(1024)(128)(4,1)}), s8[4194304]{0:T(1024)(128)(4,1)S(1)}, s32[]{:S(2)}) async-start(s8[14680064]{0:T(1024)(128)(4,1)} %bitcast.3), calls=%async_computation.4 | async-start | bytes 8388608
  21.3 20.3 %slice-start.5 = ((s8[14680064]{0:T(1024)(128)(4,1)}), s8[4194304]{0:T(1024)(128)(4,1)S(1)}, s32[]{:S(2)}) async-start(s8[14680064]{0:T(1024)(128)(4,1)} %bitcast.3), calls=%async_computation.5 | async-start | bytes 8388608
  21.3 20.3 %slice-start.8 = ((s8[14680064]{0:T(1024)(128)(4,1)}), s8[4194304]{0:T(1024)(128)(4,1)S(1)}, s32[]{:S(2)}) async-start(s8[14680064]{0:T(1024)(128)(4,1)} %bitcast.5), calls=%async_computation.8 | async-start | bytes 8388608
  21.3 20.3 %slice-start.9 = ((s8[14680064]{0:T(1024)(128)(4,1)}), s8[4194304]{0:T(1024)(128)(4,1)S(1)}, s32[]{:S(2)}) async-start(s8[14680064]{0:T(1024)(128)(4,1)} %bitcast.5), calls=%async_computation.9 | async-start | bytes 8388608
  22.6 4.5 %collective-permute-start.8 = (bf16[16,896]{1,0:T(8,128)(2,1)S(1)}, bf16[16,896]{1,0:T(8,128)(2,1)S(1)}, u32[]{:S(2)}, u32[]{:S(2)}) collective-permute-start(bf16[16,896]{1,0:T(8,128)(2,1)S(1)} %get-tuple-element.18), channel_id=1, source_target_pairs={{0,4},{2,6},{4,0},{6,2},{8,12},{10,14},{12,8},{14,10},{1,5},{3,7},... | collective-permute-start | bytes 86024 | tf_op jit(solution)/shard_map/ppermute | solution.py:17
  22.7 4.9 %collective-permute-start.9 = (bf16[16,896]{1,0:T(8,128)(2,1)S(1)}, bf16[16,896]{1,0:T(8,128)(2,1)S(1)}, u32[]{:S(2)}, u32[]{:S(2)}) collective-permute-start(bf16[16,896]{1,0:T(8,128)(2,1)S(1)} %get-tuple-element.19), channel_id=1, source_target_pairs={{0,8},{2,10},{4,12},{6,14},{8,0},{10,2},{12,4},{14,6},{1,9},{3,11}... | collective-permute-start | bytes 86024 | tf_op jit(solution)/shard_map/ppermute | solution.py:17
  24.8 5.7 %collective-permute-start.10 = (bf16[16,896]{1,0:T(8,128)(2,1)S(1)}, bf16[16,896]{1,0:T(8,128)(2,1)S(1)}, u32[]{:S(2)}, u32[]{:S(2)}) collective-permute-start(bf16[16,896]{1,0:T(8,128)(2,1)S(1)} %get-tuple-element.20), channel_id=1, source_target_pairs={{0,12},{2,14},{4,8},{6,10},{8,4},{10,6},{12,0},{14,2},{1,13},{3,15... | collective-permute-start | bytes 86024 | tf_op jit(solution)/shard_map/ppermute | solution.py:17
  30.5 11.1 %slice-start.6 = ((s8[14680064]{0:T(1024)(128)(4,1)}), s8[4194304]{0:T(1024)(128)(4,1)S(1)}, s32[]{:S(2)}) async-start(s8[14680064]{0:T(1024)(128)(4,1)} %bitcast.3), calls=%async_computation.6 | async-start | bytes 8388608
  30.5 11.1 %slice-start.10 = ((s8[14680064]{0:T(1024)(128)(4,1)}), s8[4194304]{0:T(1024)(128)(4,1)S(1)}, s32[]{:S(2)}) async-start(s8[14680064]{0:T(1024)(128)(4,1)} %bitcast.5), calls=%async_computation.10 | async-start | bytes 8388608
  30.5 3.9 %collective-permute-start.11 = (bf16[16,896]{1,0:T(8,128)(2,1)S(1)}, bf16[16,896]{1,0:T(8,128)(2,1)S(1)}, u32[]{:S(2)}, u32[]{:S(2)}) collective-permute-start(bf16[16,896]{1,0:T(8,128)(2,1)S(1)} %get-tuple-element.22), channel_id=1, source_target_pairs={{0,2},{2,0},{4,6},{6,4},{8,10},{10,8},{12,14},{14,12},{1,3},{3,1},... | collective-permute-start | bytes 86024 | tf_op jit(solution)/shard_map/ppermute | solution.py:17
  34.4 7.2 %slice-start.7 = ((s8[14680064]{0:T(1024)(128)(4,1)}), s8[2097152]{0:T(1024)(128)(4,1)S(1)}, s32[]{:S(2)}) async-start(s8[14680064]{0:T(1024)(128)(4,1)} %bitcast.3), calls=%async_computation.7 | async-start | bytes 4194304
  34.4 7.2 %slice-start.11 = ((s8[14680064]{0:T(1024)(128)(4,1)}), s8[2097152]{0:T(1024)(128)(4,1)S(1)}, s32[]{:S(2)}) async-start(s8[14680064]{0:T(1024)(128)(4,1)} %bitcast.5), calls=%async_computation.11 | async-start | bytes 4194304
  34.4 6.1 %collective-permute-start.14 = (bf16[16,896]{1,0:T(8,128)(2,1)S(1)}, bf16[16,896]{1,0:T(8,128)(2,1)S(1)}, u32[]{:S(2)}, u32[]{:S(2)}) collective-permute-start(bf16[16,896]{1,0:T(8,128)(2,1)S(1)} %shard_map.72.refs_0_), channel_id=1, source_target_pairs={{0,12},{2,14},{4,8},{6,10},{8,4},{10,6},{12,0},{14,2},{1,13},{3,15... | collective-permute-start | bytes 86024 | tf_op jit(solution)/shard_map/ppermute | solution.py:17
  36.8 4.8 %collective-permute-start.13 = (bf16[16,896]{1,0:T(8,128)(2,1)S(1)}, bf16[16,896]{1,0:T(8,128)(2,1)S(1)}, u32[]{:S(2)}, u32[]{:S(2)}) collective-permute-start(bf16[16,896]{1,0:T(8,128)(2,1)S(1)} %shard_map.72.refs_0_), channel_id=1, source_target_pairs={{0,8},{2,10},{4,12},{6,14},{8,0},{10,2},{12,4},{14,6},{1,9},{3,11}... | collective-permute-start | bytes 86024 | tf_op jit(solution)/shard_map/ppermute | solution.py:17
  36.8 4.8 %collective-permute-start.12 = (bf16[16,896]{1,0:T(8,128)(2,1)S(1)}, bf16[16,896]{1,0:T(8,128)(2,1)S(1)}, u32[]{:S(2)}, u32[]{:S(2)}) collective-permute-start(bf16[16,896]{1,0:T(8,128)(2,1)S(1)} %shard_map.72.refs_0_), channel_id=1, source_target_pairs={{0,4},{2,6},{4,0},{6,2},{8,12},{10,14},{12,8},{14,10},{1,5},{3,7},... | collective-permute-start | bytes 86024 | tf_op jit(solution)/shard_map/ppermute | solution.py:17

commit v7 on v6

--- a/solution.py
+++ b/solution.py
@@ -165,24 +165,19 @@
 
 
 def sum_kernel(own, *refs):
-    *terms, out, sent = refs
+    *terms, out = refs
     total = own[...]
     for ref in terms:
         total = total + ref[...]
     out[...] = total
-    sent[...] = total.astype(sent.dtype)
 
 
 def add_up(terms):
-    shape = terms[0].shape
     return pl.pallas_call(
         sum_kernel,
-        out_shape=[
-            jax.ShapeDtypeStruct(shape, jnp.float32),
-            jax.ShapeDtypeStruct(shape, jnp.bfloat16),
-        ],
+        out_shape=jax.ShapeDtypeStruct(terms[0].shape, jnp.float32),
         in_specs=[WHOLE] * len(terms),
-        out_specs=[WHOLE] * 2,
+        out_specs=WHOLE,
         cost_estimate=waits(8),
         compiler_params=params(4),
     )(*terms)
@@ -193,8 +188,7 @@
     total = total[...]
     for ref in near:
         half = ref.shape[0] // 2
-        term = ref[...].astype(jnp.float32)
-        total = total + jnp.concatenate([term[half:], term[:half]])
+        total = total + jnp.concatenate([ref[half:], ref[:half]])
     out[...] = (total - rows[...].astype(jnp.float32)).astype(out.dtype)
 
 
@@ -213,8 +207,8 @@
     if lax.axis_size("latent") > DIRECT:
         return lax.psum_scatter(sums[0], "latent", scatter_dimension=0, tiled=True), []
     terms = [sums[0]] + [swap(s, "latent", mask) for s, mask in zip(sums[1:], far_masks())]
-    total, sent = add_up(terms)
-    return total, [swap(sent, "latent", 1)]
+    total = add_up(terms)
+    return total, [swap(total, "latent", 1)]
 
 
 def adam_kernel(codes_t, m, v, *refs):
@@ -239,13 +233,15 @@
         err[...] = stack(blocks)
         product[...] = multiply(0)
 
+    a, p, q, eps = (jnp.asarray(x, out.dtype) for x in (a, p, q, eps))
+
     def direction(c, start):
         at = pl.ds(pl.multiple_of(start, slab), slab)
-        first = m[at, :].astype(jnp.float32) * a + c
-        second = v[at, :].astype(jnp.float32) * p + (c * c) * q
-        inverse = lax.rsqrt(second)
-        x = inverse * eps
-        return (first * (inverse * (1.0 - x * (1.0 - x)))).astype(out.dtype)
+        c = c.astype(out.dtype)
+        first = m[at, :] * a + c
+        second = v[at, :] * p + (c * c) * q
+        root = second * lax.rsqrt(second)
+        return first * pl.reciprocal(root + eps, approx=True)
 
     c = product[...]
     done = []

time: 59.8 us -> 55.4 us (0.926)
  Pallas kernels: 25.1 us -> 20.3 us
    pallas_call x1, Pallas kernels: 17.9 us -> 13.2 us  [adam(): pl.pallas_call(adam_kernel, grid=(lat // rows,), out_shape=jax.ShapeDtype...]
  transfers between devices with their start and end apart: 15 -> 15, of which waited for: 10 -> 10; matrix products, arithmetic and copies ran while one was open for 0% -> 0% of each run, Pallas kernels for 7% -> 8%
where the time goes in v7:
time: 55.4 us; the launch traced here: 55.1 us
  Pallas kernels  20.3 us (37%)
  starting transfers between devices  17.7 us (32%)
  waiting for transfers between devices  15.3 us (28%)
  local copies, waits for them, and re-layouts  1.63 us (3%)
    ppermute x15, starting transfers between devices, swap(): return lax.ppermute(value, axis, [(i, i ^ mask) for i in range(n)])  17.7 us
    ppermute x15, waiting for transfers between devices, swap(): return lax.ppermute(value, axis, [(i, i ^ mask) for i in range(n)])  15.3 us
    pallas_call x1, Pallas kernels, adam(): pl.pallas_call(adam_kernel, grid=(lat // rows,), out_shape=jax.ShapeDtype...  13.2 us
    pallas_call x2, Pallas kernels, encode(): pl.pallas_call(functools.partial(encode_kernel, first), out_shape=jax.Sha...  2.84 us
    pallas_call x2, Pallas kernels, decode(): pl.pallas_call(functools.partial(decode_kernel, first, len(given)), out_s...  2.58 us
    pallas_call x1, Pallas kernels, turn(): pl.pallas_call(functools.partial(turn_kernel, min(512, lat)), out_shape=j...  1.68 us
    unnamed x30, local copies, waits for them, and re-layouts  1.63 us
  transfers between devices with their start and end apart: 15, of which 10 were waited for; matrix products, arithmetic and copies ran while one was open for 0% of the time, Pallas kernels for 8%

profile of v7, /device:TPU:0, one launch (start us, length us, event | category | flops | bytes accessed | tf_op | source)
XLA Modules:
  0.0 55.1 jit_solution(346464780034340705)
XLA Ops:
  0.0 0.5 collective-permute-start
  0.5 2.6 %collective-permute-start.2 = (bf16[4,1792]{1,0:T(4,128)(2,1)}, bf16[4,1792]{1,0:T(4,128)(2,1)S(1)}, u32[]{:S(2)}, u32[]{:S(2)}) collective-permute-start(bf16[4,1792]{1,0:T(4,128)(2,1)} %x.1), channel_id=1, source_target_pairs={{0,3},{1,2},{2,1},{3,0},{4,7},{5,6},{6,5},{7,4},{8,11},{9,10},{10,... | collective-permute-start | bytes 43016 | tf_op jit(solution)/shard_map/ppermute | solution.py:17
  3.1 0.1 collective-permute-start.1
  3.1 1.5 %copy-done.2 = bf16[4,1792]{1,0:T(4,128)(2,1)S(1)} copy-done((bf16[4,1792]{1,0:T(4,128)(2,1)S(1)}, bf16[4,1792]{1,0:T(4,128)(2,1)}, u32[]{:S(2)}) %copy-start.2) | copy-done | bytes 14360
  4.6 0.1 collective-permute-done.2.refs_3_
  4.7 2.3 %collective-permute-done.1.refs_2_ = bf16[4,1792]{1,0:T(4,128)(2,1)S(1)} collective-permute-done((bf16[4,1792]{1,0:T(4,128)(2,1)}, bf16[4,1792]{1,0:T(4,128)(2,1)S(1)}, u32[]{:S(2)}, u32[]{:S(2)}) %collective-permute-start.1) | collective-permute-done | bytes 14368 | tf_op jit(solution)/shard_map/ppermute | solution.py:17
  7.0 3.7 %collective-permute-start.5 = (bf16[16,896]{1,0:T(8,128)(2,1)S(1)}, bf16[16,896]{1,0:T(8,128)(2,1)S(1)}, u32[]{:S(2)}, u32[]{:S(2)}) collective-permute-start(bf16[16,896]{1,0:T(8,128)(2,1)S(1)} %shard_map.65.refs_0_.rows), channel_id=1, source_target_pairs={{0,12},{2,14},{4,8},{6,10},{8,4},{10,6},{12,0},{14,2},{1,13},{3,15... | collective-permute-start | bytes 86024 | tf_op jit(solution)/shard_map/ppermute | solution.py:17
  10.7 0.8 %collective-permute-start.3 = (bf16[16,896]{1,0:T(8,128)(2,1)S(1)}, bf16[16,896]{1,0:T(8,128)(2,1)S(1)}, u32[]{:S(2)}, u32[]{:S(2)}) collective-permute-start(bf16[16,896]{1,0:T(8,128)(2,1)S(1)} %shard_map.65.refs_0_.rows), channel_id=1, source_target_pairs={{0,4},{2,6},{4,0},{6,2},{8,12},{10,14},{12,8},{14,10},{1,5},{3,7},... | collective-permute-start | bytes 86024 | tf_op jit(solution)/shard_map/ppermute | solution.py:17
  11.5 1.3 %collective-permute-done.5.refs_3_ = bf16[16,896]{1,0:T(8,128)(2,1)S(1)} collective-permute-done((bf16[16,896]{1,0:T(8,128)(2,1)S(1)}, bf16[16,896]{1,0:T(8,128)(2,1)S(1)}, u32[]{:S(2)}, u32[]{:S(2)}) %collective-permute-start.5) | collective-permute-done | bytes 28704 | tf_op jit(solution)/shard_map/ppermute | solution.py:17
  12.8 2.7 %collective-permute-done.4.refs_2_ = bf16[16,896]{1,0:T(8,128)(2,1)S(1)} collective-permute-done((bf16[16,896]{1,0:T(8,128)(2,1)S(1)}, bf16[16,896]{1,0:T(8,128)(2,1)S(1)}, u32[]{:S(2)}, u32[]{:S(2)}) %collective-permute-start.4) | collective-permute-done | bytes 28704 | tf_op jit(solution)/shard_map/ppermute | solution.py:17
  15.5 1.4 %shard_map.66.mine = f32[64,4096]{1,0:T(8,128)S(1)} custom-call(bf16[16,896]{1,0:T(8,128)(2,1)S(1)} %shard_map.65.refs_0_.rows, bf16[16,896]{1,0:T(8,128)(2,1)S(1)} %collective-permute-done.3.refs_1_, bf16[16,896]{1,0:T(8,128)(2,1)S(1)} %collective-permute-done.4.refs_2_, bf16[16,896]{1,0:T(8,128)(2,1)S(1)} %collective-permute-done.5.refs_3_, ...), custom_call_target="tpu_custom_call" | custom-call | flops 2449999872 | bytes 7340032 | tf_op jit(solution)/shard_map/pallas_call | solution.py:101
  16.9 0.0 slice-start.2
  16.9 0.1 collective-permute-start.6
  17.0 1.4 %shard_map.68.mine = f32[64,4096]{1,0:T(8,128)S(1)} custom-call(bf16[16,896]{1,0:T(8,128)(2,1)S(1)} %shard_map.65.refs_0_.rows, bf16[16,896]{1,0:T(8,128)(2,1)S(1)} %collective-permute-done.3.refs_1_, bf16[16,896]{1,0:T(8,128)(2,1)S(1)} %collective-permute-done.4.refs_2_, bf16[16,896]{1,0:T(8,128)(2,1)S(1)} %collective-permute-done.5.refs_3_, ...), custom_call_target="tpu_custom_call" | custom-call | flops 2449999872 | bytes 7340032 | tf_op jit(solution)/shard_map/pallas_call | solution.py:101
  18.4 0.6 %collective-permute-start.7 = (f32[64,4096]{1,0:T(8,128)S(1)}, f32[64,4096]{1,0:T(8,128)S(1)}, u32[]{:S(2)}, u32[]{:S(2)}) collective-permute-start(f32[64,4096]{1,0:T(8,128)S(1)} %shard_map.68.mine), channel_id=1, source_target_pairs={{0,1},{1,0},{2,3},{3,2},{4,5},{5,4},{6,7},{7,6},{8,9},{9,8},{10,11... | collective-permute-start | bytes 3145736 | tf_op jit(solution)/shard_map/ppermute | solution.py:17
  19.0 0.7 %collective-permute-done.6.theirs = f32[64,4096]{1,0:T(8,128)S(1)} collective-permute-done((f32[64,4096]{1,0:T(8,128)S(1)}, f32[64,4096]{1,0:T(8,128)S(1)}, u32[]{:S(2)}, u32[]{:S(2)}) %collective-permute-start.6) | collective-permute-done | bytes 1048608 | tf_op jit(solution)/shard_map/ppermute | solution.py:17
  19.7 0.1 slice-done.3
  19.8 1.3 %shard_map.67 = (bf16[64,4096]{1,0:T(8,128)(2,1)S(1)}, f32[64,896]{1,0:T(8,128)S(1)}) custom-call(f32[64,4096]{1,0:T(8,128)S(1)} %shard_map.66.mine, f32[64,4096]{1,0:T(8,128)S(1)} %collective-permute-done.6.theirs, f32[1,8192]{1,0:T(1,128)S(1)} %bitcast.7, bf16[8192,896]{1,0:T(8,128)(2,1)S(1)} %bitcast.2), custom_call_target="tpu_custom_call" | custom-call | flops 2449999872 | bytes 7340032 | tf_op jit(solution)/shard_map/pallas_call | solution.py:132
  21.1 0.2 collective-permute-done.7.theirs
  21.3 1.3 %shard_map.69 = (bf16[64,4096]{1,0:T(8,128)(2,1)S(1)}, f32[16,896]{1,0:T(8,128)S(1)}, bf16[16,896]{1,0:T(8,128)(2,1)S(1)}, bf16[16,896]{1,0:T(8,128)(2,1)S(1)}, bf16[16,896]{1,0:T(8,128)(2,1)S(1)}) custom-call(f32[64,4096]{1,0:T(8,128)S(1)} %shard_map.68.mine, f32[64,4096]{1,0:T(8,128)S(1)} %collective-permute-done.7.theirs, f32[1,8192]{1,0:T(1,128)S(1)} %bitcast.8, ...), custom_call_target="tpu_custom_call" | custom-call | flops 2449999872 | bytes 7340032 | tf_op jit(solution)/shard_map/pallas_call | solution.py:132
  22.6 0.1 collective-permute-start.8
  22.7 2.1 %collective-permute-start.9 = (bf16[16,896]{1,0:T(8,128)(2,1)S(1)}, bf16[16,896]{1,0:T(8,128)(2,1)S(1)}, u32[]{:S(2)}, u32[]{:S(2)}) collective-permute-start(bf16[16,896]{1,0:T(8,128)(2,1)S(1)} %get-tuple-element.17), channel_id=1, source_target_pairs={{0,8},{2,10},{4,12},{6,14},{8,0},{10,2},{12,4},{14,6},{1,9},{3,11}... | collective-permute-start | bytes 86024 | tf_op jit(solution)/shard_map/ppermute | solution.py:17
  24.8 2.3 %collective-permute-start.10 = (bf16[16,896]{1,0:T(8,128)(2,1)S(1)}, bf16[16,896]{1,0:T(8,128)(2,1)S(1)}, u32[]{:S(2)}, u32[]{:S(2)}) collective-permute-start(bf16[16,896]{1,0:T(8,128)(2,1)S(1)} %get-tuple-element.18), channel_id=1, source_target_pairs={{0,12},{2,14},{4,8},{6,10},{8,4},{10,6},{12,0},{14,2},{1,13},{3,15... | collective-permute-start | bytes 86024 | tf_op jit(solution)/shard_map/ppermute | solution.py:17
  27.1 0.5 collective-permute-done.9.refs_1_
  27.5 2.9 %collective-permute-done.10.refs_2_ = bf16[16,896]{1,0:T(8,128)(2,1)S(1)} collective-permute-done((bf16[16,896]{1,0:T(8,128)(2,1)S(1)}, bf16[16,896]{1,0:T(8,128)(2,1)S(1)}, u32[]{:S(2)}, u32[]{:S(2)}) %collective-permute-start.10) | collective-permute-done | bytes 28704 | tf_op jit(solution)/shard_map/ppermute | solution.py:17
  30.5 0.6 %collective-permute-start.11 = (f32[16,896]{1,0:T(8,128)S(1)}, f32[16,896]{1,0:T(8,128)S(1)}, u32[]{:S(2)}, u32[]{:S(2)}) collective-permute-start(f32[16,896]{1,0:T(8,128)S(1)} %shard_map.71.total), channel_id=1, source_target_pairs={{0,2},{2,0},{4,6},{6,4},{8,10},{10,8},{12,14},{14,12},{1,3},{3,1},... | collective-permute-start | bytes 172040 | tf_op jit(solution)/shard_map/ppermute | solution.py:17
  31.1 3.6 %collective-permute-done.11.refs_0_ = f32[16,896]{1,0:T(8,128)S(1)} collective-permute-done((f32[16,896]{1,0:T(8,128)S(1)}, f32[16,896]{1,0:T(8,128)S(1)}, u32[]{:S(2)}, u32[]{:S(2)}) %collective-permute-start.11) | collective-permute-done | bytes 57376 | tf_op jit(solution)/shard_map/ppermute | solution.py:17
  34.8 2.3 %collective-permute-start.14 = (bf16[16,896]{1,0:T(8,128)(2,1)S(1)}, bf16[16,896]{1,0:T(8,128)(2,1)S(1)}, u32[]{:S(2)}, u32[]{:S(2)}) collective-permute-start(bf16[16,896]{1,0:T(8,128)(2,1)S(1)} %shard_map.72.refs_0_), channel_id=1, source_target_pairs={{0,12},{2,14},{4,8},{6,10},{8,4},{10,6},{12,0},{14,2},{1,13},{3,15... | collective-permute-start | bytes 86024 | tf_op jit(solution)/shard_map/ppermute | solution.py:17
  37.1 2.1 %collective-permute-start.12 = (bf16[16,896]{1,0:T(8,128)(2,1)S(1)}, bf16[16,896]{1,0:T(8,128)(2,1)S(1)}, u32[]{:S(2)}, u32[]{:S(2)}) collective-permute-start(bf16[16,896]{1,0:T(8,128)(2,1)S(1)} %shard_map.72.refs_0_), channel_id=1, source_target_pairs={{0,4},{2,6},{4,0},{6,2},{8,12},{10,14},{12,8},{14,10},{1,5},{3,7},... | collective-permute-start | bytes 86024 | tf_op jit(solution)/shard_map/ppermute | solution.py:17
  39.2 1.7 %shard_map.70.codes_t = bf16[8192,64]{1,0:T(8,128)(2,1)S(1)} custom-call(bf16[64,4096]{1,0:T(8,128)(2,1)S(1)} %get-tuple-element.12.refs_0_, bf16[64,4096]{1,0:T(8,128)(2,1)S(1)} %get-tuple-element.14.refs_1_), custom_call_target="tpu_custom_call" | custom-call | flops 1400000000 | bytes 4194304 | tf_op jit(solution)/shard_map/pallas_call | solution.py:157
  40.9 1.0 %collective-permute-done.13.refs_2_ = bf16[16,896]{1,0:T(8,128)(2,1)S(1)} collective-permute-done((bf16[16,896]{1,0:T(8,128)(2,1)S(1)}, bf16[16,896]{1,0:T(8,128)(2,1)S(1)}, u32[]{:S(2)}, u32[]{:S(2)}) %collective-permute-start.13) | collective-permute-done | bytes 28704 | tf_op jit(solution)/shard_map/ppermute | solution.py:17
  42.0 13.2 %shard_map.73 = bf16[8192,896]{1,0:T(8,128)(2,1)} custom-call(bf16[8192,64]{1,0:T(8,128)(2,1)S(1)} %shard_map.70.codes_t, bf16[8192,896]{1,0:T(8,128)(2,1)S(1)} %bitcast.4, bf16[8192,896]{1,0:T(8,128)(2,1)S(1)} %bitcast.6, bf16[16,896]{1,0:T(8,128)(2,1)S(1)} %shard_map.72.refs_0_, bf16[16,896]{1,0:T(8,128)(2,1)S(1)} %collective-permute-done.12.refs_1_, ...), custom_call_target="tpu_custom_call" | custom-call | tf_op jit(solution)/shard_map/pallas_call | solution.py:265
  (41 shorter events, 0.1 us)
Async XLA Ops:
  0.0 15.5 %copy-start = (bf16[896,8192]{1,0:T(8,128)(2,1)S(1)}, bf16[896,8192]{1,0:T(8,128)(2,1)}, u32[]{:S(2)}) copy-start(bf16[896,8192]{1,0:T(8,128)(2,1)} %refs_4_.3) | copy-start | bytes 44040196
  0.0 4.6 %collective-permute-start = (bf16[4,1792]{1,0:T(4,128)(2,1)}, bf16[4,1792]{1,0:T(4,128)(2,1)S(1)}, u32[]{:S(2)}, u32[]{:S(2)}) collective-permute-start(bf16[4,1792]{1,0:T(4,128)(2,1)} %x.1), channel_id=1, source_target_pairs={{0,1},{1,0},{2,3},{3,2},{4,5},{5,4},{6,7},{7,6},{8,9},{9,8},{10,11... | collective-permute-start | bytes 43016 | tf_op jit(solution)/shard_map/ppermute | solution.py:17
  0.5 4.2 %collective-permute-start.2 = (bf16[4,1792]{1,0:T(4,128)(2,1)}, bf16[4,1792]{1,0:T(4,128)(2,1)S(1)}, u32[]{:S(2)}, u32[]{:S(2)}) collective-permute-start(bf16[4,1792]{1,0:T(4,128)(2,1)} %x.1), channel_id=1, source_target_pairs={{0,3},{1,2},{2,1},{3,0},{4,7},{5,6},{6,5},{7,4},{8,11},{9,10},{10,... | collective-permute-start | bytes 43016 | tf_op jit(solution)/shard_map/ppermute | solution.py:17
  3.1 3.9 %collective-permute-start.1 = (bf16[4,1792]{1,0:T(4,128)(2,1)}, bf16[4,1792]{1,0:T(4,128)(2,1)S(1)}, u32[]{:S(2)}, u32[]{:S(2)}) collective-permute-start(bf16[4,1792]{1,0:T(4,128)(2,1)} %x.1), channel_id=1, source_target_pairs={{0,2},{1,3},{2,0},{3,1},{4,6},{5,7},{6,4},{7,5},{8,10},{9,11},{10,... | collective-permute-start | bytes 43016 | tf_op jit(solution)/shard_map/ppermute | solution.py:17
  3.1 1.5 %copy-start.2 = (bf16[4,1792]{1,0:T(4,128)(2,1)S(1)}, bf16[4,1792]{1,0:T(4,128)(2,1)}, u32[]{:S(2)}) copy-start(bf16[4,1792]{1,0:T(4,128)(2,1)} %x.1) | copy-start | bytes 43012
  7.0 12.7 %slice-start = ((s8[14680064]{0:T(1024)(128)(4,1)}), s8[4194304]{0:T(1024)(128)(4,1)S(1)}, s32[]{:S(2)}) async-start(s8[14680064]{0:T(1024)(128)(4,1)} %bitcast.1), calls=%async_computation | async-start | bytes 8388608
  7.0 12.6 %slice-start.1 = ((s8[14680064]{0:T(1024)(128)(4,1)}), s8[4194304]{0:T(1024)(128)(4,1)S(1)}, s32[]{:S(2)}) async-start(s8[14680064]{0:T(1024)(128)(4,1)} %bitcast.1), calls=%async_computation.1 | async-start | bytes 8388608
  7.0 12.6 %copy-start.1 = (f32[8192]{0:T(1024)S(1)}, f32[8192]{0:T(1024)}, u32[]{:S(2)}) copy-start(f32[8192]{0:T(1024)} %param.8) | copy-start | bytes 98308
  7.0 5.7 %collective-permute-start.5 = (bf16[16,896]{1,0:T(8,128)(2,1)S(1)}, bf16[16,896]{1,0:T(8,128)(2,1)S(1)}, u32[]{:S(2)}, u32[]{:S(2)}) collective-permute-start(bf16[16,896]{1,0:T(8,128)(2,1)S(1)} %shard_map.65.refs_0_.rows), channel_id=1, source_target_pairs={{0,12},{2,14},{4,8},{6,10},{8,4},{10,6},{12,0},{14,2},{1,13},{3,15... | collective-permute-start | bytes 86024 | tf_op jit(solution)/shard_map/ppermute | solution.py:17
  10.7 4.8 %collective-permute-start.4 = (bf16[16,896]{1,0:T(8,128)(2,1)S(1)}, bf16[16,896]{1,0:T(8,128)(2,1)S(1)}, u32[]{:S(2)}, u32[]{:S(2)}) collective-permute-start(bf16[16,896]{1,0:T(8,128)(2,1)S(1)} %shard_map.65.refs_0_.rows), channel_id=1, source_target_pairs={{0,8},{2,10},{4,12},{6,14},{8,0},{10,2},{12,4},{14,6},{1,9},{3,11}... | collective-permute-start | bytes 86024 | tf_op jit(solution)/shard_map/ppermute | solution.py:17
  10.7 4.8 %collective-permute-start.3 = (bf16[16,896]{1,0:T(8,128)(2,1)S(1)}, bf16[16,896]{1,0:T(8,128)(2,1)S(1)}, u32[]{:S(2)}, u32[]{:S(2)}) collective-permute-start(bf16[16,896]{1,0:T(8,128)(2,1)S(1)} %shard_map.65.refs_0_.rows), channel_id=1, source_target_pairs={{0,4},{2,6},{4,0},{6,2},{8,12},{10,14},{12,8},{14,10},{1,5},{3,7},... | collective-permute-start | bytes 86024 | tf_op jit(solution)/shard_map/ppermute | solution.py:17
  16.9 2.8 %slice-start.2 = ((s8[14680064]{0:T(1024)(128)(4,1)}), s8[4194304]{0:T(1024)(128)(4,1)S(1)}, s32[]{:S(2)}) async-start(s8[14680064]{0:T(1024)(128)(4,1)} %bitcast.1), calls=%async_computation.2 | async-start | bytes 8388608
  16.9 2.9 %slice-start.3 = ((s8[14680064]{0:T(1024)(128)(4,1)}), s8[2097152]{0:T(1024)(128)(4,1)S(1)}, s32[]{:S(2)}) async-start(s8[14680064]{0:T(1024)(128)(4,1)} %bitcast.1), calls=%async_computation.3 | async-start | bytes 4194304
  16.9 2.7 %collective-permute-start.6 = (f32[64,4096]{1,0:T(8,128)S(1)}, f32[64,4096]{1,0:T(8,128)S(1)}, u32[]{:S(2)}, u32[]{:S(2)}) collective-permute-start(f32[64,4096]{1,0:T(8,128)S(1)} %shard_map.66.mine), channel_id=1, source_target_pairs={{0,1},{1,0},{2,3},{3,2},{4,5},{5,4},{6,7},{7,6},{8,9},{9,8},{10,11... | collective-permute-start | bytes 3145736 | tf_op jit(solution)/shard_map/ppermute | solution.py:17
  18.4 2.8 %collective-permute-start.7 = (f32[64,4096]{1,0:T(8,128)S(1)}, f32[64,4096]{1,0:T(8,128)S(1)}, u32[]{:S(2)}, u32[]{:S(2)}) collective-permute-start(f32[64,4096]{1,0:T(8,128)S(1)} %shard_map.68.mine), channel_id=1, source_target_pairs={{0,1},{1,0},{2,3},{3,2},{4,5},{5,4},{6,7},{7,6},{8,9},{9,8},{10,11... | collective-permute-start | bytes 3145736 | tf_op jit(solution)/shard_map/ppermute | solution.py:17
  21.3 20.6 %slice-start.4 = ((s8[14680064]{0:T(1024)(128)(4,1)}), s8[4194304]{0:T(1024)(128)(4,1)S(1)}, s32[]{:S(2)}) async-start(s8[14680064]{0:T(1024)(128)(4,1)} %bitcast.3), calls=%async_computation.4 | async-start | bytes 8388608
  21.3 20.6 %slice-start.5 = ((s8[14680064]{0:T(1024)(128)(4,1)}), s8[4194304]{0:T(1024)(128)(4,1)S(1)}, s32[]{:S(2)}) async-start(s8[14680064]{0:T(1024)(128)(4,1)} %bitcast.3), calls=%async_computation.5 | async-start | bytes 8388608
  21.3 20.6 %slice-start.8 = ((s8[14680064]{0:T(1024)(128)(4,1)}), s8[4194304]{0:T(1024)(128)(4,1)S(1)}, s32[]{:S(2)}) async-start(s8[14680064]{0:T(1024)(128)(4,1)} %bitcast.5), calls=%async_computation.8 | async-start | bytes 8388608
  21.3 20.6 %slice-start.9 = ((s8[14680064]{0:T(1024)(128)(4,1)}), s8[4194304]{0:T(1024)(128)(4,1)S(1)}, s32[]{:S(2)}) async-start(s8[14680064]{0:T(1024)(128)(4,1)} %bitcast.5), calls=%async_computation.9 | async-start | bytes 8388608
  22.6 4.5 %collective-permute-start.8 = (bf16[16,896]{1,0:T(8,128)(2,1)S(1)}, bf16[16,896]{1,0:T(8,128)(2,1)S(1)}, u32[]{:S(2)}, u32[]{:S(2)}) collective-permute-start(bf16[16,896]{1,0:T(8,128)(2,1)S(1)} %get-tuple-element.16), channel_id=1, source_target_pairs={{0,4},{2,6},{4,0},{6,2},{8,12},{10,14},{12,8},{14,10},{1,5},{3,7},... | collective-permute-start | bytes 86024 | tf_op jit(solution)/shard_map/ppermute | solution.py:17
  22.7 4.9 %collective-permute-start.9 = (bf16[16,896]{1,0:T(8,128)(2,1)S(1)}, bf16[16,896]{1,0:T(8,128)(2,1)S(1)}, u32[]{:S(2)}, u32[]{:S(2)}) collective-permute-start(bf16[16,896]{1,0:T(8,128)(2,1)S(1)} %get-tuple-element.17), channel_id=1, source_target_pairs={{0,8},{2,10},{4,12},{6,14},{8,0},{10,2},{12,4},{14,6},{1,9},{3,11}... | collective-permute-start | bytes 86024 | tf_op jit(solution)/shard_map/ppermute | solution.py:17
  24.8 5.7 %collective-permute-start.10 = (bf16[16,896]{1,0:T(8,128)(2,1)S(1)}, bf16[16,896]{1,0:T(8,128)(2,1)S(1)}, u32[]{:S(2)}, u32[]{:S(2)}) collective-permute-start(bf16[16,896]{1,0:T(8,128)(2,1)S(1)} %get-tuple-element.18), channel_id=1, source_target_pairs={{0,12},{2,14},{4,8},{6,10},{8,4},{10,6},{12,0},{14,2},{1,13},{3,15... | collective-permute-start | bytes 86024 | tf_op jit(solution)/shard_map/ppermute | solution.py:17
  30.5 11.5 %slice-start.6 = ((s8[14680064]{0:T(1024)(128)(4,1)}), s8[4194304]{0:T(1024)(128)(4,1)S(1)}, s32[]{:S(2)}) async-start(s8[14680064]{0:T(1024)(128)(4,1)} %bitcast.3), calls=%async_computation.6 | async-start | bytes 8388608
  30.5 11.5 %slice-start.10 = ((s8[14680064]{0:T(1024)(128)(4,1)}), s8[4194304]{0:T(1024)(128)(4,1)S(1)}, s32[]{:S(2)}) async-start(s8[14680064]{0:T(1024)(128)(4,1)} %bitcast.5), calls=%async_computation.10 | async-start | bytes 8388608
  30.5 11.5 %slice-start.7 = ((s8[14680064]{0:T(1024)(128)(4,1)}), s8[2097152]{0:T(1024)(128)(4,1)S(1)}, s32[]{:S(2)}) async-start(s8[14680064]{0:T(1024)(128)(4,1)} %bitcast.3), calls=%async_computation.7 | async-start | bytes 4194304
  30.5 11.5 %slice-start.11 = ((s8[14680064]{0:T(1024)(128)(4,1)}), s8[2097152]{0:T(1024)(128)(4,1)S(1)}, s32[]{:S(2)}) async-start(s8[14680064]{0:T(1024)(128)(4,1)} %bitcast.5), calls=%async_computation.11 | async-start | bytes 4194304
  30.5 4.2 %collective-permute-start.11 = (f32[16,896]{1,0:T(8,128)S(1)}, f32[16,896]{1,0:T(8,128)S(1)}, u32[]{:S(2)}, u32[]{:S(2)}) collective-permute-start(f32[16,896]{1,0:T(8,128)S(1)} %shard_map.71.total), channel_id=1, source_target_pairs={{0,2},{2,0},{4,6},{6,4},{8,10},{10,8},{12,14},{14,12},{1,3},{3,1},... | collective-permute-start | bytes 172040 | tf_op jit(solution)/shard_map/ppermute | solution.py:17
  34.8 6.1 %collective-permute-start.14 = (bf16[16,896]{1,0:T(8,128)(2,1)S(1)}, bf16[16,896]{1,0:T(8,128)(2,1)S(1)}, u32[]{:S(2)}, u32[]{:S(2)}) collective-permute-start(bf16[16,896]{1,0:T(8,128)(2,1)S(1)} %shard_map.72.refs_0_), channel_id=1, source_target_pairs={{0,12},{2,14},{4,8},{6,10},{8,4},{10,6},{12,0},{14,2},{1,13},{3,15... | collective-permute-start | bytes 86024 | tf_op jit(solution)/shard_map/ppermute | solution.py:17
  37.1 4.8 %collective-permute-start.13 = (bf16[16,896]{1,0:T(8,128)(2,1)S(1)}, bf16[16,896]{1,0:T(8,128)(2,1)S(1)}, u32[]{:S(2)}, u32[]{:S(2)}) collective-permute-start(bf16[16,896]{1,0:T(8,128)(2,1)S(1)} %shard_map.72.refs_0_), channel_id=1, source_target_pairs={{0,8},{2,10},{4,12},{6,14},{8,0},{10,2},{12,4},{14,6},{1,9},{3,11}... | collective-permute-start | bytes 86024 | tf_op jit(solution)/shard_map/ppermute | solution.py:17
  37.1 4.8 %collective-permute-start.12 = (bf16[16,896]{1,0:T(8,128)(2,1)S(1)}, bf16[16,896]{1,0:T(8,128)(2,1)S(1)}, u32[]{:S(2)}, u32[]{:S(2)}) collective-permute-start(bf16[16,896]{1,0:T(8,128)(2,1)S(1)} %shard_map.72.refs_0_), channel_id=1, source_target_pairs={{0,4},{2,6},{4,0},{6,2},{8,12},{10,14},{12,8},{14,10},{1,5},{3,7},... | collective-permute-start | bytes 86024 | tf_op jit(solution)/shard_map/ppermute | solution.py:17

commit v8 on v7

--- a/solution.py
+++ b/solution.py
@@ -8,6 +8,7 @@
 from jax.sharding import PartitionSpec as P
 
 MIB = 1 << 20
+PARTS = 2
 WHOLE = pl.BlockSpec(memory_space=pltpu.VMEM)
 DIRECT = 8
 
@@ -212,51 +213,42 @@
 
 
 def adam_kernel(codes_t, m, v, *refs):
-    *blocks, out, product, err = refs
+    *blocks, out, even, odd, err = refs
+    products = (even, odd)
     tokens = codes_t.shape[1]
     b = 0.1 / (1.0 - 0.9**10) / tokens
     a = 0.9 / (1.0 - 0.9**10) / b
     p = 0.999 / (1.0 - 0.999**10) / b**2
     q = 0.001 / (1.0 - 0.999**10) / tokens**2 / b**2
-    eps = 1e-8 / b
+    a, p, q, eps = (jnp.asarray(x, out.dtype) for x in (a, p, q, 1e-8 / b))
     i, last = pl.program_id(0), pl.num_programs(0) - 1
     rows = out.shape[0]
-    part = product.shape[0]
+    part = even.shape[0]
     slab = 16
 
-    def multiply(start):
+    def multiply(start, product):
         at = pl.ds(pl.multiple_of(start, part), part)
-        return jnp.dot(codes_t[at, :], err[...], preferred_element_type=jnp.float32)
+        c = jnp.dot(codes_t[at, :], err[...], preferred_element_type=jnp.float32)
+        product[...] = c.astype(product.dtype)
 
     @pl.when(i == 0)
     def _():
         err[...] = stack(blocks)
-        product[...] = multiply(0)
-
-    a, p, q, eps = (jnp.asarray(x, out.dtype) for x in (a, p, q, eps))
-
-    def direction(c, start):
-        at = pl.ds(pl.multiple_of(start, slab), slab)
-        c = c.astype(out.dtype)
-        first = m[at, :] * a + c
-        second = v[at, :] * p + (c * c) * q
-        root = second * lax.rsqrt(second)
-        return first * pl.reciprocal(root + eps, approx=True)
-
-    c = product[...]
-    done = []
-    for k in range(0, rows, part):
-        if k + part < rows:
-            later = multiply(i * rows + k + part)
+        multiply(0, even)
+
+    for k in range(2):
+        if k == 0:
+            multiply(i * rows + part, odd)
         else:
-            later = multiply(jnp.minimum(i + 1, last) * rows)
-        steps = [(k + r, direction(c[r : r + slab], i * rows + k + r)) for r in range(0, part, slab)]
-        for r, step in done:
-            out[r : r + slab, :] = step
-        done, c = steps, later
-    for r, step in done:
-        out[r : r + slab, :] = step
-    product[...] = c
+            multiply(jnp.minimum(i + 1, last) * rows, even)
+        for r in range(0, part, slab):
+            at = pl.ds(pl.multiple_of(i * rows + k * part + r, slab), slab)
+            c = products[k][r : r + slab, :]
+            first = m[at, :] * a + c
+            second = v[at, :] * p + (c * c) * q
+            root = second * lax.rsqrt(second)
+            step = first * pl.reciprocal(root + eps, approx=True)
+            out[k * part + r : k * part + r + slab, :] = step
 
 
 def adam(codes_t, blocks, m, v):
@@ -268,10 +260,8 @@
         out_shape=jax.ShapeDtypeStruct(m.shape, jnp.bfloat16),
         in_specs=[WHOLE] * (3 + len(blocks)),
         out_specs=pl.BlockSpec((rows, half), lambda i: (i, 0)),
-        scratch_shapes=[
-            pltpu.VMEM((64, half), jnp.float32),
-            pltpu.VMEM((codes_t.shape[1], half), jnp.bfloat16),
-        ],
+        scratch_shapes=[pltpu.VMEM((rows // 2, half), jnp.bfloat16)] * 2
+        + [pltpu.VMEM((codes_t.shape[1], half), jnp.bfloat16)],
         compiler_params=params(12),
     )(codes_t, resident(m), resident(v), *blocks)
 
@@ -280,14 +270,14 @@
     direct = lax.axis_size("latent") <= DIRECT
     rows = near_rows(acts, 2 if direct else 1)
     blocks = spread(rows)
-    part = w_enc.shape[1] // 2
-    mine = [encode(blocks, w_enc, k * part, part) for k in range(2)]
+    part = w_enc.shape[1] // PARTS
+    mine = [encode(blocks, w_enc, k * part, part) for k in range(PARTS)]
     theirs = [swap(x, "dp", 1) for x in mine]
-    codes, sums = [None, None], []
-    for k in range(2):
-        codes[k], sums = decode(
-            mine[k], theirs[k], b_enc, w_dec, k * part, sums, len(blocks) if k else 1
-        )
+    codes, sums = [], []
+    for k in range(PARTS):
+        far = len(blocks) if k == PARTS - 1 else 1
+        block, sums = decode(mine[k], theirs[k], b_enc, w_dec, k * part, sums, far)
+        codes.append(block)
     codes_t = turn(*codes)
     total, near = reduce_rows(sums)
     err = spread(error(total, near, rows))

time: 55.4 us -> 54.6 us (0.986)
  Pallas kernels: 20.3 us -> 19.5 us
    pallas_call x1, Pallas kernels: 13.2 us -> 12.4 us  [adam(): pl.pallas_call(adam_kernel, grid=(lat // rows,), out_shape=jax.ShapeDtype...]
where the time goes in v8:
time: 54.6 us; the launch traced here: 54.3 us
  Pallas kernels  19.5 us (36%)
  starting transfers between devices  17.7 us (32%)
  waiting for transfers between devices  15.3 us (28%)
  local copies, waits for them, and re-layouts  1.63 us (3%)
    ppermute x15, starting transfers between devices, swap(): return lax.ppermute(value, axis, [(i, i ^ mask) for i in range(n)])  17.7 us
    ppermute x15, waiting for transfers between devices, swap(): return lax.ppermute(value, axis, [(i, i ^ mask) for i in range(n)])  15.3 us
    pallas_call x1, Pallas kernels, adam(): pl.pallas_call(adam_kernel, grid=(lat // rows,), out_shape=jax.ShapeDtype...  12.4 us
    pallas_call x2, Pallas kernels, encode(): pl.pallas_call(functools.partial(encode_kernel, first), out_shape=jax.Sha...  2.84 us
    pallas_call x2, Pallas kernels, decode(): pl.pallas_call(functools.partial(decode_kernel, first, len(given)), out_s...  2.58 us
    pallas_call x1, Pallas kernels, turn(): pl.pallas_call(functools.partial(turn_kernel, min(512, lat)), out_shape=j...  1.68 us
    unnamed x30, local copies, waits for them, and re-layouts  1.63 us
  transfers between devices with their start and end apart: 15, of which 10 were waited for; matrix products, arithmetic and copies ran while one was open for 0% of the time, Pallas kernels for 8%

profile of v8, /device:TPU:0, one launch (start us, length us, event | category | flops | bytes accessed | tf_op | source)
XLA Modules:
  0.0 54.3 jit_solution(1317564926155306434)
XLA Ops:
  0.0 0.5 collective-permute-start
  0.5 2.6 %collective-permute-start.2 = (bf16[4,1792]{1,0:T(4,128)(2,1)}, bf16[4,1792]{1,0:T(4,128)(2,1)S(1)}, u32[]{:S(2)}, u32[]{:S(2)}) collective-permute-start(bf16[4,1792]{1,0:T(4,128)(2,1)} %x.1), channel_id=1, source_target_pairs={{0,3},{1,2},{2,1},{3,0},{4,7},{5,6},{6,5},{7,4},{8,11},{9,10},{10,... | collective-permute-start | bytes 43016 | tf_op jit(solution)/shard_map/ppermute | solution.py:18
  3.1 0.1 collective-permute-start.1
  3.1 1.5 %copy-done.2 = bf16[4,1792]{1,0:T(4,128)(2,1)S(1)} copy-done((bf16[4,1792]{1,0:T(4,128)(2,1)S(1)}, bf16[4,1792]{1,0:T(4,128)(2,1)}, u32[]{:S(2)}) %copy-start.2) | copy-done | bytes 14360
  4.6 0.1 collective-permute-done.2.refs_3_
  4.7 2.3 %collective-permute-done.1.refs_2_ = bf16[4,1792]{1,0:T(4,128)(2,1)S(1)} collective-permute-done((bf16[4,1792]{1,0:T(4,128)(2,1)}, bf16[4,1792]{1,0:T(4,128)(2,1)S(1)}, u32[]{:S(2)}, u32[]{:S(2)}) %collective-permute-start.1) | collective-permute-done | bytes 14368 | tf_op jit(solution)/shard_map/ppermute | solution.py:18
  7.0 3.7 %collective-permute-start.5 = (bf16[16,896]{1,0:T(8,128)(2,1)S(1)}, bf16[16,896]{1,0:T(8,128)(2,1)S(1)}, u32[]{:S(2)}, u32[]{:S(2)}) collective-permute-start(bf16[16,896]{1,0:T(8,128)(2,1)S(1)} %shard_map.65.refs_0_.rows), channel_id=1, source_target_pairs={{0,12},{2,14},{4,8},{6,10},{8,4},{10,6},{12,0},{14,2},{1,13},{3,15... | collective-permute-start | bytes 86024 | tf_op jit(solution)/shard_map/ppermute | solution.py:18
  10.7 0.8 %collective-permute-start.3 = (bf16[16,896]{1,0:T(8,128)(2,1)S(1)}, bf16[16,896]{1,0:T(8,128)(2,1)S(1)}, u32[]{:S(2)}, u32[]{:S(2)}) collective-permute-start(bf16[16,896]{1,0:T(8,128)(2,1)S(1)} %shard_map.65.refs_0_.rows), channel_id=1, source_target_pairs={{0,4},{2,6},{4,0},{6,2},{8,12},{10,14},{12,8},{14,10},{1,5},{3,7},... | collective-permute-start | bytes 86024 | tf_op jit(solution)/shard_map/ppermute | solution.py:18
  11.5 1.3 %collective-permute-done.5.refs_3_ = bf16[16,896]{1,0:T(8,128)(2,1)S(1)} collective-permute-done((bf16[16,896]{1,0:T(8,128)(2,1)S(1)}, bf16[16,896]{1,0:T(8,128)(2,1)S(1)}, u32[]{:S(2)}, u32[]{:S(2)}) %collective-permute-start.5) | collective-permute-done | bytes 28704 | tf_op jit(solution)/shard_map/ppermute | solution.py:18
  12.8 2.7 %collective-permute-done.4.refs_2_ = bf16[16,896]{1,0:T(8,128)(2,1)S(1)} collective-permute-done((bf16[16,896]{1,0:T(8,128)(2,1)S(1)}, bf16[16,896]{1,0:T(8,128)(2,1)S(1)}, u32[]{:S(2)}, u32[]{:S(2)}) %collective-permute-start.4) | collective-permute-done | bytes 28704 | tf_op jit(solution)/shard_map/ppermute | solution.py:18
  15.5 1.4 %shard_map.66.mine = f32[64,4096]{1,0:T(8,128)S(1)} custom-call(bf16[16,896]{1,0:T(8,128)(2,1)S(1)} %shard_map.65.refs_0_.rows, bf16[16,896]{1,0:T(8,128)(2,1)S(1)} %collective-permute-done.3.refs_1_, bf16[16,896]{1,0:T(8,128)(2,1)S(1)} %collective-permute-done.4.refs_2_, bf16[16,896]{1,0:T(8,128)(2,1)S(1)} %collective-permute-done.5.refs_3_, ...), custom_call_target="tpu_custom_call" | custom-call | flops 2449999872 | bytes 7340032 | tf_op jit(solution)/shard_map/pallas_call | solution.py:102
  16.9 0.1 collective-permute-start.6
  17.0 1.4 %shard_map.68.mine = f32[64,4096]{1,0:T(8,128)S(1)} custom-call(bf16[16,896]{1,0:T(8,128)(2,1)S(1)} %shard_map.65.refs_0_.rows, bf16[16,896]{1,0:T(8,128)(2,1)S(1)} %collective-permute-done.3.refs_1_, bf16[16,896]{1,0:T(8,128)(2,1)S(1)} %collective-permute-done.4.refs_2_, bf16[16,896]{1,0:T(8,128)(2,1)S(1)} %collective-permute-done.5.refs_3_, ...), custom_call_target="tpu_custom_call" | custom-call | flops 2449999872 | bytes 7340032 | tf_op jit(solution)/shard_map/pallas_call | solution.py:102
  18.4 0.6 %collective-permute-start.7 = (f32[64,4096]{1,0:T(8,128)S(1)}, f32[64,4096]{1,0:T(8,128)S(1)}, u32[]{:S(2)}, u32[]{:S(2)}) collective-permute-start(f32[64,4096]{1,0:T(8,128)S(1)} %shard_map.68.mine), channel_id=1, source_target_pairs={{0,1},{1,0},{2,3},{3,2},{4,5},{5,4},{6,7},{7,6},{8,9},{9,8},{10,11... | collective-permute-start | bytes 3145736 | tf_op jit(solution)/shard_map/ppermute | solution.py:18
  19.0 0.7 %collective-permute-done.6.theirs = f32[64,4096]{1,0:T(8,128)S(1)} collective-permute-done((f32[64,4096]{1,0:T(8,128)S(1)}, f32[64,4096]{1,0:T(8,128)S(1)}, u32[]{:S(2)}, u32[]{:S(2)}) %collective-permute-start.6) | collective-permute-done | bytes 1048608 | tf_op jit(solution)/shard_map/ppermute | solution.py:18
  19.7 0.1 slice-done.3
  19.8 1.3 %shard_map.67 = (bf16[64,4096]{1,0:T(8,128)(2,1)S(1)}, f32[64,896]{1,0:T(8,128)S(1)}) custom-call(f32[64,4096]{1,0:T(8,128)S(1)} %shard_map.66.mine, f32[64,4096]{1,0:T(8,128)S(1)} %collective-permute-done.6.theirs, f32[1,8192]{1,0:T(1,128)S(1)} %bitcast.7, bf16[8192,896]{1,0:T(8,128)(2,1)S(1)} %bitcast.2), custom_call_target="tpu_custom_call" | custom-call | flops 2449999872 | bytes 7340032 | tf_op jit(solution)/shard_map/pallas_call | solution.py:133
  21.1 0.2 collective-permute-done.7.theirs
  21.3 1.3 %shard_map.69 = (bf16[64,4096]{1,0:T(8,128)(2,1)S(1)}, f32[16,896]{1,0:T(8,128)S(1)}, bf16[16,896]{1,0:T(8,128)(2,1)S(1)}, bf16[16,896]{1,0:T(8,128)(2,1)S(1)}, bf16[16,896]{1,0:T(8,128)(2,1)S(1)}) custom-call(f32[64,4096]{1,0:T(8,128)S(1)} %shard_map.68.mine, f32[64,4096]{1,0:T(8,128)S(1)} %collective-permute-done.7.theirs, f32[1,8192]{1,0:T(1,128)S(1)} %bitcast.8, ...), custom_call_target="tpu_custom_call" | custom-call | flops 2449999872 | bytes 7340032 | tf_op jit(solution)/shard_map/pallas_call | solution.py:133
  22.6 0.1 collective-permute-start.8
  22.7 2.1 %collective-permute-start.9 = (bf16[16,896]{1,0:T(8,128)(2,1)S(1)}, bf16[16,896]{1,0:T(8,128)(2,1)S(1)}, u32[]{:S(2)}, u32[]{:S(2)}) collective-permute-start(bf16[16,896]{1,0:T(8,128)(2,1)S(1)} %get-tuple-element.17), channel_id=1, source_target_pairs={{0,8},{2,10},{4,12},{6,14},{8,0},{10,2},{12,4},{14,6},{1,9},{3,11}... | collective-permute-start | bytes 86024 | tf_op jit(solution)/shard_map/ppermute | solution.py:18
  24.8 2.3 %collective-permute-start.10 = (bf16[16,896]{1,0:T(8,128)(2,1)S(1)}, bf16[16,896]{1,0:T(8,128)(2,1)S(1)}, u32[]{:S(2)}, u32[]{:S(2)}) collective-permute-start(bf16[16,896]{1,0:T(8,128)(2,1)S(1)} %get-tuple-element.18), channel_id=1, source_target_pairs={{0,12},{2,14},{4,8},{6,10},{8,4},{10,6},{12,0},{14,2},{1,13},{3,15... | collective-permute-start | bytes 86024 | tf_op jit(solution)/shard_map/ppermute | solution.py:18
  27.1 0.5 collective-permute-done.9.refs_1_
  27.5 2.9 %collective-permute-done.10.refs_2_ = bf16[16,896]{1,0:T(8,128)(2,1)S(1)} collective-permute-done((bf16[16,896]{1,0:T(8,128)(2,1)S(1)}, bf16[16,896]{1,0:T(8,128)(2,1)S(1)}, u32[]{:S(2)}, u32[]{:S(2)}) %collective-permute-start.10) | collective-permute-done | bytes 28704 | tf_op jit(solution)/shard_map/ppermute | solution.py:18
  30.5 0.0 slice-start.11
  30.5 0.6 %collective-permute-start.11 = (f32[16,896]{1,0:T(8,128)S(1)}, f32[16,896]{1,0:T(8,128)S(1)}, u32[]{:S(2)}, u32[]{:S(2)}) collective-permute-start(f32[16,896]{1,0:T(8,128)S(1)} %shard_map.71.total), channel_id=1, source_target_pairs={{0,2},{2,0},{4,6},{6,4},{8,10},{10,8},{12,14},{14,12},{1,3},{3,1},... | collective-permute-start | bytes 172040 | tf_op jit(solution)/shard_map/ppermute | solution.py:18
  31.1 3.6 %collective-permute-done.11.refs_0_ = f32[16,896]{1,0:T(8,128)S(1)} collective-permute-done((f32[16,896]{1,0:T(8,128)S(1)}, f32[16,896]{1,0:T(8,128)S(1)}, u32[]{:S(2)}, u32[]{:S(2)}) %collective-permute-start.11) | collective-permute-done | bytes 57376 | tf_op jit(solution)/shard_map/ppermute | solution.py:18
  34.8 2.3 %collective-permute-start.14 = (bf16[16,896]{1,0:T(8,128)(2,1)S(1)}, bf16[16,896]{1,0:T(8,128)(2,1)S(1)}, u32[]{:S(2)}, u32[]{:S(2)}) collective-permute-start(bf16[16,896]{1,0:T(8,128)(2,1)S(1)} %shard_map.72.refs_0_), channel_id=1, source_target_pairs={{0,12},{2,14},{4,8},{6,10},{8,4},{10,6},{12,0},{14,2},{1,13},{3,15... | collective-permute-start | bytes 86024 | tf_op jit(solution)/shard_map/ppermute | solution.py:18
  37.1 2.1 %collective-permute-start.12 = (bf16[16,896]{1,0:T(8,128)(2,1)S(1)}, bf16[16,896]{1,0:T(8,128)(2,1)S(1)}, u32[]{:S(2)}, u32[]{:S(2)}) collective-permute-start(bf16[16,896]{1,0:T(8,128)(2,1)S(1)} %shard_map.72.refs_0_), channel_id=1, source_target_pairs={{0,4},{2,6},{4,0},{6,2},{8,12},{10,14},{12,8},{14,10},{1,5},{3,7},... | collective-permute-start | bytes 86024 | tf_op jit(solution)/shard_map/ppermute | solution.py:18
  39.2 1.7 %shard_map.70.codes_t = bf16[8192,64]{1,0:T(8,128)(2,1)S(1)} custom-call(bf16[64,4096]{1,0:T(8,128)(2,1)S(1)} %get-tuple-element.12.refs_0_, bf16[64,4096]{1,0:T(8,128)(2,1)S(1)} %get-tuple-element.14.refs_1_), custom_call_target="tpu_custom_call" | custom-call | flops 1400000000 | bytes 4194304 | tf_op jit(solution)/shard_map/pallas_call | solution.py:158
  40.9 1.0 %collective-permute-done.13.refs_2_ = bf16[16,896]{1,0:T(8,128)(2,1)S(1)} collective-permute-done((bf16[16,896]{1,0:T(8,128)(2,1)S(1)}, bf16[16,896]{1,0:T(8,128)(2,1)S(1)}, u32[]{:S(2)}, u32[]{:S(2)}) %collective-permute-start.13) | collective-permute-done | bytes 28704 | tf_op jit(solution)/shard_map/ppermute | solution.py:18
  42.0 12.4 %shard_map.73 = bf16[8192,896]{1,0:T(8,128)(2,1)} custom-call(bf16[8192,64]{1,0:T(8,128)(2,1)S(1)} %shard_map.70.codes_t, bf16[8192,896]{1,0:T(8,128)(2,1)S(1)} %bitcast.4, bf16[8192,896]{1,0:T(8,128)(2,1)S(1)} %bitcast.6, bf16[16,896]{1,0:T(8,128)(2,1)S(1)} %shard_map.72.refs_0_, bf16[16,896]{1,0:T(8,128)(2,1)S(1)} %collective-permute-done.12.refs_1_, ...), custom_call_target="tpu_custom_call" | custom-call | tf_op jit(solution)/shard_map/pallas_call | solution.py:257
  (41 shorter events, 0.1 us)
Async XLA Ops:
  0.0 15.5 %copy-start = (bf16[896,8192]{1,0:T(8,128)(2,1)S(1)}, bf16[896,8192]{1,0:T(8,128)(2,1)}, u32[]{:S(2)}) copy-start(bf16[896,8192]{1,0:T(8,128)(2,1)} %refs_4_.3) | copy-start | bytes 44040196
  0.0 4.6 %collective-permute-start = (bf16[4,1792]{1,0:T(4,128)(2,1)}, bf16[4,1792]{1,0:T(4,128)(2,1)S(1)}, u32[]{:S(2)}, u32[]{:S(2)}) collective-permute-start(bf16[4,1792]{1,0:T(4,128)(2,1)} %x.1), channel_id=1, source_target_pairs={{0,1},{1,0},{2,3},{3,2},{4,5},{5,4},{6,7},{7,6},{8,9},{9,8},{10,11... | collective-permute-start | bytes 43016 | tf_op jit(solution)/shard_map/ppermute | solution.py:18
  0.5 4.2 %collective-permute-start.2 = (bf16[4,1792]{1,0:T(4,128)(2,1)}, bf16[4,1792]{1,0:T(4,128)(2,1)S(1)}, u32[]{:S(2)}, u32[]{:S(2)}) collective-permute-start(bf16[4,1792]{1,0:T(4,128)(2,1)} %x.1), channel_id=1, source_target_pairs={{0,3},{1,2},{2,1},{3,0},{4,7},{5,6},{6,5},{7,4},{8,11},{9,10},{10,... | collective-permute-start | bytes 43016 | tf_op jit(solution)/shard_map/ppermute | solution.py:18
  3.1 3.9 %collective-permute-start.1 = (bf16[4,1792]{1,0:T(4,128)(2,1)}, bf16[4,1792]{1,0:T(4,128)(2,1)S(1)}, u32[]{:S(2)}, u32[]{:S(2)}) collective-permute-start(bf16[4,1792]{1,0:T(4,128)(2,1)} %x.1), channel_id=1, source_target_pairs={{0,2},{1,3},{2,0},{3,1},{4,6},{5,7},{6,4},{7,5},{8,10},{9,11},{10,... | collective-permute-start | bytes 43016 | tf_op jit(solution)/shard_map/ppermute | solution.py:18
  3.1 1.5 %copy-start.2 = (bf16[4,1792]{1,0:T(4,128)(2,1)S(1)}, bf16[4,1792]{1,0:T(4,128)(2,1)}, u32[]{:S(2)}) copy-start(bf16[4,1792]{1,0:T(4,128)(2,1)} %x.1) | copy-start | bytes 43012
  7.0 12.7 %slice-start = ((s8[14680064]{0:T(1024)(128)(4,1)}), s8[4194304]{0:T(1024)(128)(4,1)S(1)}, s32[]{:S(2)}) async-start(s8[14680064]{0:T(1024)(128)(4,1)} %bitcast.1), calls=%async_computation | async-start | bytes 8388608
  7.0 12.6 %slice-start.1 = ((s8[14680064]{0:T(1024)(128)(4,1)}), s8[4194304]{0:T(1024)(128)(4,1)S(1)}, s32[]{:S(2)}) async-start(s8[14680064]{0:T(1024)(128)(4,1)} %bitcast.1), calls=%async_computation.1 | async-start | bytes 8388608
  7.0 12.6 %copy-start.1 = (f32[8192]{0:T(1024)S(1)}, f32[8192]{0:T(1024)}, u32[]{:S(2)}) copy-start(f32[8192]{0:T(1024)} %param.8) | copy-start | bytes 98308
  7.0 5.7 %collective-permute-start.5 = (bf16[16,896]{1,0:T(8,128)(2,1)S(1)}, bf16[16,896]{1,0:T(8,128)(2,1)S(1)}, u32[]{:S(2)}, u32[]{:S(2)}) collective-permute-start(bf16[16,896]{1,0:T(8,128)(2,1)S(1)} %shard_map.65.refs_0_.rows), channel_id=1, source_target_pairs={{0,12},{2,14},{4,8},{6,10},{8,4},{10,6},{12,0},{14,2},{1,13},{3,15... | collective-permute-start | bytes 86024 | tf_op jit(solution)/shard_map/ppermute | solution.py:18
  10.7 4.8 %collective-permute-start.4 = (bf16[16,896]{1,0:T(8,128)(2,1)S(1)}, bf16[16,896]{1,0:T(8,128)(2,1)S(1)}, u32[]{:S(2)}, u32[]{:S(2)}) collective-permute-start(bf16[16,896]{1,0:T(8,128)(2,1)S(1)} %shard_map.65.refs_0_.rows), channel_id=1, source_target_pairs={{0,8},{2,10},{4,12},{6,14},{8,0},{10,2},{12,4},{14,6},{1,9},{3,11}... | collective-permute-start | bytes 86024 | tf_op jit(solution)/shard_map/ppermute | solution.py:18
  10.7 4.8 %collective-permute-start.3 = (bf16[16,896]{1,0:T(8,128)(2,1)S(1)}, bf16[16,896]{1,0:T(8,128)(2,1)S(1)}, u32[]{:S(2)}, u32[]{:S(2)}) collective-permute-start(bf16[16,896]{1,0:T(8,128)(2,1)S(1)} %shard_map.65.refs_0_.rows), channel_id=1, source_target_pairs={{0,4},{2,6},{4,0},{6,2},{8,12},{10,14},{12,8},{14,10},{1,5},{3,7},... | collective-permute-start | bytes 86024 | tf_op jit(solution)/shard_map/ppermute | solution.py:18
  16.9 2.8 %slice-start.2 = ((s8[14680064]{0:T(1024)(128)(4,1)}), s8[4194304]{0:T(1024)(128)(4,1)S(1)}, s32[]{:S(2)}) async-start(s8[14680064]{0:T(1024)(128)(4,1)} %bitcast.1), calls=%async_computation.2 | async-start | bytes 8388608
  16.9 2.9 %slice-start.3 = ((s8[14680064]{0:T(1024)(128)(4,1)}), s8[2097152]{0:T(1024)(128)(4,1)S(1)}, s32[]{:S(2)}) async-start(s8[14680064]{0:T(1024)(128)(4,1)} %bitcast.1), calls=%async_computation.3 | async-start | bytes 4194304
  16.9 2.7 %collective-permute-start.6 = (f32[64,4096]{1,0:T(8,128)S(1)}, f32[64,4096]{1,0:T(8,128)S(1)}, u32[]{:S(2)}, u32[]{:S(2)}) collective-permute-start(f32[64,4096]{1,0:T(8,128)S(1)} %shard_map.66.mine), channel_id=1, source_target_pairs={{0,1},{1,0},{2,3},{3,2},{4,5},{5,4},{6,7},{7,6},{8,9},{9,8},{10,11... | collective-permute-start | bytes 3145736 | tf_op jit(solution)/shard_map/ppermute | solution.py:18
  18.4 2.8 %collective-permute-start.7 = (f32[64,4096]{1,0:T(8,128)S(1)}, f32[64,4096]{1,0:T(8,128)S(1)}, u32[]{:S(2)}, u32[]{:S(2)}) collective-permute-start(f32[64,4096]{1,0:T(8,128)S(1)} %shard_map.68.mine), channel_id=1, source_target_pairs={{0,1},{1,0},{2,3},{3,2},{4,5},{5,4},{6,7},{7,6},{8,9},{9,8},{10,11... | collective-permute-start | bytes 3145736 | tf_op jit(solution)/shard_map/ppermute | solution.py:18
  21.3 20.6 %slice-start.4 = ((s8[14680064]{0:T(1024)(128)(4,1)}), s8[4194304]{0:T(1024)(128)(4,1)S(1)}, s32[]{:S(2)}) async-start(s8[14680064]{0:T(1024)(128)(4,1)} %bitcast.3), calls=%async_computation.4 | async-start | bytes 8388608
  21.3 20.6 %slice-start.5 = ((s8[14680064]{0:T(1024)(128)(4,1)}), s8[4194304]{0:T(1024)(128)(4,1)S(1)}, s32[]{:S(2)}) async-start(s8[14680064]{0:T(1024)(128)(4,1)} %bitcast.3), calls=%async_computation.5 | async-start | bytes 8388608
  21.3 20.6 %slice-start.8 = ((s8[14680064]{0:T(1024)(128)(4,1)}), s8[4194304]{0:T(1024)(128)(4,1)S(1)}, s32[]{:S(2)}) async-start(s8[14680064]{0:T(1024)(128)(4,1)} %bitcast.5), calls=%async_computation.8 | async-start | bytes 8388608
  21.3 20.6 %slice-start.9 = ((s8[14680064]{0:T(1024)(128)(4,1)}), s8[4194304]{0:T(1024)(128)(4,1)S(1)}, s32[]{:S(2)}) async-start(s8[14680064]{0:T(1024)(128)(4,1)} %bitcast.5), calls=%async_computation.9 | async-start | bytes 8388608
  22.6 4.5 %collective-permute-start.8 = (bf16[16,896]{1,0:T(8,128)(2,1)S(1)}, bf16[16,896]{1,0:T(8,128)(2,1)S(1)}, u32[]{:S(2)}, u32[]{:S(2)}) collective-permute-start(bf16[16,896]{1,0:T(8,128)(2,1)S(1)} %get-tuple-element.16), channel_id=1, source_target_pairs={{0,4},{2,6},{4,0},{6,2},{8,12},{10,14},{12,8},{14,10},{1,5},{3,7},... | collective-permute-start | bytes 86024 | tf_op jit(solution)/shard_map/ppermute | solution.py:18
  22.7 4.9 %collective-permute-start.9 = (bf16[16,896]{1,0:T(8,128)(2,1)S(1)}, bf16[16,896]{1,0:T(8,128)(2,1)S(1)}, u32[]{:S(2)}, u32[]{:S(2)}) collective-permute-start(bf16[16,896]{1,0:T(8,128)(2,1)S(1)} %get-tuple-element.17), channel_id=1, source_target_pairs={{0,8},{2,10},{4,12},{6,14},{8,0},{10,2},{12,4},{14,6},{1,9},{3,11}... | collective-permute-start | bytes 86024 | tf_op jit(solution)/shard_map/ppermute | solution.py:18
  24.8 5.7 %collective-permute-start.10 = (bf16[16,896]{1,0:T(8,128)(2,1)S(1)}, bf16[16,896]{1,0:T(8,128)(2,1)S(1)}, u32[]{:S(2)}, u32[]{:S(2)}) collective-permute-start(bf16[16,896]{1,0:T(8,128)(2,1)S(1)} %get-tuple-element.18), channel_id=1, source_target_pairs={{0,12},{2,14},{4,8},{6,10},{8,4},{10,6},{12,0},{14,2},{1,13},{3,15... | collective-permute-start | bytes 86024 | tf_op jit(solution)/shard_map/ppermute | solution.py:18
  30.5 11.5 %slice-start.6 = ((s8[14680064]{0:T(1024)(128)(4,1)}), s8[4194304]{0:T(1024)(128)(4,1)S(1)}, s32[]{:S(2)}) async-start(s8[14680064]{0:T(1024)(128)(4,1)} %bitcast.3), calls=%async_computation.6 | async-start | bytes 8388608
  30.5 11.5 %slice-start.10 = ((s8[14680064]{0:T(1024)(128)(4,1)}), s8[4194304]{0:T(1024)(128)(4,1)S(1)}, s32[]{:S(2)}) async-start(s8[14680064]{0:T(1024)(128)(4,1)} %bitcast.5), calls=%async_computation.10 | async-start | bytes 8388608
  30.5 11.5 %slice-start.7 = ((s8[14680064]{0:T(1024)(128)(4,1)}), s8[2097152]{0:T(1024)(128)(4,1)S(1)}, s32[]{:S(2)}) async-start(s8[14680064]{0:T(1024)(128)(4,1)} %bitcast.3), calls=%async_computation.7 | async-start | bytes 4194304
  30.5 11.5 %slice-start.11 = ((s8[14680064]{0:T(1024)(128)(4,1)}), s8[2097152]{0:T(1024)(128)(4,1)S(1)}, s32[]{:S(2)}) async-start(s8[14680064]{0:T(1024)(128)(4,1)} %bitcast.5), calls=%async_computation.11 | async-start | bytes 4194304
  30.5 4.2 %collective-permute-start.11 = (f32[16,896]{1,0:T(8,128)S(1)}, f32[16,896]{1,0:T(8,128)S(1)}, u32[]{:S(2)}, u32[]{:S(2)}) collective-permute-start(f32[16,896]{1,0:T(8,128)S(1)} %shard_map.71.total), channel_id=1, source_target_pairs={{0,2},{2,0},{4,6},{6,4},{8,10},{10,8},{12,14},{14,12},{1,3},{3,1},... | collective-permute-start | bytes 172040 | tf_op jit(solution)/shard_map/ppermute | solution.py:18
  34.8 6.1 %collective-permute-start.14 = (bf16[16,896]{1,0:T(8,128)(2,1)S(1)}, bf16[16,896]{1,0:T(8,128)(2,1)S(1)}, u32[]{:S(2)}, u32[]{:S(2)}) collective-permute-start(bf16[16,896]{1,0:T(8,128)(2,1)S(1)} %shard_map.72.refs_0_), channel_id=1, source_target_pairs={{0,12},{2,14},{4,8},{6,10},{8,4},{10,6},{12,0},{14,2},{1,13},{3,15... | collective-permute-start | bytes 86024 | tf_op jit(solution)/shard_map/ppermute | solution.py:18
  37.1 4.8 %collective-permute-start.13 = (bf16[16,896]{1,0:T(8,128)(2,1)S(1)}, bf16[16,896]{1,0:T(8,128)(2,1)S(1)}, u32[]{:S(2)}, u32[]{:S(2)}) collective-permute-start(bf16[16,896]{1,0:T(8,128)(2,1)S(1)} %shard_map.72.refs_0_), channel_id=1, source_target_pairs={{0,8},{2,10},{4,12},{6,14},{8,0},{10,2},{12,4},{14,6},{1,9},{3,11}... | collective-permute-start | bytes 86024 | tf_op jit(solution)/shard_map/ppermute | solution.py:18
  37.1 4.8 %collective-permute-start.12 = (bf16[16,896]{1,0:T(8,128)(2,1)S(1)}, bf16[16,896]{1,0:T(8,128)(2,1)S(1)}, u32[]{:S(2)}, u32[]{:S(2)}) collective-permute-start(bf16[16,896]{1,0:T(8,128)(2,1)S(1)} %shard_map.72.refs_0_), channel_id=1, source_target_pairs={{0,4},{2,6},{4,0},{6,2},{8,12},{10,14},{12,8},{14,10},{1,5},{3,7},... | collective-permute-start | bytes 86024 | tf_op jit(solution)/shard_map/ppermute | solution.py:18

commit v9 on v8

--- a/solution.py
+++ b/solution.py
@@ -224,31 +224,45 @@
     i, last = pl.program_id(0), pl.num_programs(0) - 1
     rows = out.shape[0]
     part = even.shape[0]
-    slab = 16
-
-    def multiply(start, product):
+    slab, ahead = 16, 8
+    slabs = part // slab
+
+    def multiply(start):
         at = pl.ds(pl.multiple_of(start, part), part)
         c = jnp.dot(codes_t[at, :], err[...], preferred_element_type=jnp.float32)
-        product[...] = c.astype(product.dtype)
+        return c.astype(out.dtype)
+
+    def direction(k, j):
+        at = pl.ds(pl.multiple_of(i * rows + k * part + j * slab, slab), slab)
+        c = products[k][j * slab : (j + 1) * slab, :]
+        first = m[at, :] * a + c
+        second = v[at, :] * p + (c * c) * q
+        root = second * lax.rsqrt(second)
+        return first * pl.reciprocal(root + eps, approx=True)
 
     @pl.when(i == 0)
     def _():
         err[...] = stack(blocks)
-        multiply(0, even)
+        even[...] = multiply(0)
+
+    ready = []
+
+    def store():
+        at, step = ready.pop(0)
+        out[at : at + slab, :] = step
 
     for k in range(2):
-        if k == 0:
-            multiply(i * rows + part, odd)
-        else:
-            multiply(jnp.minimum(i + 1, last) * rows, even)
-        for r in range(0, part, slab):
-            at = pl.ds(pl.multiple_of(i * rows + k * part + r, slab), slab)
-            c = products[k][r : r + slab, :]
-            first = m[at, :] * a + c
-            second = v[at, :] * p + (c * c) * q
-            root = second * lax.rsqrt(second)
-            step = first * pl.reciprocal(root + eps, approx=True)
-            out[k * part + r : k * part + r + slab, :] = step
+        later = multiply(i * rows + part if k == 0 else jnp.minimum(i + 1, last) * rows)
+        into = products[1 - k]
+        for j in range(slabs):
+            ready.append((k * part + j * slab, direction(k, j)))
+            if len(ready) > ahead:
+                store()
+            if 2 * j >= slabs:
+                at = (2 * j - slabs) * slab
+                into[at : at + 2 * slab, :] = later[at : at + 2 * slab]
+    while ready:
+        store()
 
 
 def adam(codes_t, blocks, m, v):

time: 54.6 us -> 54.6 us (level)
  no operation moved by 1% of the time
where the time goes in v9:
time: 54.6 us; the launch traced here: 54.3 us
  Pallas kernels  19.5 us (36%)
  starting transfers between devices  17.7 us (32%)
  waiting for transfers between devices  15.3 us (28%)
  local copies, waits for them, and re-layouts  1.63 us (3%)
    ppermute x15, starting transfers between devices, swap(): return lax.ppermute(value, axis, [(i, i ^ mask) for i in range(n)])  17.7 us
    ppermute x15, waiting for transfers between devices, swap(): return lax.ppermute(value, axis, [(i, i ^ mask) for i in range(n)])  15.3 us
    pallas_call x1, Pallas kernels, adam(): pl.pallas_call(adam_kernel, grid=(lat // rows,), out_shape=jax.ShapeDtype...  12.4 us
    pallas_call x2, Pallas kernels, encode(): pl.pallas_call(functools.partial(encode_kernel, first), out_shape=jax.Sha...  2.84 us
    pallas_call x2, Pallas kernels, decode(): pl.pallas_call(functools.partial(decode_kernel, first, len(given)), out_s...  2.58 us
    pallas_call x1, Pallas kernels, turn(): pl.pallas_call(functools.partial(turn_kernel, min(512, lat)), out_shape=j...  1.68 us
    unnamed x30, local copies, waits for them, and re-layouts  1.63 us
  transfers between devices with their start and end apart: 15, of which 10 were waited for; matrix products, arithmetic and copies ran while one was open for 0% of the time, Pallas kernels for 8%

profile of v9, /device:TPU:0, one launch (start us, length us, event | category | flops | bytes accessed | tf_op | source)
XLA Modules:
  0.0 54.3 jit_solution(1317564926155306434)
XLA Ops:
  0.0 0.5 collective-permute-start
  0.5 2.6 %collective-permute-start.2 = (bf16[4,1792]{1,0:T(4,128)(2,1)}, bf16[4,1792]{1,0:T(4,128)(2,1)S(1)}, u32[]{:S(2)}, u32[]{:S(2)}) collective-permute-start(bf16[4,1792]{1,0:T(4,128)(2,1)} %x.1), channel_id=1, source_target_pairs={{0,3},{1,2},{2,1},{3,0},{4,7},{5,6},{6,5},{7,4},{8,11},{9,10},{10,... | collective-permute-start | bytes 43016 | tf_op jit(solution)/shard_map/ppermute | solution.py:18
  3.1 0.1 collective-permute-start.1
  3.1 1.5 %copy-done.2 = bf16[4,1792]{1,0:T(4,128)(2,1)S(1)} copy-done((bf16[4,1792]{1,0:T(4,128)(2,1)S(1)}, bf16[4,1792]{1,0:T(4,128)(2,1)}, u32[]{:S(2)}) %copy-start.2) | copy-done | bytes 14360
  4.6 0.1 collective-permute-done.2.refs_3_
  4.7 2.3 %collective-permute-done.1.refs_2_ = bf16[4,1792]{1,0:T(4,128)(2,1)S(1)} collective-permute-done((bf16[4,1792]{1,0:T(4,128)(2,1)}, bf16[4,1792]{1,0:T(4,128)(2,1)S(1)}, u32[]{:S(2)}, u32[]{:S(2)}) %collective-permute-start.1) | collective-permute-done | bytes 14368 | tf_op jit(solution)/shard_map/ppermute | solution.py:18
  7.0 3.7 %collective-permute-start.5 = (bf16[16,896]{1,0:T(8,128)(2,1)S(1)}, bf16[16,896]{1,0:T(8,128)(2,1)S(1)}, u32[]{:S(2)}, u32[]{:S(2)}) collective-permute-start(bf16[16,896]{1,0:T(8,128)(2,1)S(1)} %shard_map.65.refs_0_.rows), channel_id=1, source_target_pairs={{0,12},{2,14},{4,8},{6,10},{8,4},{10,6},{12,0},{14,2},{1,13},{3,15... | collective-permute-start | bytes 86024 | tf_op jit(solution)/shard_map/ppermute | solution.py:18
  10.7 0.8 %collective-permute-start.3 = (bf16[16,896]{1,0:T(8,128)(2,1)S(1)}, bf16[16,896]{1,0:T(8,128)(2,1)S(1)}, u32[]{:S(2)}, u32[]{:S(2)}) collective-permute-start(bf16[16,896]{1,0:T(8,128)(2,1)S(1)} %shard_map.65.refs_0_.rows), channel_id=1, source_target_pairs={{0,4},{2,6},{4,0},{6,2},{8,12},{10,14},{12,8},{14,10},{1,5},{3,7},... | collective-permute-start | bytes 86024 | tf_op jit(solution)/shard_map/ppermute | solution.py:18
  11.5 1.3 %collective-permute-done.5.refs_3_ = bf16[16,896]{1,0:T(8,128)(2,1)S(1)} collective-permute-done((bf16[16,896]{1,0:T(8,128)(2,1)S(1)}, bf16[16,896]{1,0:T(8,128)(2,1)S(1)}, u32[]{:S(2)}, u32[]{:S(2)}) %collective-permute-start.5) | collective-permute-done | bytes 28704 | tf_op jit(solution)/shard_map/ppermute | solution.py:18
  12.8 2.7 %collective-permute-done.4.refs_2_ = bf16[16,896]{1,0:T(8,128)(2,1)S(1)} collective-permute-done((bf16[16,896]{1,0:T(8,128)(2,1)S(1)}, bf16[16,896]{1,0:T(8,128)(2,1)S(1)}, u32[]{:S(2)}, u32[]{:S(2)}) %collective-permute-start.4) | collective-permute-done | bytes 28704 | tf_op jit(solution)/shard_map/ppermute | solution.py:18
  15.5 1.4 %shard_map.66.mine = f32[64,4096]{1,0:T(8,128)S(1)} custom-call(bf16[16,896]{1,0:T(8,128)(2,1)S(1)} %shard_map.65.refs_0_.rows, bf16[16,896]{1,0:T(8,128)(2,1)S(1)} %collective-permute-done.3.refs_1_, bf16[16,896]{1,0:T(8,128)(2,1)S(1)} %collective-permute-done.4.refs_2_, bf16[16,896]{1,0:T(8,128)(2,1)S(1)} %collective-permute-done.5.refs_3_, ...), custom_call_target="tpu_custom_call" | custom-call | flops 2449999872 | bytes 7340032 | tf_op jit(solution)/shard_map/pallas_call | solution.py:102
  16.9 0.1 collective-permute-start.6
  17.0 1.4 %shard_map.68.mine = f32[64,4096]{1,0:T(8,128)S(1)} custom-call(bf16[16,896]{1,0:T(8,128)(2,1)S(1)} %shard_map.65.refs_0_.rows, bf16[16,896]{1,0:T(8,128)(2,1)S(1)} %collective-permute-done.3.refs_1_, bf16[16,896]{1,0:T(8,128)(2,1)S(1)} %collective-permute-done.4.refs_2_, bf16[16,896]{1,0:T(8,128)(2,1)S(1)} %collective-permute-done.5.refs_3_, ...), custom_call_target="tpu_custom_call" | custom-call | flops 2449999872 | bytes 7340032 | tf_op jit(solution)/shard_map/pallas_call | solution.py:102
  18.4 0.6 %collective-permute-start.7 = (f32[64,4096]{1,0:T(8,128)S(1)}, f32[64,4096]{1,0:T(8,128)S(1)}, u32[]{:S(2)}, u32[]{:S(2)}) collective-permute-start(f32[64,4096]{1,0:T(8,128)S(1)} %shard_map.68.mine), channel_id=1, source_target_pairs={{0,1},{1,0},{2,3},{3,2},{4,5},{5,4},{6,7},{7,6},{8,9},{9,8},{10,11... | collective-permute-start | bytes 3145736 | tf_op jit(solution)/shard_map/ppermute | solution.py:18
  19.0 0.7 %collective-permute-done.6.theirs = f32[64,4096]{1,0:T(8,128)S(1)} collective-permute-done((f32[64,4096]{1,0:T(8,128)S(1)}, f32[64,4096]{1,0:T(8,128)S(1)}, u32[]{:S(2)}, u32[]{:S(2)}) %collective-permute-start.6) | collective-permute-done | bytes 1048608 | tf_op jit(solution)/shard_map/ppermute | solution.py:18
  19.7 0.1 slice-done.3
  19.8 1.3 %shard_map.67 = (bf16[64,4096]{1,0:T(8,128)(2,1)S(1)}, f32[64,896]{1,0:T(8,128)S(1)}) custom-call(f32[64,4096]{1,0:T(8,128)S(1)} %shard_map.66.mine, f32[64,4096]{1,0:T(8,128)S(1)} %collective-permute-done.6.theirs, f32[1,8192]{1,0:T(1,128)S(1)} %bitcast.7, bf16[8192,896]{1,0:T(8,128)(2,1)S(1)} %bitcast.2), custom_call_target="tpu_custom_call" | custom-call | flops 2449999872 | bytes 7340032 | tf_op jit(solution)/shard_map/pallas_call | solution.py:133
  21.1 0.2 collective-permute-done.7.theirs
  21.3 1.3 %shard_map.69 = (bf16[64,4096]{1,0:T(8,128)(2,1)S(1)}, f32[16,896]{1,0:T(8,128)S(1)}, bf16[16,896]{1,0:T(8,128)(2,1)S(1)}, bf16[16,896]{1,0:T(8,128)(2,1)S(1)}, bf16[16,896]{1,0:T(8,128)(2,1)S(1)}) custom-call(f32[64,4096]{1,0:T(8,128)S(1)} %shard_map.68.mine, f32[64,4096]{1,0:T(8,128)S(1)} %collective-permute-done.7.theirs, f32[1,8192]{1,0:T(1,128)S(1)} %bitcast.8, ...), custom_call_target="tpu_custom_call" | custom-call | flops 2449999872 | bytes 7340032 | tf_op jit(solution)/shard_map/pallas_call | solution.py:133
  22.6 0.1 collective-permute-start.8
  22.7 2.1 %collective-permute-start.9 = (bf16[16,896]{1,0:T(8,128)(2,1)S(1)}, bf16[16,896]{1,0:T(8,128)(2,1)S(1)}, u32[]{:S(2)}, u32[]{:S(2)}) collective-permute-start(bf16[16,896]{1,0:T(8,128)(2,1)S(1)} %get-tuple-element.17), channel_id=1, source_target_pairs={{0,8},{2,10},{4,12},{6,14},{8,0},{10,2},{12,4},{14,6},{1,9},{3,11}... | collective-permute-start | bytes 86024 | tf_op jit(solution)/shard_map/ppermute | solution.py:18
  24.8 2.3 %collective-permute-start.10 = (bf16[16,896]{1,0:T(8,128)(2,1)S(1)}, bf16[16,896]{1,0:T(8,128)(2,1)S(1)}, u32[]{:S(2)}, u32[]{:S(2)}) collective-permute-start(bf16[16,896]{1,0:T(8,128)(2,1)S(1)} %get-tuple-element.18), channel_id=1, source_target_pairs={{0,12},{2,14},{4,8},{6,10},{8,4},{10,6},{12,0},{14,2},{1,13},{3,15... | collective-permute-start | bytes 86024 | tf_op jit(solution)/shard_map/ppermute | solution.py:18
  27.1 0.5 collective-permute-done.9.refs_1_
  27.5 2.9 %collective-permute-done.10.refs_2_ = bf16[16,896]{1,0:T(8,128)(2,1)S(1)} collective-permute-done((bf16[16,896]{1,0:T(8,128)(2,1)S(1)}, bf16[16,896]{1,0:T(8,128)(2,1)S(1)}, u32[]{:S(2)}, u32[]{:S(2)}) %collective-permute-start.10) | collective-permute-done | bytes 28704 | tf_op jit(solution)/shard_map/ppermute | solution.py:18
  30.5 0.0 slice-start.11
  30.5 0.6 %collective-permute-start.11 = (f32[16,896]{1,0:T(8,128)S(1)}, f32[16,896]{1,0:T(8,128)S(1)}, u32[]{:S(2)}, u32[]{:S(2)}) collective-permute-start(f32[16,896]{1,0:T(8,128)S(1)} %shard_map.71.total), channel_id=1, source_target_pairs={{0,2},{2,0},{4,6},{6,4},{8,10},{10,8},{12,14},{14,12},{1,3},{3,1},... | collective-permute-start | bytes 172040 | tf_op jit(solution)/shard_map/ppermute | solution.py:18
  31.1 3.6 %collective-permute-done.11.refs_0_ = f32[16,896]{1,0:T(8,128)S(1)} collective-permute-done((f32[16,896]{1,0:T(8,128)S(1)}, f32[16,896]{1,0:T(8,128)S(1)}, u32[]{:S(2)}, u32[]{:S(2)}) %collective-permute-start.11) | collective-permute-done | bytes 57376 | tf_op jit(solution)/shard_map/ppermute | solution.py:18
  34.8 2.3 %collective-permute-start.14 = (bf16[16,896]{1,0:T(8,128)(2,1)S(1)}, bf16[16,896]{1,0:T(8,128)(2,1)S(1)}, u32[]{:S(2)}, u32[]{:S(2)}) collective-permute-start(bf16[16,896]{1,0:T(8,128)(2,1)S(1)} %shard_map.72.refs_0_), channel_id=1, source_target_pairs={{0,12},{2,14},{4,8},{6,10},{8,4},{10,6},{12,0},{14,2},{1,13},{3,15... | collective-permute-start | bytes 86024 | tf_op jit(solution)/shard_map/ppermute | solution.py:18
  37.1 2.1 %collective-permute-start.12 = (bf16[16,896]{1,0:T(8,128)(2,1)S(1)}, bf16[16,896]{1,0:T(8,128)(2,1)S(1)}, u32[]{:S(2)}, u32[]{:S(2)}) collective-permute-start(bf16[16,896]{1,0:T(8,128)(2,1)S(1)} %shard_map.72.refs_0_), channel_id=1, source_target_pairs={{0,4},{2,6},{4,0},{6,2},{8,12},{10,14},{12,8},{14,10},{1,5},{3,7},... | collective-permute-start | bytes 86024 | tf_op jit(solution)/shard_map/ppermute | solution.py:18
  39.2 1.7 %shard_map.70.codes_t = bf16[8192,64]{1,0:T(8,128)(2,1)S(1)} custom-call(bf16[64,4096]{1,0:T(8,128)(2,1)S(1)} %get-tuple-element.12.refs_0_, bf16[64,4096]{1,0:T(8,128)(2,1)S(1)} %get-tuple-element.14.refs_1_), custom_call_target="tpu_custom_call" | custom-call | flops 1400000000 | bytes 4194304 | tf_op jit(solution)/shard_map/pallas_call | solution.py:158
  40.9 1.0 %collective-permute-done.13.refs_2_ = bf16[16,896]{1,0:T(8,128)(2,1)S(1)} collective-permute-done((bf16[16,896]{1,0:T(8,128)(2,1)S(1)}, bf16[16,896]{1,0:T(8,128)(2,1)S(1)}, u32[]{:S(2)}, u32[]{:S(2)}) %collective-permute-start.13) | collective-permute-done | bytes 28704 | tf_op jit(solution)/shard_map/ppermute | solution.py:18
  42.0 12.4 %shard_map.73 = bf16[8192,896]{1,0:T(8,128)(2,1)} custom-call(bf16[8192,64]{1,0:T(8,128)(2,1)S(1)} %shard_map.70.codes_t, bf16[8192,896]{1,0:T(8,128)(2,1)S(1)} %bitcast.4, bf16[8192,896]{1,0:T(8,128)(2,1)S(1)} %bitcast.6, bf16[16,896]{1,0:T(8,128)(2,1)S(1)} %shard_map.72.refs_0_, bf16[16,896]{1,0:T(8,128)(2,1)S(1)} %collective-permute-done.12.refs_1_, ...), custom_call_target="tpu_custom_call" | custom-call | tf_op jit(solution)/shard_map/pallas_call | solution.py:271
  (41 shorter events, 0.1 us)
Async XLA Ops:
  0.0 15.5 %copy-start = (bf16[896,8192]{1,0:T(8,128)(2,1)S(1)}, bf16[896,8192]{1,0:T(8,128)(2,1)}, u32[]{:S(2)}) copy-start(bf16[896,8192]{1,0:T(8,128)(2,1)} %refs_4_.3) | copy-start | bytes 44040196
  0.0 4.6 %collective-permute-start = (bf16[4,1792]{1,0:T(4,128)(2,1)}, bf16[4,1792]{1,0:T(4,128)(2,1)S(1)}, u32[]{:S(2)}, u32[]{:S(2)}) collective-permute-start(bf16[4,1792]{1,0:T(4,128)(2,1)} %x.1), channel_id=1, source_target_pairs={{0,1},{1,0},{2,3},{3,2},{4,5},{5,4},{6,7},{7,6},{8,9},{9,8},{10,11... | collective-permute-start | bytes 43016 | tf_op jit(solution)/shard_map/ppermute | solution.py:18
  0.5 4.2 %collective-permute-start.2 = (bf16[4,1792]{1,0:T(4,128)(2,1)}, bf16[4,1792]{1,0:T(4,128)(2,1)S(1)}, u32[]{:S(2)}, u32[]{:S(2)}) collective-permute-start(bf16[4,1792]{1,0:T(4,128)(2,1)} %x.1), channel_id=1, source_target_pairs={{0,3},{1,2},{2,1},{3,0},{4,7},{5,6},{6,5},{7,4},{8,11},{9,10},{10,... | collective-permute-start | bytes 43016 | tf_op jit(solution)/shard_map/ppermute | solution.py:18
  3.1 3.9 %collective-permute-start.1 = (bf16[4,1792]{1,0:T(4,128)(2,1)}, bf16[4,1792]{1,0:T(4,128)(2,1)S(1)}, u32[]{:S(2)}, u32[]{:S(2)}) collective-permute-start(bf16[4,1792]{1,0:T(4,128)(2,1)} %x.1), channel_id=1, source_target_pairs={{0,2},{1,3},{2,0},{3,1},{4,6},{5,7},{6,4},{7,5},{8,10},{9,11},{10,... | collective-permute-start | bytes 43016 | tf_op jit(solution)/shard_map/ppermute | solution.py:18
  3.1 1.5 %copy-start.2 = (bf16[4,1792]{1,0:T(4,128)(2,1)S(1)}, bf16[4,1792]{1,0:T(4,128)(2,1)}, u32[]{:S(2)}) copy-start(bf16[4,1792]{1,0:T(4,128)(2,1)} %x.1) | copy-start | bytes 43012
  7.0 12.7 %slice-start = ((s8[14680064]{0:T(1024)(128)(4,1)}), s8[4194304]{0:T(1024)(128)(4,1)S(1)}, s32[]{:S(2)}) async-start(s8[14680064]{0:T(1024)(128)(4,1)} %bitcast.1), calls=%async_computation | async-start | bytes 8388608
  7.0 12.6 %slice-start.1 = ((s8[14680064]{0:T(1024)(128)(4,1)}), s8[4194304]{0:T(1024)(128)(4,1)S(1)}, s32[]{:S(2)}) async-start(s8[14680064]{0:T(1024)(128)(4,1)} %bitcast.1), calls=%async_computation.1 | async-start | bytes 8388608
  7.0 12.6 %copy-start.1 = (f32[8192]{0:T(1024)S(1)}, f32[8192]{0:T(1024)}, u32[]{:S(2)}) copy-start(f32[8192]{0:T(1024)} %param.8) | copy-start | bytes 98308
  7.0 5.7 %collective-permute-start.5 = (bf16[16,896]{1,0:T(8,128)(2,1)S(1)}, bf16[16,896]{1,0:T(8,128)(2,1)S(1)}, u32[]{:S(2)}, u32[]{:S(2)}) collective-permute-start(bf16[16,896]{1,0:T(8,128)(2,1)S(1)} %shard_map.65.refs_0_.rows), channel_id=1, source_target_pairs={{0,12},{2,14},{4,8},{6,10},{8,4},{10,6},{12,0},{14,2},{1,13},{3,15... | collective-permute-start | bytes 86024 | tf_op jit(solution)/shard_map/ppermute | solution.py:18
  10.7 4.8 %collective-permute-start.4 = (bf16[16,896]{1,0:T(8,128)(2,1)S(1)}, bf16[16,896]{1,0:T(8,128)(2,1)S(1)}, u32[]{:S(2)}, u32[]{:S(2)}) collective-permute-start(bf16[16,896]{1,0:T(8,128)(2,1)S(1)} %shard_map.65.refs_0_.rows), channel_id=1, source_target_pairs={{0,8},{2,10},{4,12},{6,14},{8,0},{10,2},{12,4},{14,6},{1,9},{3,11}... | collective-permute-start | bytes 86024 | tf_op jit(solution)/shard_map/ppermute | solution.py:18
  10.7 4.8 %collective-permute-start.3 = (bf16[16,896]{1,0:T(8,128)(2,1)S(1)}, bf16[16,896]{1,0:T(8,128)(2,1)S(1)}, u32[]{:S(2)}, u32[]{:S(2)}) collective-permute-start(bf16[16,896]{1,0:T(8,128)(2,1)S(1)} %shard_map.65.refs_0_.rows), channel_id=1, source_target_pairs={{0,4},{2,6},{4,0},{6,2},{8,12},{10,14},{12,8},{14,10},{1,5},{3,7},... | collective-permute-start | bytes 86024 | tf_op jit(solution)/shard_map/ppermute | solution.py:18
  16.9 2.8 %slice-start.2 = ((s8[14680064]{0:T(1024)(128)(4,1)}), s8[4194304]{0:T(1024)(128)(4,1)S(1)}, s32[]{:S(2)}) async-start(s8[14680064]{0:T(1024)(128)(4,1)} %bitcast.1), calls=%async_computation.2 | async-start | bytes 8388608
  16.9 2.9 %slice-start.3 = ((s8[14680064]{0:T(1024)(128)(4,1)}), s8[2097152]{0:T(1024)(128)(4,1)S(1)}, s32[]{:S(2)}) async-start(s8[14680064]{0:T(1024)(128)(4,1)} %bitcast.1), calls=%async_computation.3 | async-start | bytes 4194304
  16.9 2.7 %collective-permute-start.6 = (f32[64,4096]{1,0:T(8,128)S(1)}, f32[64,4096]{1,0:T(8,128)S(1)}, u32[]{:S(2)}, u32[]{:S(2)}) collective-permute-start(f32[64,4096]{1,0:T(8,128)S(1)} %shard_map.66.mine), channel_id=1, source_target_pairs={{0,1},{1,0},{2,3},{3,2},{4,5},{5,4},{6,7},{7,6},{8,9},{9,8},{10,11... | collective-permute-start | bytes 3145736 | tf_op jit(solution)/shard_map/ppermute | solution.py:18
  18.4 2.8 %collective-permute-start.7 = (f32[64,4096]{1,0:T(8,128)S(1)}, f32[64,4096]{1,0:T(8,128)S(1)}, u32[]{:S(2)}, u32[]{:S(2)}) collective-permute-start(f32[64,4096]{1,0:T(8,128)S(1)} %shard_map.68.mine), channel_id=1, source_target_pairs={{0,1},{1,0},{2,3},{3,2},{4,5},{5,4},{6,7},{7,6},{8,9},{9,8},{10,11... | collective-permute-start | bytes 3145736 | tf_op jit(solution)/shard_map/ppermute | solution.py:18
  21.3 20.6 %slice-start.4 = ((s8[14680064]{0:T(1024)(128)(4,1)}), s8[4194304]{0:T(1024)(128)(4,1)S(1)}, s32[]{:S(2)}) async-start(s8[14680064]{0:T(1024)(128)(4,1)} %bitcast.3), calls=%async_computation.4 | async-start | bytes 8388608
  21.3 20.6 %slice-start.5 = ((s8[14680064]{0:T(1024)(128)(4,1)}), s8[4194304]{0:T(1024)(128)(4,1)S(1)}, s32[]{:S(2)}) async-start(s8[14680064]{0:T(1024)(128)(4,1)} %bitcast.3), calls=%async_computation.5 | async-start | bytes 8388608
  21.3 20.6 %slice-start.8 = ((s8[14680064]{0:T(1024)(128)(4,1)}), s8[4194304]{0:T(1024)(128)(4,1)S(1)}, s32[]{:S(2)}) async-start(s8[14680064]{0:T(1024)(128)(4,1)} %bitcast.5), calls=%async_computation.8 | async-start | bytes 8388608
  21.3 20.6 %slice-start.9 = ((s8[14680064]{0:T(1024)(128)(4,1)}), s8[4194304]{0:T(1024)(128)(4,1)S(1)}, s32[]{:S(2)}) async-start(s8[14680064]{0:T(1024)(128)(4,1)} %bitcast.5), calls=%async_computation.9 | async-start | bytes 8388608
  22.6 4.5 %collective-permute-start.8 = (bf16[16,896]{1,0:T(8,128)(2,1)S(1)}, bf16[16,896]{1,0:T(8,128)(2,1)S(1)}, u32[]{:S(2)}, u32[]{:S(2)}) collective-permute-start(bf16[16,896]{1,0:T(8,128)(2,1)S(1)} %get-tuple-element.16), channel_id=1, source_target_pairs={{0,4},{2,6},{4,0},{6,2},{8,12},{10,14},{12,8},{14,10},{1,5},{3,7},... | collective-permute-start | bytes 86024 | tf_op jit(solution)/shard_map/ppermute | solution.py:18
  22.7 4.9 %collective-permute-start.9 = (bf16[16,896]{1,0:T(8,128)(2,1)S(1)}, bf16[16,896]{1,0:T(8,128)(2,1)S(1)}, u32[]{:S(2)}, u32[]{:S(2)}) collective-permute-start(bf16[16,896]{1,0:T(8,128)(2,1)S(1)} %get-tuple-element.17), channel_id=1, source_target_pairs={{0,8},{2,10},{4,12},{6,14},{8,0},{10,2},{12,4},{14,6},{1,9},{3,11}... | collective-permute-start | bytes 86024 | tf_op jit(solution)/shard_map/ppermute | solution.py:18
  24.8 5.7 %collective-permute-start.10 = (bf16[16,896]{1,0:T(8,128)(2,1)S(1)}, bf16[16,896]{1,0:T(8,128)(2,1)S(1)}, u32[]{:S(2)}, u32[]{:S(2)}) collective-permute-start(bf16[16,896]{1,0:T(8,128)(2,1)S(1)} %get-tuple-element.18), channel_id=1, source_target_pairs={{0,12},{2,14},{4,8},{6,10},{8,4},{10,6},{12,0},{14,2},{1,13},{3,15... | collective-permute-start | bytes 86024 | tf_op jit(solution)/shard_map/ppermute | solution.py:18
  30.5 11.5 %slice-start.6 = ((s8[14680064]{0:T(1024)(128)(4,1)}), s8[4194304]{0:T(1024)(128)(4,1)S(1)}, s32[]{:S(2)}) async-start(s8[14680064]{0:T(1024)(128)(4,1)} %bitcast.3), calls=%async_computation.6 | async-start | bytes 8388608
  30.5 11.5 %slice-start.10 = ((s8[14680064]{0:T(1024)(128)(4,1)}), s8[4194304]{0:T(1024)(128)(4,1)S(1)}, s32[]{:S(2)}) async-start(s8[14680064]{0:T(1024)(128)(4,1)} %bitcast.5), calls=%async_computation.10 | async-start | bytes 8388608
  30.5 11.5 %slice-start.7 = ((s8[14680064]{0:T(1024)(128)(4,1)}), s8[2097152]{0:T(1024)(128)(4,1)S(1)}, s32[]{:S(2)}) async-start(s8[14680064]{0:T(1024)(128)(4,1)} %bitcast.3), calls=%async_computation.7 | async-start | bytes 4194304
  30.5 11.5 %slice-start.11 = ((s8[14680064]{0:T(1024)(128)(4,1)}), s8[2097152]{0:T(1024)(128)(4,1)S(1)}, s32[]{:S(2)}) async-start(s8[14680064]{0:T(1024)(128)(4,1)} %bitcast.5), calls=%async_computation.11 | async-start | bytes 4194304
  30.5 4.2 %collective-permute-start.11 = (f32[16,896]{1,0:T(8,128)S(1)}, f32[16,896]{1,0:T(8,128)S(1)}, u32[]{:S(2)}, u32[]{:S(2)}) collective-permute-start(f32[16,896]{1,0:T(8,128)S(1)} %shard_map.71.total), channel_id=1, source_target_pairs={{0,2},{2,0},{4,6},{6,4},{8,10},{10,8},{12,14},{14,12},{1,3},{3,1},... | collective-permute-start | bytes 172040 | tf_op jit(solution)/shard_map/ppermute | solution.py:18
  34.8 6.1 %collective-permute-start.14 = (bf16[16,896]{1,0:T(8,128)(2,1)S(1)}, bf16[16,896]{1,0:T(8,128)(2,1)S(1)}, u32[]{:S(2)}, u32[]{:S(2)}) collective-permute-start(bf16[16,896]{1,0:T(8,128)(2,1)S(1)} %shard_map.72.refs_0_), channel_id=1, source_target_pairs={{0,12},{2,14},{4,8},{6,10},{8,4},{10,6},{12,0},{14,2},{1,13},{3,15... | collective-permute-start | bytes 86024 | tf_op jit(solution)/shard_map/ppermute | solution.py:18
  37.1 4.8 %collective-permute-start.13 = (bf16[16,896]{1,0:T(8,128)(2,1)S(1)}, bf16[16,896]{1,0:T(8,128)(2,1)S(1)}, u32[]{:S(2)}, u32[]{:S(2)}) collective-permute-start(bf16[16,896]{1,0:T(8,128)(2,1)S(1)} %shard_map.72.refs_0_), channel_id=1, source_target_pairs={{0,8},{2,10},{4,12},{6,14},{8,0},{10,2},{12,4},{14,6},{1,9},{3,11}... | collective-permute-start | bytes 86024 | tf_op jit(solution)/shard_map/ppermute | solution.py:18
  37.1 4.8 %collective-permute-start.12 = (bf16[16,896]{1,0:T(8,128)(2,1)S(1)}, bf16[16,896]{1,0:T(8,128)(2,1)S(1)}, u32[]{:S(2)}, u32[]{:S(2)}) collective-permute-start(bf16[16,896]{1,0:T(8,128)(2,1)S(1)} %shard_map.72.refs_0_), channel_id=1, source_target_pairs={{0,4},{2,6},{4,0},{6,2},{8,12},{10,14},{12,8},{14,10},{1,5},{3,7},... | collective-permute-start | bytes 86024 | tf_op jit(solution)/shard_map/ppermute | solution.py:18

commit v10 on v8

--- a/solution.py
+++ b/solution.py
@@ -213,7 +213,7 @@
 
 
 def adam_kernel(codes_t, m, v, *refs):
-    *blocks, out, even, odd, err = refs
+    *blocks, out, even, odd, err, ready, sems = refs
     products = (even, odd)
     tokens = codes_t.shape[1]
     b = 0.1 / (1.0 - 0.9**10) / tokens
@@ -221,10 +221,20 @@
     p = 0.999 / (1.0 - 0.999**10) / b**2
     q = 0.001 / (1.0 - 0.999**10) / tokens**2 / b**2
     a, p, q, eps = (jnp.asarray(x, out.dtype) for x in (a, p, q, 1e-8 / b))
-    i, last = pl.program_id(0), pl.num_programs(0) - 1
-    rows = out.shape[0]
+    i, steps = pl.program_id(0), pl.num_programs(0)
+    rows, half = ready.shape[1:]
     part = even.shape[0]
+    pieces = sems.shape[1]
+    piece = rows // pieces
     slab = 16
+    slot = lax.rem(i, 2)
+
+    def sent(step, k):
+        slot = lax.rem(step, 2)
+        at = pl.ds(pl.multiple_of(step * rows + k * piece, piece), piece)
+        return pltpu.make_async_copy(
+            ready.at[slot, pl.ds(k * piece, piece)], out.at[at], sems.at[slot, k]
+        )
 
     def multiply(start, product):
         at = pl.ds(pl.multiple_of(start, part), part)
@@ -236,19 +246,35 @@
         err[...] = stack(blocks)
         multiply(0, even)
 
-    for k in range(2):
-        if k == 0:
+    @pl.when(i >= 2)
+    def _():
+        for k in range(pieces):
+            sent(i - 2, k).wait()
+
+    for r in range(0, rows, slab):
+        if r == 0:
             multiply(i * rows + part, odd)
-        else:
-            multiply(jnp.minimum(i + 1, last) * rows, even)
-        for r in range(0, part, slab):
-            at = pl.ds(pl.multiple_of(i * rows + k * part + r, slab), slab)
-            c = products[k][r : r + slab, :]
-            first = m[at, :] * a + c
-            second = v[at, :] * p + (c * c) * q
-            root = second * lax.rsqrt(second)
-            step = first * pl.reciprocal(root + eps, approx=True)
-            out[k * part + r : k * part + r + slab, :] = step
+        if r == part:
+            multiply(jnp.minimum(i + 1, steps - 1) * rows, even)
+        at = pl.ds(pl.multiple_of(i * rows + r, slab), slab)
+        c = products[r // part][r % part : r % part + slab, :]
+        first = m[at, :] * a + c
+        second = v[at, :] * p + (c * c) * q
+        root = second * lax.rsqrt(second)
+        step = first * pl.reciprocal(root + eps, approx=True)
+        ready[slot, r : r + slab, :] = step
+        if (r + slab) % piece == 0:
+            sent(i, r // piece).start()
+
+    @pl.when(i == steps - 1)
+    def _():
+        for k in range(pieces):
+            sent(i, k).wait()
+
+    @pl.when((i == steps - 1) & (i >= 1))
+    def _():
+        for k in range(pieces):
+            sent(i - 1, k).wait()
 
 
 def adam(codes_t, blocks, m, v):
@@ -259,9 +285,13 @@
         grid=(lat // rows,),
         out_shape=jax.ShapeDtypeStruct(m.shape, jnp.bfloat16),
         in_specs=[WHOLE] * (3 + len(blocks)),
-        out_specs=pl.BlockSpec((rows, half), lambda i: (i, 0)),
+        out_specs=pl.BlockSpec(memory_space=pl.ANY),
         scratch_shapes=[pltpu.VMEM((rows // 2, half), jnp.bfloat16)] * 2
-        + [pltpu.VMEM((codes_t.shape[1], half), jnp.bfloat16)],
+        + [
+            pltpu.VMEM((codes_t.shape[1], half), jnp.bfloat16),
+            pltpu.VMEM((2, rows, half), jnp.bfloat16),
+            pltpu.SemaphoreType.DMA((2, 4)),
+        ],
         compiler_params=params(12),
     )(codes_t, resident(m), resident(v), *blocks)
 

time: 54.6 us -> 55.4 us (1.015)
  Pallas kernels: 19.5 us -> 20.3 us
    pallas_call x1, Pallas kernels: 12.4 us -> 13.2 us  [adam(): pl.pallas_call(adam_kernel, grid=(lat // rows,), out_shape=jax.ShapeDtype...]
where the time goes in v10:
time: 55.4 us; the launch traced here: 55.2 us
  Pallas kernels  20.3 us (37%)
  starting transfers between devices  17.7 us (32%)
  waiting for transfers between devices  15.3 us (28%)
  local copies, waits for them, and re-layouts  1.63 us (3%)
    ppermute x15, starting transfers between devices, swap(): return lax.ppermute(value, axis, [(i, i ^ mask) for i in range(n)])  17.7 us
    ppermute x15, waiting for transfers between devices, swap(): return lax.ppermute(value, axis, [(i, i ^ mask) for i in range(n)])  15.3 us
    pallas_call x1, Pallas kernels, adam(): pl.pallas_call(adam_kernel, grid=(lat // rows,), out_shape=jax.ShapeDtype...  13.2 us
    pallas_call x2, Pallas kernels, encode(): pl.pallas_call(functools.partial(encode_kernel, first), out_shape=jax.Sha...  2.84 us
    pallas_call x2, Pallas kernels, decode(): pl.pallas_call(functools.partial(decode_kernel, first, len(given)), out_s...  2.58 us
    pallas_call x1, Pallas kernels, turn(): pl.pallas_call(functools.partial(turn_kernel, min(512, lat)), out_shape=j...  1.68 us
    unnamed x30, local copies, waits for them, and re-layouts  1.63 us
  transfers between devices with their start and end apart: 15, of which 10 were waited for; matrix products, arithmetic and copies ran while one was open for 0% of the time, Pallas kernels for 8%

profile of v10, /device:TPU:0, one launch (start us, length us, event | category | flops | bytes accessed | tf_op | source)
XLA Modules:
  0.0 55.2 jit_solution(4880076732781475857)
XLA Ops:
  0.0 0.5 collective-permute-start
  0.5 2.6 %collective-permute-start.2 = (bf16[4,1792]{1,0:T(4,128)(2,1)}, bf16[4,1792]{1,0:T(4,128)(2,1)S(1)}, u32[]{:S(2)}, u32[]{:S(2)}) collective-permute-start(bf16[4,1792]{1,0:T(4,128)(2,1)} %x.1), channel_id=1, source_target_pairs={{0,3},{1,2},{2,1},{3,0},{4,7},{5,6},{6,5},{7,4},{8,11},{9,10},{10,... | collective-permute-start | bytes 43016 | tf_op jit(solution)/shard_map/ppermute | solution.py:18
  3.1 0.1 collective-permute-start.1
  3.1 1.5 %copy-done.2 = bf16[4,1792]{1,0:T(4,128)(2,1)S(1)} copy-done((bf16[4,1792]{1,0:T(4,128)(2,1)S(1)}, bf16[4,1792]{1,0:T(4,128)(2,1)}, u32[]{:S(2)}) %copy-start.2) | copy-done | bytes 14360
  4.6 0.1 collective-permute-done.2.refs_3_
  4.7 2.3 %collective-permute-done.1.refs_2_ = bf16[4,1792]{1,0:T(4,128)(2,1)S(1)} collective-permute-done((bf16[4,1792]{1,0:T(4,128)(2,1)}, bf16[4,1792]{1,0:T(4,128)(2,1)S(1)}, u32[]{:S(2)}, u32[]{:S(2)}) %collective-permute-start.1) | collective-permute-done | bytes 14368 | tf_op jit(solution)/shard_map/ppermute | solution.py:18
  7.0 3.7 %collective-permute-start.5 = (bf16[16,896]{1,0:T(8,128)(2,1)S(1)}, bf16[16,896]{1,0:T(8,128)(2,1)S(1)}, u32[]{:S(2)}, u32[]{:S(2)}) collective-permute-start(bf16[16,896]{1,0:T(8,128)(2,1)S(1)} %shard_map.65.refs_0_.rows), channel_id=1, source_target_pairs={{0,12},{2,14},{4,8},{6,10},{8,4},{10,6},{12,0},{14,2},{1,13},{3,15... | collective-permute-start | bytes 86024 | tf_op jit(solution)/shard_map/ppermute | solution.py:18
  10.7 0.8 %collective-permute-start.3 = (bf16[16,896]{1,0:T(8,128)(2,1)S(1)}, bf16[16,896]{1,0:T(8,128)(2,1)S(1)}, u32[]{:S(2)}, u32[]{:S(2)}) collective-permute-start(bf16[16,896]{1,0:T(8,128)(2,1)S(1)} %shard_map.65.refs_0_.rows), channel_id=1, source_target_pairs={{0,4},{2,6},{4,0},{6,2},{8,12},{10,14},{12,8},{14,10},{1,5},{3,7},... | collective-permute-start | bytes 86024 | tf_op jit(solution)/shard_map/ppermute | solution.py:18
  11.5 1.3 %collective-permute-done.5.refs_3_ = bf16[16,896]{1,0:T(8,128)(2,1)S(1)} collective-permute-done((bf16[16,896]{1,0:T(8,128)(2,1)S(1)}, bf16[16,896]{1,0:T(8,128)(2,1)S(1)}, u32[]{:S(2)}, u32[]{:S(2)}) %collective-permute-start.5) | collective-permute-done | bytes 28704 | tf_op jit(solution)/shard_map/ppermute | solution.py:18
  12.8 2.7 %collective-permute-done.4.refs_2_ = bf16[16,896]{1,0:T(8,128)(2,1)S(1)} collective-permute-done((bf16[16,896]{1,0:T(8,128)(2,1)S(1)}, bf16[16,896]{1,0:T(8,128)(2,1)S(1)}, u32[]{:S(2)}, u32[]{:S(2)}) %collective-permute-start.4) | collective-permute-done | bytes 28704 | tf_op jit(solution)/shard_map/ppermute | solution.py:18
  15.5 1.4 %shard_map.66.mine = f32[64,4096]{1,0:T(8,128)S(1)} custom-call(bf16[16,896]{1,0:T(8,128)(2,1)S(1)} %shard_map.65.refs_0_.rows, bf16[16,896]{1,0:T(8,128)(2,1)S(1)} %collective-permute-done.3.refs_1_, bf16[16,896]{1,0:T(8,128)(2,1)S(1)} %collective-permute-done.4.refs_2_, bf16[16,896]{1,0:T(8,128)(2,1)S(1)} %collective-permute-done.5.refs_3_, ...), custom_call_target="tpu_custom_call" | custom-call | flops 2449999872 | bytes 7340032 | tf_op jit(solution)/shard_map/pallas_call | solution.py:102
  16.9 0.0 slice-start.2
  16.9 0.1 collective-permute-start.6
  17.0 1.4 %shard_map.68.mine = f32[64,4096]{1,0:T(8,128)S(1)} custom-call(bf16[16,896]{1,0:T(8,128)(2,1)S(1)} %shard_map.65.refs_0_.rows, bf16[16,896]{1,0:T(8,128)(2,1)S(1)} %collective-permute-done.3.refs_1_, bf16[16,896]{1,0:T(8,128)(2,1)S(1)} %collective-permute-done.4.refs_2_, bf16[16,896]{1,0:T(8,128)(2,1)S(1)} %collective-permute-done.5.refs_3_, ...), custom_call_target="tpu_custom_call" | custom-call | flops 2449999872 | bytes 7340032 | tf_op jit(solution)/shard_map/pallas_call | solution.py:102
  18.4 0.6 %collective-permute-start.7 = (f32[64,4096]{1,0:T(8,128)S(1)}, f32[64,4096]{1,0:T(8,128)S(1)}, u32[]{:S(2)}, u32[]{:S(2)}) collective-permute-start(f32[64,4096]{1,0:T(8,128)S(1)} %shard_map.68.mine), channel_id=1, source_target_pairs={{0,1},{1,0},{2,3},{3,2},{4,5},{5,4},{6,7},{7,6},{8,9},{9,8},{10,11... | collective-permute-start | bytes 3145736 | tf_op jit(solution)/shard_map/ppermute | solution.py:18
  19.0 0.7 %collective-permute-done.6.theirs = f32[64,4096]{1,0:T(8,128)S(1)} collective-permute-done((f32[64,4096]{1,0:T(8,128)S(1)}, f32[64,4096]{1,0:T(8,128)S(1)}, u32[]{:S(2)}, u32[]{:S(2)}) %collective-permute-start.6) | collective-permute-done | bytes 1048608 | tf_op jit(solution)/shard_map/ppermute | solution.py:18
  19.7 0.1 slice-done.3
  19.8 1.3 %shard_map.67 = (bf16[64,4096]{1,0:T(8,128)(2,1)S(1)}, f32[64,896]{1,0:T(8,128)S(1)}) custom-call(f32[64,4096]{1,0:T(8,128)S(1)} %shard_map.66.mine, f32[64,4096]{1,0:T(8,128)S(1)} %collective-permute-done.6.theirs, f32[1,8192]{1,0:T(1,128)S(1)} %bitcast.7, bf16[8192,896]{1,0:T(8,128)(2,1)S(1)} %bitcast.2), custom_call_target="tpu_custom_call" | custom-call | flops 2449999872 | bytes 7340032 | tf_op jit(solution)/shard_map/pallas_call | solution.py:133
  21.1 0.2 collective-permute-done.7.theirs
  21.3 1.3 %shard_map.69 = (bf16[64,4096]{1,0:T(8,128)(2,1)S(1)}, f32[16,896]{1,0:T(8,128)S(1)}, bf16[16,896]{1,0:T(8,128)(2,1)S(1)}, bf16[16,896]{1,0:T(8,128)(2,1)S(1)}, bf16[16,896]{1,0:T(8,128)(2,1)S(1)}) custom-call(f32[64,4096]{1,0:T(8,128)S(1)} %shard_map.68.mine, f32[64,4096]{1,0:T(8,128)S(1)} %collective-permute-done.7.theirs, f32[1,8192]{1,0:T(1,128)S(1)} %bitcast.8, ...), custom_call_target="tpu_custom_call" | custom-call | flops 2449999872 | bytes 7340032 | tf_op jit(solution)/shard_map/pallas_call | solution.py:133
  22.6 0.1 collective-permute-start.8
  22.7 2.1 %collective-permute-start.9 = (bf16[16,896]{1,0:T(8,128)(2,1)S(1)}, bf16[16,896]{1,0:T(8,128)(2,1)S(1)}, u32[]{:S(2)}, u32[]{:S(2)}) collective-permute-start(bf16[16,896]{1,0:T(8,128)(2,1)S(1)} %get-tuple-element.17), channel_id=1, source_target_pairs={{0,8},{2,10},{4,12},{6,14},{8,0},{10,2},{12,4},{14,6},{1,9},{3,11}... | collective-permute-start | bytes 86024 | tf_op jit(solution)/shard_map/ppermute | solution.py:18
  24.8 2.3 %collective-permute-start.10 = (bf16[16,896]{1,0:T(8,128)(2,1)S(1)}, bf16[16,896]{1,0:T(8,128)(2,1)S(1)}, u32[]{:S(2)}, u32[]{:S(2)}) collective-permute-start(bf16[16,896]{1,0:T(8,128)(2,1)S(1)} %get-tuple-element.18), channel_id=1, source_target_pairs={{0,12},{2,14},{4,8},{6,10},{8,4},{10,6},{12,0},{14,2},{1,13},{3,15... | collective-permute-start | bytes 86024 | tf_op jit(solution)/shard_map/ppermute | solution.py:18
  27.1 0.5 collective-permute-done.9.refs_1_
  27.5 2.9 %collective-permute-done.10.refs_2_ = bf16[16,896]{1,0:T(8,128)(2,1)S(1)} collective-permute-done((bf16[16,896]{1,0:T(8,128)(2,1)S(1)}, bf16[16,896]{1,0:T(8,128)(2,1)S(1)}, u32[]{:S(2)}, u32[]{:S(2)}) %collective-permute-start.10) | collective-permute-done | bytes 28704 | tf_op jit(solution)/shard_map/ppermute | solution.py:18
  30.5 0.6 %collective-permute-start.11 = (f32[16,896]{1,0:T(8,128)S(1)}, f32[16,896]{1,0:T(8,128)S(1)}, u32[]{:S(2)}, u32[]{:S(2)}) collective-permute-start(f32[16,896]{1,0:T(8,128)S(1)} %shard_map.71.total), channel_id=1, source_target_pairs={{0,2},{2,0},{4,6},{6,4},{8,10},{10,8},{12,14},{14,12},{1,3},{3,1},... | collective-permute-start | bytes 172040 | tf_op jit(solution)/shard_map/ppermute | solution.py:18
  31.1 3.6 %collective-permute-done.11.refs_0_ = f32[16,896]{1,0:T(8,128)S(1)} collective-permute-done((f32[16,896]{1,0:T(8,128)S(1)}, f32[16,896]{1,0:T(8,128)S(1)}, u32[]{:S(2)}, u32[]{:S(2)}) %collective-permute-start.11) | collective-permute-done | bytes 57376 | tf_op jit(solution)/shard_map/ppermute | solution.py:18
  34.8 2.3 %collective-permute-start.14 = (bf16[16,896]{1,0:T(8,128)(2,1)S(1)}, bf16[16,896]{1,0:T(8,128)(2,1)S(1)}, u32[]{:S(2)}, u32[]{:S(2)}) collective-permute-start(bf16[16,896]{1,0:T(8,128)(2,1)S(1)} %shard_map.72.refs_0_), channel_id=1, source_target_pairs={{0,12},{2,14},{4,8},{6,10},{8,4},{10,6},{12,0},{14,2},{1,13},{3,15... | collective-permute-start | bytes 86024 | tf_op jit(solution)/shard_map/ppermute | solution.py:18
  37.1 2.1 %collective-permute-start.12 = (bf16[16,896]{1,0:T(8,128)(2,1)S(1)}, bf16[16,896]{1,0:T(8,128)(2,1)S(1)}, u32[]{:S(2)}, u32[]{:S(2)}) collective-permute-start(bf16[16,896]{1,0:T(8,128)(2,1)S(1)} %shard_map.72.refs_0_), channel_id=1, source_target_pairs={{0,4},{2,6},{4,0},{6,2},{8,12},{10,14},{12,8},{14,10},{1,5},{3,7},... | collective-permute-start | bytes 86024 | tf_op jit(solution)/shard_map/ppermute | solution.py:18
  39.2 1.7 %shard_map.70.codes_t = bf16[8192,64]{1,0:T(8,128)(2,1)S(1)} custom-call(bf16[64,4096]{1,0:T(8,128)(2,1)S(1)} %get-tuple-element.12.refs_0_, bf16[64,4096]{1,0:T(8,128)(2,1)S(1)} %get-tuple-element.14.refs_1_), custom_call_target="tpu_custom_call" | custom-call | flops 1400000000 | bytes 4194304 | tf_op jit(solution)/shard_map/pallas_call | solution.py:158
  40.9 1.0 %collective-permute-done.13.refs_2_ = bf16[16,896]{1,0:T(8,128)(2,1)S(1)} collective-permute-done((bf16[16,896]{1,0:T(8,128)(2,1)S(1)}, bf16[16,896]{1,0:T(8,128)(2,1)S(1)}, u32[]{:S(2)}, u32[]{:S(2)}) %collective-permute-start.13) | collective-permute-done | bytes 28704 | tf_op jit(solution)/shard_map/ppermute | solution.py:18
  42.0 13.2 %shard_map.73 = bf16[8192,896]{1,0:T(8,128)(2,1)} custom-call(bf16[8192,64]{1,0:T(8,128)(2,1)S(1)} %shard_map.70.codes_t, bf16[8192,896]{1,0:T(8,128)(2,1)S(1)} %bitcast.4, bf16[8192,896]{1,0:T(8,128)(2,1)S(1)} %bitcast.6, bf16[16,896]{1,0:T(8,128)(2,1)S(1)} %shard_map.72.refs_0_, bf16[16,896]{1,0:T(8,128)(2,1)S(1)} %collective-permute-done.12.refs_1_, ...), custom_call_target="tpu_custom_call" | custom-call | tf_op jit(solution)/shard_map/pallas_call | solution.py:283
  (41 shorter events, 0.1 us)
Async XLA Ops:
  0.0 15.5 %copy-start = (bf16[896,8192]{1,0:T(8,128)(2,1)S(1)}, bf16[896,8192]{1,0:T(8,128)(2,1)}, u32[]{:S(2)}) copy-start(bf16[896,8192]{1,0:T(8,128)(2,1)} %refs_4_.3) | copy-start | bytes 44040196
  0.0 4.6 %collective-permute-start = (bf16[4,1792]{1,0:T(4,128)(2,1)}, bf16[4,1792]{1,0:T(4,128)(2,1)S(1)}, u32[]{:S(2)}, u32[]{:S(2)}) collective-permute-start(bf16[4,1792]{1,0:T(4,128)(2,1)} %x.1), channel_id=1, source_target_pairs={{0,1},{1,0},{2,3},{3,2},{4,5},{5,4},{6,7},{7,6},{8,9},{9,8},{10,11... | collective-permute-start | bytes 43016 | tf_op jit(solution)/shard_map/ppermute | solution.py:18
  0.5 4.2 %collective-permute-start.2 = (bf16[4,1792]{1,0:T(4,128)(2,1)}, bf16[4,1792]{1,0:T(4,128)(2,1)S(1)}, u32[]{:S(2)}, u32[]{:S(2)}) collective-permute-start(bf16[4,1792]{1,0:T(4,128)(2,1)} %x.1), channel_id=1, source_target_pairs={{0,3},{1,2},{2,1},{3,0},{4,7},{5,6},{6,5},{7,4},{8,11},{9,10},{10,... | collective-permute-start | bytes 43016 | tf_op jit(solution)/shard_map/ppermute | solution.py:18
  3.1 3.9 %collective-permute-start.1 = (bf16[4,1792]{1,0:T(4,128)(2,1)}, bf16[4,1792]{1,0:T(4,128)(2,1)S(1)}, u32[]{:S(2)}, u32[]{:S(2)}) collective-permute-start(bf16[4,1792]{1,0:T(4,128)(2,1)} %x.1), channel_id=1, source_target_pairs={{0,2},{1,3},{2,0},{3,1},{4,6},{5,7},{6,4},{7,5},{8,10},{9,11},{10,... | collective-permute-start | bytes 43016 | tf_op jit(solution)/shard_map/ppermute | solution.py:18
  3.1 1.5 %copy-start.2 = (bf16[4,1792]{1,0:T(4,128)(2,1)S(1)}, bf16[4,1792]{1,0:T(4,128)(2,1)}, u32[]{:S(2)}) copy-start(bf16[4,1792]{1,0:T(4,128)(2,1)} %x.1) | copy-start | bytes 43012
  7.0 12.7 %slice-start = ((s8[14680064]{0:T(1024)(128)(4,1)}), s8[4194304]{0:T(1024)(128)(4,1)S(1)}, s32[]{:S(2)}) async-start(s8[14680064]{0:T(1024)(128)(4,1)} %bitcast.1), calls=%async_computation | async-start | bytes 8388608
  7.0 12.6 %slice-start.1 = ((s8[14680064]{0:T(1024)(128)(4,1)}), s8[4194304]{0:T(1024)(128)(4,1)S(1)}, s32[]{:S(2)}) async-start(s8[14680064]{0:T(1024)(128)(4,1)} %bitcast.1), calls=%async_computation.1 | async-start | bytes 8388608
  7.0 12.6 %copy-start.1 = (f32[8192]{0:T(1024)S(1)}, f32[8192]{0:T(1024)}, u32[]{:S(2)}) copy-start(f32[8192]{0:T(1024)} %param.8) | copy-start | bytes 98308
  7.0 5.7 %collective-permute-start.5 = (bf16[16,896]{1,0:T(8,128)(2,1)S(1)}, bf16[16,896]{1,0:T(8,128)(2,1)S(1)}, u32[]{:S(2)}, u32[]{:S(2)}) collective-permute-start(bf16[16,896]{1,0:T(8,128)(2,1)S(1)} %shard_map.65.refs_0_.rows), channel_id=1, source_target_pairs={{0,12},{2,14},{4,8},{6,10},{8,4},{10,6},{12,0},{14,2},{1,13},{3,15... | collective-permute-start | bytes 86024 | tf_op jit(solution)/shard_map/ppermute | solution.py:18
  10.7 4.8 %collective-permute-start.4 = (bf16[16,896]{1,0:T(8,128)(2,1)S(1)}, bf16[16,896]{1,0:T(8,128)(2,1)S(1)}, u32[]{:S(2)}, u32[]{:S(2)}) collective-permute-start(bf16[16,896]{1,0:T(8,128)(2,1)S(1)} %shard_map.65.refs_0_.rows), channel_id=1, source_target_pairs={{0,8},{2,10},{4,12},{6,14},{8,0},{10,2},{12,4},{14,6},{1,9},{3,11}... | collective-permute-start | bytes 86024 | tf_op jit(solution)/shard_map/ppermute | solution.py:18
  10.7 4.8 %collective-permute-start.3 = (bf16[16,896]{1,0:T(8,128)(2,1)S(1)}, bf16[16,896]{1,0:T(8,128)(2,1)S(1)}, u32[]{:S(2)}, u32[]{:S(2)}) collective-permute-start(bf16[16,896]{1,0:T(8,128)(2,1)S(1)} %shard_map.65.refs_0_.rows), channel_id=1, source_target_pairs={{0,4},{2,6},{4,0},{6,2},{8,12},{10,14},{12,8},{14,10},{1,5},{3,7},... | collective-permute-start | bytes 86024 | tf_op jit(solution)/shard_map/ppermute | solution.py:18
  16.9 2.8 %slice-start.2 = ((s8[14680064]{0:T(1024)(128)(4,1)}), s8[4194304]{0:T(1024)(128)(4,1)S(1)}, s32[]{:S(2)}) async-start(s8[14680064]{0:T(1024)(128)(4,1)} %bitcast.1), calls=%async_computation.2 | async-start | bytes 8388608
  16.9 2.9 %slice-start.3 = ((s8[14680064]{0:T(1024)(128)(4,1)}), s8[2097152]{0:T(1024)(128)(4,1)S(1)}, s32[]{:S(2)}) async-start(s8[14680064]{0:T(1024)(128)(4,1)} %bitcast.1), calls=%async_computation.3 | async-start | bytes 4194304
  16.9 2.7 %collective-permute-start.6 = (f32[64,4096]{1,0:T(8,128)S(1)}, f32[64,4096]{1,0:T(8,128)S(1)}, u32[]{:S(2)}, u32[]{:S(2)}) collective-permute-start(f32[64,4096]{1,0:T(8,128)S(1)} %shard_map.66.mine), channel_id=1, source_target_pairs={{0,1},{1,0},{2,3},{3,2},{4,5},{5,4},{6,7},{7,6},{8,9},{9,8},{10,11... | collective-permute-start | bytes 3145736 | tf_op jit(solution)/shard_map/ppermute | solution.py:18
  18.4 2.8 %collective-permute-start.7 = (f32[64,4096]{1,0:T(8,128)S(1)}, f32[64,4096]{1,0:T(8,128)S(1)}, u32[]{:S(2)}, u32[]{:S(2)}) collective-permute-start(f32[64,4096]{1,0:T(8,128)S(1)} %shard_map.68.mine), channel_id=1, source_target_pairs={{0,1},{1,0},{2,3},{3,2},{4,5},{5,4},{6,7},{7,6},{8,9},{9,8},{10,11... | collective-permute-start | bytes 3145736 | tf_op jit(solution)/shard_map/ppermute | solution.py:18
  21.3 20.6 %slice-start.4 = ((s8[14680064]{0:T(1024)(128)(4,1)}), s8[4194304]{0:T(1024)(128)(4,1)S(1)}, s32[]{:S(2)}) async-start(s8[14680064]{0:T(1024)(128)(4,1)} %bitcast.3), calls=%async_computation.4 | async-start | bytes 8388608
  21.3 20.6 %slice-start.5 = ((s8[14680064]{0:T(1024)(128)(4,1)}), s8[4194304]{0:T(1024)(128)(4,1)S(1)}, s32[]{:S(2)}) async-start(s8[14680064]{0:T(1024)(128)(4,1)} %bitcast.3), calls=%async_computation.5 | async-start | bytes 8388608
  21.3 20.6 %slice-start.8 = ((s8[14680064]{0:T(1024)(128)(4,1)}), s8[4194304]{0:T(1024)(128)(4,1)S(1)}, s32[]{:S(2)}) async-start(s8[14680064]{0:T(1024)(128)(4,1)} %bitcast.5), calls=%async_computation.8 | async-start | bytes 8388608
  21.3 20.6 %slice-start.9 = ((s8[14680064]{0:T(1024)(128)(4,1)}), s8[4194304]{0:T(1024)(128)(4,1)S(1)}, s32[]{:S(2)}) async-start(s8[14680064]{0:T(1024)(128)(4,1)} %bitcast.5), calls=%async_computation.9 | async-start | bytes 8388608
  22.6 4.5 %collective-permute-start.8 = (bf16[16,896]{1,0:T(8,128)(2,1)S(1)}, bf16[16,896]{1,0:T(8,128)(2,1)S(1)}, u32[]{:S(2)}, u32[]{:S(2)}) collective-permute-start(bf16[16,896]{1,0:T(8,128)(2,1)S(1)} %get-tuple-element.16), channel_id=1, source_target_pairs={{0,4},{2,6},{4,0},{6,2},{8,12},{10,14},{12,8},{14,10},{1,5},{3,7},... | collective-permute-start | bytes 86024 | tf_op jit(solution)/shard_map/ppermute | solution.py:18
  22.7 4.9 %collective-permute-start.9 = (bf16[16,896]{1,0:T(8,128)(2,1)S(1)}, bf16[16,896]{1,0:T(8,128)(2,1)S(1)}, u32[]{:S(2)}, u32[]{:S(2)}) collective-permute-start(bf16[16,896]{1,0:T(8,128)(2,1)S(1)} %get-tuple-element.17), channel_id=1, source_target_pairs={{0,8},{2,10},{4,12},{6,14},{8,0},{10,2},{12,4},{14,6},{1,9},{3,11}... | collective-permute-start | bytes 86024 | tf_op jit(solution)/shard_map/ppermute | solution.py:18
  24.8 5.7 %collective-permute-start.10 = (bf16[16,896]{1,0:T(8,128)(2,1)S(1)}, bf16[16,896]{1,0:T(8,128)(2,1)S(1)}, u32[]{:S(2)}, u32[]{:S(2)}) collective-permute-start(bf16[16,896]{1,0:T(8,128)(2,1)S(1)} %get-tuple-element.18), channel_id=1, source_target_pairs={{0,12},{2,14},{4,8},{6,10},{8,4},{10,6},{12,0},{14,2},{1,13},{3,15... | collective-permute-start | bytes 86024 | tf_op jit(solution)/shard_map/ppermute | solution.py:18
  30.5 11.5 %slice-start.6 = ((s8[14680064]{0:T(1024)(128)(4,1)}), s8[4194304]{0:T(1024)(128)(4,1)S(1)}, s32[]{:S(2)}) async-start(s8[14680064]{0:T(1024)(128)(4,1)} %bitcast.3), calls=%async_computation.6 | async-start | bytes 8388608
  30.5 11.5 %slice-start.10 = ((s8[14680064]{0:T(1024)(128)(4,1)}), s8[4194304]{0:T(1024)(128)(4,1)S(1)}, s32[]{:S(2)}) async-start(s8[14680064]{0:T(1024)(128)(4,1)} %bitcast.5), calls=%async_computation.10 | async-start | bytes 8388608
  30.5 11.5 %slice-start.7 = ((s8[14680064]{0:T(1024)(128)(4,1)}), s8[2097152]{0:T(1024)(128)(4,1)S(1)}, s32[]{:S(2)}) async-start(s8[14680064]{0:T(1024)(128)(4,1)} %bitcast.3), calls=%async_computation.7 | async-start | bytes 4194304
  30.5 11.5 %slice-start.11 = ((s8[14680064]{0:T(1024)(128)(4,1)}), s8[2097152]{0:T(1024)(128)(4,1)S(1)}, s32[]{:S(2)}) async-start(s8[14680064]{0:T(1024)(128)(4,1)} %bitcast.5), calls=%async_computation.11 | async-start | bytes 4194304
  30.5 4.2 %collective-permute-start.11 = (f32[16,896]{1,0:T(8,128)S(1)}, f32[16,896]{1,0:T(8,128)S(1)}, u32[]{:S(2)}, u32[]{:S(2)}) collective-permute-start(f32[16,896]{1,0:T(8,128)S(1)} %shard_map.71.total), channel_id=1, source_target_pairs={{0,2},{2,0},{4,6},{6,4},{8,10},{10,8},{12,14},{14,12},{1,3},{3,1},... | collective-permute-start | bytes 172040 | tf_op jit(solution)/shard_map/ppermute | solution.py:18
  34.8 6.1 %collective-permute-start.14 = (bf16[16,896]{1,0:T(8,128)(2,1)S(1)}, bf16[16,896]{1,0:T(8,128)(2,1)S(1)}, u32[]{:S(2)}, u32[]{:S(2)}) collective-permute-start(bf16[16,896]{1,0:T(8,128)(2,1)S(1)} %shard_map.72.refs_0_), channel_id=1, source_target_pairs={{0,12},{2,14},{4,8},{6,10},{8,4},{10,6},{12,0},{14,2},{1,13},{3,15... | collective-permute-start | bytes 86024 | tf_op jit(solution)/shard_map/ppermute | solution.py:18
  37.1 4.8 %collective-permute-start.13 = (bf16[16,896]{1,0:T(8,128)(2,1)S(1)}, bf16[16,896]{1,0:T(8,128)(2,1)S(1)}, u32[]{:S(2)}, u32[]{:S(2)}) collective-permute-start(bf16[16,896]{1,0:T(8,128)(2,1)S(1)} %shard_map.72.refs_0_), channel_id=1, source_target_pairs={{0,8},{2,10},{4,12},{6,14},{8,0},{10,2},{12,4},{14,6},{1,9},{3,11}... | collective-permute-start | bytes 86024 | tf_op jit(solution)/shard_map/ppermute | solution.py:18
  37.1 4.8 %collective-permute-start.12 = (bf16[16,896]{1,0:T(8,128)(2,1)S(1)}, bf16[16,896]{1,0:T(8,128)(2,1)S(1)}, u32[]{:S(2)}, u32[]{:S(2)}) collective-permute-start(bf16[16,896]{1,0:T(8,128)(2,1)S(1)} %shard_map.72.refs_0_), channel_id=1, source_target_pairs={{0,4},{2,6},{4,0},{6,2},{8,12},{10,14},{12,8},{14,10},{1,5},{3,7},... | collective-permute-start | bytes 86024 | tf_op jit(solution)/shard_map/ppermute | solution.py:18

commit v11 on v8

--- a/solution.py
+++ b/solution.py
@@ -217,10 +217,11 @@
     products = (even, odd)
     tokens = codes_t.shape[1]
     b = 0.1 / (1.0 - 0.9**10) / tokens
-    a = 0.9 / (1.0 - 0.9**10) / b
-    p = 0.999 / (1.0 - 0.999**10) / b**2
-    q = 0.001 / (1.0 - 0.999**10) / tokens**2 / b**2
-    a, p, q, eps = (jnp.asarray(x, out.dtype) for x in (a, p, q, 1e-8 / b))
+    a = 0.9 / 0.1 * tokens
+    p = 0.999 / 0.001 * tokens**2
+    scale = b / (0.001 / (1.0 - 0.999**10) / tokens**2) ** 0.5
+    eps = 1e-8 / b * scale**2
+    a, p, scale, eps = (jnp.asarray(x, out.dtype) for x in (a, p, scale, eps))
     i, last = pl.program_id(0), pl.num_programs(0) - 1
     rows = out.shape[0]
     part = even.shape[0]
@@ -245,9 +246,9 @@
             at = pl.ds(pl.multiple_of(i * rows + k * part + r, slab), slab)
             c = products[k][r : r + slab, :]
             first = m[at, :] * a + c
-            second = v[at, :] * p + (c * c) * q
-            root = second * lax.rsqrt(second)
-            step = first * pl.reciprocal(root + eps, approx=True)
+            second = v[at, :] * p + c * c
+            inverse = lax.rsqrt(second)
+            step = first * (inverse * (scale - inverse * eps))
             out[k * part + r : k * part + r + slab, :] = step
 
 

time: 54.6 us -> 53 us (0.971)
  Pallas kernels: 19.5 us -> 17.9 us
    pallas_call x1, Pallas kernels: 12.4 us -> 10.8 us  [adam(): pl.pallas_call(adam_kernel, grid=(lat // rows,), out_shape=jax.ShapeDtype...]
where the time goes in v11:
time: 53 us; the launch traced here: 52.8 us
  Pallas kernels  17.9 us (34%)
  starting transfers between devices  17.7 us (33%)
  waiting for transfers between devices  15.3 us (29%)
  local copies, waits for them, and re-layouts  1.63 us (3%)
    ppermute x15, starting transfers between devices, swap(): return lax.ppermute(value, axis, [(i, i ^ mask) for i in range(n)])  17.7 us
    ppermute x15, waiting for transfers between devices, swap(): return lax.ppermute(value, axis, [(i, i ^ mask) for i in range(n)])  15.3 us
    pallas_call x1, Pallas kernels, adam(): pl.pallas_call(adam_kernel, grid=(lat // rows,), out_shape=jax.ShapeDtype...  10.8 us
    pallas_call x2, Pallas kernels, encode(): pl.pallas_call(functools.partial(encode_kernel, first), out_shape=jax.Sha...  2.84 us
    pallas_call x2, Pallas kernels, decode(): pl.pallas_call(functools.partial(decode_kernel, first, len(given)), out_s...  2.58 us
    pallas_call x1, Pallas kernels, turn(): pl.pallas_call(functools.partial(turn_kernel, min(512, lat)), out_shape=j...  1.68 us
    unnamed x30, local copies, waits for them, and re-layouts  1.63 us
  transfers between devices with their start and end apart: 15, of which 10 were waited for; matrix products, arithmetic and copies ran while one was open for 0% of the time, Pallas kernels for 8%

profile of v11, /device:TPU:0, one launch (start us, length us, event | category | flops | bytes accessed | tf_op | source)
XLA Modules:
  0.0 52.8 jit_solution(14110249482354094264)
XLA Ops:
  0.0 0.5 collective-permute-start
  0.5 2.6 %collective-permute-start.2 = (bf16[4,1792]{1,0:T(4,128)(2,1)}, bf16[4,1792]{1,0:T(4,128)(2,1)S(1)}, u32[]{:S(2)}, u32[]{:S(2)}) collective-permute-start(bf16[4,1792]{1,0:T(4,128)(2,1)} %x.1), channel_id=1, source_target_pairs={{0,3},{1,2},{2,1},{3,0},{4,7},{5,6},{6,5},{7,4},{8,11},{9,10},{10,... | collective-permute-start | bytes 43016 | tf_op jit(solution)/shard_map/ppermute | solution.py:18
  3.1 0.1 collective-permute-start.1
  3.1 1.5 %copy-done.2 = bf16[4,1792]{1,0:T(4,128)(2,1)S(1)} copy-done((bf16[4,1792]{1,0:T(4,128)(2,1)S(1)}, bf16[4,1792]{1,0:T(4,128)(2,1)}, u32[]{:S(2)}) %copy-start.2) | copy-done | bytes 14360
  4.6 0.1 collective-permute-done.2.refs_3_
  4.7 2.3 %collective-permute-done.1.refs_2_ = bf16[4,1792]{1,0:T(4,128)(2,1)S(1)} collective-permute-done((bf16[4,1792]{1,0:T(4,128)(2,1)}, bf16[4,1792]{1,0:T(4,128)(2,1)S(1)}, u32[]{:S(2)}, u32[]{:S(2)}) %collective-permute-start.1) | collective-permute-done | bytes 14368 | tf_op jit(solution)/shard_map/ppermute | solution.py:18
  7.0 3.7 %collective-permute-start.5 = (bf16[16,896]{1,0:T(8,128)(2,1)S(1)}, bf16[16,896]{1,0:T(8,128)(2,1)S(1)}, u32[]{:S(2)}, u32[]{:S(2)}) collective-permute-start(bf16[16,896]{1,0:T(8,128)(2,1)S(1)} %shard_map.65.refs_0_.rows), channel_id=1, source_target_pairs={{0,12},{2,14},{4,8},{6,10},{8,4},{10,6},{12,0},{14,2},{1,13},{3,15... | collective-permute-start | bytes 86024 | tf_op jit(solution)/shard_map/ppermute | solution.py:18
  10.7 0.8 %collective-permute-start.3 = (bf16[16,896]{1,0:T(8,128)(2,1)S(1)}, bf16[16,896]{1,0:T(8,128)(2,1)S(1)}, u32[]{:S(2)}, u32[]{:S(2)}) collective-permute-start(bf16[16,896]{1,0:T(8,128)(2,1)S(1)} %shard_map.65.refs_0_.rows), channel_id=1, source_target_pairs={{0,4},{2,6},{4,0},{6,2},{8,12},{10,14},{12,8},{14,10},{1,5},{3,7},... | collective-permute-start | bytes 86024 | tf_op jit(solution)/shard_map/ppermute | solution.py:18
  11.5 1.3 %collective-permute-done.5.refs_3_ = bf16[16,896]{1,0:T(8,128)(2,1)S(1)} collective-permute-done((bf16[16,896]{1,0:T(8,128)(2,1)S(1)}, bf16[16,896]{1,0:T(8,128)(2,1)S(1)}, u32[]{:S(2)}, u32[]{:S(2)}) %collective-permute-start.5) | collective-permute-done | bytes 28704 | tf_op jit(solution)/shard_map/ppermute | solution.py:18
  12.8 2.7 %collective-permute-done.4.refs_2_ = bf16[16,896]{1,0:T(8,128)(2,1)S(1)} collective-permute-done((bf16[16,896]{1,0:T(8,128)(2,1)S(1)}, bf16[16,896]{1,0:T(8,128)(2,1)S(1)}, u32[]{:S(2)}, u32[]{:S(2)}) %collective-permute-start.4) | collective-permute-done | bytes 28704 | tf_op jit(solution)/shard_map/ppermute | solution.py:18
  15.5 1.4 %shard_map.66.mine = f32[64,4096]{1,0:T(8,128)S(1)} custom-call(bf16[16,896]{1,0:T(8,128)(2,1)S(1)} %shard_map.65.refs_0_.rows, bf16[16,896]{1,0:T(8,128)(2,1)S(1)} %collective-permute-done.3.refs_1_, bf16[16,896]{1,0:T(8,128)(2,1)S(1)} %collective-permute-done.4.refs_2_, bf16[16,896]{1,0:T(8,128)(2,1)S(1)} %collective-permute-done.5.refs_3_, ...), custom_call_target="tpu_custom_call" | custom-call | flops 2449999872 | bytes 7340032 | tf_op jit(solution)/shard_map/pallas_call | solution.py:102
  16.9 0.1 collective-permute-start.6
  17.0 1.4 %shard_map.68.mine = f32[64,4096]{1,0:T(8,128)S(1)} custom-call(bf16[16,896]{1,0:T(8,128)(2,1)S(1)} %shard_map.65.refs_0_.rows, bf16[16,896]{1,0:T(8,128)(2,1)S(1)} %collective-permute-done.3.refs_1_, bf16[16,896]{1,0:T(8,128)(2,1)S(1)} %collective-permute-done.4.refs_2_, bf16[16,896]{1,0:T(8,128)(2,1)S(1)} %collective-permute-done.5.refs_3_, ...), custom_call_target="tpu_custom_call" | custom-call | flops 2449999872 | bytes 7340032 | tf_op jit(solution)/shard_map/pallas_call | solution.py:102
  18.4 0.6 %collective-permute-start.7 = (f32[64,4096]{1,0:T(8,128)S(1)}, f32[64,4096]{1,0:T(8,128)S(1)}, u32[]{:S(2)}, u32[]{:S(2)}) collective-permute-start(f32[64,4096]{1,0:T(8,128)S(1)} %shard_map.68.mine), channel_id=1, source_target_pairs={{0,1},{1,0},{2,3},{3,2},{4,5},{5,4},{6,7},{7,6},{8,9},{9,8},{10,11... | collective-permute-start | bytes 3145736 | tf_op jit(solution)/shard_map/ppermute | solution.py:18
  19.0 0.7 %collective-permute-done.6.theirs = f32[64,4096]{1,0:T(8,128)S(1)} collective-permute-done((f32[64,4096]{1,0:T(8,128)S(1)}, f32[64,4096]{1,0:T(8,128)S(1)}, u32[]{:S(2)}, u32[]{:S(2)}) %collective-permute-start.6) | collective-permute-done | bytes 1048608 | tf_op jit(solution)/shard_map/ppermute | solution.py:18
  19.7 0.1 slice-done.3
  19.8 1.3 %shard_map.67 = (bf16[64,4096]{1,0:T(8,128)(2,1)S(1)}, f32[64,896]{1,0:T(8,128)S(1)}) custom-call(f32[64,4096]{1,0:T(8,128)S(1)} %shard_map.66.mine, f32[64,4096]{1,0:T(8,128)S(1)} %collective-permute-done.6.theirs, f32[1,8192]{1,0:T(1,128)S(1)} %bitcast.7, bf16[8192,896]{1,0:T(8,128)(2,1)S(1)} %bitcast.2), custom_call_target="tpu_custom_call" | custom-call | flops 2449999872 | bytes 7340032 | tf_op jit(solution)/shard_map/pallas_call | solution.py:133
  21.1 0.2 collective-permute-done.7.theirs
  21.3 1.3 %shard_map.69 = (bf16[64,4096]{1,0:T(8,128)(2,1)S(1)}, f32[16,896]{1,0:T(8,128)S(1)}, bf16[16,896]{1,0:T(8,128)(2,1)S(1)}, bf16[16,896]{1,0:T(8,128)(2,1)S(1)}, bf16[16,896]{1,0:T(8,128)(2,1)S(1)}) custom-call(f32[64,4096]{1,0:T(8,128)S(1)} %shard_map.68.mine, f32[64,4096]{1,0:T(8,128)S(1)} %collective-permute-done.7.theirs, f32[1,8192]{1,0:T(1,128)S(1)} %bitcast.8, ...), custom_call_target="tpu_custom_call" | custom-call | flops 2449999872 | bytes 7340032 | tf_op jit(solution)/shard_map/pallas_call | solution.py:133
  22.6 0.1 collective-permute-start.8
  22.7 2.1 %collective-permute-start.9 = (bf16[16,896]{1,0:T(8,128)(2,1)S(1)}, bf16[16,896]{1,0:T(8,128)(2,1)S(1)}, u32[]{:S(2)}, u32[]{:S(2)}) collective-permute-start(bf16[16,896]{1,0:T(8,128)(2,1)S(1)} %get-tuple-element.17), channel_id=1, source_target_pairs={{0,8},{2,10},{4,12},{6,14},{8,0},{10,2},{12,4},{14,6},{1,9},{3,11}... | collective-permute-start | bytes 86024 | tf_op jit(solution)/shard_map/ppermute | solution.py:18
  24.8 2.3 %collective-permute-start.10 = (bf16[16,896]{1,0:T(8,128)(2,1)S(1)}, bf16[16,896]{1,0:T(8,128)(2,1)S(1)}, u32[]{:S(2)}, u32[]{:S(2)}) collective-permute-start(bf16[16,896]{1,0:T(8,128)(2,1)S(1)} %get-tuple-element.18), channel_id=1, source_target_pairs={{0,12},{2,14},{4,8},{6,10},{8,4},{10,6},{12,0},{14,2},{1,13},{3,15... | collective-permute-start | bytes 86024 | tf_op jit(solution)/shard_map/ppermute | solution.py:18
  27.1 0.5 collective-permute-done.9.refs_1_
  27.5 2.9 %collective-permute-done.10.refs_2_ = bf16[16,896]{1,0:T(8,128)(2,1)S(1)} collective-permute-done((bf16[16,896]{1,0:T(8,128)(2,1)S(1)}, bf16[16,896]{1,0:T(8,128)(2,1)S(1)}, u32[]{:S(2)}, u32[]{:S(2)}) %collective-permute-start.10) | collective-permute-done | bytes 28704 | tf_op jit(solution)/shard_map/ppermute | solution.py:18
  30.5 0.0 slice-start.11
  30.5 0.6 %collective-permute-start.11 = (f32[16,896]{1,0:T(8,128)S(1)}, f32[16,896]{1,0:T(8,128)S(1)}, u32[]{:S(2)}, u32[]{:S(2)}) collective-permute-start(f32[16,896]{1,0:T(8,128)S(1)} %shard_map.71.total), channel_id=1, source_target_pairs={{0,2},{2,0},{4,6},{6,4},{8,10},{10,8},{12,14},{14,12},{1,3},{3,1},... | collective-permute-start | bytes 172040 | tf_op jit(solution)/shard_map/ppermute | solution.py:18
  31.1 3.6 %collective-permute-done.11.refs_0_ = f32[16,896]{1,0:T(8,128)S(1)} collective-permute-done((f32[16,896]{1,0:T(8,128)S(1)}, f32[16,896]{1,0:T(8,128)S(1)}, u32[]{:S(2)}, u32[]{:S(2)}) %collective-permute-start.11) | collective-permute-done | bytes 57376 | tf_op jit(solution)/shard_map/ppermute | solution.py:18
  34.8 2.3 %collective-permute-start.14 = (bf16[16,896]{1,0:T(8,128)(2,1)S(1)}, bf16[16,896]{1,0:T(8,128)(2,1)S(1)}, u32[]{:S(2)}, u32[]{:S(2)}) collective-permute-start(bf16[16,896]{1,0:T(8,128)(2,1)S(1)} %shard_map.72.refs_0_), channel_id=1, source_target_pairs={{0,12},{2,14},{4,8},{6,10},{8,4},{10,6},{12,0},{14,2},{1,13},{3,15... | collective-permute-start | bytes 86024 | tf_op jit(solution)/shard_map/ppermute | solution.py:18
  37.1 2.1 %collective-permute-start.12 = (bf16[16,896]{1,0:T(8,128)(2,1)S(1)}, bf16[16,896]{1,0:T(8,128)(2,1)S(1)}, u32[]{:S(2)}, u32[]{:S(2)}) collective-permute-start(bf16[16,896]{1,0:T(8,128)(2,1)S(1)} %shard_map.72.refs_0_), channel_id=1, source_target_pairs={{0,4},{2,6},{4,0},{6,2},{8,12},{10,14},{12,8},{14,10},{1,5},{3,7},... | collective-permute-start | bytes 86024 | tf_op jit(solution)/shard_map/ppermute | solution.py:18
  39.2 1.7 %shard_map.70.codes_t = bf16[8192,64]{1,0:T(8,128)(2,1)S(1)} custom-call(bf16[64,4096]{1,0:T(8,128)(2,1)S(1)} %get-tuple-element.12.refs_0_, bf16[64,4096]{1,0:T(8,128)(2,1)S(1)} %get-tuple-element.14.refs_1_), custom_call_target="tpu_custom_call" | custom-call | flops 1400000000 | bytes 4194304 | tf_op jit(solution)/shard_map/pallas_call | solution.py:158
  40.9 1.0 %collective-permute-done.13.refs_2_ = bf16[16,896]{1,0:T(8,128)(2,1)S(1)} collective-permute-done((bf16[16,896]{1,0:T(8,128)(2,1)S(1)}, bf16[16,896]{1,0:T(8,128)(2,1)S(1)}, u32[]{:S(2)}, u32[]{:S(2)}) %collective-permute-start.13) | collective-permute-done | bytes 28704 | tf_op jit(solution)/shard_map/ppermute | solution.py:18
  42.0 10.8 %shard_map.73 = bf16[8192,896]{1,0:T(8,128)(2,1)} custom-call(bf16[8192,64]{1,0:T(8,128)(2,1)S(1)} %shard_map.70.codes_t, bf16[8192,896]{1,0:T(8,128)(2,1)S(1)} %bitcast.4, bf16[8192,896]{1,0:T(8,128)(2,1)S(1)} %bitcast.6, bf16[16,896]{1,0:T(8,128)(2,1)S(1)} %shard_map.72.refs_0_, bf16[16,896]{1,0:T(8,128)(2,1)S(1)} %collective-permute-done.12.refs_1_, ...), custom_call_target="tpu_custom_call" | custom-call | tf_op jit(solution)/shard_map/pallas_call | solution.py:258
  (41 shorter events, 0.1 us)
Async XLA Ops:
  0.0 15.5 %copy-start = (bf16[896,8192]{1,0:T(8,128)(2,1)S(1)}, bf16[896,8192]{1,0:T(8,128)(2,1)}, u32[]{:S(2)}) copy-start(bf16[896,8192]{1,0:T(8,128)(2,1)} %refs_4_.3) | copy-start | bytes 44040196
  0.0 4.6 %collective-permute-start = (bf16[4,1792]{1,0:T(4,128)(2,1)}, bf16[4,1792]{1,0:T(4,128)(2,1)S(1)}, u32[]{:S(2)}, u32[]{:S(2)}) collective-permute-start(bf16[4,1792]{1,0:T(4,128)(2,1)} %x.1), channel_id=1, source_target_pairs={{0,1},{1,0},{2,3},{3,2},{4,5},{5,4},{6,7},{7,6},{8,9},{9,8},{10,11... | collective-permute-start | bytes 43016 | tf_op jit(solution)/shard_map/ppermute | solution.py:18
  0.5 4.2 %collective-permute-start.2 = (bf16[4,1792]{1,0:T(4,128)(2,1)}, bf16[4,1792]{1,0:T(4,128)(2,1)S(1)}, u32[]{:S(2)}, u32[]{:S(2)}) collective-permute-start(bf16[4,1792]{1,0:T(4,128)(2,1)} %x.1), channel_id=1, source_target_pairs={{0,3},{1,2},{2,1},{3,0},{4,7},{5,6},{6,5},{7,4},{8,11},{9,10},{10,... | collective-permute-start | bytes 43016 | tf_op jit(solution)/shard_map/ppermute | solution.py:18
  3.1 3.9 %collective-permute-start.1 = (bf16[4,1792]{1,0:T(4,128)(2,1)}, bf16[4,1792]{1,0:T(4,128)(2,1)S(1)}, u32[]{:S(2)}, u32[]{:S(2)}) collective-permute-start(bf16[4,1792]{1,0:T(4,128)(2,1)} %x.1), channel_id=1, source_target_pairs={{0,2},{1,3},{2,0},{3,1},{4,6},{5,7},{6,4},{7,5},{8,10},{9,11},{10,... | collective-permute-start | bytes 43016 | tf_op jit(solution)/shard_map/ppermute | solution.py:18
  3.1 1.5 %copy-start.2 = (bf16[4,1792]{1,0:T(4,128)(2,1)S(1)}, bf16[4,1792]{1,0:T(4,128)(2,1)}, u32[]{:S(2)}) copy-start(bf16[4,1792]{1,0:T(4,128)(2,1)} %x.1) | copy-start | bytes 43012
  7.0 12.7 %slice-start = ((s8[14680064]{0:T(1024)(128)(4,1)}), s8[4194304]{0:T(1024)(128)(4,1)S(1)}, s32[]{:S(2)}) async-start(s8[14680064]{0:T(1024)(128)(4,1)} %bitcast.1), calls=%async_computation | async-start | bytes 8388608
  7.0 12.6 %slice-start.1 = ((s8[14680064]{0:T(1024)(128)(4,1)}), s8[4194304]{0:T(1024)(128)(4,1)S(1)}, s32[]{:S(2)}) async-start(s8[14680064]{0:T(1024)(128)(4,1)} %bitcast.1), calls=%async_computation.1 | async-start | bytes 8388608
  7.0 12.6 %copy-start.1 = (f32[8192]{0:T(1024)S(1)}, f32[8192]{0:T(1024)}, u32[]{:S(2)}) copy-start(f32[8192]{0:T(1024)} %param.8) | copy-start | bytes 98308
  7.0 5.7 %collective-permute-start.5 = (bf16[16,896]{1,0:T(8,128)(2,1)S(1)}, bf16[16,896]{1,0:T(8,128)(2,1)S(1)}, u32[]{:S(2)}, u32[]{:S(2)}) collective-permute-start(bf16[16,896]{1,0:T(8,128)(2,1)S(1)} %shard_map.65.refs_0_.rows), channel_id=1, source_target_pairs={{0,12},{2,14},{4,8},{6,10},{8,4},{10,6},{12,0},{14,2},{1,13},{3,15... | collective-permute-start | bytes 86024 | tf_op jit(solution)/shard_map/ppermute | solution.py:18
  10.7 4.8 %collective-permute-start.4 = (bf16[16,896]{1,0:T(8,128)(2,1)S(1)}, bf16[16,896]{1,0:T(8,128)(2,1)S(1)}, u32[]{:S(2)}, u32[]{:S(2)}) collective-permute-start(bf16[16,896]{1,0:T(8,128)(2,1)S(1)} %shard_map.65.refs_0_.rows), channel_id=1, source_target_pairs={{0,8},{2,10},{4,12},{6,14},{8,0},{10,2},{12,4},{14,6},{1,9},{3,11}... | collective-permute-start | bytes 86024 | tf_op jit(solution)/shard_map/ppermute | solution.py:18
  10.7 4.8 %collective-permute-start.3 = (bf16[16,896]{1,0:T(8,128)(2,1)S(1)}, bf16[16,896]{1,0:T(8,128)(2,1)S(1)}, u32[]{:S(2)}, u32[]{:S(2)}) collective-permute-start(bf16[16,896]{1,0:T(8,128)(2,1)S(1)} %shard_map.65.refs_0_.rows), channel_id=1, source_target_pairs={{0,4},{2,6},{4,0},{6,2},{8,12},{10,14},{12,8},{14,10},{1,5},{3,7},... | collective-permute-start | bytes 86024 | tf_op jit(solution)/shard_map/ppermute | solution.py:18
  16.9 2.8 %slice-start.2 = ((s8[14680064]{0:T(1024)(128)(4,1)}), s8[4194304]{0:T(1024)(128)(4,1)S(1)}, s32[]{:S(2)}) async-start(s8[14680064]{0:T(1024)(128)(4,1)} %bitcast.1), calls=%async_computation.2 | async-start | bytes 8388608
  16.9 2.9 %slice-start.3 = ((s8[14680064]{0:T(1024)(128)(4,1)}), s8[2097152]{0:T(1024)(128)(4,1)S(1)}, s32[]{:S(2)}) async-start(s8[14680064]{0:T(1024)(128)(4,1)} %bitcast.1), calls=%async_computation.3 | async-start | bytes 4194304
  16.9 2.7 %collective-permute-start.6 = (f32[64,4096]{1,0:T(8,128)S(1)}, f32[64,4096]{1,0:T(8,128)S(1)}, u32[]{:S(2)}, u32[]{:S(2)}) collective-permute-start(f32[64,4096]{1,0:T(8,128)S(1)} %shard_map.66.mine), channel_id=1, source_target_pairs={{0,1},{1,0},{2,3},{3,2},{4,5},{5,4},{6,7},{7,6},{8,9},{9,8},{10,11... | collective-permute-start | bytes 3145736 | tf_op jit(solution)/shard_map/ppermute | solution.py:18
  18.4 2.8 %collective-permute-start.7 = (f32[64,4096]{1,0:T(8,128)S(1)}, f32[64,4096]{1,0:T(8,128)S(1)}, u32[]{:S(2)}, u32[]{:S(2)}) collective-permute-start(f32[64,4096]{1,0:T(8,128)S(1)} %shard_map.68.mine), channel_id=1, source_target_pairs={{0,1},{1,0},{2,3},{3,2},{4,5},{5,4},{6,7},{7,6},{8,9},{9,8},{10,11... | collective-permute-start | bytes 3145736 | tf_op jit(solution)/shard_map/ppermute | solution.py:18
  21.3 20.6 %slice-start.4 = ((s8[14680064]{0:T(1024)(128)(4,1)}), s8[4194304]{0:T(1024)(128)(4,1)S(1)}, s32[]{:S(2)}) async-start(s8[14680064]{0:T(1024)(128)(4,1)} %bitcast.3), calls=%async_computation.4 | async-start | bytes 8388608
  21.3 20.6 %slice-start.5 = ((s8[14680064]{0:T(1024)(128)(4,1)}), s8[4194304]{0:T(1024)(128)(4,1)S(1)}, s32[]{:S(2)}) async-start(s8[14680064]{0:T(1024)(128)(4,1)} %bitcast.3), calls=%async_computation.5 | async-start | bytes 8388608
  21.3 20.6 %slice-start.8 = ((s8[14680064]{0:T(1024)(128)(4,1)}), s8[4194304]{0:T(1024)(128)(4,1)S(1)}, s32[]{:S(2)}) async-start(s8[14680064]{0:T(1024)(128)(4,1)} %bitcast.5), calls=%async_computation.8 | async-start | bytes 8388608
  21.3 20.6 %slice-start.9 = ((s8[14680064]{0:T(1024)(128)(4,1)}), s8[4194304]{0:T(1024)(128)(4,1)S(1)}, s32[]{:S(2)}) async-start(s8[14680064]{0:T(1024)(128)(4,1)} %bitcast.5), calls=%async_computation.9 | async-start | bytes 8388608
  22.6 4.5 %collective-permute-start.8 = (bf16[16,896]{1,0:T(8,128)(2,1)S(1)}, bf16[16,896]{1,0:T(8,128)(2,1)S(1)}, u32[]{:S(2)}, u32[]{:S(2)}) collective-permute-start(bf16[16,896]{1,0:T(8,128)(2,1)S(1)} %get-tuple-element.16), channel_id=1, source_target_pairs={{0,4},{2,6},{4,0},{6,2},{8,12},{10,14},{12,8},{14,10},{1,5},{3,7},... | collective-permute-start | bytes 86024 | tf_op jit(solution)/shard_map/ppermute | solution.py:18
  22.7 4.9 %collective-permute-start.9 = (bf16[16,896]{1,0:T(8,128)(2,1)S(1)}, bf16[16,896]{1,0:T(8,128)(2,1)S(1)}, u32[]{:S(2)}, u32[]{:S(2)}) collective-permute-start(bf16[16,896]{1,0:T(8,128)(2,1)S(1)} %get-tuple-element.17), channel_id=1, source_target_pairs={{0,8},{2,10},{4,12},{6,14},{8,0},{10,2},{12,4},{14,6},{1,9},{3,11}... | collective-permute-start | bytes 86024 | tf_op jit(solution)/shard_map/ppermute | solution.py:18
  24.8 5.7 %collective-permute-start.10 = (bf16[16,896]{1,0:T(8,128)(2,1)S(1)}, bf16[16,896]{1,0:T(8,128)(2,1)S(1)}, u32[]{:S(2)}, u32[]{:S(2)}) collective-permute-start(bf16[16,896]{1,0:T(8,128)(2,1)S(1)} %get-tuple-element.18), channel_id=1, source_target_pairs={{0,12},{2,14},{4,8},{6,10},{8,4},{10,6},{12,0},{14,2},{1,13},{3,15... | collective-permute-start | bytes 86024 | tf_op jit(solution)/shard_map/ppermute | solution.py:18
  30.5 11.5 %slice-start.6 = ((s8[14680064]{0:T(1024)(128)(4,1)}), s8[4194304]{0:T(1024)(128)(4,1)S(1)}, s32[]{:S(2)}) async-start(s8[14680064]{0:T(1024)(128)(4,1)} %bitcast.3), calls=%async_computation.6 | async-start | bytes 8388608
  30.5 11.5 %slice-start.10 = ((s8[14680064]{0:T(1024)(128)(4,1)}), s8[4194304]{0:T(1024)(128)(4,1)S(1)}, s32[]{:S(2)}) async-start(s8[14680064]{0:T(1024)(128)(4,1)} %bitcast.5), calls=%async_computation.10 | async-start | bytes 8388608
  30.5 11.5 %slice-start.7 = ((s8[14680064]{0:T(1024)(128)(4,1)}), s8[2097152]{0:T(1024)(128)(4,1)S(1)}, s32[]{:S(2)}) async-start(s8[14680064]{0:T(1024)(128)(4,1)} %bitcast.3), calls=%async_computation.7 | async-start | bytes 4194304
  30.5 11.5 %slice-start.11 = ((s8[14680064]{0:T(1024)(128)(4,1)}), s8[2097152]{0:T(1024)(128)(4,1)S(1)}, s32[]{:S(2)}) async-start(s8[14680064]{0:T(1024)(128)(4,1)} %bitcast.5), calls=%async_computation.11 | async-start | bytes 4194304
  30.5 4.2 %collective-permute-start.11 = (f32[16,896]{1,0:T(8,128)S(1)}, f32[16,896]{1,0:T(8,128)S(1)}, u32[]{:S(2)}, u32[]{:S(2)}) collective-permute-start(f32[16,896]{1,0:T(8,128)S(1)} %shard_map.71.total), channel_id=1, source_target_pairs={{0,2},{2,0},{4,6},{6,4},{8,10},{10,8},{12,14},{14,12},{1,3},{3,1},... | collective-permute-start | bytes 172040 | tf_op jit(solution)/shard_map/ppermute | solution.py:18
  34.8 6.1 %collective-permute-start.14 = (bf16[16,896]{1,0:T(8,128)(2,1)S(1)}, bf16[16,896]{1,0:T(8,128)(2,1)S(1)}, u32[]{:S(2)}, u32[]{:S(2)}) collective-permute-start(bf16[16,896]{1,0:T(8,128)(2,1)S(1)} %shard_map.72.refs_0_), channel_id=1, source_target_pairs={{0,12},{2,14},{4,8},{6,10},{8,4},{10,6},{12,0},{14,2},{1,13},{3,15... | collective-permute-start | bytes 86024 | tf_op jit(solution)/shard_map/ppermute | solution.py:18
  37.1 4.8 %collective-permute-start.13 = (bf16[16,896]{1,0:T(8,128)(2,1)S(1)}, bf16[16,896]{1,0:T(8,128)(2,1)S(1)}, u32[]{:S(2)}, u32[]{:S(2)}) collective-permute-start(bf16[16,896]{1,0:T(8,128)(2,1)S(1)} %shard_map.72.refs_0_), channel_id=1, source_target_pairs={{0,8},{2,10},{4,12},{6,14},{8,0},{10,2},{12,4},{14,6},{1,9},{3,11}... | collective-permute-start | bytes 86024 | tf_op jit(solution)/shard_map/ppermute | solution.py:18
  37.1 4.8 %collective-permute-start.12 = (bf16[16,896]{1,0:T(8,128)(2,1)S(1)}, bf16[16,896]{1,0:T(8,128)(2,1)S(1)}, u32[]{:S(2)}, u32[]{:S(2)}) collective-permute-start(bf16[16,896]{1,0:T(8,128)(2,1)S(1)} %shard_map.72.refs_0_), channel_id=1, source_target_pairs={{0,4},{2,6},{4,0},{6,2},{8,12},{10,14},{12,8},{14,10},{1,5},{3,7},... | collective-permute-start | bytes 86024 | tf_op jit(solution)/shard_map/ppermute | solution.py:18

commit v12 on v11

--- a/solution.py
+++ b/solution.py
@@ -184,18 +184,18 @@
     )(*terms)
 
 
-def error_kernel(total, rows, *refs):
+def error_kernel(factor, total, rows, *refs):
     *near, out = refs
     total = total[...]
     for ref in near:
         half = ref.shape[0] // 2
         total = total + jnp.concatenate([ref[half:], ref[:half]])
-    out[...] = (total - rows[...].astype(jnp.float32)).astype(out.dtype)
-
-
-def error(total, near, rows):
-    return pl.pallas_call(
-        error_kernel,
+    out[...] = ((total - rows[...].astype(jnp.float32)) * factor).astype(out.dtype)
+
+
+def error(total, near, rows, factor):
+    return pl.pallas_call(
+        functools.partial(error_kernel, factor),
         out_shape=jax.ShapeDtypeStruct(rows.shape, rows.dtype),
         in_specs=[WHOLE] * (2 + len(near)),
         out_specs=WHOLE,
@@ -215,13 +215,11 @@
 def adam_kernel(codes_t, m, v, *refs):
     *blocks, out, even, odd, err = refs
     products = (even, odd)
-    tokens = codes_t.shape[1]
-    b = 0.1 / (1.0 - 0.9**10) / tokens
-    a = 0.9 / 0.1 * tokens
-    p = 0.999 / 0.001 * tokens**2
-    scale = b / (0.001 / (1.0 - 0.999**10) / tokens**2) ** 0.5
-    eps = 1e-8 / b * scale**2
-    a, p, scale, eps = (jnp.asarray(x, out.dtype) for x in (a, p, scale, eps))
+    b1, b2 = 1.0 - 0.9**10, 1.0 - 0.999**10
+    p = 0.999 / 0.081
+    scale = 0.9 / b1 / (0.081 / b2) ** 0.5
+    eps = 1e-8 / (0.9 / b1) * scale**2
+    p, scale, eps = (jnp.asarray(x, out.dtype) for x in (p, scale, eps))
     i, last = pl.program_id(0), pl.num_programs(0) - 1
     rows = out.shape[0]
     part = even.shape[0]
@@ -245,7 +243,7 @@
         for r in range(0, part, slab):
             at = pl.ds(pl.multiple_of(i * rows + k * part + r, slab), slab)
             c = products[k][r : r + slab, :]
-            first = m[at, :] * a + c
+            first = m[at, :] + c
             second = v[at, :] * p + c * c
             inverse = lax.rsqrt(second)
             step = first * (inverse * (scale - inverse * eps))
@@ -281,7 +279,8 @@
         codes.append(block)
     codes_t = turn(*codes)
     total, near = reduce_rows(sums)
-    err = spread(error(total, near, rows))
+    factor = 0.1 / 0.9 / codes_t.shape[1]
+    err = spread(error(total, near, rows, factor))
     return adam(codes_t, err, dec_m, dec_v)
 
 

time: 53 us -> 52.6 us (level)
  no operation moved by 1% of the time
where the time goes in v12:
time: 52.6 us; the launch traced here: 52.3 us
  starting transfers between devices  17.7 us (34%)
  Pallas kernels  17.5 us (33%)
  waiting for transfers between devices  15.3 us (29%)
  local copies, waits for them, and re-layouts  1.63 us (3%)
    ppermute x15, starting transfers between devices, swap(): return lax.ppermute(value, axis, [(i, i ^ mask) for i in range(n)])  17.7 us
    ppermute x15, waiting for transfers between devices, swap(): return lax.ppermute(value, axis, [(i, i ^ mask) for i in range(n)])  15.3 us
    pallas_call x1, Pallas kernels, adam(): pl.pallas_call(adam_kernel, grid=(lat // rows,), out_shape=jax.ShapeDtype...  10.4 us
    pallas_call x2, Pallas kernels, encode(): pl.pallas_call(functools.partial(encode_kernel, first), out_shape=jax.Sha...  2.84 us
    pallas_call x2, Pallas kernels, decode(): pl.pallas_call(functools.partial(decode_kernel, first, len(given)), out_s...  2.58 us
    pallas_call x1, Pallas kernels, turn(): pl.pallas_call(functools.partial(turn_kernel, min(512, lat)), out_shape=j...  1.68 us
    unnamed x30, local copies, waits for them, and re-layouts  1.63 us
  transfers between devices with their start and end apart: 15, of which 10 were waited for; matrix products, arithmetic and copies ran while one was open for 0% of the time, Pallas kernels for 8%

profile of v12, /device:TPU:0, one launch (start us, length us, event | category | flops | bytes accessed | tf_op | source)
XLA Modules:
  0.0 52.3 jit_solution(4336597583787458251)
XLA Ops:
  0.0 0.5 collective-permute-start
  0.5 2.6 %collective-permute-start.2 = (bf16[4,1792]{1,0:T(4,128)(2,1)}, bf16[4,1792]{1,0:T(4,128)(2,1)S(1)}, u32[]{:S(2)}, u32[]{:S(2)}) collective-permute-start(bf16[4,1792]{1,0:T(4,128)(2,1)} %x.1), channel_id=1, source_target_pairs={{0,3},{1,2},{2,1},{3,0},{4,7},{5,6},{6,5},{7,4},{8,11},{9,10},{10,... | collective-permute-start | bytes 43016 | tf_op jit(solution)/shard_map/ppermute | solution.py:18
  3.1 0.1 collective-permute-start.1
  3.1 1.5 %copy-done.2 = bf16[4,1792]{1,0:T(4,128)(2,1)S(1)} copy-done((bf16[4,1792]{1,0:T(4,128)(2,1)S(1)}, bf16[4,1792]{1,0:T(4,128)(2,1)}, u32[]{:S(2)}) %copy-start.2) | copy-done | bytes 14360
  4.6 0.1 collective-permute-done.2.refs_3_
  4.7 2.3 %collective-permute-done.1.refs_2_ = bf16[4,1792]{1,0:T(4,128)(2,1)S(1)} collective-permute-done((bf16[4,1792]{1,0:T(4,128)(2,1)}, bf16[4,1792]{1,0:T(4,128)(2,1)S(1)}, u32[]{:S(2)}, u32[]{:S(2)}) %collective-permute-start.1) | collective-permute-done | bytes 14368 | tf_op jit(solution)/shard_map/ppermute | solution.py:18
  7.0 3.7 %collective-permute-start.5 = (bf16[16,896]{1,0:T(8,128)(2,1)S(1)}, bf16[16,896]{1,0:T(8,128)(2,1)S(1)}, u32[]{:S(2)}, u32[]{:S(2)}) collective-permute-start(bf16[16,896]{1,0:T(8,128)(2,1)S(1)} %shard_map.65.refs_0_.rows), channel_id=1, source_target_pairs={{0,12},{2,14},{4,8},{6,10},{8,4},{10,6},{12,0},{14,2},{1,13},{3,15... | collective-permute-start | bytes 86024 | tf_op jit(solution)/shard_map/ppermute | solution.py:18
  10.7 0.8 %collective-permute-start.3 = (bf16[16,896]{1,0:T(8,128)(2,1)S(1)}, bf16[16,896]{1,0:T(8,128)(2,1)S(1)}, u32[]{:S(2)}, u32[]{:S(2)}) collective-permute-start(bf16[16,896]{1,0:T(8,128)(2,1)S(1)} %shard_map.65.refs_0_.rows), channel_id=1, source_target_pairs={{0,4},{2,6},{4,0},{6,2},{8,12},{10,14},{12,8},{14,10},{1,5},{3,7},... | collective-permute-start | bytes 86024 | tf_op jit(solution)/shard_map/ppermute | solution.py:18
  11.5 1.3 %collective-permute-done.5.refs_3_ = bf16[16,896]{1,0:T(8,128)(2,1)S(1)} collective-permute-done((bf16[16,896]{1,0:T(8,128)(2,1)S(1)}, bf16[16,896]{1,0:T(8,128)(2,1)S(1)}, u32[]{:S(2)}, u32[]{:S(2)}) %collective-permute-start.5) | collective-permute-done | bytes 28704 | tf_op jit(solution)/shard_map/ppermute | solution.py:18
  12.8 2.7 %collective-permute-done.4.refs_2_ = bf16[16,896]{1,0:T(8,128)(2,1)S(1)} collective-permute-done((bf16[16,896]{1,0:T(8,128)(2,1)S(1)}, bf16[16,896]{1,0:T(8,128)(2,1)S(1)}, u32[]{:S(2)}, u32[]{:S(2)}) %collective-permute-start.4) | collective-permute-done | bytes 28704 | tf_op jit(solution)/shard_map/ppermute | solution.py:18
  15.5 1.4 %shard_map.66.mine = f32[64,4096]{1,0:T(8,128)S(1)} custom-call(bf16[16,896]{1,0:T(8,128)(2,1)S(1)} %shard_map.65.refs_0_.rows, bf16[16,896]{1,0:T(8,128)(2,1)S(1)} %collective-permute-done.3.refs_1_, bf16[16,896]{1,0:T(8,128)(2,1)S(1)} %collective-permute-done.4.refs_2_, bf16[16,896]{1,0:T(8,128)(2,1)S(1)} %collective-permute-done.5.refs_3_, ...), custom_call_target="tpu_custom_call" | custom-call | flops 2449999872 | bytes 7340032 | tf_op jit(solution)/shard_map/pallas_call | solution.py:102
  16.9 0.1 collective-permute-start.6
  17.0 1.4 %shard_map.68.mine = f32[64,4096]{1,0:T(8,128)S(1)} custom-call(bf16[16,896]{1,0:T(8,128)(2,1)S(1)} %shard_map.65.refs_0_.rows, bf16[16,896]{1,0:T(8,128)(2,1)S(1)} %collective-permute-done.3.refs_1_, bf16[16,896]{1,0:T(8,128)(2,1)S(1)} %collective-permute-done.4.refs_2_, bf16[16,896]{1,0:T(8,128)(2,1)S(1)} %collective-permute-done.5.refs_3_, ...), custom_call_target="tpu_custom_call" | custom-call | flops 2449999872 | bytes 7340032 | tf_op jit(solution)/shard_map/pallas_call | solution.py:102
  18.4 0.6 %collective-permute-start.7 = (f32[64,4096]{1,0:T(8,128)S(1)}, f32[64,4096]{1,0:T(8,128)S(1)}, u32[]{:S(2)}, u32[]{:S(2)}) collective-permute-start(f32[64,4096]{1,0:T(8,128)S(1)} %shard_map.68.mine), channel_id=1, source_target_pairs={{0,1},{1,0},{2,3},{3,2},{4,5},{5,4},{6,7},{7,6},{8,9},{9,8},{10,11... | collective-permute-start | bytes 3145736 | tf_op jit(solution)/shard_map/ppermute | solution.py:18
  19.0 0.7 %collective-permute-done.6.theirs = f32[64,4096]{1,0:T(8,128)S(1)} collective-permute-done((f32[64,4096]{1,0:T(8,128)S(1)}, f32[64,4096]{1,0:T(8,128)S(1)}, u32[]{:S(2)}, u32[]{:S(2)}) %collective-permute-start.6) | collective-permute-done | bytes 1048608 | tf_op jit(solution)/shard_map/ppermute | solution.py:18
  19.7 0.1 slice-done.3
  19.8 1.3 %shard_map.67 = (bf16[64,4096]{1,0:T(8,128)(2,1)S(1)}, f32[64,896]{1,0:T(8,128)S(1)}) custom-call(f32[64,4096]{1,0:T(8,128)S(1)} %shard_map.66.mine, f32[64,4096]{1,0:T(8,128)S(1)} %collective-permute-done.6.theirs, f32[1,8192]{1,0:T(1,128)S(1)} %bitcast.7, bf16[8192,896]{1,0:T(8,128)(2,1)S(1)} %bitcast.2), custom_call_target="tpu_custom_call" | custom-call | flops 2449999872 | bytes 7340032 | tf_op jit(solution)/shard_map/pallas_call | solution.py:133
  21.1 0.2 collective-permute-done.7.theirs
  21.3 1.3 %shard_map.69 = (bf16[64,4096]{1,0:T(8,128)(2,1)S(1)}, f32[16,896]{1,0:T(8,128)S(1)}, bf16[16,896]{1,0:T(8,128)(2,1)S(1)}, bf16[16,896]{1,0:T(8,128)(2,1)S(1)}, bf16[16,896]{1,0:T(8,128)(2,1)S(1)}) custom-call(f32[64,4096]{1,0:T(8,128)S(1)} %shard_map.68.mine, f32[64,4096]{1,0:T(8,128)S(1)} %collective-permute-done.7.theirs, f32[1,8192]{1,0:T(1,128)S(1)} %bitcast.8, ...), custom_call_target="tpu_custom_call" | custom-call | flops 2449999872 | bytes 7340032 | tf_op jit(solution)/shard_map/pallas_call | solution.py:133
  22.6 0.1 collective-permute-start.8
  22.7 2.1 %collective-permute-start.9 = (bf16[16,896]{1,0:T(8,128)(2,1)S(1)}, bf16[16,896]{1,0:T(8,128)(2,1)S(1)}, u32[]{:S(2)}, u32[]{:S(2)}) collective-permute-start(bf16[16,896]{1,0:T(8,128)(2,1)S(1)} %get-tuple-element.17), channel_id=1, source_target_pairs={{0,8},{2,10},{4,12},{6,14},{8,0},{10,2},{12,4},{14,6},{1,9},{3,11}... | collective-permute-start | bytes 86024 | tf_op jit(solution)/shard_map/ppermute | solution.py:18
  24.8 2.3 %collective-permute-start.10 = (bf16[16,896]{1,0:T(8,128)(2,1)S(1)}, bf16[16,896]{1,0:T(8,128)(2,1)S(1)}, u32[]{:S(2)}, u32[]{:S(2)}) collective-permute-start(bf16[16,896]{1,0:T(8,128)(2,1)S(1)} %get-tuple-element.18), channel_id=1, source_target_pairs={{0,12},{2,14},{4,8},{6,10},{8,4},{10,6},{12,0},{14,2},{1,13},{3,15... | collective-permute-start | bytes 86024 | tf_op jit(solution)/shard_map/ppermute | solution.py:18
  27.1 0.5 collective-permute-done.9.refs_1_
  27.5 2.9 %collective-permute-done.10.refs_2_ = bf16[16,896]{1,0:T(8,128)(2,1)S(1)} collective-permute-done((bf16[16,896]{1,0:T(8,128)(2,1)S(1)}, bf16[16,896]{1,0:T(8,128)(2,1)S(1)}, u32[]{:S(2)}, u32[]{:S(2)}) %collective-permute-start.10) | collective-permute-done | bytes 28704 | tf_op jit(solution)/shard_map/ppermute | solution.py:18
  30.5 0.0 slice-start.11
  30.5 0.6 %collective-permute-start.11 = (f32[16,896]{1,0:T(8,128)S(1)}, f32[16,896]{1,0:T(8,128)S(1)}, u32[]{:S(2)}, u32[]{:S(2)}) collective-permute-start(f32[16,896]{1,0:T(8,128)S(1)} %shard_map.71.total), channel_id=1, source_target_pairs={{0,2},{2,0},{4,6},{6,4},{8,10},{10,8},{12,14},{14,12},{1,3},{3,1},... | collective-permute-start | bytes 172040 | tf_op jit(solution)/shard_map/ppermute | solution.py:18
  31.1 3.6 %collective-permute-done.11.refs_0_ = f32[16,896]{1,0:T(8,128)S(1)} collective-permute-done((f32[16,896]{1,0:T(8,128)S(1)}, f32[16,896]{1,0:T(8,128)S(1)}, u32[]{:S(2)}, u32[]{:S(2)}) %collective-permute-start.11) | collective-permute-done | bytes 57376 | tf_op jit(solution)/shard_map/ppermute | solution.py:18
  34.8 2.4 %collective-permute-start.14 = (bf16[16,896]{1,0:T(8,128)(2,1)S(1)}, bf16[16,896]{1,0:T(8,128)(2,1)S(1)}, u32[]{:S(2)}, u32[]{:S(2)}) collective-permute-start(bf16[16,896]{1,0:T(8,128)(2,1)S(1)} %shard_map.72.refs_0_), channel_id=1, source_target_pairs={{0,12},{2,14},{4,8},{6,10},{8,4},{10,6},{12,0},{14,2},{1,13},{3,15... | collective-permute-start | bytes 86024 | tf_op jit(solution)/shard_map/ppermute | solution.py:18
  37.1 2.1 %collective-permute-start.12 = (bf16[16,896]{1,0:T(8,128)(2,1)S(1)}, bf16[16,896]{1,0:T(8,128)(2,1)S(1)}, u32[]{:S(2)}, u32[]{:S(2)}) collective-permute-start(bf16[16,896]{1,0:T(8,128)(2,1)S(1)} %shard_map.72.refs_0_), channel_id=1, source_target_pairs={{0,4},{2,6},{4,0},{6,2},{8,12},{10,14},{12,8},{14,10},{1,5},{3,7},... | collective-permute-start | bytes 86024 | tf_op jit(solution)/shard_map/ppermute | solution.py:18
  39.2 1.7 %shard_map.70.codes_t = bf16[8192,64]{1,0:T(8,128)(2,1)S(1)} custom-call(bf16[64,4096]{1,0:T(8,128)(2,1)S(1)} %get-tuple-element.12.refs_0_, bf16[64,4096]{1,0:T(8,128)(2,1)S(1)} %get-tuple-element.14.refs_1_), custom_call_target="tpu_custom_call" | custom-call | flops 1400000000 | bytes 4194304 | tf_op jit(solution)/shard_map/pallas_call | solution.py:158
  40.9 1.0 %collective-permute-done.13.refs_2_ = bf16[16,896]{1,0:T(8,128)(2,1)S(1)} collective-permute-done((bf16[16,896]{1,0:T(8,128)(2,1)S(1)}, bf16[16,896]{1,0:T(8,128)(2,1)S(1)}, u32[]{:S(2)}, u32[]{:S(2)}) %collective-permute-start.13) | collective-permute-done | bytes 28704 | tf_op jit(solution)/shard_map/ppermute | solution.py:18
  42.0 10.4 %shard_map.73 = bf16[8192,896]{1,0:T(8,128)(2,1)} custom-call(bf16[8192,64]{1,0:T(8,128)(2,1)S(1)} %shard_map.70.codes_t, bf16[8192,896]{1,0:T(8,128)(2,1)S(1)} %bitcast.4, bf16[8192,896]{1,0:T(8,128)(2,1)S(1)} %bitcast.6, bf16[16,896]{1,0:T(8,128)(2,1)S(1)} %shard_map.72.refs_0_, bf16[16,896]{1,0:T(8,128)(2,1)S(1)} %collective-permute-done.12.refs_1_, ...), custom_call_target="tpu_custom_call" | custom-call | tf_op jit(solution)/shard_map/pallas_call | solution.py:256
  (41 shorter events, 0.1 us)
Async XLA Ops:
  0.0 15.5 %copy-start = (bf16[896,8192]{1,0:T(8,128)(2,1)S(1)}, bf16[896,8192]{1,0:T(8,128)(2,1)}, u32[]{:S(2)}) copy-start(bf16[896,8192]{1,0:T(8,128)(2,1)} %refs_4_.3) | copy-start | bytes 44040196
  0.0 4.6 %collective-permute-start = (bf16[4,1792]{1,0:T(4,128)(2,1)}, bf16[4,1792]{1,0:T(4,128)(2,1)S(1)}, u32[]{:S(2)}, u32[]{:S(2)}) collective-permute-start(bf16[4,1792]{1,0:T(4,128)(2,1)} %x.1), channel_id=1, source_target_pairs={{0,1},{1,0},{2,3},{3,2},{4,5},{5,4},{6,7},{7,6},{8,9},{9,8},{10,11... | collective-permute-start | bytes 43016 | tf_op jit(solution)/shard_map/ppermute | solution.py:18
  0.5 4.2 %collective-permute-start.2 = (bf16[4,1792]{1,0:T(4,128)(2,1)}, bf16[4,1792]{1,0:T(4,128)(2,1)S(1)}, u32[]{:S(2)}, u32[]{:S(2)}) collective-permute-start(bf16[4,1792]{1,0:T(4,128)(2,1)} %x.1), channel_id=1, source_target_pairs={{0,3},{1,2},{2,1},{3,0},{4,7},{5,6},{6,5},{7,4},{8,11},{9,10},{10,... | collective-permute-start | bytes 43016 | tf_op jit(solution)/shard_map/ppermute | solution.py:18
  3.1 3.9 %collective-permute-start.1 = (bf16[4,1792]{1,0:T(4,128)(2,1)}, bf16[4,1792]{1,0:T(4,128)(2,1)S(1)}, u32[]{:S(2)}, u32[]{:S(2)}) collective-permute-start(bf16[4,1792]{1,0:T(4,128)(2,1)} %x.1), channel_id=1, source_target_pairs={{0,2},{1,3},{2,0},{3,1},{4,6},{5,7},{6,4},{7,5},{8,10},{9,11},{10,... | collective-permute-start | bytes 43016 | tf_op jit(solution)/shard_map/ppermute | solution.py:18
  3.1 1.5 %copy-start.2 = (bf16[4,1792]{1,0:T(4,128)(2,1)S(1)}, bf16[4,1792]{1,0:T(4,128)(2,1)}, u32[]{:S(2)}) copy-start(bf16[4,1792]{1,0:T(4,128)(2,1)} %x.1) | copy-start | bytes 43012
  7.0 12.7 %slice-start = ((s8[14680064]{0:T(1024)(128)(4,1)}), s8[4194304]{0:T(1024)(128)(4,1)S(1)}, s32[]{:S(2)}) async-start(s8[14680064]{0:T(1024)(128)(4,1)} %bitcast.1), calls=%async_computation | async-start | bytes 8388608
  7.0 12.6 %slice-start.1 = ((s8[14680064]{0:T(1024)(128)(4,1)}), s8[4194304]{0:T(1024)(128)(4,1)S(1)}, s32[]{:S(2)}) async-start(s8[14680064]{0:T(1024)(128)(4,1)} %bitcast.1), calls=%async_computation.1 | async-start | bytes 8388608
  7.0 12.6 %copy-start.1 = (f32[8192]{0:T(1024)S(1)}, f32[8192]{0:T(1024)}, u32[]{:S(2)}) copy-start(f32[8192]{0:T(1024)} %param.8) | copy-start | bytes 98308
  7.0 5.7 %collective-permute-start.5 = (bf16[16,896]{1,0:T(8,128)(2,1)S(1)}, bf16[16,896]{1,0:T(8,128)(2,1)S(1)}, u32[]{:S(2)}, u32[]{:S(2)}) collective-permute-start(bf16[16,896]{1,0:T(8,128)(2,1)S(1)} %shard_map.65.refs_0_.rows), channel_id=1, source_target_pairs={{0,12},{2,14},{4,8},{6,10},{8,4},{10,6},{12,0},{14,2},{1,13},{3,15... | collective-permute-start | bytes 86024 | tf_op jit(solution)/shard_map/ppermute | solution.py:18
  10.7 4.8 %collective-permute-start.4 = (bf16[16,896]{1,0:T(8,128)(2,1)S(1)}, bf16[16,896]{1,0:T(8,128)(2,1)S(1)}, u32[]{:S(2)}, u32[]{:S(2)}) collective-permute-start(bf16[16,896]{1,0:T(8,128)(2,1)S(1)} %shard_map.65.refs_0_.rows), channel_id=1, source_target_pairs={{0,8},{2,10},{4,12},{6,14},{8,0},{10,2},{12,4},{14,6},{1,9},{3,11}... | collective-permute-start | bytes 86024 | tf_op jit(solution)/shard_map/ppermute | solution.py:18
  10.7 4.8 %collective-permute-start.3 = (bf16[16,896]{1,0:T(8,128)(2,1)S(1)}, bf16[16,896]{1,0:T(8,128)(2,1)S(1)}, u32[]{:S(2)}, u32[]{:S(2)}) collective-permute-start(bf16[16,896]{1,0:T(8,128)(2,1)S(1)} %shard_map.65.refs_0_.rows), channel_id=1, source_target_pairs={{0,4},{2,6},{4,0},{6,2},{8,12},{10,14},{12,8},{14,10},{1,5},{3,7},... | collective-permute-start | bytes 86024 | tf_op jit(solution)/shard_map/ppermute | solution.py:18
  16.9 2.8 %slice-start.2 = ((s8[14680064]{0:T(1024)(128)(4,1)}), s8[4194304]{0:T(1024)(128)(4,1)S(1)}, s32[]{:S(2)}) async-start(s8[14680064]{0:T(1024)(128)(4,1)} %bitcast.1), calls=%async_computation.2 | async-start | bytes 8388608
  16.9 2.9 %slice-start.3 = ((s8[14680064]{0:T(1024)(128)(4,1)}), s8[2097152]{0:T(1024)(128)(4,1)S(1)}, s32[]{:S(2)}) async-start(s8[14680064]{0:T(1024)(128)(4,1)} %bitcast.1), calls=%async_computation.3 | async-start | bytes 4194304
  16.9 2.7 %collective-permute-start.6 = (f32[64,4096]{1,0:T(8,128)S(1)}, f32[64,4096]{1,0:T(8,128)S(1)}, u32[]{:S(2)}, u32[]{:S(2)}) collective-permute-start(f32[64,4096]{1,0:T(8,128)S(1)} %shard_map.66.mine), channel_id=1, source_target_pairs={{0,1},{1,0},{2,3},{3,2},{4,5},{5,4},{6,7},{7,6},{8,9},{9,8},{10,11... | collective-permute-start | bytes 3145736 | tf_op jit(solution)/shard_map/ppermute | solution.py:18
  18.4 2.8 %collective-permute-start.7 = (f32[64,4096]{1,0:T(8,128)S(1)}, f32[64,4096]{1,0:T(8,128)S(1)}, u32[]{:S(2)}, u32[]{:S(2)}) collective-permute-start(f32[64,4096]{1,0:T(8,128)S(1)} %shard_map.68.mine), channel_id=1, source_target_pairs={{0,1},{1,0},{2,3},{3,2},{4,5},{5,4},{6,7},{7,6},{8,9},{9,8},{10,11... | collective-permute-start | bytes 3145736 | tf_op jit(solution)/shard_map/ppermute | solution.py:18
  21.3 20.6 %slice-start.4 = ((s8[14680064]{0:T(1024)(128)(4,1)}), s8[4194304]{0:T(1024)(128)(4,1)S(1)}, s32[]{:S(2)}) async-start(s8[14680064]{0:T(1024)(128)(4,1)} %bitcast.3), calls=%async_computation.4 | async-start | bytes 8388608
  21.3 20.6 %slice-start.5 = ((s8[14680064]{0:T(1024)(128)(4,1)}), s8[4194304]{0:T(1024)(128)(4,1)S(1)}, s32[]{:S(2)}) async-start(s8[14680064]{0:T(1024)(128)(4,1)} %bitcast.3), calls=%async_computation.5 | async-start | bytes 8388608
  21.3 20.6 %slice-start.8 = ((s8[14680064]{0:T(1024)(128)(4,1)}), s8[4194304]{0:T(1024)(128)(4,1)S(1)}, s32[]{:S(2)}) async-start(s8[14680064]{0:T(1024)(128)(4,1)} %bitcast.5), calls=%async_computation.8 | async-start | bytes 8388608
  21.3 20.6 %slice-start.9 = ((s8[14680064]{0:T(1024)(128)(4,1)}), s8[4194304]{0:T(1024)(128)(4,1)S(1)}, s32[]{:S(2)}) async-start(s8[14680064]{0:T(1024)(128)(4,1)} %bitcast.5), calls=%async_computation.9 | async-start | bytes 8388608
  22.6 4.5 %collective-permute-start.8 = (bf16[16,896]{1,0:T(8,128)(2,1)S(1)}, bf16[16,896]{1,0:T(8,128)(2,1)S(1)}, u32[]{:S(2)}, u32[]{:S(2)}) collective-permute-start(bf16[16,896]{1,0:T(8,128)(2,1)S(1)} %get-tuple-element.16), channel_id=1, source_target_pairs={{0,4},{2,6},{4,0},{6,2},{8,12},{10,14},{12,8},{14,10},{1,5},{3,7},... | collective-permute-start | bytes 86024 | tf_op jit(solution)/shard_map/ppermute | solution.py:18
  22.7 4.9 %collective-permute-start.9 = (bf16[16,896]{1,0:T(8,128)(2,1)S(1)}, bf16[16,896]{1,0:T(8,128)(2,1)S(1)}, u32[]{:S(2)}, u32[]{:S(2)}) collective-permute-start(bf16[16,896]{1,0:T(8,128)(2,1)S(1)} %get-tuple-element.17), channel_id=1, source_target_pairs={{0,8},{2,10},{4,12},{6,14},{8,0},{10,2},{12,4},{14,6},{1,9},{3,11}... | collective-permute-start | bytes 86024 | tf_op jit(solution)/shard_map/ppermute | solution.py:18
  24.8 5.7 %collective-permute-start.10 = (bf16[16,896]{1,0:T(8,128)(2,1)S(1)}, bf16[16,896]{1,0:T(8,128)(2,1)S(1)}, u32[]{:S(2)}, u32[]{:S(2)}) collective-permute-start(bf16[16,896]{1,0:T(8,128)(2,1)S(1)} %get-tuple-element.18), channel_id=1, source_target_pairs={{0,12},{2,14},{4,8},{6,10},{8,4},{10,6},{12,0},{14,2},{1,13},{3,15... | collective-permute-start | bytes 86024 | tf_op jit(solution)/shard_map/ppermute | solution.py:18
  30.5 11.5 %slice-start.6 = ((s8[14680064]{0:T(1024)(128)(4,1)}), s8[4194304]{0:T(1024)(128)(4,1)S(1)}, s32[]{:S(2)}) async-start(s8[14680064]{0:T(1024)(128)(4,1)} %bitcast.3), calls=%async_computation.6 | async-start | bytes 8388608
  30.5 11.5 %slice-start.10 = ((s8[14680064]{0:T(1024)(128)(4,1)}), s8[4194304]{0:T(1024)(128)(4,1)S(1)}, s32[]{:S(2)}) async-start(s8[14680064]{0:T(1024)(128)(4,1)} %bitcast.5), calls=%async_computation.10 | async-start | bytes 8388608
  30.5 11.5 %slice-start.7 = ((s8[14680064]{0:T(1024)(128)(4,1)}), s8[2097152]{0:T(1024)(128)(4,1)S(1)}, s32[]{:S(2)}) async-start(s8[14680064]{0:T(1024)(128)(4,1)} %bitcast.3), calls=%async_computation.7 | async-start | bytes 4194304
  30.5 11.5 %slice-start.11 = ((s8[14680064]{0:T(1024)(128)(4,1)}), s8[2097152]{0:T(1024)(128)(4,1)S(1)}, s32[]{:S(2)}) async-start(s8[14680064]{0:T(1024)(128)(4,1)} %bitcast.5), calls=%async_computation.11 | async-start | bytes 4194304
  30.5 4.2 %collective-permute-start.11 = (f32[16,896]{1,0:T(8,128)S(1)}, f32[16,896]{1,0:T(8,128)S(1)}, u32[]{:S(2)}, u32[]{:S(2)}) collective-permute-start(f32[16,896]{1,0:T(8,128)S(1)} %shard_map.71.total), channel_id=1, source_target_pairs={{0,2},{2,0},{4,6},{6,4},{8,10},{10,8},{12,14},{14,12},{1,3},{3,1},... | collective-permute-start | bytes 172040 | tf_op jit(solution)/shard_map/ppermute | solution.py:18
  34.8 6.1 %collective-permute-start.14 = (bf16[16,896]{1,0:T(8,128)(2,1)S(1)}, bf16[16,896]{1,0:T(8,128)(2,1)S(1)}, u32[]{:S(2)}, u32[]{:S(2)}) collective-permute-start(bf16[16,896]{1,0:T(8,128)(2,1)S(1)} %shard_map.72.refs_0_), channel_id=1, source_target_pairs={{0,12},{2,14},{4,8},{6,10},{8,4},{10,6},{12,0},{14,2},{1,13},{3,15... | collective-permute-start | bytes 86024 | tf_op jit(solution)/shard_map/ppermute | solution.py:18
  37.1 4.8 %collective-permute-start.13 = (bf16[16,896]{1,0:T(8,128)(2,1)S(1)}, bf16[16,896]{1,0:T(8,128)(2,1)S(1)}, u32[]{:S(2)}, u32[]{:S(2)}) collective-permute-start(bf16[16,896]{1,0:T(8,128)(2,1)S(1)} %shard_map.72.refs_0_), channel_id=1, source_target_pairs={{0,8},{2,10},{4,12},{6,14},{8,0},{10,2},{12,4},{14,6},{1,9},{3,11}... | collective-permute-start | bytes 86024 | tf_op jit(solution)/shard_map/ppermute | solution.py:18
  37.1 4.8 %collective-permute-start.12 = (bf16[16,896]{1,0:T(8,128)(2,1)S(1)}, bf16[16,896]{1,0:T(8,128)(2,1)S(1)}, u32[]{:S(2)}, u32[]{:S(2)}) collective-permute-start(bf16[16,896]{1,0:T(8,128)(2,1)S(1)} %shard_map.72.refs_0_), channel_id=1, source_target_pairs={{0,4},{2,6},{4,0},{6,2},{8,12},{10,14},{12,8},{14,10},{1,5},{3,7},... | collective-permute-start | bytes 86024 | tf_op jit(solution)/shard_map/ppermute | solution.py:18

commit v13 on v12

--- a/solution.py
+++ b/solution.py
@@ -223,24 +223,25 @@
     i, last = pl.program_id(0), pl.num_programs(0) - 1
     rows = out.shape[0]
     part = even.shape[0]
-    slab = 16
-
-    def multiply(start, product):
-        at = pl.ds(pl.multiple_of(start, part), part)
+    slab, group = 32, part // 2
+
+    def multiply(start, product, g):
+        at = pl.ds(pl.multiple_of(start + g, group), group)
         c = jnp.dot(codes_t[at, :], err[...], preferred_element_type=jnp.float32)
-        product[...] = c.astype(product.dtype)
+        product[g : g + group, :] = c.astype(product.dtype)
 
     @pl.when(i == 0)
     def _():
         err[...] = stack(blocks)
-        multiply(0, even)
+        for g in range(0, part, group):
+            multiply(0, even, g)
 
     for k in range(2):
-        if k == 0:
-            multiply(i * rows + part, odd)
-        else:
-            multiply(jnp.minimum(i + 1, last) * rows, even)
         for r in range(0, part, slab):
+            if r % group == 0 and k == 0:
+                multiply(i * rows + part, odd, r)
+            elif r % group == 0:
+                multiply(jnp.minimum(i + 1, last) * rows, even, r)
             at = pl.ds(pl.multiple_of(i * rows + k * part + r, slab), slab)
             c = products[k][r : r + slab, :]
             first = m[at, :] + c

time: 52.6 us -> 52.7 us (level)
  no operation moved by 1% of the time
where the time goes in v13:
time: 52.7 us; the launch traced here: 52.4 us
  starting transfers between devices  17.7 us (34%)
  Pallas kernels  17.6 us (33%)
  waiting for transfers between devices  15.3 us (29%)
  local copies, waits for them, and re-layouts  1.63 us (3%)
    ppermute x15, starting transfers between devices, swap(): return lax.ppermute(value, axis, [(i, i ^ mask) for i in range(n)])  17.7 us
    ppermute x15, waiting for transfers between devices, swap(): return lax.ppermute(value, axis, [(i, i ^ mask) for i in range(n)])  15.3 us
    pallas_call x1, Pallas kernels, adam(): pl.pallas_call(adam_kernel, grid=(lat // rows,), out_shape=jax.ShapeDtype...  10.5 us
    pallas_call x2, Pallas kernels, encode(): pl.pallas_call(functools.partial(encode_kernel, first), out_shape=jax.Sha...  2.84 us
    pallas_call x2, Pallas kernels, decode(): pl.pallas_call(functools.partial(decode_kernel, first, len(given)), out_s...  2.58 us
    pallas_call x1, Pallas kernels, turn(): pl.pallas_call(functools.partial(turn_kernel, min(512, lat)), out_shape=j...  1.68 us
    unnamed x30, local copies, waits for them, and re-layouts  1.63 us
  transfers between devices with their start and end apart: 15, of which 10 were waited for; matrix products, arithmetic and copies ran while one was open for 0% of the time, Pallas kernels for 8%

profile of v13, /device:TPU:0, one launch (start us, length us, event | category | flops | bytes accessed | tf_op | source)
XLA Modules:
  0.0 52.4 jit_solution(9884280380742839224)
XLA Ops:
  0.0 0.5 collective-permute-start
  0.5 2.6 %collective-permute-start.2 = (bf16[4,1792]{1,0:T(4,128)(2,1)}, bf16[4,1792]{1,0:T(4,128)(2,1)S(1)}, u32[]{:S(2)}, u32[]{:S(2)}) collective-permute-start(bf16[4,1792]{1,0:T(4,128)(2,1)} %x.1), channel_id=1, source_target_pairs={{0,3},{1,2},{2,1},{3,0},{4,7},{5,6},{6,5},{7,4},{8,11},{9,10},{10,... | collective-permute-start | bytes 43016 | tf_op jit(solution)/shard_map/ppermute | solution.py:18
  3.1 0.1 collective-permute-start.1
  3.1 1.5 %copy-done.2 = bf16[4,1792]{1,0:T(4,128)(2,1)S(1)} copy-done((bf16[4,1792]{1,0:T(4,128)(2,1)S(1)}, bf16[4,1792]{1,0:T(4,128)(2,1)}, u32[]{:S(2)}) %copy-start.2) | copy-done | bytes 14360
  4.6 0.1 collective-permute-done.2.refs_3_
  4.7 2.3 %collective-permute-done.1.refs_2_ = bf16[4,1792]{1,0:T(4,128)(2,1)S(1)} collective-permute-done((bf16[4,1792]{1,0:T(4,128)(2,1)}, bf16[4,1792]{1,0:T(4,128)(2,1)S(1)}, u32[]{:S(2)}, u32[]{:S(2)}) %collective-permute-start.1) | collective-permute-done | bytes 14368 | tf_op jit(solution)/shard_map/ppermute | solution.py:18
  7.0 3.7 %collective-permute-start.5 = (bf16[16,896]{1,0:T(8,128)(2,1)S(1)}, bf16[16,896]{1,0:T(8,128)(2,1)S(1)}, u32[]{:S(2)}, u32[]{:S(2)}) collective-permute-start(bf16[16,896]{1,0:T(8,128)(2,1)S(1)} %shard_map.65.refs_0_.rows), channel_id=1, source_target_pairs={{0,12},{2,14},{4,8},{6,10},{8,4},{10,6},{12,0},{14,2},{1,13},{3,15... | collective-permute-start | bytes 86024 | tf_op jit(solution)/shard_map/ppermute | solution.py:18
  10.7 0.8 %collective-permute-start.3 = (bf16[16,896]{1,0:T(8,128)(2,1)S(1)}, bf16[16,896]{1,0:T(8,128)(2,1)S(1)}, u32[]{:S(2)}, u32[]{:S(2)}) collective-permute-start(bf16[16,896]{1,0:T(8,128)(2,1)S(1)} %shard_map.65.refs_0_.rows), channel_id=1, source_target_pairs={{0,4},{2,6},{4,0},{6,2},{8,12},{10,14},{12,8},{14,10},{1,5},{3,7},... | collective-permute-start | bytes 86024 | tf_op jit(solution)/shard_map/ppermute | solution.py:18
  11.5 1.3 %collective-permute-done.5.refs_3_ = bf16[16,896]{1,0:T(8,128)(2,1)S(1)} collective-permute-done((bf16[16,896]{1,0:T(8,128)(2,1)S(1)}, bf16[16,896]{1,0:T(8,128)(2,1)S(1)}, u32[]{:S(2)}, u32[]{:S(2)}) %collective-permute-start.5) | collective-permute-done | bytes 28704 | tf_op jit(solution)/shard_map/ppermute | solution.py:18
  12.8 2.7 %collective-permute-done.4.refs_2_ = bf16[16,896]{1,0:T(8,128)(2,1)S(1)} collective-permute-done((bf16[16,896]{1,0:T(8,128)(2,1)S(1)}, bf16[16,896]{1,0:T(8,128)(2,1)S(1)}, u32[]{:S(2)}, u32[]{:S(2)}) %collective-permute-start.4) | collective-permute-done | bytes 28704 | tf_op jit(solution)/shard_map/ppermute | solution.py:18
  15.5 1.4 %shard_map.66.mine = f32[64,4096]{1,0:T(8,128)S(1)} custom-call(bf16[16,896]{1,0:T(8,128)(2,1)S(1)} %shard_map.65.refs_0_.rows, bf16[16,896]{1,0:T(8,128)(2,1)S(1)} %collective-permute-done.3.refs_1_, bf16[16,896]{1,0:T(8,128)(2,1)S(1)} %collective-permute-done.4.refs_2_, bf16[16,896]{1,0:T(8,128)(2,1)S(1)} %collective-permute-done.5.refs_3_, ...), custom_call_target="tpu_custom_call" | custom-call | flops 2449999872 | bytes 7340032 | tf_op jit(solution)/shard_map/pallas_call | solution.py:102
  16.9 0.1 collective-permute-start.6
  17.0 1.4 %shard_map.68.mine = f32[64,4096]{1,0:T(8,128)S(1)} custom-call(bf16[16,896]{1,0:T(8,128)(2,1)S(1)} %shard_map.65.refs_0_.rows, bf16[16,896]{1,0:T(8,128)(2,1)S(1)} %collective-permute-done.3.refs_1_, bf16[16,896]{1,0:T(8,128)(2,1)S(1)} %collective-permute-done.4.refs_2_, bf16[16,896]{1,0:T(8,128)(2,1)S(1)} %collective-permute-done.5.refs_3_, ...), custom_call_target="tpu_custom_call" | custom-call | flops 2449999872 | bytes 7340032 | tf_op jit(solution)/shard_map/pallas_call | solution.py:102
  18.4 0.6 %collective-permute-start.7 = (f32[64,4096]{1,0:T(8,128)S(1)}, f32[64,4096]{1,0:T(8,128)S(1)}, u32[]{:S(2)}, u32[]{:S(2)}) collective-permute-start(f32[64,4096]{1,0:T(8,128)S(1)} %shard_map.68.mine), channel_id=1, source_target_pairs={{0,1},{1,0},{2,3},{3,2},{4,5},{5,4},{6,7},{7,6},{8,9},{9,8},{10,11... | collective-permute-start | bytes 3145736 | tf_op jit(solution)/shard_map/ppermute | solution.py:18
  19.0 0.7 %collective-permute-done.6.theirs = f32[64,4096]{1,0:T(8,128)S(1)} collective-permute-done((f32[64,4096]{1,0:T(8,128)S(1)}, f32[64,4096]{1,0:T(8,128)S(1)}, u32[]{:S(2)}, u32[]{:S(2)}) %collective-permute-start.6) | collective-permute-done | bytes 1048608 | tf_op jit(solution)/shard_map/ppermute | solution.py:18
  19.7 0.1 slice-done.3
  19.8 1.3 %shard_map.67 = (bf16[64,4096]{1,0:T(8,128)(2,1)S(1)}, f32[64,896]{1,0:T(8,128)S(1)}) custom-call(f32[64,4096]{1,0:T(8,128)S(1)} %shard_map.66.mine, f32[64,4096]{1,0:T(8,128)S(1)} %collective-permute-done.6.theirs, f32[1,8192]{1,0:T(1,128)S(1)} %bitcast.7, bf16[8192,896]{1,0:T(8,128)(2,1)S(1)} %bitcast.2), custom_call_target="tpu_custom_call" | custom-call | flops 2449999872 | bytes 7340032 | tf_op jit(solution)/shard_map/pallas_call | solution.py:133
  21.1 0.2 collective-permute-done.7.theirs
  21.3 1.3 %shard_map.69 = (bf16[64,4096]{1,0:T(8,128)(2,1)S(1)}, f32[16,896]{1,0:T(8,128)S(1)}, bf16[16,896]{1,0:T(8,128)(2,1)S(1)}, bf16[16,896]{1,0:T(8,128)(2,1)S(1)}, bf16[16,896]{1,0:T(8,128)(2,1)S(1)}) custom-call(f32[64,4096]{1,0:T(8,128)S(1)} %shard_map.68.mine, f32[64,4096]{1,0:T(8,128)S(1)} %collective-permute-done.7.theirs, f32[1,8192]{1,0:T(1,128)S(1)} %bitcast.8, ...), custom_call_target="tpu_custom_call" | custom-call | flops 2449999872 | bytes 7340032 | tf_op jit(solution)/shard_map/pallas_call | solution.py:133
  22.6 0.1 collective-permute-start.8
  22.7 2.1 %collective-permute-start.9 = (bf16[16,896]{1,0:T(8,128)(2,1)S(1)}, bf16[16,896]{1,0:T(8,128)(2,1)S(1)}, u32[]{:S(2)}, u32[]{:S(2)}) collective-permute-start(bf16[16,896]{1,0:T(8,128)(2,1)S(1)} %get-tuple-element.17), channel_id=1, source_target_pairs={{0,8},{2,10},{4,12},{6,14},{8,0},{10,2},{12,4},{14,6},{1,9},{3,11}... | collective-permute-start | bytes 86024 | tf_op jit(solution)/shard_map/ppermute | solution.py:18
  24.8 2.3 %collective-permute-start.10 = (bf16[16,896]{1,0:T(8,128)(2,1)S(1)}, bf16[16,896]{1,0:T(8,128)(2,1)S(1)}, u32[]{:S(2)}, u32[]{:S(2)}) collective-permute-start(bf16[16,896]{1,0:T(8,128)(2,1)S(1)} %get-tuple-element.18), channel_id=1, source_target_pairs={{0,12},{2,14},{4,8},{6,10},{8,4},{10,6},{12,0},{14,2},{1,13},{3,15... | collective-permute-start | bytes 86024 | tf_op jit(solution)/shard_map/ppermute | solution.py:18
  27.1 0.5 collective-permute-done.9.refs_1_
  27.5 2.9 %collective-permute-done.10.refs_2_ = bf16[16,896]{1,0:T(8,128)(2,1)S(1)} collective-permute-done((bf16[16,896]{1,0:T(8,128)(2,1)S(1)}, bf16[16,896]{1,0:T(8,128)(2,1)S(1)}, u32[]{:S(2)}, u32[]{:S(2)}) %collective-permute-start.10) | collective-permute-done | bytes 28704 | tf_op jit(solution)/shard_map/ppermute | solution.py:18
  30.5 0.0 slice-start.7
  30.5 0.6 %collective-permute-start.11 = (f32[16,896]{1,0:T(8,128)S(1)}, f32[16,896]{1,0:T(8,128)S(1)}, u32[]{:S(2)}, u32[]{:S(2)}) collective-permute-start(f32[16,896]{1,0:T(8,128)S(1)} %shard_map.71.total), channel_id=1, source_target_pairs={{0,2},{2,0},{4,6},{6,4},{8,10},{10,8},{12,14},{14,12},{1,3},{3,1},... | collective-permute-start | bytes 172040 | tf_op jit(solution)/shard_map/ppermute | solution.py:18
  31.1 3.6 %collective-permute-done.11.refs_0_ = f32[16,896]{1,0:T(8,128)S(1)} collective-permute-done((f32[16,896]{1,0:T(8,128)S(1)}, f32[16,896]{1,0:T(8,128)S(1)}, u32[]{:S(2)}, u32[]{:S(2)}) %collective-permute-start.11) | collective-permute-done | bytes 57376 | tf_op jit(solution)/shard_map/ppermute | solution.py:18
  34.8 2.4 %collective-permute-start.14 = (bf16[16,896]{1,0:T(8,128)(2,1)S(1)}, bf16[16,896]{1,0:T(8,128)(2,1)S(1)}, u32[]{:S(2)}, u32[]{:S(2)}) collective-permute-start(bf16[16,896]{1,0:T(8,128)(2,1)S(1)} %shard_map.72.refs_0_), channel_id=1, source_target_pairs={{0,12},{2,14},{4,8},{6,10},{8,4},{10,6},{12,0},{14,2},{1,13},{3,15... | collective-permute-start | bytes 86024 | tf_op jit(solution)/shard_map/ppermute | solution.py:18
  37.1 2.1 %collective-permute-start.12 = (bf16[16,896]{1,0:T(8,128)(2,1)S(1)}, bf16[16,896]{1,0:T(8,128)(2,1)S(1)}, u32[]{:S(2)}, u32[]{:S(2)}) collective-permute-start(bf16[16,896]{1,0:T(8,128)(2,1)S(1)} %shard_map.72.refs_0_), channel_id=1, source_target_pairs={{0,4},{2,6},{4,0},{6,2},{8,12},{10,14},{12,8},{14,10},{1,5},{3,7},... | collective-permute-start | bytes 86024 | tf_op jit(solution)/shard_map/ppermute | solution.py:18
  39.2 1.7 %shard_map.70.codes_t = bf16[8192,64]{1,0:T(8,128)(2,1)S(1)} custom-call(bf16[64,4096]{1,0:T(8,128)(2,1)S(1)} %get-tuple-element.12.refs_0_, bf16[64,4096]{1,0:T(8,128)(2,1)S(1)} %get-tuple-element.14.refs_1_), custom_call_target="tpu_custom_call" | custom-call | flops 1400000000 | bytes 4194304 | tf_op jit(solution)/shard_map/pallas_call | solution.py:158
  40.9 1.0 %collective-permute-done.13.refs_2_ = bf16[16,896]{1,0:T(8,128)(2,1)S(1)} collective-permute-done((bf16[16,896]{1,0:T(8,128)(2,1)S(1)}, bf16[16,896]{1,0:T(8,128)(2,1)S(1)}, u32[]{:S(2)}, u32[]{:S(2)}) %collective-permute-start.13) | collective-permute-done | bytes 28704 | tf_op jit(solution)/shard_map/ppermute | solution.py:18
  42.0 10.5 %shard_map.73 = bf16[8192,896]{1,0:T(8,128)(2,1)} custom-call(bf16[8192,64]{1,0:T(8,128)(2,1)S(1)} %shard_map.70.codes_t, bf16[8192,896]{1,0:T(8,128)(2,1)S(1)} %bitcast.4, bf16[8192,896]{1,0:T(8,128)(2,1)S(1)} %bitcast.6, bf16[16,896]{1,0:T(8,128)(2,1)S(1)} %shard_map.72.refs_0_, bf16[16,896]{1,0:T(8,128)(2,1)S(1)} %collective-permute-done.12.refs_1_, ...), custom_call_target="tpu_custom_call" | custom-call | tf_op jit(solution)/shard_map/pallas_call | solution.py:257
  (41 shorter events, 0.1 us)
Async XLA Ops:
  0.0 15.5 %copy-start = (bf16[896,8192]{1,0:T(8,128)(2,1)S(1)}, bf16[896,8192]{1,0:T(8,128)(2,1)}, u32[]{:S(2)}) copy-start(bf16[896,8192]{1,0:T(8,128)(2,1)} %refs_4_.3) | copy-start | bytes 44040196
  0.0 4.6 %collective-permute-start = (bf16[4,1792]{1,0:T(4,128)(2,1)}, bf16[4,1792]{1,0:T(4,128)(2,1)S(1)}, u32[]{:S(2)}, u32[]{:S(2)}) collective-permute-start(bf16[4,1792]{1,0:T(4,128)(2,1)} %x.1), channel_id=1, source_target_pairs={{0,1},{1,0},{2,3},{3,2},{4,5},{5,4},{6,7},{7,6},{8,9},{9,8},{10,11... | collective-permute-start | bytes 43016 | tf_op jit(solution)/shard_map/ppermute | solution.py:18
  0.5 4.2 %collective-permute-start.2 = (bf16[4,1792]{1,0:T(4,128)(2,1)}, bf16[4,1792]{1,0:T(4,128)(2,1)S(1)}, u32[]{:S(2)}, u32[]{:S(2)}) collective-permute-start(bf16[4,1792]{1,0:T(4,128)(2,1)} %x.1), channel_id=1, source_target_pairs={{0,3},{1,2},{2,1},{3,0},{4,7},{5,6},{6,5},{7,4},{8,11},{9,10},{10,... | collective-permute-start | bytes 43016 | tf_op jit(solution)/shard_map/ppermute | solution.py:18
  3.1 3.9 %collective-permute-start.1 = (bf16[4,1792]{1,0:T(4,128)(2,1)}, bf16[4,1792]{1,0:T(4,128)(2,1)S(1)}, u32[]{:S(2)}, u32[]{:S(2)}) collective-permute-start(bf16[4,1792]{1,0:T(4,128)(2,1)} %x.1), channel_id=1, source_target_pairs={{0,2},{1,3},{2,0},{3,1},{4,6},{5,7},{6,4},{7,5},{8,10},{9,11},{10,... | collective-permute-start | bytes 43016 | tf_op jit(solution)/shard_map/ppermute | solution.py:18
  3.1 1.5 %copy-start.2 = (bf16[4,1792]{1,0:T(4,128)(2,1)S(1)}, bf16[4,1792]{1,0:T(4,128)(2,1)}, u32[]{:S(2)}) copy-start(bf16[4,1792]{1,0:T(4,128)(2,1)} %x.1) | copy-start | bytes 43012
  7.0 12.7 %slice-start = ((s8[14680064]{0:T(1024)(128)(4,1)}), s8[4194304]{0:T(1024)(128)(4,1)S(1)}, s32[]{:S(2)}) async-start(s8[14680064]{0:T(1024)(128)(4,1)} %bitcast.1), calls=%async_computation | async-start | bytes 8388608
  7.0 12.6 %slice-start.1 = ((s8[14680064]{0:T(1024)(128)(4,1)}), s8[4194304]{0:T(1024)(128)(4,1)S(1)}, s32[]{:S(2)}) async-start(s8[14680064]{0:T(1024)(128)(4,1)} %bitcast.1), calls=%async_computation.1 | async-start | bytes 8388608
  7.0 12.6 %copy-start.1 = (f32[8192]{0:T(1024)S(1)}, f32[8192]{0:T(1024)}, u32[]{:S(2)}) copy-start(f32[8192]{0:T(1024)} %param.8) | copy-start | bytes 98308
  7.0 5.7 %collective-permute-start.5 = (bf16[16,896]{1,0:T(8,128)(2,1)S(1)}, bf16[16,896]{1,0:T(8,128)(2,1)S(1)}, u32[]{:S(2)}, u32[]{:S(2)}) collective-permute-start(bf16[16,896]{1,0:T(8,128)(2,1)S(1)} %shard_map.65.refs_0_.rows), channel_id=1, source_target_pairs={{0,12},{2,14},{4,8},{6,10},{8,4},{10,6},{12,0},{14,2},{1,13},{3,15... | collective-permute-start | bytes 86024 | tf_op jit(solution)/shard_map/ppermute | solution.py:18
  10.7 4.8 %collective-permute-start.4 = (bf16[16,896]{1,0:T(8,128)(2,1)S(1)}, bf16[16,896]{1,0:T(8,128)(2,1)S(1)}, u32[]{:S(2)}, u32[]{:S(2)}) collective-permute-start(bf16[16,896]{1,0:T(8,128)(2,1)S(1)} %shard_map.65.refs_0_.rows), channel_id=1, source_target_pairs={{0,8},{2,10},{4,12},{6,14},{8,0},{10,2},{12,4},{14,6},{1,9},{3,11}... | collective-permute-start | bytes 86024 | tf_op jit(solution)/shard_map/ppermute | solution.py:18
  10.7 4.8 %collective-permute-start.3 = (bf16[16,896]{1,0:T(8,128)(2,1)S(1)}, bf16[16,896]{1,0:T(8,128)(2,1)S(1)}, u32[]{:S(2)}, u32[]{:S(2)}) collective-permute-start(bf16[16,896]{1,0:T(8,128)(2,1)S(1)} %shard_map.65.refs_0_.rows), channel_id=1, source_target_pairs={{0,4},{2,6},{4,0},{6,2},{8,12},{10,14},{12,8},{14,10},{1,5},{3,7},... | collective-permute-start | bytes 86024 | tf_op jit(solution)/shard_map/ppermute | solution.py:18
  16.9 2.8 %slice-start.2 = ((s8[14680064]{0:T(1024)(128)(4,1)}), s8[4194304]{0:T(1024)(128)(4,1)S(1)}, s32[]{:S(2)}) async-start(s8[14680064]{0:T(1024)(128)(4,1)} %bitcast.1), calls=%async_computation.2 | async-start | bytes 8388608
  16.9 2.9 %slice-start.3 = ((s8[14680064]{0:T(1024)(128)(4,1)}), s8[2097152]{0:T(1024)(128)(4,1)S(1)}, s32[]{:S(2)}) async-start(s8[14680064]{0:T(1024)(128)(4,1)} %bitcast.1), calls=%async_computation.3 | async-start | bytes 4194304
  16.9 2.7 %collective-permute-start.6 = (f32[64,4096]{1,0:T(8,128)S(1)}, f32[64,4096]{1,0:T(8,128)S(1)}, u32[]{:S(2)}, u32[]{:S(2)}) collective-permute-start(f32[64,4096]{1,0:T(8,128)S(1)} %shard_map.66.mine), channel_id=1, source_target_pairs={{0,1},{1,0},{2,3},{3,2},{4,5},{5,4},{6,7},{7,6},{8,9},{9,8},{10,11... | collective-permute-start | bytes 3145736 | tf_op jit(solution)/shard_map/ppermute | solution.py:18
  18.4 2.8 %collective-permute-start.7 = (f32[64,4096]{1,0:T(8,128)S(1)}, f32[64,4096]{1,0:T(8,128)S(1)}, u32[]{:S(2)}, u32[]{:S(2)}) collective-permute-start(f32[64,4096]{1,0:T(8,128)S(1)} %shard_map.68.mine), channel_id=1, source_target_pairs={{0,1},{1,0},{2,3},{3,2},{4,5},{5,4},{6,7},{7,6},{8,9},{9,8},{10,11... | collective-permute-start | bytes 3145736 | tf_op jit(solution)/shard_map/ppermute | solution.py:18
  21.3 20.6 %slice-start.4 = ((s8[14680064]{0:T(1024)(128)(4,1)}), s8[4194304]{0:T(1024)(128)(4,1)S(1)}, s32[]{:S(2)}) async-start(s8[14680064]{0:T(1024)(128)(4,1)} %bitcast.3), calls=%async_computation.4 | async-start | bytes 8388608
  21.3 20.6 %slice-start.5 = ((s8[14680064]{0:T(1024)(128)(4,1)}), s8[4194304]{0:T(1024)(128)(4,1)S(1)}, s32[]{:S(2)}) async-start(s8[14680064]{0:T(1024)(128)(4,1)} %bitcast.3), calls=%async_computation.5 | async-start | bytes 8388608
  21.3 20.6 %slice-start.8 = ((s8[14680064]{0:T(1024)(128)(4,1)}), s8[4194304]{0:T(1024)(128)(4,1)S(1)}, s32[]{:S(2)}) async-start(s8[14680064]{0:T(1024)(128)(4,1)} %bitcast.5), calls=%async_computation.8 | async-start | bytes 8388608
  21.3 20.6 %slice-start.9 = ((s8[14680064]{0:T(1024)(128)(4,1)}), s8[4194304]{0:T(1024)(128)(4,1)S(1)}, s32[]{:S(2)}) async-start(s8[14680064]{0:T(1024)(128)(4,1)} %bitcast.5), calls=%async_computation.9 | async-start | bytes 8388608
  22.6 4.5 %collective-permute-start.8 = (bf16[16,896]{1,0:T(8,128)(2,1)S(1)}, bf16[16,896]{1,0:T(8,128)(2,1)S(1)}, u32[]{:S(2)}, u32[]{:S(2)}) collective-permute-start(bf16[16,896]{1,0:T(8,128)(2,1)S(1)} %get-tuple-element.16), channel_id=1, source_target_pairs={{0,4},{2,6},{4,0},{6,2},{8,12},{10,14},{12,8},{14,10},{1,5},{3,7},... | collective-permute-start | bytes 86024 | tf_op jit(solution)/shard_map/ppermute | solution.py:18
  22.7 4.9 %collective-permute-start.9 = (bf16[16,896]{1,0:T(8,128)(2,1)S(1)}, bf16[16,896]{1,0:T(8,128)(2,1)S(1)}, u32[]{:S(2)}, u32[]{:S(2)}) collective-permute-start(bf16[16,896]{1,0:T(8,128)(2,1)S(1)} %get-tuple-element.17), channel_id=1, source_target_pairs={{0,8},{2,10},{4,12},{6,14},{8,0},{10,2},{12,4},{14,6},{1,9},{3,11}... | collective-permute-start | bytes 86024 | tf_op jit(solution)/shard_map/ppermute | solution.py:18
  24.8 5.7 %collective-permute-start.10 = (bf16[16,896]{1,0:T(8,128)(2,1)S(1)}, bf16[16,896]{1,0:T(8,128)(2,1)S(1)}, u32[]{:S(2)}, u32[]{:S(2)}) collective-permute-start(bf16[16,896]{1,0:T(8,128)(2,1)S(1)} %get-tuple-element.18), channel_id=1, source_target_pairs={{0,12},{2,14},{4,8},{6,10},{8,4},{10,6},{12,0},{14,2},{1,13},{3,15... | collective-permute-start | bytes 86024 | tf_op jit(solution)/shard_map/ppermute | solution.py:18
  30.5 11.5 %slice-start.6 = ((s8[14680064]{0:T(1024)(128)(4,1)}), s8[4194304]{0:T(1024)(128)(4,1)S(1)}, s32[]{:S(2)}) async-start(s8[14680064]{0:T(1024)(128)(4,1)} %bitcast.3), calls=%async_computation.6 | async-start | bytes 8388608
  30.5 11.5 %slice-start.10 = ((s8[14680064]{0:T(1024)(128)(4,1)}), s8[4194304]{0:T(1024)(128)(4,1)S(1)}, s32[]{:S(2)}) async-start(s8[14680064]{0:T(1024)(128)(4,1)} %bitcast.5), calls=%async_computation.10 | async-start | bytes 8388608
  30.5 11.5 %slice-start.7 = ((s8[14680064]{0:T(1024)(128)(4,1)}), s8[2097152]{0:T(1024)(128)(4,1)S(1)}, s32[]{:S(2)}) async-start(s8[14680064]{0:T(1024)(128)(4,1)} %bitcast.3), calls=%async_computation.7 | async-start | bytes 4194304
  30.5 11.5 %slice-start.11 = ((s8[14680064]{0:T(1024)(128)(4,1)}), s8[2097152]{0:T(1024)(128)(4,1)S(1)}, s32[]{:S(2)}) async-start(s8[14680064]{0:T(1024)(128)(4,1)} %bitcast.5), calls=%async_computation.11 | async-start | bytes 4194304
  30.5 4.2 %collective-permute-start.11 = (f32[16,896]{1,0:T(8,128)S(1)}, f32[16,896]{1,0:T(8,128)S(1)}, u32[]{:S(2)}, u32[]{:S(2)}) collective-permute-start(f32[16,896]{1,0:T(8,128)S(1)} %shard_map.71.total), channel_id=1, source_target_pairs={{0,2},{2,0},{4,6},{6,4},{8,10},{10,8},{12,14},{14,12},{1,3},{3,1},... | collective-permute-start | bytes 172040 | tf_op jit(solution)/shard_map/ppermute | solution.py:18
  34.8 6.1 %collective-permute-start.14 = (bf16[16,896]{1,0:T(8,128)(2,1)S(1)}, bf16[16,896]{1,0:T(8,128)(2,1)S(1)}, u32[]{:S(2)}, u32[]{:S(2)}) collective-permute-start(bf16[16,896]{1,0:T(8,128)(2,1)S(1)} %shard_map.72.refs_0_), channel_id=1, source_target_pairs={{0,12},{2,14},{4,8},{6,10},{8,4},{10,6},{12,0},{14,2},{1,13},{3,15... | collective-permute-start | bytes 86024 | tf_op jit(solution)/shard_map/ppermute | solution.py:18
  37.1 4.8 %collective-permute-start.13 = (bf16[16,896]{1,0:T(8,128)(2,1)S(1)}, bf16[16,896]{1,0:T(8,128)(2,1)S(1)}, u32[]{:S(2)}, u32[]{:S(2)}) collective-permute-start(bf16[16,896]{1,0:T(8,128)(2,1)S(1)} %shard_map.72.refs_0_), channel_id=1, source_target_pairs={{0,8},{2,10},{4,12},{6,14},{8,0},{10,2},{12,4},{14,6},{1,9},{3,11}... | collective-permute-start | bytes 86024 | tf_op jit(solution)/shard_map/ppermute | solution.py:18
  37.1 4.8 %collective-permute-start.12 = (bf16[16,896]{1,0:T(8,128)(2,1)S(1)}, bf16[16,896]{1,0:T(8,128)(2,1)S(1)}, u32[]{:S(2)}, u32[]{:S(2)}) collective-permute-start(bf16[16,896]{1,0:T(8,128)(2,1)S(1)} %shard_map.72.refs_0_), channel_id=1, source_target_pairs={{0,4},{2,6},{4,0},{6,2},{8,12},{10,14},{12,8},{14,10},{1,5},{3,7},... | collective-permute-start | bytes 86024 | tf_op jit(solution)/shard_map/ppermute | solution.py:18

commit v14 on v12

--- a/solution.py
+++ b/solution.py
@@ -252,7 +252,7 @@
 
 def adam(codes_t, blocks, m, v):
     lat, half = m.shape
-    rows = min(1024, lat)
+    rows = min(512, lat)
     return pl.pallas_call(
         adam_kernel,
         grid=(lat // rows,),

time: 52.6 us -> 54.9 us (1.044)
  Pallas kernels: 17.5 us -> 19.9 us
    pallas_call x1, Pallas kernels: 10.4 us -> 12.7 us  [adam(): pl.pallas_call(adam_kernel, grid=(lat // rows,), out_shape=jax.ShapeDtype...]
where the time goes in v14:
time: 54.9 us; the launch traced here: 54.7 us
  Pallas kernels  19.9 us (36%)
  starting transfers between devices  17.7 us (32%)
  waiting for transfers between devices  15.3 us (28%)
  local copies, waits for them, and re-layouts  1.63 us (3%)
    ppermute x15, starting transfers between devices, swap(): return lax.ppermute(value, axis, [(i, i ^ mask) for i in range(n)])  17.7 us
    ppermute x15, waiting for transfers between devices, swap(): return lax.ppermute(value, axis, [(i, i ^ mask) for i in range(n)])  15.3 us
    pallas_call x1, Pallas kernels, adam(): pl.pallas_call(adam_kernel, grid=(lat // rows,), out_shape=jax.ShapeDtype...  12.7 us
    pallas_call x2, Pallas kernels, encode(): pl.pallas_call(functools.partial(encode_kernel, first), out_shape=jax.Sha...  2.84 us
    pallas_call x2, Pallas kernels, decode(): pl.pallas_call(functools.partial(decode_kernel, first, len(given)), out_s...  2.58 us
    pallas_call x1, Pallas kernels, turn(): pl.pallas_call(functools.partial(turn_kernel, min(512, lat)), out_shape=j...  1.68 us
    unnamed x30, local copies, waits for them, and re-layouts  1.63 us
  transfers between devices with their start and end apart: 15, of which 10 were waited for; matrix products, arithmetic and copies ran while one was open for 0% of the time, Pallas kernels for 8%

profile of v14, /device:TPU:0, one launch (start us, length us, event | category | flops | bytes accessed | tf_op | source)
XLA Modules:
  0.0 54.7 jit_solution(4546359341887197662)
XLA Ops:
  0.0 0.5 collective-permute-start
  0.5 2.6 %collective-permute-start.2 = (bf16[4,1792]{1,0:T(4,128)(2,1)}, bf16[4,1792]{1,0:T(4,128)(2,1)S(1)}, u32[]{:S(2)}, u32[]{:S(2)}) collective-permute-start(bf16[4,1792]{1,0:T(4,128)(2,1)} %x.1), channel_id=1, source_target_pairs={{0,3},{1,2},{2,1},{3,0},{4,7},{5,6},{6,5},{7,4},{8,11},{9,10},{10,... | collective-permute-start | bytes 43016 | tf_op jit(solution)/shard_map/ppermute | solution.py:18
  3.1 0.1 collective-permute-start.1
  3.1 1.5 %copy-done.2 = bf16[4,1792]{1,0:T(4,128)(2,1)S(1)} copy-done((bf16[4,1792]{1,0:T(4,128)(2,1)S(1)}, bf16[4,1792]{1,0:T(4,128)(2,1)}, u32[]{:S(2)}) %copy-start.2) | copy-done | bytes 14360
  4.6 0.1 collective-permute-done.2.refs_3_
  4.7 2.3 %collective-permute-done.1.refs_2_ = bf16[4,1792]{1,0:T(4,128)(2,1)S(1)} collective-permute-done((bf16[4,1792]{1,0:T(4,128)(2,1)}, bf16[4,1792]{1,0:T(4,128)(2,1)S(1)}, u32[]{:S(2)}, u32[]{:S(2)}) %collective-permute-start.1) | collective-permute-done | bytes 14368 | tf_op jit(solution)/shard_map/ppermute | solution.py:18
  7.0 3.7 %collective-permute-start.5 = (bf16[16,896]{1,0:T(8,128)(2,1)S(1)}, bf16[16,896]{1,0:T(8,128)(2,1)S(1)}, u32[]{:S(2)}, u32[]{:S(2)}) collective-permute-start(bf16[16,896]{1,0:T(8,128)(2,1)S(1)} %shard_map.65.refs_0_.rows), channel_id=1, source_target_pairs={{0,12},{2,14},{4,8},{6,10},{8,4},{10,6},{12,0},{14,2},{1,13},{3,15... | collective-permute-start | bytes 86024 | tf_op jit(solution)/shard_map/ppermute | solution.py:18
  10.7 0.8 %collective-permute-start.3 = (bf16[16,896]{1,0:T(8,128)(2,1)S(1)}, bf16[16,896]{1,0:T(8,128)(2,1)S(1)}, u32[]{:S(2)}, u32[]{:S(2)}) collective-permute-start(bf16[16,896]{1,0:T(8,128)(2,1)S(1)} %shard_map.65.refs_0_.rows), channel_id=1, source_target_pairs={{0,4},{2,6},{4,0},{6,2},{8,12},{10,14},{12,8},{14,10},{1,5},{3,7},... | collective-permute-start | bytes 86024 | tf_op jit(solution)/shard_map/ppermute | solution.py:18
  11.5 1.3 %collective-permute-done.5.refs_3_ = bf16[16,896]{1,0:T(8,128)(2,1)S(1)} collective-permute-done((bf16[16,896]{1,0:T(8,128)(2,1)S(1)}, bf16[16,896]{1,0:T(8,128)(2,1)S(1)}, u32[]{:S(2)}, u32[]{:S(2)}) %collective-permute-start.5) | collective-permute-done | bytes 28704 | tf_op jit(solution)/shard_map/ppermute | solution.py:18
  12.8 2.7 %collective-permute-done.4.refs_2_ = bf16[16,896]{1,0:T(8,128)(2,1)S(1)} collective-permute-done((bf16[16,896]{1,0:T(8,128)(2,1)S(1)}, bf16[16,896]{1,0:T(8,128)(2,1)S(1)}, u32[]{:S(2)}, u32[]{:S(2)}) %collective-permute-start.4) | collective-permute-done | bytes 28704 | tf_op jit(solution)/shard_map/ppermute | solution.py:18
  15.5 1.4 %shard_map.66.mine = f32[64,4096]{1,0:T(8,128)S(1)} custom-call(bf16[16,896]{1,0:T(8,128)(2,1)S(1)} %shard_map.65.refs_0_.rows, bf16[16,896]{1,0:T(8,128)(2,1)S(1)} %collective-permute-done.3.refs_1_, bf16[16,896]{1,0:T(8,128)(2,1)S(1)} %collective-permute-done.4.refs_2_, bf16[16,896]{1,0:T(8,128)(2,1)S(1)} %collective-permute-done.5.refs_3_, ...), custom_call_target="tpu_custom_call" | custom-call | flops 2449999872 | bytes 7340032 | tf_op jit(solution)/shard_map/pallas_call | solution.py:102
  16.9 0.1 collective-permute-start.6
  17.0 1.4 %shard_map.68.mine = f32[64,4096]{1,0:T(8,128)S(1)} custom-call(bf16[16,896]{1,0:T(8,128)(2,1)S(1)} %shard_map.65.refs_0_.rows, bf16[16,896]{1,0:T(8,128)(2,1)S(1)} %collective-permute-done.3.refs_1_, bf16[16,896]{1,0:T(8,128)(2,1)S(1)} %collective-permute-done.4.refs_2_, bf16[16,896]{1,0:T(8,128)(2,1)S(1)} %collective-permute-done.5.refs_3_, ...), custom_call_target="tpu_custom_call" | custom-call | flops 2449999872 | bytes 7340032 | tf_op jit(solution)/shard_map/pallas_call | solution.py:102
  18.4 0.6 %collective-permute-start.7 = (f32[64,4096]{1,0:T(8,128)S(1)}, f32[64,4096]{1,0:T(8,128)S(1)}, u32[]{:S(2)}, u32[]{:S(2)}) collective-permute-start(f32[64,4096]{1,0:T(8,128)S(1)} %shard_map.68.mine), channel_id=1, source_target_pairs={{0,1},{1,0},{2,3},{3,2},{4,5},{5,4},{6,7},{7,6},{8,9},{9,8},{10,11... | collective-permute-start | bytes 3145736 | tf_op jit(solution)/shard_map/ppermute | solution.py:18
  19.0 0.7 %collective-permute-done.6.theirs = f32[64,4096]{1,0:T(8,128)S(1)} collective-permute-done((f32[64,4096]{1,0:T(8,128)S(1)}, f32[64,4096]{1,0:T(8,128)S(1)}, u32[]{:S(2)}, u32[]{:S(2)}) %collective-permute-start.6) | collective-permute-done | bytes 1048608 | tf_op jit(solution)/shard_map/ppermute | solution.py:18
  19.7 0.1 slice-done.3
  19.8 1.3 %shard_map.67 = (bf16[64,4096]{1,0:T(8,128)(2,1)S(1)}, f32[64,896]{1,0:T(8,128)S(1)}) custom-call(f32[64,4096]{1,0:T(8,128)S(1)} %shard_map.66.mine, f32[64,4096]{1,0:T(8,128)S(1)} %collective-permute-done.6.theirs, f32[1,8192]{1,0:T(1,128)S(1)} %bitcast.7, bf16[8192,896]{1,0:T(8,128)(2,1)S(1)} %bitcast.2), custom_call_target="tpu_custom_call" | custom-call | flops 2449999872 | bytes 7340032 | tf_op jit(solution)/shard_map/pallas_call | solution.py:133
  21.1 0.2 collective-permute-done.7.theirs
  21.3 1.3 %shard_map.69 = (bf16[64,4096]{1,0:T(8,128)(2,1)S(1)}, f32[16,896]{1,0:T(8,128)S(1)}, bf16[16,896]{1,0:T(8,128)(2,1)S(1)}, bf16[16,896]{1,0:T(8,128)(2,1)S(1)}, bf16[16,896]{1,0:T(8,128)(2,1)S(1)}) custom-call(f32[64,4096]{1,0:T(8,128)S(1)} %shard_map.68.mine, f32[64,4096]{1,0:T(8,128)S(1)} %collective-permute-done.7.theirs, f32[1,8192]{1,0:T(1,128)S(1)} %bitcast.8, ...), custom_call_target="tpu_custom_call" | custom-call | flops 2449999872 | bytes 7340032 | tf_op jit(solution)/shard_map/pallas_call | solution.py:133
  22.6 0.1 collective-permute-start.8
  22.7 2.1 %collective-permute-start.9 = (bf16[16,896]{1,0:T(8,128)(2,1)S(1)}, bf16[16,896]{1,0:T(8,128)(2,1)S(1)}, u32[]{:S(2)}, u32[]{:S(2)}) collective-permute-start(bf16[16,896]{1,0:T(8,128)(2,1)S(1)} %get-tuple-element.17), channel_id=1, source_target_pairs={{0,8},{2,10},{4,12},{6,14},{8,0},{10,2},{12,4},{14,6},{1,9},{3,11}... | collective-permute-start | bytes 86024 | tf_op jit(solution)/shard_map/ppermute | solution.py:18
  24.8 2.3 %collective-permute-start.10 = (bf16[16,896]{1,0:T(8,128)(2,1)S(1)}, bf16[16,896]{1,0:T(8,128)(2,1)S(1)}, u32[]{:S(2)}, u32[]{:S(2)}) collective-permute-start(bf16[16,896]{1,0:T(8,128)(2,1)S(1)} %get-tuple-element.18), channel_id=1, source_target_pairs={{0,12},{2,14},{4,8},{6,10},{8,4},{10,6},{12,0},{14,2},{1,13},{3,15... | collective-permute-start | bytes 86024 | tf_op jit(solution)/shard_map/ppermute | solution.py:18
  27.1 0.5 collective-permute-done.9.refs_1_
  27.5 2.9 %collective-permute-done.10.refs_2_ = bf16[16,896]{1,0:T(8,128)(2,1)S(1)} collective-permute-done((bf16[16,896]{1,0:T(8,128)(2,1)S(1)}, bf16[16,896]{1,0:T(8,128)(2,1)S(1)}, u32[]{:S(2)}, u32[]{:S(2)}) %collective-permute-start.10) | collective-permute-done | bytes 28704 | tf_op jit(solution)/shard_map/ppermute | solution.py:18
  30.5 0.0 slice-start.11
  30.5 0.6 %collective-permute-start.11 = (f32[16,896]{1,0:T(8,128)S(1)}, f32[16,896]{1,0:T(8,128)S(1)}, u32[]{:S(2)}, u32[]{:S(2)}) collective-permute-start(f32[16,896]{1,0:T(8,128)S(1)} %shard_map.71.total), channel_id=1, source_target_pairs={{0,2},{2,0},{4,6},{6,4},{8,10},{10,8},{12,14},{14,12},{1,3},{3,1},... | collective-permute-start | bytes 172040 | tf_op jit(solution)/shard_map/ppermute | solution.py:18
  31.1 3.6 %collective-permute-done.11.refs_0_ = f32[16,896]{1,0:T(8,128)S(1)} collective-permute-done((f32[16,896]{1,0:T(8,128)S(1)}, f32[16,896]{1,0:T(8,128)S(1)}, u32[]{:S(2)}, u32[]{:S(2)}) %collective-permute-start.11) | collective-permute-done | bytes 57376 | tf_op jit(solution)/shard_map/ppermute | solution.py:18
  34.8 2.4 %collective-permute-start.14 = (bf16[16,896]{1,0:T(8,128)(2,1)S(1)}, bf16[16,896]{1,0:T(8,128)(2,1)S(1)}, u32[]{:S(2)}, u32[]{:S(2)}) collective-permute-start(bf16[16,896]{1,0:T(8,128)(2,1)S(1)} %shard_map.72.refs_0_), channel_id=1, source_target_pairs={{0,12},{2,14},{4,8},{6,10},{8,4},{10,6},{12,0},{14,2},{1,13},{3,15... | collective-permute-start | bytes 86024 | tf_op jit(solution)/shard_map/ppermute | solution.py:18
  37.1 2.1 %collective-permute-start.12 = (bf16[16,896]{1,0:T(8,128)(2,1)S(1)}, bf16[16,896]{1,0:T(8,128)(2,1)S(1)}, u32[]{:S(2)}, u32[]{:S(2)}) collective-permute-start(bf16[16,896]{1,0:T(8,128)(2,1)S(1)} %shard_map.72.refs_0_), channel_id=1, source_target_pairs={{0,4},{2,6},{4,0},{6,2},{8,12},{10,14},{12,8},{14,10},{1,5},{3,7},... | collective-permute-start | bytes 86024 | tf_op jit(solution)/shard_map/ppermute | solution.py:18
  39.2 1.7 %shard_map.70.codes_t = bf16[8192,64]{1,0:T(8,128)(2,1)S(1)} custom-call(bf16[64,4096]{1,0:T(8,128)(2,1)S(1)} %get-tuple-element.12.refs_0_, bf16[64,4096]{1,0:T(8,128)(2,1)S(1)} %get-tuple-element.14.refs_1_), custom_call_target="tpu_custom_call" | custom-call | flops 1400000000 | bytes 4194304 | tf_op jit(solution)/shard_map/pallas_call | solution.py:158
  40.9 1.0 %collective-permute-done.13.refs_2_ = bf16[16,896]{1,0:T(8,128)(2,1)S(1)} collective-permute-done((bf16[16,896]{1,0:T(8,128)(2,1)S(1)}, bf16[16,896]{1,0:T(8,128)(2,1)S(1)}, u32[]{:S(2)}, u32[]{:S(2)}) %collective-permute-start.13) | collective-permute-done | bytes 28704 | tf_op jit(solution)/shard_map/ppermute | solution.py:18
  42.0 12.7 %shard_map.73 = bf16[8192,896]{1,0:T(8,128)(2,1)} custom-call(bf16[8192,64]{1,0:T(8,128)(2,1)S(1)} %shard_map.70.codes_t, bf16[8192,896]{1,0:T(8,128)(2,1)S(1)} %bitcast.4, bf16[8192,896]{1,0:T(8,128)(2,1)S(1)} %bitcast.6, bf16[16,896]{1,0:T(8,128)(2,1)S(1)} %shard_map.72.refs_0_, bf16[16,896]{1,0:T(8,128)(2,1)S(1)} %collective-permute-done.12.refs_1_, ...), custom_call_target="tpu_custom_call" | custom-call | tf_op jit(solution)/shard_map/pallas_call | solution.py:256
  (41 shorter events, 0.1 us)
Async XLA Ops:
  0.0 15.5 %copy-start = (bf16[896,8192]{1,0:T(8,128)(2,1)S(1)}, bf16[896,8192]{1,0:T(8,128)(2,1)}, u32[]{:S(2)}) copy-start(bf16[896,8192]{1,0:T(8,128)(2,1)} %refs_4_.3) | copy-start | bytes 44040196
  0.0 4.6 %collective-permute-start = (bf16[4,1792]{1,0:T(4,128)(2,1)}, bf16[4,1792]{1,0:T(4,128)(2,1)S(1)}, u32[]{:S(2)}, u32[]{:S(2)}) collective-permute-start(bf16[4,1792]{1,0:T(4,128)(2,1)} %x.1), channel_id=1, source_target_pairs={{0,1},{1,0},{2,3},{3,2},{4,5},{5,4},{6,7},{7,6},{8,9},{9,8},{10,11... | collective-permute-start | bytes 43016 | tf_op jit(solution)/shard_map/ppermute | solution.py:18
  0.5 4.2 %collective-permute-start.2 = (bf16[4,1792]{1,0:T(4,128)(2,1)}, bf16[4,1792]{1,0:T(4,128)(2,1)S(1)}, u32[]{:S(2)}, u32[]{:S(2)}) collective-permute-start(bf16[4,1792]{1,0:T(4,128)(2,1)} %x.1), channel_id=1, source_target_pairs={{0,3},{1,2},{2,1},{3,0},{4,7},{5,6},{6,5},{7,4},{8,11},{9,10},{10,... | collective-permute-start | bytes 43016 | tf_op jit(solution)/shard_map/ppermute | solution.py:18
  3.1 3.9 %collective-permute-start.1 = (bf16[4,1792]{1,0:T(4,128)(2,1)}, bf16[4,1792]{1,0:T(4,128)(2,1)S(1)}, u32[]{:S(2)}, u32[]{:S(2)}) collective-permute-start(bf16[4,1792]{1,0:T(4,128)(2,1)} %x.1), channel_id=1, source_target_pairs={{0,2},{1,3},{2,0},{3,1},{4,6},{5,7},{6,4},{7,5},{8,10},{9,11},{10,... | collective-permute-start | bytes 43016 | tf_op jit(solution)/shard_map/ppermute | solution.py:18
  3.1 1.5 %copy-start.2 = (bf16[4,1792]{1,0:T(4,128)(2,1)S(1)}, bf16[4,1792]{1,0:T(4,128)(2,1)}, u32[]{:S(2)}) copy-start(bf16[4,1792]{1,0:T(4,128)(2,1)} %x.1) | copy-start | bytes 43012
  7.0 12.7 %slice-start = ((s8[14680064]{0:T(1024)(128)(4,1)}), s8[4194304]{0:T(1024)(128)(4,1)S(1)}, s32[]{:S(2)}) async-start(s8[14680064]{0:T(1024)(128)(4,1)} %bitcast.1), calls=%async_computation | async-start | bytes 8388608
  7.0 12.6 %slice-start.1 = ((s8[14680064]{0:T(1024)(128)(4,1)}), s8[4194304]{0:T(1024)(128)(4,1)S(1)}, s32[]{:S(2)}) async-start(s8[14680064]{0:T(1024)(128)(4,1)} %bitcast.1), calls=%async_computation.1 | async-start | bytes 8388608
  7.0 12.6 %copy-start.1 = (f32[8192]{0:T(1024)S(1)}, f32[8192]{0:T(1024)}, u32[]{:S(2)}) copy-start(f32[8192]{0:T(1024)} %param.8) | copy-start | bytes 98308
  7.0 5.7 %collective-permute-start.5 = (bf16[16,896]{1,0:T(8,128)(2,1)S(1)}, bf16[16,896]{1,0:T(8,128)(2,1)S(1)}, u32[]{:S(2)}, u32[]{:S(2)}) collective-permute-start(bf16[16,896]{1,0:T(8,128)(2,1)S(1)} %shard_map.65.refs_0_.rows), channel_id=1, source_target_pairs={{0,12},{2,14},{4,8},{6,10},{8,4},{10,6},{12,0},{14,2},{1,13},{3,15... | collective-permute-start | bytes 86024 | tf_op jit(solution)/shard_map/ppermute | solution.py:18
  10.7 4.8 %collective-permute-start.4 = (bf16[16,896]{1,0:T(8,128)(2,1)S(1)}, bf16[16,896]{1,0:T(8,128)(2,1)S(1)}, u32[]{:S(2)}, u32[]{:S(2)}) collective-permute-start(bf16[16,896]{1,0:T(8,128)(2,1)S(1)} %shard_map.65.refs_0_.rows), channel_id=1, source_target_pairs={{0,8},{2,10},{4,12},{6,14},{8,0},{10,2},{12,4},{14,6},{1,9},{3,11}... | collective-permute-start | bytes 86024 | tf_op jit(solution)/shard_map/ppermute | solution.py:18
  10.7 4.8 %collective-permute-start.3 = (bf16[16,896]{1,0:T(8,128)(2,1)S(1)}, bf16[16,896]{1,0:T(8,128)(2,1)S(1)}, u32[]{:S(2)}, u32[]{:S(2)}) collective-permute-start(bf16[16,896]{1,0:T(8,128)(2,1)S(1)} %shard_map.65.refs_0_.rows), channel_id=1, source_target_pairs={{0,4},{2,6},{4,0},{6,2},{8,12},{10,14},{12,8},{14,10},{1,5},{3,7},... | collective-permute-start | bytes 86024 | tf_op jit(solution)/shard_map/ppermute | solution.py:18
  16.9 2.8 %slice-start.2 = ((s8[14680064]{0:T(1024)(128)(4,1)}), s8[4194304]{0:T(1024)(128)(4,1)S(1)}, s32[]{:S(2)}) async-start(s8[14680064]{0:T(1024)(128)(4,1)} %bitcast.1), calls=%async_computation.2 | async-start | bytes 8388608
  16.9 2.9 %slice-start.3 = ((s8[14680064]{0:T(1024)(128)(4,1)}), s8[2097152]{0:T(1024)(128)(4,1)S(1)}, s32[]{:S(2)}) async-start(s8[14680064]{0:T(1024)(128)(4,1)} %bitcast.1), calls=%async_computation.3 | async-start | bytes 4194304
  16.9 2.7 %collective-permute-start.6 = (f32[64,4096]{1,0:T(8,128)S(1)}, f32[64,4096]{1,0:T(8,128)S(1)}, u32[]{:S(2)}, u32[]{:S(2)}) collective-permute-start(f32[64,4096]{1,0:T(8,128)S(1)} %shard_map.66.mine), channel_id=1, source_target_pairs={{0,1},{1,0},{2,3},{3,2},{4,5},{5,4},{6,7},{7,6},{8,9},{9,8},{10,11... | collective-permute-start | bytes 3145736 | tf_op jit(solution)/shard_map/ppermute | solution.py:18
  18.4 2.8 %collective-permute-start.7 = (f32[64,4096]{1,0:T(8,128)S(1)}, f32[64,4096]{1,0:T(8,128)S(1)}, u32[]{:S(2)}, u32[]{:S(2)}) collective-permute-start(f32[64,4096]{1,0:T(8,128)S(1)} %shard_map.68.mine), channel_id=1, source_target_pairs={{0,1},{1,0},{2,3},{3,2},{4,5},{5,4},{6,7},{7,6},{8,9},{9,8},{10,11... | collective-permute-start | bytes 3145736 | tf_op jit(solution)/shard_map/ppermute | solution.py:18
  21.3 20.6 %slice-start.4 = ((s8[14680064]{0:T(1024)(128)(4,1)}), s8[4194304]{0:T(1024)(128)(4,1)S(1)}, s32[]{:S(2)}) async-start(s8[14680064]{0:T(1024)(128)(4,1)} %bitcast.3), calls=%async_computation.4 | async-start | bytes 8388608
  21.3 20.6 %slice-start.5 = ((s8[14680064]{0:T(1024)(128)(4,1)}), s8[4194304]{0:T(1024)(128)(4,1)S(1)}, s32[]{:S(2)}) async-start(s8[14680064]{0:T(1024)(128)(4,1)} %bitcast.3), calls=%async_computation.5 | async-start | bytes 8388608
  21.3 20.6 %slice-start.8 = ((s8[14680064]{0:T(1024)(128)(4,1)}), s8[4194304]{0:T(1024)(128)(4,1)S(1)}, s32[]{:S(2)}) async-start(s8[14680064]{0:T(1024)(128)(4,1)} %bitcast.5), calls=%async_computation.8 | async-start | bytes 8388608
  21.3 20.6 %slice-start.9 = ((s8[14680064]{0:T(1024)(128)(4,1)}), s8[4194304]{0:T(1024)(128)(4,1)S(1)}, s32[]{:S(2)}) async-start(s8[14680064]{0:T(1024)(128)(4,1)} %bitcast.5), calls=%async_computation.9 | async-start | bytes 8388608
  22.6 4.5 %collective-permute-start.8 = (bf16[16,896]{1,0:T(8,128)(2,1)S(1)}, bf16[16,896]{1,0:T(8,128)(2,1)S(1)}, u32[]{:S(2)}, u32[]{:S(2)}) collective-permute-start(bf16[16,896]{1,0:T(8,128)(2,1)S(1)} %get-tuple-element.16), channel_id=1, source_target_pairs={{0,4},{2,6},{4,0},{6,2},{8,12},{10,14},{12,8},{14,10},{1,5},{3,7},... | collective-permute-start | bytes 86024 | tf_op jit(solution)/shard_map/ppermute | solution.py:18
  22.7 4.9 %collective-permute-start.9 = (bf16[16,896]{1,0:T(8,128)(2,1)S(1)}, bf16[16,896]{1,0:T(8,128)(2,1)S(1)}, u32[]{:S(2)}, u32[]{:S(2)}) collective-permute-start(bf16[16,896]{1,0:T(8,128)(2,1)S(1)} %get-tuple-element.17), channel_id=1, source_target_pairs={{0,8},{2,10},{4,12},{6,14},{8,0},{10,2},{12,4},{14,6},{1,9},{3,11}... | collective-permute-start | bytes 86024 | tf_op jit(solution)/shard_map/ppermute | solution.py:18
  24.8 5.7 %collective-permute-start.10 = (bf16[16,896]{1,0:T(8,128)(2,1)S(1)}, bf16[16,896]{1,0:T(8,128)(2,1)S(1)}, u32[]{:S(2)}, u32[]{:S(2)}) collective-permute-start(bf16[16,896]{1,0:T(8,128)(2,1)S(1)} %get-tuple-element.18), channel_id=1, source_target_pairs={{0,12},{2,14},{4,8},{6,10},{8,4},{10,6},{12,0},{14,2},{1,13},{3,15... | collective-permute-start | bytes 86024 | tf_op jit(solution)/shard_map/ppermute | solution.py:18
  30.5 11.5 %slice-start.6 = ((s8[14680064]{0:T(1024)(128)(4,1)}), s8[4194304]{0:T(1024)(128)(4,1)S(1)}, s32[]{:S(2)}) async-start(s8[14680064]{0:T(1024)(128)(4,1)} %bitcast.3), calls=%async_computation.6 | async-start | bytes 8388608
  30.5 11.5 %slice-start.10 = ((s8[14680064]{0:T(1024)(128)(4,1)}), s8[4194304]{0:T(1024)(128)(4,1)S(1)}, s32[]{:S(2)}) async-start(s8[14680064]{0:T(1024)(128)(4,1)} %bitcast.5), calls=%async_computation.10 | async-start | bytes 8388608
  30.5 11.5 %slice-start.7 = ((s8[14680064]{0:T(1024)(128)(4,1)}), s8[2097152]{0:T(1024)(128)(4,1)S(1)}, s32[]{:S(2)}) async-start(s8[14680064]{0:T(1024)(128)(4,1)} %bitcast.3), calls=%async_computation.7 | async-start | bytes 4194304
  30.5 11.5 %slice-start.11 = ((s8[14680064]{0:T(1024)(128)(4,1)}), s8[2097152]{0:T(1024)(128)(4,1)S(1)}, s32[]{:S(2)}) async-start(s8[14680064]{0:T(1024)(128)(4,1)} %bitcast.5), calls=%async_computation.11 | async-start | bytes 4194304
  30.5 4.2 %collective-permute-start.11 = (f32[16,896]{1,0:T(8,128)S(1)}, f32[16,896]{1,0:T(8,128)S(1)}, u32[]{:S(2)}, u32[]{:S(2)}) collective-permute-start(f32[16,896]{1,0:T(8,128)S(1)} %shard_map.71.total), channel_id=1, source_target_pairs={{0,2},{2,0},{4,6},{6,4},{8,10},{10,8},{12,14},{14,12},{1,3},{3,1},... | collective-permute-start | bytes 172040 | tf_op jit(solution)/shard_map/ppermute | solution.py:18
  34.8 6.1 %collective-permute-start.14 = (bf16[16,896]{1,0:T(8,128)(2,1)S(1)}, bf16[16,896]{1,0:T(8,128)(2,1)S(1)}, u32[]{:S(2)}, u32[]{:S(2)}) collective-permute-start(bf16[16,896]{1,0:T(8,128)(2,1)S(1)} %shard_map.72.refs_0_), channel_id=1, source_target_pairs={{0,12},{2,14},{4,8},{6,10},{8,4},{10,6},{12,0},{14,2},{1,13},{3,15... | collective-permute-start | bytes 86024 | tf_op jit(solution)/shard_map/ppermute | solution.py:18
  37.1 4.8 %collective-permute-start.13 = (bf16[16,896]{1,0:T(8,128)(2,1)S(1)}, bf16[16,896]{1,0:T(8,128)(2,1)S(1)}, u32[]{:S(2)}, u32[]{:S(2)}) collective-permute-start(bf16[16,896]{1,0:T(8,128)(2,1)S(1)} %shard_map.72.refs_0_), channel_id=1, source_target_pairs={{0,8},{2,10},{4,12},{6,14},{8,0},{10,2},{12,4},{14,6},{1,9},{3,11}... | collective-permute-start | bytes 86024 | tf_op jit(solution)/shard_map/ppermute | solution.py:18
  37.1 4.8 %collective-permute-start.12 = (bf16[16,896]{1,0:T(8,128)(2,1)S(1)}, bf16[16,896]{1,0:T(8,128)(2,1)S(1)}, u32[]{:S(2)}, u32[]{:S(2)}) collective-permute-start(bf16[16,896]{1,0:T(8,128)(2,1)S(1)} %shard_map.72.refs_0_), channel_id=1, source_target_pairs={{0,4},{2,6},{4,0},{6,2},{8,12},{10,14},{12,8},{14,10},{1,5},{3,7},... | collective-permute-start | bytes 86024 | tf_op jit(solution)/shard_map/ppermute | solution.py:18
